TPU v7x, 256 devices: a whole 4x4x8 slice. The times are simulated.
256 devices in a mesh: tile: 16 (over y, x), cand: 1, group: 16 (over z, core).
Axes of the slice: x: 4, y: 4, z: 8, core: 2. Of those that a mesh axis runs over, the one named last changes fastest.
Arguments:
- latent: bfloat16 [64, 48, 48, 384], P(('cand', 'group'), 'tile'), may hold values from -6 to 6
- gain_first: float32 [384], replicated, may hold values from 0.25 to 1.75
- weight_first: bfloat16 [3, 3, 1152, 384], P(None, None, 'group'), may hold values from -0.0625 to 0.0625
- bias_first: float32 [384], replicated, may hold values from -0.6 to 0.6
- gain_second: float32 [384], replicated, may hold values from 0.25 to 1.75
- weight_second: bfloat16 [3, 3, 1152, 384], P(None, None, 'group'), may hold values from -0.0625 to 0.0625
- bias_second: float32 [384], replicated, may hold values from -0.6 to 0.6
Outputs:
- decoded: bfloat16 [64, 48, 48, 384], P(('cand', 'group'), 'tile')
All inputs are finite; a program needn't handle non-finite values.
Results may differ from a plain program's by a relative error of at most 0.0042.
Values may be sent and summed in bfloat16 or wider, within the bound.
No kernel may reach another device: no remote copies, remote signals or barrier semaphores. Data moves between devices by JAX's collectives and lax.ppermute only.
A program may use at most 128 MiB of HBM per device.

v0:
```python
import jax
import jax.numpy as jnp
from jax import lax
from jax.sharding import PartitionSpec as P


def shifted(value, axis, steps):
    count = lax.axis_size(axis)
    first, last = (max(0, -steps), min(count, count - steps))
    return lax.ppermute(value, axis, [(source, source + steps) for source in range(first, last)])


def with_halo(array, sides, width):
    for axis, dim in sides:
        size, length = (lax.axis_size(axis), array.shape[dim])
        up = [(i, (i + 1) % size) for i in range(size - 1)]
        down = [(j, i) for i, j in up]
        last = lax.slice_in_dim(array, length - width, length, axis=dim)
        first = lax.slice_in_dim(array, 0, width, axis=dim)
        before = lax.ppermute(last, axis, up)
        after = lax.ppermute(first, axis, down)
        array = jnp.concatenate([before, array, after], axis=dim)
    return array


def activate(values, gain):
    wide = values.astype(jnp.float32)
    scaled = wide * lax.rsqrt(jnp.mean(wide * wide, axis=-1, keepdims=True) + 1e-06) * gain
    return jax.nn.silu(scaled)


def widen(grown):
    across = grown.shape[2]
    padded = jnp.pad(grown, ((0, 0), (0, 0), (1, 1), (0, 0)))
    return jnp.concatenate([padded[:, :, k : k + across] for k in range(3)], axis=-1)


def taps(joined, piece):
    count = joined.shape[0] - 2
    tall = joined.shape[1] - 2
    across = joined.shape[2]
    inner = piece.shape[2]
    total = jnp.zeros((count * tall * across, piece.shape[3]), jnp.float32)
    for step_t in range(3):
        for step_r in range(3):
            window = joined[step_t : step_t + count, step_r : step_r + tall].reshape(-1, inner)
            total = total + jnp.dot(
                window, piece[step_t, step_r], preferred_element_type=jnp.float32
            )
    return total.reshape(count, tall, across, piece.shape[3])


def local(latent, gain_first, weight_first, bias_first, gain_second, weight_second, bias_second):
    frames, rows, width, chans = latent.shape
    depth = 1
    first = activate(latent, gain_first).astype(jnp.bfloat16)
    earlier = shifted(first[frames - 2 :], "group", 1)
    stacked = jnp.concatenate([earlier, first], axis=0)
    grown = with_halo(stacked, (("tile", 1),), depth)
    joined_first = widen(grown)
    hidden = (
        taps(joined_first, lax.all_gather(weight_first, "group", axis=2, tiled=True)) + bias_first
    )
    second = activate(hidden, gain_second)
    second = second.astype(jnp.bfloat16)
    later = shifted(second[frames - 2 :], "group", 1)
    second = jnp.concatenate([later, second], axis=0)
    second = with_halo(second, (("tile", 1),), 1)
    joined_second = widen(second)
    branch = taps(joined_second, lax.all_gather(weight_second, "group", axis=2, tiled=True))
    result = latent.astype(jnp.float32) + branch + bias_second
    return result.astype(jnp.bfloat16)


def solution(mesh):
    return jax.shard_map(
        local,
        mesh=mesh,
        in_specs=(
            P(("cand", "group"), "tile", None, None),
            P(),
            P(None, None, "group", None),
            P(),
            P(),
            P(None, None, "group", None),
            P(),
        ),
        out_specs=P(("cand", "group"), "tile", None, None),
        check_vma=False,
    )
```

profile of v0, /device:TPU:1, one launch (start us, length us, event | category | flops | bytes accessed | tf_op | source)
XLA Modules:
  0.0 144.1 jit_solution(16453270550773001904)
XLA Ops:
  8.0 1.2 fusion.25
  9.6 4.9 %collective-permute-start = (bf16[2,3,48,384]{3,2,1,0:T(8,128)(2,1)S(1)}, bf16[2,3,48,384]{3,2,1,0:T(8,128)(2,1)S(1)}, u32[]{:S(2)}, u32[]{:S(2)}) collective-permute-start(bf16[2,3,48,384]{3,2,1,0:T(8,128)(2,1)S(1)} %slice.186), channel_id=1, source_target_pairs={{0,1},{1,2},{2,3},{3,4},{4,5},{5,6},{6,7},{7,8},{8,9},{9,10},{10,1... | collective-permute-start | bytes 663560 | tf_op jit(solution)/shard_map/ppermute | solution.py:10
  14.5 2.9 %collective-permute-done = bf16[2,3,48,384]{3,2,1,0:T(8,128)(2,1)S(1)} collective-permute-done((bf16[2,3,48,384]{3,2,1,0:T(8,128)(2,1)S(1)}, bf16[2,3,48,384]{3,2,1,0:T(8,128)(2,1)S(1)}, u32[]{:S(2)}, u32[]{:S(2)}) %collective-permute-start) | collective-permute-done | bytes 221216 | tf_op jit(solution)/shard_map/ppermute | solution.py:10
  17.5 3.1 %collective-permute-start.1 = (bf16[6,1,48,384]{3,2,1,0:T(8,128)(2,1)S(1)}, bf16[6,1,48,384]{3,2,1,0:T(8,128)(2,1)S(1)}, u32[]{:S(2)}, u32[]{:S(2)}) collective-permute-start(bf16[6,1,48,384]{3,2,1,0:T(8,128)(2,1)S(1)} %get-tuple-element.29), channel_id=1, source_target_pairs={{0,16},{16,32},{32,48},{48,64},{64,80},{80,96},{96,112},{112,128},... | collective-permute-start | bytes 663560 | tf_op jit(solution)/shard_map/ppermute | solution.py:20
  20.6 1.3 collective-permute-start.2
  21.9 1.5 %collective-permute-done.1 = bf16[6,1,48,384]{3,2,1,0:T(8,128)(2,1)S(1)} collective-permute-done((bf16[6,1,48,384]{3,2,1,0:T(8,128)(2,1)S(1)}, bf16[6,1,48,384]{3,2,1,0:T(8,128)(2,1)S(1)}, u32[]{:S(2)}, u32[]{:S(2)}) %collective-permute-start.1) | collective-permute-done | bytes 221216 | tf_op jit(solution)/shard_map/ppermute | solution.py:20
  23.4 4.2 %collective-permute-done.2 = bf16[6,1,48,384]{3,2,1,0:T(8,128)(2,1)S(1)} collective-permute-done((bf16[6,1,48,384]{3,2,1,0:T(8,128)(2,1)S(1)}, bf16[6,1,48,384]{3,2,1,0:T(8,128)(2,1)S(1)}, u32[]{:S(2)}, u32[]{:S(2)}) %collective-permute-start.2) | collective-permute-done | bytes 221216 | tf_op jit(solution)/shard_map/ppermute | solution.py:21
  29.3 3.7 %fusion.52 = (bf16[4,3,48,1152]{3,2,1,0:T(8,128)(2,1)S(1)}, bf16[4,3,48,1152]{3,2,1,0:T(8,128)(2,1)}, bf16[4,3,48,1152]{3,2,1,0:T(8,128)(2,1)}, bf16[4,3,48,1152...) fusion(bf16[6,5,48,1152]{3,2,1,0:T(8,128)(2,1)S(1)} %pad_maximu, ...), kind=kLoop, calls=%fused_computation.89 | loop fusion | bytes 23887872 | tf_op jit(solution)/shard_map/slice | solution.py:46
  33.0 34.3 %all-gather.3.cloned.1.call-done = bf16[3,3,1152,384]{3,2,1,0:T(8,128)(2,1)} async-done(((bf16[3,3,72,384]{3,2,1,0:T(8,128)(2,1)}), bf16[3,3,1152,384]{3,2,1,0:T(8,128)(2,1)}) %all-gather.3.cloned.1.call-update) | async-done | bytes 7962640 | tf_op jit(solution)/shard_map/all_gather | solution.py:62
  67.3 2.6 %fusion.43 = f32[576,384]{1,0:T(8,128)S(1)} fusion(bf16[576,1152]{1,0:T(8,128)(2,1)} %bitcast.112, bf16[3,3,1152,384]{3,2,1,0:T(8,128)(2,1)} %all-gather.3.cloned.1.call-done), kind=kOutput, calls=%fused_computation.64 | convolution fusion | flops 509607936 | bytes 3096576 | tf_op jit(solution)/shard_map/dot_general | solution.py:47
  69.9 2.8 %fusion.44 = f32[576,384]{1,0:T(8,128)S(1)} fusion(bf16[576,1152]{1,0:T(8,128)(2,1)S(1)} %bitcast.110, bf16[3,3,1152,384]{3,2,1,0:T(8,128)(2,1)} %all-gather.3.cloned.1.call-done), kind=kOutput, calls=%fused_computation.66 | convolution fusion | flops 509607936 | bytes 3096576 | tf_op jit(solution)/shard_map/dot_general | solution.py:47
  79.8 1.3 multiply_reduce_fusion
  81.6 1.9 %collective-permute-start.3 = (bf16[2,3,48,384]{3,2,1,0:T(8,128)(2,1)S(1)}, bf16[2,3,48,384]{3,2,1,0:T(8,128)(2,1)S(1)}, u32[]{:S(2)}, u32[]{:S(2)}) collective-permute-start(bf16[2,3,48,384]{3,2,1,0:T(8,128)(2,1)S(1)} %slice.207), channel_id=1, source_target_pairs={{0,1},{1,2},{2,3},{3,4},{4,5},{5,6},{6,7},{7,8},{8,9},{9,10},{10,1... | collective-permute-start | bytes 663560 | tf_op jit(solution)/shard_map/ppermute | solution.py:10
  83.5 6.4 %collective-permute-done.3 = bf16[2,3,48,384]{3,2,1,0:T(8,128)(2,1)S(1)} collective-permute-done((bf16[2,3,48,384]{3,2,1,0:T(8,128)(2,1)S(1)}, bf16[2,3,48,384]{3,2,1,0:T(8,128)(2,1)S(1)}, u32[]{:S(2)}, u32[]{:S(2)}) %collective-permute-start.3) | collective-permute-done | bytes 221216 | tf_op jit(solution)/shard_map/ppermute | solution.py:10
  90.0 3.1 %collective-permute-start.4 = (bf16[6,1,48,384]{3,2,1,0:T(8,128)(2,1)S(1)}, bf16[6,1,48,384]{3,2,1,0:T(8,128)(2,1)S(1)}, u32[]{:S(2)}, u32[]{:S(2)}) collective-permute-start(bf16[6,1,48,384]{3,2,1,0:T(8,128)(2,1)S(1)} %get-tuple-element.27), channel_id=1, source_target_pairs={{0,16},{16,32},{32,48},{48,64},{64,80},{80,96},{96,112},{112,128},... | collective-permute-start | bytes 663560 | tf_op jit(solution)/shard_map/ppermute | solution.py:20
  93.1 1.5 %collective-permute-start.5 = (bf16[6,1,48,384]{3,2,1,0:T(8,128)(2,1)S(1)}, bf16[6,1,48,384]{3,2,1,0:T(8,128)(2,1)S(1)}, u32[]{:S(2)}, u32[]{:S(2)}) collective-permute-start(bf16[6,1,48,384]{3,2,1,0:T(8,128)(2,1)S(1)} %get-tuple-element.28), channel_id=1, source_target_pairs={{16,0},{32,16},{48,32},{64,48},{80,64},{96,80},{112,96},{128,112},... | collective-permute-start | bytes 663560 | tf_op jit(solution)/shard_map/ppermute | solution.py:21
  94.6 1.4 collective-permute-done.4
  96.0 4.2 %collective-permute-done.5 = bf16[6,1,48,384]{3,2,1,0:T(8,128)(2,1)S(1)} collective-permute-done((bf16[6,1,48,384]{3,2,1,0:T(8,128)(2,1)S(1)}, bf16[6,1,48,384]{3,2,1,0:T(8,128)(2,1)S(1)}, u32[]{:S(2)}, u32[]{:S(2)}) %collective-permute-start.5) | collective-permute-done | bytes 221216 | tf_op jit(solution)/shard_map/ppermute | solution.py:21
  101.8 3.7 %fusion.51 = (bf16[4,3,48,1152]{3,2,1,0:T(8,128)(2,1)S(1)}, bf16[4,3,48,1152]{3,2,1,0:T(8,128)(2,1)}, bf16[4,3,48,1152]{3,2,1,0:T(8,128)(2,1)}, bf16[4,3,48,1152...) fusion(bf16[6,5,48,1152]{3,2,1,0:T(8,128)(2,1)S(1)} %pad_maximu, ...), kind=kLoop, calls=%fused_computation.88 | loop fusion | bytes 23887872 | tf_op jit(solution)/shard_map/slice | solution.py:46
  105.5 17.3 %all-gather.5.cloned.1.call-done = bf16[3,3,1152,384]{3,2,1,0:T(8,128)(2,1)} async-done(((bf16[3,3,72,384]{3,2,1,0:T(8,128)(2,1)}), bf16[3,3,1152,384]{3,2,1,0:T(8,128)(2,1)}) %all-gather.5.cloned.1.call-update) | async-done | bytes 7962640 | tf_op jit(solution)/shard_map/all_gather | solution.py:70
  122.8 2.6 %fusion.35 = f32[576,384]{1,0:T(8,128)S(1)} fusion(bf16[576,1152]{1,0:T(8,128)(2,1)} %bitcast.113, bf16[3,3,1152,384]{3,2,1,0:T(8,128)(2,1)} %all-gather.5.cloned.1.call-done), kind=kOutput, calls=%fused_computation.47 | convolution fusion | flops 509607936 | bytes 3096576 | tf_op jit(solution)/shard_map/dot_general | solution.py:47
  125.4 2.8 %fusion.36 = f32[576,384]{1,0:T(8,128)S(1)} fusion(bf16[576,1152]{1,0:T(8,128)(2,1)S(1)} %bitcast.111, bf16[3,3,1152,384]{3,2,1,0:T(8,128)(2,1)} %all-gather.5.cloned.1.call-done), kind=kOutput, calls=%fused_computation.49 | convolution fusion | flops 509607936 | bytes 3096576 | tf_op jit(solution)/shard_map/dot_general | solution.py:47
  135.3 1.1 fusion.21
  136.4 0.9 fusion.34
  (69 shorter events, 19.6 us)
Async XLA Ops:
  6.5 2.7 %copy-start = (bf16[4,3,48,384]{3,2,1,0:T(8,128)(2,1)S(1)}, bf16[4,3,48,384]{3,2,1,0:T(8,128)(2,1)}, u32[]{:S(2)}) copy-start(bf16[4,3,48,384]{3,2,1,0:T(8,128)(2,1)} %param.7) | copy-start | bytes 1327108
  6.5 2.7 %copy-start.16 = (f32[384]{0:T(512)S(1)}, f32[384]{0:T(512)}, u32[]{:S(2)}) copy-start(f32[384]{0:T(512)} %param.8) | copy-start | bytes 4612
  6.5 60.8 %all-gather.3.cloned.1.call-start = ((), (), s32[]{:S(2)}) async-start(), calls=%async_computation | async-start | bytes 8460288 | tf_op jit(solution)/shard_map/all_gather | solution.py:62
  7.3 115.5 %all-gather.5.cloned.1.call-start = ((), (), s32[]{:S(2)}) async-start(), calls=%async_computation.1 | async-start | bytes 8460288 | tf_op jit(solution)/shard_map/all_gather | solution.py:70
  9.6 7.8 %collective-permute-start = (bf16[2,3,48,384]{3,2,1,0:T(8,128)(2,1)S(1)}, bf16[2,3,48,384]{3,2,1,0:T(8,128)(2,1)S(1)}, u32[]{:S(2)}, u32[]{:S(2)}) collective-permute-start(bf16[2,3,48,384]{3,2,1,0:T(8,128)(2,1)S(1)} %slice.186), channel_id=1, source_target_pairs={{0,1},{1,2},{2,3},{3,4},{4,5},{5,6},{6,7},{7,8},{8,9},{9,10},{10,1... | collective-permute-start | bytes 663560 | tf_op jit(solution)/shard_map/ppermute | solution.py:10
  17.5 6.0 %collective-permute-start.1 = (bf16[6,1,48,384]{3,2,1,0:T(8,128)(2,1)S(1)}, bf16[6,1,48,384]{3,2,1,0:T(8,128)(2,1)S(1)}, u32[]{:S(2)}, u32[]{:S(2)}) collective-permute-start(bf16[6,1,48,384]{3,2,1,0:T(8,128)(2,1)S(1)} %get-tuple-element.29), channel_id=1, source_target_pairs={{0,16},{16,32},{32,48},{48,64},{64,80},{80,96},{96,112},{112,128},... | collective-permute-start | bytes 663560 | tf_op jit(solution)/shard_map/ppermute | solution.py:20
  20.6 7.1 %collective-permute-start.2 = (bf16[6,1,48,384]{3,2,1,0:T(8,128)(2,1)S(1)}, bf16[6,1,48,384]{3,2,1,0:T(8,128)(2,1)S(1)}, u32[]{:S(2)}, u32[]{:S(2)}) collective-permute-start(bf16[6,1,48,384]{3,2,1,0:T(8,128)(2,1)S(1)} %get-tuple-element.30), channel_id=1, source_target_pairs={{16,0},{32,16},{48,32},{64,48},{80,64},{96,80},{112,96},{128,112},... | collective-permute-start | bytes 663560 | tf_op jit(solution)/shard_map/ppermute | solution.py:21
  67.3 2.6 %copy-start.11 = (bf16[4,3,48,1152]{3,2,1,0:T(8,128)(2,1)S(1)}, bf16[4,3,48,1152]{3,2,1,0:T(8,128)(2,1)}, u32[]{:S(2)}) copy-start(bf16[4,3,48,1152]{3,2,1,0:T(8,128)(2,1)} %get-tuple-element.16) | copy-start | bytes 3981316
  67.3 5.4 %copy-start.14 = (bf16[3,3,1152,384]{3,2,1,0:T(8,128)(2,1)S(1)}, bf16[3,3,1152,384]{3,2,1,0:T(8,128)(2,1)}, u32[]{:S(2)}) copy-start(bf16[3,3,1152,384]{3,2,1,0:T(8,128)(2,1)} %all-gather.3.cloned.1.call-done) | copy-start | bytes 23887876
  69.9 2.8 %copy-start.9 = (bf16[4,3,48,1152]{3,2,1,0:T(8,128)(2,1)S(1)}, bf16[4,3,48,1152]{3,2,1,0:T(8,128)(2,1)}, u32[]{:S(2)}) copy-start(bf16[4,3,48,1152]{3,2,1,0:T(8,128)(2,1)} %get-tuple-element.17) | copy-start | bytes 3981316
  72.7 1.3 copy-start.7
  74.0 1.3 copy-start.5
  75.4 1.3 copy-start.3
  76.7 1.3 copy-start.1
  79.8 1.4 copy-start.17
  81.6 8.4 %collective-permute-start.3 = (bf16[2,3,48,384]{3,2,1,0:T(8,128)(2,1)S(1)}, bf16[2,3,48,384]{3,2,1,0:T(8,128)(2,1)S(1)}, u32[]{:S(2)}, u32[]{:S(2)}) collective-permute-start(bf16[2,3,48,384]{3,2,1,0:T(8,128)(2,1)S(1)} %slice.207), channel_id=1, source_target_pairs={{0,1},{1,2},{2,3},{3,4},{4,5},{5,6},{6,7},{7,8},{8,9},{9,10},{10,1... | collective-permute-start | bytes 663560 | tf_op jit(solution)/shard_map/ppermute | solution.py:10
  90.0 6.0 %collective-permute-start.4 = (bf16[6,1,48,384]{3,2,1,0:T(8,128)(2,1)S(1)}, bf16[6,1,48,384]{3,2,1,0:T(8,128)(2,1)S(1)}, u32[]{:S(2)}, u32[]{:S(2)}) collective-permute-start(bf16[6,1,48,384]{3,2,1,0:T(8,128)(2,1)S(1)} %get-tuple-element.27), channel_id=1, source_target_pairs={{0,16},{16,32},{32,48},{48,64},{64,80},{80,96},{96,112},{112,128},... | collective-permute-start | bytes 663560 | tf_op jit(solution)/shard_map/ppermute | solution.py:20
  93.1 7.1 %collective-permute-start.5 = (bf16[6,1,48,384]{3,2,1,0:T(8,128)(2,1)S(1)}, bf16[6,1,48,384]{3,2,1,0:T(8,128)(2,1)S(1)}, u32[]{:S(2)}, u32[]{:S(2)}) collective-permute-start(bf16[6,1,48,384]{3,2,1,0:T(8,128)(2,1)S(1)} %get-tuple-element.28), channel_id=1, source_target_pairs={{16,0},{32,16},{48,32},{64,48},{80,64},{96,80},{112,96},{128,112},... | collective-permute-start | bytes 663560 | tf_op jit(solution)/shard_map/ppermute | solution.py:21
  122.8 2.6 %copy-start.12 = (bf16[4,3,48,1152]{3,2,1,0:T(8,128)(2,1)S(1)}, bf16[4,3,48,1152]{3,2,1,0:T(8,128)(2,1)}, u32[]{:S(2)}) copy-start(bf16[4,3,48,1152]{3,2,1,0:T(8,128)(2,1)} %get-tuple-element.7) | copy-start | bytes 3981316
  122.8 5.4 %copy-start.13 = (bf16[3,3,1152,384]{3,2,1,0:T(8,128)(2,1)S(1)}, bf16[3,3,1152,384]{3,2,1,0:T(8,128)(2,1)}, u32[]{:S(2)}) copy-start(bf16[3,3,1152,384]{3,2,1,0:T(8,128)(2,1)} %all-gather.5.cloned.1.call-done) | copy-start | bytes 23887876
  125.4 2.8 %copy-start.10 = (bf16[4,3,48,1152]{3,2,1,0:T(8,128)(2,1)S(1)}, bf16[4,3,48,1152]{3,2,1,0:T(8,128)(2,1)}, u32[]{:S(2)}) copy-start(bf16[4,3,48,1152]{3,2,1,0:T(8,128)(2,1)} %get-tuple-element.8) | copy-start | bytes 3981316
  128.2 1.3 copy-start.8
  129.5 1.3 copy-start.6
  130.8 1.3 copy-start.4
  (3 other events, 3.3 us)
Sparse Core Ops, SparseCore 0:
  9.1 58.1 all-gather.2
  69.1 53.6 all-gather.4
where the time goes:
time: 145 us; the launch traced here: 144 us
  waiting for transfers between devices  73.7 us (51%)
  matrix products  23.5 us (16%)
  starting transfers between devices  15.9 us (11%)
  between operations  13.8 us (10%)
  local copies, waits for them, and re-layouts  12.3 us (8%)
  other arithmetic  4.8 us (3%)
    all_gather x1, waiting for transfers between devices, local(): lax.all_gather(weight_first, 'group', axis=2, tiled=True)  34.3 us
    dot_general x18, matrix products, taps(): jnp.dot(window, piece[step_t, step_r], preferred_element_type=jnp.float32)  23.5 us
    all_gather x1, waiting for transfers between devices, local(): lax.all_gather(weight_second, 'group', axis=2, tiled=True)  17.3 us
    ppermute x2, waiting for transfers between devices, shifted(): lax.ppermute(value, axis, [(source, source + steps) for source in range(f...  9.28 us
    ppermute x2, waiting for transfers between devices, with_halo(): after = lax.ppermute(first, axis, down)  8.46 us
    slice x2, local copies, waits for them, and re-layouts, taps(): joined[step_t:step_t + count, step_r:step_r + tall].reshape(-1, inner)  7.32 us
    ppermute x2, starting transfers between devices, shifted(): lax.ppermute(value, axis, [(source, source + steps) for source in range(f...  6.86 us
    ppermute x2, starting transfers between devices, with_halo(): before = lax.ppermute(last, axis, up)  6.28 us
  transfers between devices with their start and end apart: 8, of which 8 were waited for; matrix products, arithmetic and copies ran while one was open for 17% of the time, Pallas kernels for 0%

commit v1 on v0

v1 whole, which is shorter than its diff:
```python
import functools

import jax
import jax.numpy as jnp
from jax import lax
from jax.experimental import pallas as pl
from jax.experimental.pallas import tpu as pltpu
from jax.sharding import Mesh
from jax.sharding import PartitionSpec as P

BF = jnp.bfloat16
F32 = jnp.float32
C = 384
NY, NX, NZ = 4, 4, 8
AXES = ("y", "x", "z", "c")
SLAB = 144
PIECE = 16
UNIT = SLAB + PIECE


def index(y, x, z, c):
    return ((y % NY * NX + x % NX) * NZ + z % NZ) * 2 + c


def perm(to):
    return [
        (index(y, x, z, c), index(*to(y, x, z, c)))
        for y in range(NY)
        for x in range(NX)
        for z in range(NZ)
        for c in range(2)
    ]


def along_z(steps):
    return perm(lambda y, x, z, c: (y, x, z + steps if c == 0 else z - steps, c))


Z1, Z2 = along_z(1), along_z(2)
SWAP = perm(lambda y, x, z, c: (y, x, z, 1 - c))
RING_UP = perm(lambda y, x, z, c: (y, x + 1, z, c) if c == 0 else (y + 1, x, z, c))
RING_DOWN = perm(lambda y, x, z, c: (y, x - 1, z, c) if c == 0 else (y - 1, x, z, c))


def neighbours(tile_step, group_step):
    tiles, groups = NY * NX, NZ * 2
    return [
        (t * groups + g, (t + tile_step) * groups + g + group_step)
        for t in range(tiles)
        for g in range(groups)
        if 0 <= t + tile_step < tiles and 0 <= g + group_step < groups
    ]


def send(value, pairs):
    return lax.ppermute(value, AXES, pairs)


def activate(values, gain):
    wide = values.astype(F32)
    scaled = wide * lax.rsqrt(jnp.mean(wide * wide, axis=-1, keepdims=True) + 1e-06) * gain
    return jax.nn.silu(scaled)


def after(value, *others):
    return lax.optimization_barrier((value, others))[0]


def grow(own):
    tail = own[2:]
    above = send(own[:, 1:], neighbours(1, 0))
    below = send(own[:, :2], neighbours(-1, 0))
    earlier = send(tail, neighbours(0, 1))
    corner_above = send(tail[:, 1:], neighbours(1, 1))
    corner_below = send(tail[:, :2], neighbours(-1, 1))
    return [
        jnp.concatenate([corner_above, earlier, corner_below], axis=1),
        jnp.concatenate([above[:2], own[:2], below[:2]], axis=1),
        jnp.concatenate([above[2:], own[2:], below[2:]], axis=1),
    ]


def gather(weight, z, core, tap_x, tap_y):
    first_core = core == 0
    local_taps = [lax.dynamic_slice_in_dim(weight, tap, 1, axis=0)[0] for tap in (tap_x, tap_y)]
    own = jnp.stack([*local_taps, weight[0]])
    other = send(own, SWAP)
    slab = jnp.concatenate(
        [jnp.where(first_core, own, other), jnp.where(first_core, other, own)], axis=1
    )
    piece = [
        lax.dynamic_slice_in_dim(slab[2], (tap - 1) * PIECE, PIECE, axis=0) for tap in (tap_x, tap_y)
    ]
    both = jnp.concatenate([slab[0], piece[0], slab[1], piece[1], slab[2, 8 * PIECE :]], axis=0)

    def mine(value):
        return jnp.where(first_core, value[:UNIT], value[UNIT : 2 * UNIT])

    one, two = send(both, Z1), send(both, Z2)
    three = send(two, Z1)
    four = send(jnp.concatenate([mine(two), two[2 * UNIT :]], axis=0), Z2)
    sent = [one, two, three]
    other = [send(v, SWAP) for v in sent]
    plus = [jnp.where(first_core, o, s) for s, o in zip(sent, other)]
    minus = [jnp.where(first_core, s, o) for s, o in zip(sent, other)]
    turn = lax.rem(NZ - z, NZ)

    def in_order(pick, four):
        parts = [pick(both), *map(pick, plus), four, *map(pick, minus[::-1])]
        return lax.dynamic_slice_in_dim(jnp.stack(parts + parts), turn, NZ, axis=0)

    last = in_order(lambda v: v[2 * UNIT :], four[UNIT:])
    chunk = in_order(mine, four[:UNIT])
    up, down = send(chunk, RING_UP), send(chunk, RING_DOWN)
    far_up, far_down = send(up[: NZ // 2], RING_UP), send(down[NZ // 2 :], RING_DOWN)
    pieces = [chunk, up, down, far_up, far_down]
    return [*pieces, *(send(v, SWAP) for v in pieces), last], both


def assemble_kernel(where, *refs):
    *arrays, last, whole, sems = refs
    copies = []

    def fetch(src, dst):
        copy = pltpu.make_async_copy(src, dst, sems.at[len(copies)])
        copy.start()
        copies.append(copy)

    half = NZ // 2
    for k, src in enumerate(arrays):
        tap = where[k - k // 5 - k % 5 // 4]
        slabs = {3: pl.ds(0, half), 4: pl.ds(half, half)}.get(k % 5, pl.ds(0, NZ))
        piece = pl.ds(pl.multiple_of((tap - 1) * PIECE, PIECE), PIECE)
        fetch(src.at[:, pl.ds(0, SLAB)], whole.at[tap, slabs])
        fetch(src.at[:, pl.ds(SLAB, PIECE)], whole.at[0, slabs, piece])
    fetch(last, whole.at[0, :, pl.ds(8 * PIECE, PIECE)])
    for copy in copies:
        copy.wait()


ANY = pl.BlockSpec(memory_space=pl.ANY)
VMEM = pl.BlockSpec(memory_space=pltpu.VMEM)
SMEM = pl.BlockSpec(memory_space=pltpu.SMEM)


def assemble(arrays, where):
    whole = pl.pallas_call(
        assemble_kernel,
        out_shape=jax.ShapeDtypeStruct((9, NZ, SLAB, C), BF),
        in_specs=[SMEM, *[ANY] * len(arrays)],
        out_specs=VMEM,
        scratch_shapes=[pltpu.SemaphoreType.DMA((2 * len(arrays) - 1,))],
        compiler_params=pltpu.CompilerParams(vmem_limit_bytes=12 * 2**20),
        name="assemble",
    )(where, *arrays)
    return whole.reshape(9, 3 * C, C)


def convolve(frames, rows, whole, wide):
    size = 2 * rows * 48
    for t in range(3):
        left = jnp.concatenate(
            [
                jnp.concatenate(
                    [frames[f][k : k + rows].reshape(rows * 48, C) for f in (t, t + 1)], axis=0
                )
                for k in range(3)
            ],
            axis=1,
        )
        right = jnp.concatenate(
            [
                jnp.concatenate([whole(3 * t + k)[d * C : (d + 1) * C] for d in range(3)], axis=1)
                for k in range(3)
            ],
            axis=0,
        )
        part = jnp.dot(left, right, preferred_element_type=F32)
        if t == 0:
            wide[...] = part
        else:
            wide[...] += part
    column = lax.broadcasted_iota(jnp.int32, (48, C), 0)
    lines = []
    for i in range(2 * rows):
        line = wide[48 * i : 48 * i + 48]
        before = jnp.where(column == 0, 0.0, pltpu.roll(line[:, :C], 1, 0))
        behind = jnp.where(column == 47, 0.0, pltpu.roll(line[:, 2 * C :], 47, 0))
        lines.append(before + line[:, C : 2 * C] + behind)
    return lines


def first_kernel(tile, low, high, weight, bias, gain, out, wide):
    frames = [low[0], low[1], high[0], high[1]]
    lines = convolve(frames, 5, lambda tap: weight[tap], wide)
    for i, line in enumerate(lines):
        result = activate(line + bias[...], gain[...])
        if i % 5 == 0:
            result = jnp.where(tile[0] == 0, 0.0, result)
        if i % 5 == 4:
            result = jnp.where(tile[0] == NY * NX - 1, 0.0, result)
        out[i // 5, i % 5] = result.astype(BF)


def conv_first(low, high, weight, bias, gain, tile):
    return pl.pallas_call(
        first_kernel,
        out_shape=jax.ShapeDtypeStruct((2, 5, 48, C), BF),
        in_specs=[SMEM] + [VMEM] * 5,
        out_specs=VMEM,
        scratch_shapes=[pltpu.VMEM((480, 3 * C), F32)],
        compiler_params=pltpu.CompilerParams(vmem_limit_bytes=20 * 2**20),
        cost_estimate=cost(480),
        name="conv_first",
    )(tile, low, high, weight, bias, gain)


def second_kernel(start, low, high, weight, latent, bias, *refs):
    out, wide, done, sem = refs[-4:]
    frames = [low[0], low[1], high[0], high[1]]
    lines = convolve(frames, 3, lambda tap: weight[tap], wide)
    for i, line in enumerate(lines):
        at = start + 48 * i
        done[48 * i : 48 * i + 48] = (
            line + bias[...] + latent[at : at + 48].astype(F32)
        ).astype(BF)
    copy = pltpu.make_async_copy(done, out.at[pl.ds(start, 288)], sem)
    copy.start()
    copy.wait()


def conv_second(low, high, weight, latent, bias, partial):
    start = 288 if partial is None else 0
    return pl.pallas_call(
        functools.partial(second_kernel, start),
        out_shape=jax.ShapeDtypeStruct((576, C), BF),
        in_specs=[VMEM] * 5 + ([] if partial is None else [ANY]),
        out_specs=ANY,
        input_output_aliases={} if partial is None else {5: 0},
        scratch_shapes=[
            pltpu.VMEM((288, 3 * C), F32),
            pltpu.VMEM((288, C), BF),
            pltpu.SemaphoreType.DMA,
        ],
        compiler_params=pltpu.CompilerParams(vmem_limit_bytes=20 * 2**20),
        cost_estimate=cost(288),
        name="second_late" if start else "second_early",
    )(low, high, weight, latent, bias, *([] if partial is None else [partial]))


def cost(size):
    return pl.CostEstimate(
        flops=2 * size * 27 * C * C, bytes_accessed=27 * C * C * 2, transcendentals=0
    )


def local(latent, gain_first, weight_first, bias_first, gain_second, weight_second, bias_second):
    y, x, z, core = (lax.axis_index(name) for name in AXES)
    tap_x, tap_y = 1 + x, 5 + y

    def taps(step):
        across, down = 1 + lax.rem(x + step + NX, NX), 5 + lax.rem(y + step + NY, NY)
        return jnp.where(core == 0, across, down), jnp.where(core == 0, down, across)

    mine, other = zip(*(taps(step) for step in (0, -1, 1, 2)))
    where = jnp.stack([*mine, *other]).astype(jnp.int32)
    tile = (y * NX + x).astype(jnp.int32).reshape(1)
    row = lambda v: v.reshape(1, C)

    whole_first = lax.all_gather(weight_first, ("z", "c"), axis=2, tiled=True)
    pieces, both = gather(weight_second.reshape(9, 72, C), z, core, tap_x, tap_y)
    first = activate(after(latent, both), gain_first).astype(BF)
    earlier, low, high = grow(first)
    whole_second = assemble(pieces, where)

    scales = row(bias_first), row(gain_second), tile
    whole_first = whole_first.reshape(9, 3 * C, C)
    second_high = conv_first(low, high, whole_first, *scales)
    second_earlier = send(second_high, neighbours(0, 1))
    second_low = conv_first(earlier, low, whole_first, *scales)
    rest = whole_second, latent.reshape(576, C), row(bias_second)
    partial = conv_second(second_low, second_high, *rest, None)
    return conv_second(second_earlier, second_low, *rest, partial).reshape(4, 3, 48, C)


def solution(mesh):
    fine = Mesh(mesh.devices.reshape(NY, NX, NZ, 2), AXES)
    frames = P(("z", "c"), ("y", "x"), None, None)
    slices = P(None, None, ("z", "c"), None)
    return jax.shard_map(
        local,
        mesh=fine,
        in_specs=(frames, P(), slices, P(), P(), slices, P()),
        out_specs=frames,
        check_vma=False,
    )
```

time: 145 us -> 132 us (0.910)
  waiting for transfers between devices: 73.7 us -> 38.5 us
  starting transfers between devices: 15.9 us -> 47.5 us
  matrix products: 23.5 us -> 0 us
  Pallas kernels: 0 us -> 19.3 us
  other arithmetic: 4.8 us -> 1.69 us
  local copies, waits for them, and re-layouts: 12.3 us -> 10 us
    all_gather x2 -> x1, waiting for transfers between devices: 51.6 us -> 0.01 us  [local(): whole_first = lax.all_gather(weight_first, ('z', 'c'), axis=2, tiled=True)]
    ppermute x6 -> x23, starting transfers between devices: 15.9 us -> 47.5 us  [send(): return lax.ppermute(value, AXES, pairs)]
    dot_general x18 -> x0, matrix products: 23.5 us -> none  [taps(): jnp.dot(window, piece[step_t, step_r], preferred_element_type=jnp.float32)]
    pallas_call x0 -> x5, Pallas kernels: none -> 19.3 us  [the longest x2 10.2 us: conv_first(): pl.pallas_call(first_kernel, out_shape=jax.ShapeDtypeStruct((2, 5, 48, C)...]
    ppermute x6 -> x23, waiting for transfers between devices: 20.7 us -> 37.8 us  [send(): return lax.ppermute(value, AXES, pairs)]
    slice x6 -> x8, local copies, waits for them, and re-layouts: 8.64 us -> 0.29 us  [the longest x1 0.05 us: grow(): above = send(own[:, 1:], neighbours(1, 0))]
    unnamed x38 -> x33, local copies, waits for them, and re-layouts: 3.56 us -> 6.56 us
    reshape x0 -> x3, local copies, waits for them, and re-layouts: none -> 2.05 us  [local(): row = lambda v: v.reshape(1, C)]
  transfers between devices with their start and end apart: 8 -> 24, of which waited for: 8 -> 9; matrix products, arithmetic and copies ran while one was open for 17% -> 4% of each run, Pallas kernels for 0% -> 8%
where the time goes in v1:
time: 132 us; the launch traced here: 131 us
  starting transfers between devices  47.5 us (36%)
  waiting for transfers between devices  38.5 us (29%)
  Pallas kernels  19.3 us (15%)
  between operations  13.9 us (11%)
  local copies, waits for them, and re-layouts  10 us (8%)
  other arithmetic  1.69 us (1%)
    ppermute x23, starting transfers between devices, send(): return lax.ppermute(value, AXES, pairs)  47.5 us
    ppermute x23, waiting for transfers between devices, send(): return lax.ppermute(value, AXES, pairs)  37.8 us
    pallas_call x2, Pallas kernels, conv_first(): pl.pallas_call(first_kernel, out_shape=jax.ShapeDtypeStruct((2, 5, 48, C)...  10.2 us
    pallas_call x2, Pallas kernels, conv_second(): pl.pallas_call(functools.partial(second_kernel, start), out_shape=jax.Sha...  7.41 us
    unnamed x33, local copies, waits for them, and re-layouts  6.56 us
  transfers between devices with their start and end apart: 24, of which 9 were waited for; matrix products, arithmetic and copies ran while one was open for 4% of the time, Pallas kernels for 8%

profile of v1, /device:TPU:1, one launch (start us, length us, event | category | flops | bytes accessed | tf_op | source)
XLA Modules:
  0.0 130.9 jit_solution(8322010513154404686)
XLA Ops:
  8.2 3.3 %collective-permute-start = (bf16[3,72,384]{2,1,0:T(8,128)(2,1)S(1)}, bf16[3,72,384]{2,1,0:T(8,128)(2,1)S(1)}, u32[]{:S(2)}, u32[]{:S(2)}) collective-permute-start(bf16[3,72,384]{2,1,0:T(8,128)(2,1)S(1)} %pad_maximum_fusion.3), channel_id=1, source_target_pairs={{0,1},{1,0},{2,3},{3,2},{4,5},{5,4},{6,7},{7,6},{8,9},{9,8},{10,11... | collective-permute-start | bytes 497672 | tf_op jit(solution)/shard_map/ppermute | solution.py:56
  13.9 3.9 %collective-permute-start.7 = (bf16[336,384]{1,0:T(8,128)(2,1)S(1)}, bf16[336,384]{1,0:T(8,128)(2,1)S(1)}, u32[]{:S(2)}, u32[]{:S(2)}) collective-permute-start(bf16[336,384]{1,0:T(8,128)(2,1)S(1)} %constant_dynamic-update-slice_fusion), channel_id=1, source_target_pairs={{0,2},{1,15},{2,4},{3,1},{4,6},{5,3},{6,8},{7,5},{8,10},{9,7},{10,... | collective-permute-start | bytes 774152 | tf_op jit(solution)/shard_map/ppermute | solution.py:56
  20.9 3.2 %collective-permute-start.5 = (bf16[2,3,48,384]{3,2,1,0:T(8,128)(2,1)S(1)}, bf16[2,3,48,384]{3,2,1,0:T(8,128)(2,1)S(1)}, u32[]{:S(2)}, u32[]{:S(2)}) collective-permute-start(bf16[2,3,48,384]{3,2,1,0:T(8,128)(2,1)S(1)} %get-tuple-element.26), channel_id=1, source_target_pairs={{0,1},{1,2},{2,3},{3,4},{4,5},{5,6},{6,7},{7,8},{8,9},{9,10},{10,1... | collective-permute-start | bytes 663560 | tf_op jit(solution)/shard_map/ppermute | solution.py:56
  24.1 4.6 %collective-permute-start.4 = (bf16[2,2,48,384]{3,2,1,0:T(8,128)(2,1)S(1)}, bf16[2,2,48,384]{3,2,1,0:T(8,128)(2,1)S(1)}, u32[]{:S(2)}, u32[]{:S(2)}) collective-permute-start(bf16[2,2,48,384]{3,2,1,0:T(8,128)(2,1)S(1)} %get-tuple-element.24), channel_id=1, source_target_pairs={{0,17},{1,18},{2,19},{3,20},{4,21},{5,22},{6,23},{7,24},{8,25},{9,... | collective-permute-start | bytes 442376 | tf_op jit(solution)/shard_map/ppermute | solution.py:56
  30.1 6.4 %collective-permute-done.4 = bf16[2,2,48,384]{3,2,1,0:T(8,128)(2,1)S(1)} collective-permute-done((bf16[2,2,48,384]{3,2,1,0:T(8,128)(2,1)S(1)}, bf16[2,2,48,384]{3,2,1,0:T(8,128)(2,1)S(1)}, u32[]{:S(2)}, u32[]{:S(2)}) %collective-permute-start.4) | collective-permute-done | bytes 147488 | tf_op jit(solution)/shard_map/ppermute | solution.py:56
  36.5 6.3 %collective-permute-start.1 = (bf16[4,2,48,384]{3,2,1,0:T(8,128)(2,1)S(1)}, bf16[4,2,48,384]{3,2,1,0:T(8,128)(2,1)S(1)}, u32[]{:S(2)}, u32[]{:S(2)}) collective-permute-start(bf16[4,2,48,384]{3,2,1,0:T(8,128)(2,1)S(1)} %get-tuple-element.28), channel_id=1, source_target_pairs={{0,16},{1,17},{2,18},{3,19},{4,20},{5,21},{6,22},{7,23},{8,24},{9,... | collective-permute-start | bytes 884744 | tf_op jit(solution)/shard_map/ppermute | solution.py:56
  44.0 1.9 %collective-permute-start.11 = (bf16[336,384]{1,0:T(8,128)(2,1)S(1)}, bf16[336,384]{1,0:T(8,128)(2,1)S(1)}, u32[]{:S(2)}, u32[]{:S(2)}) collective-permute-start(bf16[336,384]{1,0:T(8,128)(2,1)S(1)} %collective-permute-done.9), channel_id=1, source_target_pairs={{0,2},{1,15},{2,4},{3,1},{4,6},{5,3},{6,8},{7,5},{8,10},{9,7},{10,... | collective-permute-start | bytes 774152 | tf_op jit(solution)/shard_map/ppermute | solution.py:56
  47.5 11.0 %collective-permute-done.11 = bf16[336,384]{1,0:T(8,128)(2,1)S(1)} collective-permute-done((bf16[336,384]{1,0:T(8,128)(2,1)S(1)}, bf16[336,384]{1,0:T(8,128)(2,1)S(1)}, u32[]{:S(2)}, u32[]{:S(2)}) %collective-permute-start.11) | collective-permute-done | bytes 258080 | tf_op jit(solution)/shard_map/ppermute | solution.py:56
  58.5 1.9 %collective-permute-start.12 = (bf16[336,384]{1,0:T(8,128)(2,1)S(1)}, bf16[336,384]{1,0:T(8,128)(2,1)S(1)}, u32[]{:S(2)}, u32[]{:S(2)}) collective-permute-start(bf16[336,384]{1,0:T(8,128)(2,1)S(1)} %collective-permute-done.11), channel_id=1, source_target_pairs={{0,1},{1,0},{2,3},{3,2},{4,5},{5,4},{6,7},{7,6},{8,9},{9,8},{10,11... | collective-permute-start | bytes 774152 | tf_op jit(solution)/shard_map/ppermute | solution.py:56
  62.3 6.7 %collective-permute-start.14 = (bf16[8,160,384]{2,1,0:T(8,128)(2,1)S(1)}, bf16[8,160,384]{2,1,0:T(8,128)(2,1)S(1)}, u32[]{:S(2)}, u32[]{:S(2)}) collective-permute-start(bf16[8,160,384]{2,1,0:T(8,128)(2,1)S(1)} %constant_dynamic-slice_fusion.1.refs_0_), channel_id=1, source_target_pairs={{0,16},{1,65},{2,18},{3,67},{4,20},{5,69},{6,22},{7,71},{8,24},{9,... | collective-permute-start | bytes 2949128 | tf_op jit(solution)/shard_map/ppermute | solution.py:56
  69.0 2.0 %collective-permute-start.15 = (bf16[8,160,384]{2,1,0:T(8,128)(2,1)S(1)}, bf16[8,160,384]{2,1,0:T(8,128)(2,1)S(1)}, u32[]{:S(2)}, u32[]{:S(2)}) collective-permute-start(bf16[8,160,384]{2,1,0:T(8,128)(2,1)S(1)} %constant_dynamic-slice_fusion.1.refs_0_), channel_id=1, source_target_pairs={{0,48},{1,193},{2,50},{3,195},{4,52},{5,197},{6,54},{7,199},{8,56}... | collective-permute-start | bytes 2949128 | tf_op jit(solution)/shard_map/ppermute | solution.py:56
  71.6 11.1 %collective-permute-done.14.refs_1_ = bf16[8,160,384]{2,1,0:T(8,128)(2,1)S(1)} collective-permute-done((bf16[8,160,384]{2,1,0:T(8,128)(2,1)S(1)}, bf16[8,160,384]{2,1,0:T(8,128)(2,1)S(1)}, u32[]{:S(2)}, u32[]{:S(2)}) %collective-permute-start.14) | collective-permute-done | bytes 983072 | tf_op jit(solution)/shard_map/ppermute | solution.py:56
  82.8 2.7 %collective-permute-start.17 = (bf16[4,160,384]{2,1,0:T(8,128)(2,1)S(1)}, bf16[4,160,384]{2,1,0:T(8,128)(2,1)S(1)}, u32[]{:S(2)}, u32[]{:S(2)}) collective-permute-start(bf16[4,160,384]{2,1,0:T(8,128)(2,1)S(1)} %slice.201), channel_id=1, source_target_pairs={{0,48},{1,193},{2,50},{3,195},{4,52},{5,197},{6,54},{7,199},{8,56}... | collective-permute-start | bytes 1474568 | tf_op jit(solution)/shard_map/ppermute | solution.py:56
  85.6 1.4 %collective-permute-start.19 = (bf16[8,160,384]{2,1,0:T(8,128)(2,1)S(1)}, bf16[8,160,384]{2,1,0:T(8,128)(2,1)S(1)}, u32[]{:S(2)}, u32[]{:S(2)}) collective-permute-start(bf16[8,160,384]{2,1,0:T(8,128)(2,1)S(1)} %collective-permute-done.14.refs_1_), channel_id=1, source_target_pairs={{0,1},{1,0},{2,3},{3,2},{4,5},{5,4},{6,7},{7,6},{8,9},{9,8},{10,11... | collective-permute-start | bytes 2949128 | tf_op jit(solution)/shard_map/ppermute | solution.py:56
  87.0 4.9 %collective-permute-done.16.refs_3_ = bf16[4,160,384]{2,1,0:T(8,128)(2,1)S(1)} collective-permute-done((bf16[4,160,384]{2,1,0:T(8,128)(2,1)S(1)}, bf16[4,160,384]{2,1,0:T(8,128)(2,1)S(1)}, u32[]{:S(2)}, u32[]{:S(2)}) %collective-permute-start.16) | collective-permute-done | bytes 491552 | tf_op jit(solution)/shard_map/ppermute | solution.py:56
  92.0 1.7 %collective-permute-start.21 = (bf16[4,160,384]{2,1,0:T(8,128)(2,1)S(1)}, bf16[4,160,384]{2,1,0:T(8,128)(2,1)S(1)}, u32[]{:S(2)}, u32[]{:S(2)}) collective-permute-start(bf16[4,160,384]{2,1,0:T(8,128)(2,1)S(1)} %collective-permute-done.16.refs_3_), channel_id=1, source_target_pairs={{0,1},{1,0},{2,3},{3,2},{4,5},{5,4},{6,7},{7,6},{8,9},{9,8},{10,11... | collective-permute-start | bytes 1474568 | tf_op jit(solution)/shard_map/ppermute | solution.py:56
  95.9 1.7 %assemble.1 = bf16[9,8,144,384]{3,2,1,0:T(8,128)(2,1)S(1)} custom-call(s32[8]{0:T(128)S(1)} %stack.103.where, bf16[8,160,384]{2,1,0:T(8,128)(2,1)S(1)} %constant_dynamic-slice_fusion.1.refs_0_, bf16[8,160,384]{2,1,0:T(8,128)(2,1)S(1)} %collective-permute-done.14.refs_1_, bf16[8,160,384]{2,1,0:T(8,128)(2,1)S(1)} %collective-permute-done.15.refs_2_, ...), custom_call_target="tpu_custom_call" | custom-call | tf_op jit(solution)/shard_map/assemble/pallas_call | solution.py:147
  97.6 3.1 %copy-done = bf16[9,8,144,384]{3,2,1,0:T(8,128)(2,1)} copy-done((bf16[9,8,144,384]{3,2,1,0:T(8,128)(2,1)}, bf16[9,8,144,384]{3,2,1,0:T(8,128)(2,1)S(1)}, u32[]{:S(2)}) %copy-start) | copy-done | bytes 7962648
  100.7 3.3 %copy-done.2 = bf16[3,3,1152,384]{3,2,1,0:T(8,128)(2,1)S(1)} copy-done((bf16[3,3,1152,384]{3,2,1,0:T(8,128)(2,1)S(1)}, bf16[3,3,1152,384]{3,2,1,0:T(8,128)(2,1)}, u32[]{:S(2)}) %copy-start.2) | copy-done | bytes 7962648
  103.9 5.1 %conv_first.2.high = bf16[2,5,48,384]{3,2,1,0:T(8,128)(2,1)S(1)} custom-call(s32[1]{0:T(128)} %bitcast.tile, bf16[2,7,48,384]{3,2,1,0:T(8,128)(2,1)S(1)} %get-tuple-element.36.low.high, bf16[2,7,48,384]{3,2,1,0:T(8,128)(2,1)S(1)} %get-tuple-element.37.high, bf16[9,1152,384]{2,1,0:T(8,128)(2,1)S(1)} %bitcast.114, f32[1,384]{1,0:T(1,128)S(1)} %reshape.75.bias, ...), custom_call_target="tpu_custom_call" | custom-call | flops 3822059520 | bytes 7962624 | tf_op jit(solution)/shard_map/conv_first/pallas_call | solution.py:206
  109.0 2.4 %collective-permute-start.3 = (bf16[2,5,48,384]{3,2,1,0:T(8,128)(2,1)S(1)}, bf16[2,5,48,384]{3,2,1,0:T(8,128)(2,1)S(1)}, u32[]{:S(2)}, u32[]{:S(2)}) collective-permute-start(bf16[2,5,48,384]{3,2,1,0:T(8,128)(2,1)S(1)} %conv_first.2.high), channel_id=1, source_target_pairs={{0,1},{1,2},{2,3},{3,4},{4,5},{5,6},{6,7},{7,8},{8,9},{9,10},{10,1... | collective-permute-start | bytes 1105928 | tf_op jit(solution)/shard_map/ppermute | solution.py:56
  111.5 5.1 %conv_first.3.low.high = bf16[2,5,48,384]{3,2,1,0:T(8,128)(2,1)S(1)} custom-call(s32[1]{0:T(128)} %bitcast.tile, bf16[2,7,48,384]{3,2,1,0:T(8,128)(2,1)S(1)} %pad_maximum_fusion.2.low, bf16[2,7,48,384]{3,2,1,0:T(8,128)(2,1)S(1)} %get-tuple-element.36.low.high, bf16[9,1152,384]{2,1,0:T(8,128)(2,1)S(1)} %bitcast.115, f32[1,384]{1,0:T(1,128)S(1)} %reshape.75.bias, ...), custom_call_target="tpu_custom_call" | custom-call | flops 3822059520 | bytes 7962624 | tf_op jit(solution)/shard_map/conv_first/pallas_call | solution.py:206
  116.6 3.7 %second_late.1.refs_0_ = bf16[576,384]{1,0:T(8,128)(2,1)} custom-call(bf16[2,5,48,384]{3,2,1,0:T(8,128)(2,1)S(1)} %conv_first.3.low.high, bf16[2,5,48,384]{3,2,1,0:T(8,128)(2,1)S(1)} %conv_first.2.high, bf16[9,1152,384]{2,1,0:T(8,128)(2,1)S(1)} %bitcast.110, bf16[576,384]{1,0:T(8,128)(2,1)S(1)} %bitcast.112, f32[1,384]{1,0:T(1,128)S(1)} %reshape.79.bias), custom_call_target="tpu_custom_call" | custom-call | flops 2293235712 | bytes 7962624 | tf_op jit(solution)/shard_map/second_late/pallas_call | solution.py:234
  120.4 3.7 %second_early.1 = bf16[576,384]{1,0:T(8,128)(2,1)} custom-call(bf16[2,5,48,384]{3,2,1,0:T(8,128)(2,1)S(1)} %collective-permute-done.3.low, bf16[2,5,48,384]{3,2,1,0:T(8,128)(2,1)S(1)} %conv_first.3.low.high, bf16[9,1152,384]{2,1,0:T(8,128)(2,1)S(1)} %bitcast.111, bf16[576,384]{1,0:T(8,128)(2,1)S(1)} %bitcast.113, ...), custom_call_target="tpu_custom_call", output_to_operand_aliasing={{}: (5, {})} | custom-call | flops 2293235712 | bytes 7962624 | tf_op jit(solution)/shard_map/second_early/pallas_call | solution.py:234
  (110 shorter events, 16.0 us)
Async XLA Ops:
  6.5 94.1 %all-gather.2.cloned.1.call-start = ((), (), s32[]{:S(2)}) async-start(), calls=%async_computation | async-start | bytes 8460288 | tf_op jit(solution)/shard_map/all_gather | solution.py:270
  8.2 5.5 %collective-permute-start = (bf16[3,72,384]{2,1,0:T(8,128)(2,1)S(1)}, bf16[3,72,384]{2,1,0:T(8,128)(2,1)S(1)}, u32[]{:S(2)}, u32[]{:S(2)}) collective-permute-start(bf16[3,72,384]{2,1,0:T(8,128)(2,1)S(1)} %pad_maximum_fusion.3), channel_id=1, source_target_pairs={{0,1},{1,0},{2,3},{3,2},{4,5},{5,4},{6,7},{7,6},{8,9},{9,8},{10,11... | collective-permute-start | bytes 497672 | tf_op jit(solution)/shard_map/ppermute | solution.py:56
  13.9 30.1 %collective-permute-start.7 = (bf16[336,384]{1,0:T(8,128)(2,1)S(1)}, bf16[336,384]{1,0:T(8,128)(2,1)S(1)}, u32[]{:S(2)}, u32[]{:S(2)}) collective-permute-start(bf16[336,384]{1,0:T(8,128)(2,1)S(1)} %constant_dynamic-update-slice_fusion), channel_id=1, source_target_pairs={{0,2},{1,15},{2,4},{3,1},{4,6},{5,3},{6,8},{7,5},{8,10},{9,7},{10,... | collective-permute-start | bytes 774152 | tf_op jit(solution)/shard_map/ppermute | solution.py:56
  17.8 25.0 %collective-permute-start.9 = (bf16[336,384]{1,0:T(8,128)(2,1)S(1)}, bf16[336,384]{1,0:T(8,128)(2,1)S(1)}, u32[]{:S(2)}, u32[]{:S(2)}) collective-permute-start(bf16[336,384]{1,0:T(8,128)(2,1)S(1)} %constant_dynamic-update-slice_fusion), channel_id=1, source_target_pairs={{0,4},{1,13},{2,6},{3,15},{4,8},{5,1},{6,10},{7,3},{8,12},{9,5},{1... | collective-permute-start | bytes 774152 | tf_op jit(solution)/shard_map/ppermute | solution.py:56
  19.5 9.2 %collective-permute-start.6 = (bf16[2,2,48,384]{3,2,1,0:T(8,128)(2,1)S(1)}, bf16[2,2,48,384]{3,2,1,0:T(8,128)(2,1)S(1)}, u32[]{:S(2)}, u32[]{:S(2)}) collective-permute-start(bf16[2,2,48,384]{3,2,1,0:T(8,128)(2,1)S(1)} %get-tuple-element.25), channel_id=1, source_target_pairs={{16,1},{17,2},{18,3},{19,4},{20,5},{21,6},{22,7},{23,8},{24,9},{25... | collective-permute-start | bytes 442376 | tf_op jit(solution)/shard_map/ppermute | solution.py:56
  20.9 21.9 %collective-permute-start.5 = (bf16[2,3,48,384]{3,2,1,0:T(8,128)(2,1)S(1)}, bf16[2,3,48,384]{3,2,1,0:T(8,128)(2,1)S(1)}, u32[]{:S(2)}, u32[]{:S(2)}) collective-permute-start(bf16[2,3,48,384]{3,2,1,0:T(8,128)(2,1)S(1)} %get-tuple-element.26), channel_id=1, source_target_pairs={{0,1},{1,2},{2,3},{3,4},{4,5},{5,6},{6,7},{7,8},{8,9},{9,10},{10,1... | collective-permute-start | bytes 663560 | tf_op jit(solution)/shard_map/ppermute | solution.py:56
  24.1 12.4 %collective-permute-start.4 = (bf16[2,2,48,384]{3,2,1,0:T(8,128)(2,1)S(1)}, bf16[2,2,48,384]{3,2,1,0:T(8,128)(2,1)S(1)}, u32[]{:S(2)}, u32[]{:S(2)}) collective-permute-start(bf16[2,2,48,384]{3,2,1,0:T(8,128)(2,1)S(1)} %get-tuple-element.24), channel_id=1, source_target_pairs={{0,17},{1,18},{2,19},{3,20},{4,21},{5,22},{6,23},{7,24},{8,25},{9,... | collective-permute-start | bytes 442376 | tf_op jit(solution)/shard_map/ppermute | solution.py:56
  28.8 17.1 %collective-permute-start.2 = (bf16[4,2,48,384]{3,2,1,0:T(8,128)(2,1)S(1)}, bf16[4,2,48,384]{3,2,1,0:T(8,128)(2,1)S(1)}, u32[]{:S(2)}, u32[]{:S(2)}) collective-permute-start(bf16[4,2,48,384]{3,2,1,0:T(8,128)(2,1)S(1)} %get-tuple-element.29), channel_id=1, source_target_pairs={{16,0},{17,1},{18,2},{19,3},{20,4},{21,5},{22,6},{23,7},{24,8},{25... | collective-permute-start | bytes 884744 | tf_op jit(solution)/shard_map/ppermute | solution.py:56
  36.5 9.9 %collective-permute-start.1 = (bf16[4,2,48,384]{3,2,1,0:T(8,128)(2,1)S(1)}, bf16[4,2,48,384]{3,2,1,0:T(8,128)(2,1)S(1)}, u32[]{:S(2)}, u32[]{:S(2)}) collective-permute-start(bf16[4,2,48,384]{3,2,1,0:T(8,128)(2,1)S(1)} %get-tuple-element.28), channel_id=1, source_target_pairs={{0,16},{1,17},{2,18},{3,19},{4,20},{5,21},{6,22},{7,23},{8,24},{9,... | collective-permute-start | bytes 884744 | tf_op jit(solution)/shard_map/ppermute | solution.py:56
  42.9 18.8 %collective-permute-start.13 = (bf16[176,384]{1,0:T(8,128)(2,1)S(1)}, bf16[176,384]{1,0:T(8,128)(2,1)S(1)}, u32[]{:S(2)}, u32[]{:S(2)}) collective-permute-start(bf16[176,384]{1,0:T(8,128)(2,1)S(1)} %pad_maximum_fusion.4), channel_id=1, source_target_pairs={{0,4},{1,13},{2,6},{3,15},{4,8},{5,1},{6,10},{7,3},{8,12},{9,5},{1... | collective-permute-start | bytes 405512 | tf_op jit(solution)/shard_map/ppermute | solution.py:56
  44.0 16.5 %collective-permute-start.10 = (bf16[336,384]{1,0:T(8,128)(2,1)S(1)}, bf16[336,384]{1,0:T(8,128)(2,1)S(1)}, u32[]{:S(2)}, u32[]{:S(2)}) collective-permute-start(bf16[336,384]{1,0:T(8,128)(2,1)S(1)} %collective-permute-done.9), channel_id=1, source_target_pairs={{0,1},{1,0},{2,3},{3,2},{4,5},{5,4},{6,7},{7,6},{8,9},{9,8},{10,11... | collective-permute-start | bytes 774152 | tf_op jit(solution)/shard_map/ppermute | solution.py:56
  44.0 14.5 %collective-permute-start.11 = (bf16[336,384]{1,0:T(8,128)(2,1)S(1)}, bf16[336,384]{1,0:T(8,128)(2,1)S(1)}, u32[]{:S(2)}, u32[]{:S(2)}) collective-permute-start(bf16[336,384]{1,0:T(8,128)(2,1)S(1)} %collective-permute-done.9), channel_id=1, source_target_pairs={{0,2},{1,15},{2,4},{3,1},{4,6},{5,3},{6,8},{7,5},{8,10},{9,7},{10,... | collective-permute-start | bytes 774152 | tf_op jit(solution)/shard_map/ppermute | solution.py:56
  45.9 1.5 %collective-permute-start.8 = (bf16[336,384]{1,0:T(8,128)(2,1)S(1)}, bf16[336,384]{1,0:T(8,128)(2,1)S(1)}, u32[]{:S(2)}, u32[]{:S(2)}) collective-permute-start(bf16[336,384]{1,0:T(8,128)(2,1)S(1)} %collective-permute-done.7), channel_id=1, source_target_pairs={{0,1},{1,0},{2,3},{3,2},{4,5},{5,4},{6,7},{7,6},{8,9},{9,8},{10,11... | collective-permute-start | bytes 774152 | tf_op jit(solution)/shard_map/ppermute | solution.py:56
  58.5 3.1 %collective-permute-start.12 = (bf16[336,384]{1,0:T(8,128)(2,1)S(1)}, bf16[336,384]{1,0:T(8,128)(2,1)S(1)}, u32[]{:S(2)}, u32[]{:S(2)}) collective-permute-start(bf16[336,384]{1,0:T(8,128)(2,1)S(1)} %collective-permute-done.11), channel_id=1, source_target_pairs={{0,1},{1,0},{2,3},{3,2},{4,5},{5,4},{6,7},{7,6},{8,9},{9,8},{10,11... | collective-permute-start | bytes 774152 | tf_op jit(solution)/shard_map/ppermute | solution.py:56
  62.3 20.3 %collective-permute-start.14 = (bf16[8,160,384]{2,1,0:T(8,128)(2,1)S(1)}, bf16[8,160,384]{2,1,0:T(8,128)(2,1)S(1)}, u32[]{:S(2)}, u32[]{:S(2)}) collective-permute-start(bf16[8,160,384]{2,1,0:T(8,128)(2,1)S(1)} %constant_dynamic-slice_fusion.1.refs_0_), channel_id=1, source_target_pairs={{0,16},{1,65},{2,18},{3,67},{4,20},{5,69},{6,22},{7,71},{8,24},{9,... | collective-permute-start | bytes 2949128 | tf_op jit(solution)/shard_map/ppermute | solution.py:56
  69.0 13.8 %collective-permute-start.15 = (bf16[8,160,384]{2,1,0:T(8,128)(2,1)S(1)}, bf16[8,160,384]{2,1,0:T(8,128)(2,1)S(1)}, u32[]{:S(2)}, u32[]{:S(2)}) collective-permute-start(bf16[8,160,384]{2,1,0:T(8,128)(2,1)S(1)} %constant_dynamic-slice_fusion.1.refs_0_), channel_id=1, source_target_pairs={{0,48},{1,193},{2,50},{3,195},{4,52},{5,197},{6,54},{7,199},{8,56}... | collective-permute-start | bytes 2949128 | tf_op jit(solution)/shard_map/ppermute | solution.py:56
  70.9 22.8 %collective-permute-start.18 = (bf16[8,160,384]{2,1,0:T(8,128)(2,1)S(1)}, bf16[8,160,384]{2,1,0:T(8,128)(2,1)S(1)}, u32[]{:S(2)}, u32[]{:S(2)}) collective-permute-start(bf16[8,160,384]{2,1,0:T(8,128)(2,1)S(1)} %constant_dynamic-slice_fusion.1.refs_0_), channel_id=1, source_target_pairs={{0,1},{1,0},{2,3},{3,2},{4,5},{5,4},{6,7},{7,6},{8,9},{9,8},{10,11... | collective-permute-start | bytes 2949128 | tf_op jit(solution)/shard_map/ppermute | solution.py:56
  82.7 9.3 %collective-permute-start.16 = (bf16[4,160,384]{2,1,0:T(8,128)(2,1)S(1)}, bf16[4,160,384]{2,1,0:T(8,128)(2,1)S(1)}, u32[]{:S(2)}, u32[]{:S(2)}) collective-permute-start(bf16[4,160,384]{2,1,0:T(8,128)(2,1)S(1)} %slice.200), channel_id=1, source_target_pairs={{0,16},{1,65},{2,18},{3,67},{4,20},{5,69},{6,22},{7,71},{8,24},{9,... | collective-permute-start | bytes 1474568 | tf_op jit(solution)/shard_map/ppermute | solution.py:56
  82.8 10.8 %collective-permute-start.17 = (bf16[4,160,384]{2,1,0:T(8,128)(2,1)S(1)}, bf16[4,160,384]{2,1,0:T(8,128)(2,1)S(1)}, u32[]{:S(2)}, u32[]{:S(2)}) collective-permute-start(bf16[4,160,384]{2,1,0:T(8,128)(2,1)S(1)} %slice.201), channel_id=1, source_target_pairs={{0,48},{1,193},{2,50},{3,195},{4,52},{5,197},{6,54},{7,199},{8,56}... | collective-permute-start | bytes 1474568 | tf_op jit(solution)/shard_map/ppermute | solution.py:56
  85.6 8.1 %collective-permute-start.19 = (bf16[8,160,384]{2,1,0:T(8,128)(2,1)S(1)}, bf16[8,160,384]{2,1,0:T(8,128)(2,1)S(1)}, u32[]{:S(2)}, u32[]{:S(2)}) collective-permute-start(bf16[8,160,384]{2,1,0:T(8,128)(2,1)S(1)} %collective-permute-done.14.refs_1_), channel_id=1, source_target_pairs={{0,1},{1,0},{2,3},{3,2},{4,5},{5,4},{6,7},{7,6},{8,9},{9,8},{10,11... | collective-permute-start | bytes 2949128 | tf_op jit(solution)/shard_map/ppermute | solution.py:56
  87.0 6.7 %collective-permute-start.20 = (bf16[8,160,384]{2,1,0:T(8,128)(2,1)S(1)}, bf16[8,160,384]{2,1,0:T(8,128)(2,1)S(1)}, u32[]{:S(2)}, u32[]{:S(2)}) collective-permute-start(bf16[8,160,384]{2,1,0:T(8,128)(2,1)S(1)} %collective-permute-done.15.refs_2_), channel_id=1, source_target_pairs={{0,1},{1,0},{2,3},{3,2},{4,5},{5,4},{6,7},{7,6},{8,9},{9,8},{10,11... | collective-permute-start | bytes 2949128 | tf_op jit(solution)/shard_map/ppermute | solution.py:56
  92.0 3.2 %collective-permute-start.21 = (bf16[4,160,384]{2,1,0:T(8,128)(2,1)S(1)}, bf16[4,160,384]{2,1,0:T(8,128)(2,1)S(1)}, u32[]{:S(2)}, u32[]{:S(2)}) collective-permute-start(bf16[4,160,384]{2,1,0:T(8,128)(2,1)S(1)} %collective-permute-done.16.refs_3_), channel_id=1, source_target_pairs={{0,1},{1,0},{2,3},{3,2},{4,5},{5,4},{6,7},{7,6},{8,9},{9,8},{10,11... | collective-permute-start | bytes 1474568 | tf_op jit(solution)/shard_map/ppermute | solution.py:56
  93.7 2.2 %collective-permute-start.22 = (bf16[4,160,384]{2,1,0:T(8,128)(2,1)S(1)}, bf16[4,160,384]{2,1,0:T(8,128)(2,1)S(1)}, u32[]{:S(2)}, u32[]{:S(2)}) collective-permute-start(bf16[4,160,384]{2,1,0:T(8,128)(2,1)S(1)} %collective-permute-done.17.refs_4_), channel_id=1, source_target_pairs={{0,1},{1,0},{2,3},{3,2},{4,5},{5,4},{6,7},{7,6},{8,9},{9,8},{10,11... | collective-permute-start | bytes 1474568 | tf_op jit(solution)/shard_map/ppermute | solution.py:56
  109.0 11.3 %collective-permute-start.3 = (bf16[2,5,48,384]{3,2,1,0:T(8,128)(2,1)S(1)}, bf16[2,5,48,384]{3,2,1,0:T(8,128)(2,1)S(1)}, u32[]{:S(2)}, u32[]{:S(2)}) collective-permute-start(bf16[2,5,48,384]{3,2,1,0:T(8,128)(2,1)S(1)} %conv_first.2.high), channel_id=1, source_target_pairs={{0,1},{1,2},{2,3},{3,4},{4,5},{5,6},{6,7},{7,8},{8,9},{9,10},{10,1... | collective-permute-start | bytes 1105928 | tf_op jit(solution)/shard_map/ppermute | solution.py:56
  (7 other events, 58.5 us)
Sparse Core Ops, SparseCore 0:
  9.1 66.5 all-gather.1

commit v2 on v1

--- a/solution.py
+++ b/solution.py
@@ -14,8 +14,8 @@
 NY, NX, NZ = 4, 4, 8
 AXES = ("y", "x", "z", "c")
 SLAB = 144
-PIECE = 16
-UNIT = SLAB + PIECE
+PART = 40
+BLOCK = 160
 
 
 def index(y, x, z, c):
@@ -40,6 +40,9 @@
 SWAP = perm(lambda y, x, z, c: (y, x, z, 1 - c))
 RING_UP = perm(lambda y, x, z, c: (y, x + 1, z, c) if c == 0 else (y + 1, x, z, c))
 RING_DOWN = perm(lambda y, x, z, c: (y, x - 1, z, c) if c == 0 else (y - 1, x, z, c))
+
+CROSS_UP = perm(lambda y, x, z, c: (y + 1, x, z, c) if c == 0 else (y, x + 1, z, c))
+CROSS_DOWN = perm(lambda y, x, z, c: (y - 1, x, z, c) if c == 0 else (y, x - 1, z, c))
 
 
 def neighbours(tile_step, group_step):
@@ -80,41 +83,39 @@
     ]
 
 
-def gather(weight, z, core, tap_x, tap_y):
+def gather(weight, y, x, z, core):
     first_core = core == 0
-    local_taps = [lax.dynamic_slice_in_dim(weight, tap, 1, axis=0)[0] for tap in (tap_x, tap_y)]
-    own = jnp.stack([*local_taps, weight[0]])
-    other = send(own, SWAP)
+    other = send(weight, SWAP)
     slab = jnp.concatenate(
-        [jnp.where(first_core, own, other), jnp.where(first_core, other, own)], axis=1
+        [jnp.where(first_core, weight, other), jnp.where(first_core, other, weight)], axis=1
+    ).reshape(9 * SLAB, C)
+    starts = BLOCK * 2 * y + PART * x, BLOCK * 2 * x + BLOCK + PART * y
+    both = jnp.concatenate(
+        [*(lax.dynamic_slice_in_dim(slab, at, PART, axis=0) for at in starts), slab[8 * BLOCK :]],
+        axis=0,
     )
-    piece = [
-        lax.dynamic_slice_in_dim(slab[2], (tap - 1) * PIECE, PIECE, axis=0) for tap in (tap_x, tap_y)
-    ]
-    both = jnp.concatenate([slab[0], piece[0], slab[1], piece[1], slab[2, 8 * PIECE :]], axis=0)
-
-    def mine(value):
-        return jnp.where(first_core, value[:UNIT], value[UNIT : 2 * UNIT])
-
     one, two = send(both, Z1), send(both, Z2)
-    three = send(two, Z1)
-    four = send(jnp.concatenate([mine(two), two[2 * UNIT :]], axis=0), Z2)
-    sent = [one, two, three]
-    other = [send(v, SWAP) for v in sent]
-    plus = [jnp.where(first_core, o, s) for s, o in zip(sent, other)]
-    minus = [jnp.where(first_core, s, o) for s, o in zip(sent, other)]
-    turn = lax.rem(NZ - z, NZ)
-
-    def in_order(pick, four):
-        parts = [pick(both), *map(pick, plus), four, *map(pick, minus[::-1])]
-        return lax.dynamic_slice_in_dim(jnp.stack(parts + parts), turn, NZ, axis=0)
-
-    last = in_order(lambda v: v[2 * UNIT :], four[UNIT:])
-    chunk = in_order(mine, four[:UNIT])
-    up, down = send(chunk, RING_UP), send(chunk, RING_DOWN)
-    far_up, far_down = send(up[: NZ // 2], RING_UP), send(down[NZ // 2 :], RING_DOWN)
-    pieces = [chunk, up, down, far_up, far_down]
-    return [*pieces, *(send(v, SWAP) for v in pieces), last], both
+    three, four = send(two, Z1), send(two, Z2)
+    sent = jnp.stack([one, two, three])
+    other = send(sent, SWAP)
+    plus, minus = jnp.where(first_core, other, sent), jnp.where(first_core, sent, other)
+    parts = [both, plus[0], plus[1], plus[2], four, minus[2], minus[1], minus[0]]
+    slabs = lax.dynamic_slice_in_dim(jnp.stack(parts + parts), lax.rem(NZ - z, NZ), NZ, axis=0)
+    last = slabs[:, 2 * PART :]
+    chunk = jnp.where(first_core, slabs[:, :PART], slabs[:, PART : 2 * PART])
+
+    def ring(chunk, up_pairs, down_pairs):
+        half = NZ // 2
+        up, down = send(chunk, up_pairs), send(chunk, down_pairs)
+        return up, down, send(up[:half], up_pairs), send(down[half:], down_pairs)
+
+    up, down, far_up, far_down = ring(chunk, RING_UP, RING_DOWN)
+    parts = [chunk, down, jnp.concatenate([far_up, far_down], axis=0), up]
+    spot = lax.rem(4 - jnp.where(first_core, x, y), 4)
+    turned = lax.dynamic_slice_in_dim(jnp.stack(parts + parts), spot, 4, axis=0)
+    chunk = turned.transpose(1, 0, 2, 3).reshape(NZ, BLOCK, C)
+    pieces = [chunk, *ring(chunk, CROSS_UP, CROSS_DOWN)]
+    return [*pieces, *(send(v, SWAP) for v in pieces), last], chunk
 
 
 def assemble_kernel(where, *refs):
@@ -128,12 +129,10 @@
 
     half = NZ // 2
     for k, src in enumerate(arrays):
-        tap = where[k - k // 5 - k % 5 // 4]
+        at = pl.multiple_of(where[k - k // 5 - k % 5 // 4], BLOCK)
         slabs = {3: pl.ds(0, half), 4: pl.ds(half, half)}.get(k % 5, pl.ds(0, NZ))
-        piece = pl.ds(pl.multiple_of((tap - 1) * PIECE, PIECE), PIECE)
-        fetch(src.at[:, pl.ds(0, SLAB)], whole.at[tap, slabs])
-        fetch(src.at[:, pl.ds(SLAB, PIECE)], whole.at[0, slabs, piece])
-    fetch(last, whole.at[0, :, pl.ds(8 * PIECE, PIECE)])
+        fetch(src, whole.at[slabs, pl.ds(at, BLOCK)])
+    fetch(last, whole.at[:, pl.ds(8 * BLOCK, 9 * SLAB - 8 * BLOCK)])
     for copy in copies:
         copy.wait()
 
@@ -144,16 +143,15 @@
 
 
 def assemble(arrays, where):
-    whole = pl.pallas_call(
+    return pl.pallas_call(
         assemble_kernel,
-        out_shape=jax.ShapeDtypeStruct((9, NZ, SLAB, C), BF),
+        out_shape=jax.ShapeDtypeStruct((NZ, 9 * SLAB, C), BF),
         in_specs=[SMEM, *[ANY] * len(arrays)],
         out_specs=VMEM,
-        scratch_shapes=[pltpu.SemaphoreType.DMA((2 * len(arrays) - 1,))],
+        scratch_shapes=[pltpu.SemaphoreType.DMA((len(arrays),))],
         compiler_params=pltpu.CompilerParams(vmem_limit_bytes=12 * 2**20),
         name="assemble",
     )(where, *arrays)
-    return whole.reshape(9, 3 * C, C)
 
 
 def convolve(frames, rows, whole, wide):
@@ -209,16 +207,20 @@
         in_specs=[SMEM] + [VMEM] * 5,
         out_specs=VMEM,
         scratch_shapes=[pltpu.VMEM((480, 3 * C), F32)],
-        compiler_params=pltpu.CompilerParams(vmem_limit_bytes=20 * 2**20),
+        compiler_params=pltpu.CompilerParams(vmem_limit_bytes=12 * 2**20),
         cost_estimate=cost(480),
         name="conv_first",
     )(tile, low, high, weight, bias, gain)
 
 
+def slab_rows(weight, tap):
+    return weight[:, SLAB * tap : SLAB * (tap + 1)].reshape(3 * C, C)
+
+
 def second_kernel(start, low, high, weight, latent, bias, *refs):
     out, wide, done, sem = refs[-4:]
     frames = [low[0], low[1], high[0], high[1]]
-    lines = convolve(frames, 3, lambda tap: weight[tap], wide)
+    lines = convolve(frames, 3, lambda tap: slab_rows(weight, tap), wide)
     for i, line in enumerate(lines):
         at = start + 48 * i
         done[48 * i : 48 * i + 48] = (
@@ -242,7 +244,7 @@
             pltpu.VMEM((288, C), BF),
             pltpu.SemaphoreType.DMA,
         ],
-        compiler_params=pltpu.CompilerParams(vmem_limit_bytes=20 * 2**20),
+        compiler_params=pltpu.CompilerParams(vmem_limit_bytes=12 * 2**20),
         cost_estimate=cost(288),
         name="second_late" if start else "second_early",
     )(low, high, weight, latent, bias, *([] if partial is None else [partial]))
@@ -256,28 +258,28 @@
 
 def local(latent, gain_first, weight_first, bias_first, gain_second, weight_second, bias_second):
     y, x, z, core = (lax.axis_index(name) for name in AXES)
-    tap_x, tap_y = 1 + x, 5 + y
-
-    def taps(step):
-        across, down = 1 + lax.rem(x + step + NX, NX), 5 + lax.rem(y + step + NY, NY)
-        return jnp.where(core == 0, across, down), jnp.where(core == 0, down, across)
-
-    mine, other = zip(*(taps(step) for step in (0, -1, 1, 2)))
+
+    def starts(step):
+        down, across = lax.rem(y + step + NY, NY), lax.rem(x + step + NX, NX)
+        down, across = 2 * BLOCK * down, 2 * BLOCK * across + BLOCK
+        return jnp.where(core == 0, down, across), jnp.where(core == 0, across, down)
+
+    mine, other = zip(*(starts(step) for step in (0, -1, 1, 2)))
     where = jnp.stack([*mine, *other]).astype(jnp.int32)
     tile = (y * NX + x).astype(jnp.int32).reshape(1)
     row = lambda v: v.reshape(1, C)
 
     whole_first = lax.all_gather(weight_first, ("z", "c"), axis=2, tiled=True)
-    pieces, both = gather(weight_second.reshape(9, 72, C), z, core, tap_x, tap_y)
-    first = activate(after(latent, both), gain_first).astype(BF)
+    pieces, chunk = gather(weight_second.reshape(9, 72, C), y, x, z, core)
+    first = activate(after(latent, chunk), gain_first).astype(BF)
     earlier, low, high = grow(first)
-    whole_second = assemble(pieces, where)
 
     scales = row(bias_first), row(gain_second), tile
     whole_first = whole_first.reshape(9, 3 * C, C)
     second_high = conv_first(low, high, whole_first, *scales)
     second_earlier = send(second_high, neighbours(0, 1))
     second_low = conv_first(earlier, low, whole_first, *scales)
+    whole_second = assemble(after(pieces, second_low), where)
     rest = whole_second, latent.reshape(576, C), row(bias_second)
     partial = conv_second(second_low, second_high, *rest, None)
     return conv_second(second_earlier, second_low, *rest, partial).reshape(4, 3, 48, C)

time: 132 us -> 134 us (1.015)
  waiting for transfers between devices: 38.5 us -> 23.9 us
  starting transfers between devices: 47.5 us -> 55.9 us
  other arithmetic: 1.69 us -> 6.8 us
  Pallas kernels: 19.3 us -> 20.9 us
  local copies, waits for them, and re-layouts: 10 us -> 11.5 us
    ppermute x23 -> x25, waiting for transfers between devices: 37.8 us -> 23.2 us  [send(): return lax.ppermute(value, AXES, pairs)]
    ppermute x23 -> x25, starting transfers between devices: 47.5 us -> 55.9 us  [send(): return lax.ppermute(value, AXES, pairs)]
    reshape x3, local copies, waits for them, and re-layouts: 2.05 us -> 0.01 us  [local(): row = lambda v: v.reshape(1, C)]
    concatenate x2 -> x3, other arithmetic: 0.03 us -> 1.93 us  [the longest x1 1.82 us: grow(): jnp.concatenate([above[2:], own[2:], below[2:]], axis=1)]
    concatenate x1, other arithmetic: 0.08 us -> 1.94 us  [grow(): jnp.concatenate([corner_above, earlier, corner_below], axis=1)]
    pallas_call x1, Pallas kernels: 1.71 us -> 3.28 us  [assemble(): pl.pallas_call(assemble_kernel, out_shape=jax.ShapeDtypeStruct((NZ, 9 * S...]
  transfers between devices with their start and end apart: 24 -> 26, of which waited for: 9 -> 9; matrix products, arithmetic and copies ran while one was open for 4% -> 9% of each run, Pallas kernels for 8% -> 13%
where the time goes in v2:
time: 134 us; the launch traced here: 133 us
  starting transfers between devices  55.9 us (42%)
  waiting for transfers between devices  23.9 us (18%)
  Pallas kernels  20.9 us (16%)
  between operations  13.8 us (10%)
  local copies, waits for them, and re-layouts  11.5 us (9%)
  other arithmetic  6.8 us (5%)
    ppermute x25, starting transfers between devices, send(): return lax.ppermute(value, AXES, pairs)  55.9 us
    ppermute x25, waiting for transfers between devices, send(): return lax.ppermute(value, AXES, pairs)  23.2 us
    pallas_call x2, Pallas kernels, conv_first(): pl.pallas_call(first_kernel, out_shape=jax.ShapeDtypeStruct((2, 5, 48, C)...  10.2 us
    pallas_call x2, Pallas kernels, conv_second(): pl.pallas_call(functools.partial(second_kernel, start), out_shape=jax.Sha...  7.43 us
    unnamed x33, local copies, waits for them, and re-layouts  6.67 us
    pallas_call x1, Pallas kernels, assemble(): pl.pallas_call(assemble_kernel, out_shape=jax.ShapeDtypeStruct((NZ, 9 * S...  3.28 us
  transfers between devices with their start and end apart: 26, of which 9 were waited for; matrix products, arithmetic and copies ran while one was open for 9% of the time, Pallas kernels for 13%

profile of v2, /device:TPU:1, one launch (start us, length us, event | category | flops | bytes accessed | tf_op | source)
XLA Modules:
  0.0 132.9 jit_solution(14493276454420477956)
XLA Ops:
  7.3 3.3 %collective-permute-start = (bf16[9,72,384]{2,1,0:T(8,128)(2,1)}, bf16[9,72,384]{2,1,0:T(8,128)(2,1)S(1)}, u32[]{:S(2)}, u32[]{:S(2)}) collective-permute-start(bf16[9,72,384]{2,1,0:T(8,128)(2,1)} %bitcast.62), channel_id=1, source_target_pairs={{0,1},{1,0},{2,3},{3,2},{4,5},{5,4},{6,7},{7,6},{8,9},{9,8},{10,11... | collective-permute-start | bytes 1493000 | tf_op jit(solution)/shard_map/ppermute | solution.py:59
  13.6 4.4 %collective-permute-start.2 = (bf16[96,384]{1,0:T(8,128)(2,1)S(1)}, bf16[96,384]{1,0:T(8,128)(2,1)S(1)}, u32[]{:S(2)}, u32[]{:S(2)}) collective-permute-start(bf16[96,384]{1,0:T(8,128)(2,1)S(1)} %pad_maximum_fusion.5), channel_id=1, source_target_pairs={{0,4},{1,13},{2,6},{3,15},{4,8},{5,1},{6,10},{7,3},{8,12},{9,5},{1... | collective-permute-start | bytes 221192 | tf_op jit(solution)/shard_map/ppermute | solution.py:59
  20.0 2.9 %collective-permute-start.3 = (bf16[96,384]{1,0:T(8,128)(2,1)S(1)}, bf16[96,384]{1,0:T(8,128)(2,1)S(1)}, u32[]{:S(2)}, u32[]{:S(2)}) collective-permute-start(bf16[96,384]{1,0:T(8,128)(2,1)S(1)} %collective-permute-done.2), channel_id=1, source_target_pairs={{0,2},{1,15},{2,4},{3,1},{4,6},{5,3},{6,8},{7,5},{8,10},{9,7},{10,... | collective-permute-start | bytes 221192 | tf_op jit(solution)/shard_map/ppermute | solution.py:59
  24.4 2.4 %collective-permute-start.4 = (bf16[3,96,384]{2,1,0:T(8,128)(2,1)S(1)}, bf16[3,96,384]{2,1,0:T(8,128)(2,1)S(1)}, u32[]{:S(2)}, u32[]{:S(2)}) collective-permute-start(bf16[3,96,384]{2,1,0:T(8,128)(2,1)S(1)} %pad_maximum_fusion.4), channel_id=1, source_target_pairs={{0,1},{1,0},{2,3},{3,2},{4,5},{5,4},{6,7},{7,6},{8,9},{9,8},{10,11... | collective-permute-start | bytes 663560 | tf_op jit(solution)/shard_map/ppermute | solution.py:59
  26.7 2.4 %collective-permute-start.5 = (bf16[96,384]{1,0:T(8,128)(2,1)S(1)}, bf16[96,384]{1,0:T(8,128)(2,1)S(1)}, u32[]{:S(2)}, u32[]{:S(2)}) collective-permute-start(bf16[96,384]{1,0:T(8,128)(2,1)S(1)} %collective-permute-done.2), channel_id=1, source_target_pairs={{0,4},{1,13},{2,6},{3,15},{4,8},{5,1},{6,10},{7,3},{8,12},{9,5},{1... | collective-permute-start | bytes 221192 | tf_op jit(solution)/shard_map/ppermute | solution.py:59
  29.3 4.4 %collective-permute-done.5 = bf16[96,384]{1,0:T(8,128)(2,1)S(1)} collective-permute-done((bf16[96,384]{1,0:T(8,128)(2,1)S(1)}, bf16[96,384]{1,0:T(8,128)(2,1)S(1)}, u32[]{:S(2)}, u32[]{:S(2)}) %collective-permute-start.5) | collective-permute-done | bytes 73760 | tf_op jit(solution)/shard_map/ppermute | solution.py:59
  35.1 2.7 %collective-permute-start.6 = (bf16[8,40,384]{2,1,0:T(8,128)(2,1)S(1)}, bf16[8,40,384]{2,1,0:T(8,128)(2,1)S(1)}, u32[]{:S(2)}, u32[]{:S(2)}) collective-permute-start(bf16[8,40,384]{2,1,0:T(8,128)(2,1)S(1)} %get-tuple-element.30), channel_id=1, source_target_pairs={{0,48},{1,193},{2,50},{3,195},{4,52},{5,197},{6,54},{7,199},{8,56}... | collective-permute-start | bytes 737288 | tf_op jit(solution)/shard_map/ppermute | solution.py:59
  37.8 3.1 %collective-permute-done.6 = bf16[8,40,384]{2,1,0:T(8,128)(2,1)S(1)} collective-permute-done((bf16[8,40,384]{2,1,0:T(8,128)(2,1)S(1)}, bf16[8,40,384]{2,1,0:T(8,128)(2,1)S(1)}, u32[]{:S(2)}, u32[]{:S(2)}) %collective-permute-start.6) | collective-permute-done | bytes 245792 | tf_op jit(solution)/shard_map/ppermute | solution.py:59
  40.9 3.6 %collective-permute-start.9 = (bf16[4,40,384]{2,1,0:T(8,128)(2,1)S(1)}, bf16[4,40,384]{2,1,0:T(8,128)(2,1)S(1)}, u32[]{:S(2)}, u32[]{:S(2)}) collective-permute-start(bf16[4,40,384]{2,1,0:T(8,128)(2,1)S(1)} %slice.97), channel_id=1, source_target_pairs={{0,48},{1,193},{2,50},{3,195},{4,52},{5,197},{6,54},{7,199},{8,56}... | collective-permute-start | bytes 368648 | tf_op jit(solution)/shard_map/ppermute | solution.py:59
  46.4 3.6 %collective-permute-done.8 = bf16[4,40,384]{2,1,0:T(8,128)(2,1)S(1)} collective-permute-done((bf16[4,40,384]{2,1,0:T(8,128)(2,1)S(1)}, bf16[4,40,384]{2,1,0:T(8,128)(2,1)S(1)}, u32[]{:S(2)}, u32[]{:S(2)}) %collective-permute-start.8) | collective-permute-done | bytes 122912 | tf_op jit(solution)/shard_map/ppermute | solution.py:59
  56.8 7.6 %collective-permute-start.14 = (bf16[2,3,48,384]{3,2,1,0:T(8,128)(2,1)}, bf16[2,3,48,384]{3,2,1,0:T(8,128)(2,1)}, u32[]{:S(2)}, u32[]{:S(2)}) collective-permute-start(bf16[2,3,48,384]{3,2,1,0:T(8,128)(2,1)} %get-tuple-element.37), channel_id=1, source_target_pairs={{0,1},{1,2},{2,3},{3,4},{4,5},{5,6},{6,7},{7,8},{8,9},{9,10},{10,1... | collective-permute-start | bytes 663560 | tf_op jit(solution)/shard_map/ppermute | solution.py:59
  66.6 4.7 %collective-permute-start.13 = (bf16[2,2,48,384]{3,2,1,0:T(8,128)(2,1)}, bf16[2,2,48,384]{3,2,1,0:T(8,128)(2,1)}, u32[]{:S(2)}, u32[]{:S(2)}) collective-permute-start(bf16[2,2,48,384]{3,2,1,0:T(8,128)(2,1)} %get-tuple-element.35), channel_id=1, source_target_pairs={{0,17},{1,18},{2,19},{3,20},{4,21},{5,22},{6,23},{7,24},{8,25},{9,... | collective-permute-start | bytes 442376 | tf_op jit(solution)/shard_map/ppermute | solution.py:59
  74.3 3.9 %collective-permute-start.10 = (bf16[4,2,48,384]{3,2,1,0:T(8,128)(2,1)}, bf16[4,2,48,384]{3,2,1,0:T(8,128)(2,1)S(1)}, u32[]{:S(2)}, u32[]{:S(2)}) collective-permute-start(bf16[4,2,48,384]{3,2,1,0:T(8,128)(2,1)} %get-tuple-element.39), channel_id=1, source_target_pairs={{0,16},{1,17},{2,18},{3,19},{4,20},{5,21},{6,22},{7,23},{8,24},{9,... | collective-permute-start | bytes 884744 | tf_op jit(solution)/shard_map/ppermute | solution.py:59
  78.2 1.9 %pad_maximum_fusion.3.low = bf16[2,7,48,384]{3,2,1,0:T(8,128)(2,1)} fusion(bf16[2,2,48,384]{3,2,1,0:T(8,128)(2,1)} %collective-permute-done.15, bf16[2,3,48,384]{3,2,1,0:T(8,128)(2,1)} %collective-permute-done.14, bf16[2,2,48,384]{3,2,1,0:T(8,128)(2,1)} %collective-permute-done.13), kind=kLoop, calls=%fused_computation.14 | loop fusion | flops 516096 | bytes 1032192 | tf_op jit(solution)/shard_map/concatenate | solution.py:80
  81.5 2.4 %collective-permute-start.19 = (bf16[4,160,384]{2,1,0:T(8,128)(2,1)S(1)}, bf16[4,160,384]{2,1,0:T(8,128)(2,1)}, u32[]{:S(2)}, u32[]{:S(2)}) collective-permute-start(bf16[4,160,384]{2,1,0:T(8,128)(2,1)S(1)} %slice.109), channel_id=1, source_target_pairs={{0,192},{1,49},{2,194},{3,51},{4,196},{5,53},{6,198},{7,55},{8,200... | collective-permute-start | bytes 1474568 | tf_op jit(solution)/shard_map/ppermute | solution.py:59
  86.5 1.8 %pad_maximum_fusion.2.high = bf16[2,7,48,384]{3,2,1,0:T(8,128)(2,1)} fusion(bf16[2,2,48,384]{3,2,1,0:T(8,128)(2,1)S(1)} %get-tuple-element.45, bf16[2,3,48,384]{3,2,1,0:T(8,128)(2,1)} %get-tuple-element.37, bf16[2,2,48,384]{3,2,1,0:T(8,128)(2,1)S(1)} %get-tuple-element.43), kind=kLoop, calls=%fused_computation.13 | loop fusion | flops 516096 | bytes 1032192 | tf_op jit(solution)/shard_map/concatenate | solution.py:82
  89.2 5.1 %collective-permute-done.18.refs_3_ = bf16[4,160,384]{2,1,0:T(8,128)(2,1)} collective-permute-done((bf16[4,160,384]{2,1,0:T(8,128)(2,1)S(1)}, bf16[4,160,384]{2,1,0:T(8,128)(2,1)}, u32[]{:S(2)}, u32[]{:S(2)}) %collective-permute-start.18) | collective-permute-done | bytes 491552 | tf_op jit(solution)/shard_map/ppermute | solution.py:59
  96.9 3.3 %copy-done.4 = bf16[3,3,1152,384]{3,2,1,0:T(8,128)(2,1)S(1)} copy-done((bf16[3,3,1152,384]{3,2,1,0:T(8,128)(2,1)S(1)}, bf16[3,3,1152,384]{3,2,1,0:T(8,128)(2,1)}, u32[]{:S(2)}) %copy-start.4) | copy-done | bytes 7962648
  100.2 5.1 %conv_first.2.high = bf16[2,5,48,384]{3,2,1,0:T(8,128)(2,1)S(1)} custom-call(s32[1]{0:T(128)} %bitcast.tile, bf16[2,7,48,384]{3,2,1,0:T(8,128)(2,1)S(1)} %copy-done.2, bf16[2,7,48,384]{3,2,1,0:T(8,128)(2,1)S(1)} %copy-done.3, bf16[9,1152,384]{2,1,0:T(8,128)(2,1)S(1)} %bitcast.49, f32[1,384]{1,0:T(1,128)S(1)} %reshape.44.bias, f32[1,384]{1,0:T(1,128)S(1)} %reshape.45.gain), custom_call_target="tpu_custom_call" | custom-call | flops 3822059520 | bytes 7962624 | tf_op jit(solution)/shard_map/conv_first/pallas_call | solution.py:204
  105.3 4.8 %collective-permute-start.12 = (bf16[2,5,48,384]{3,2,1,0:T(8,128)(2,1)S(1)}, bf16[2,5,48,384]{3,2,1,0:T(8,128)(2,1)S(1)}, u32[]{:S(2)}, u32[]{:S(2)}) collective-permute-start(bf16[2,5,48,384]{3,2,1,0:T(8,128)(2,1)S(1)} %conv_first.2.high), channel_id=1, source_target_pairs={{0,1},{1,2},{2,3},{3,4},{4,5},{5,6},{6,7},{7,8},{8,9},{9,10},{10,1... | collective-permute-start | bytes 1105928 | tf_op jit(solution)/shard_map/ppermute | solution.py:59
  110.1 5.1 %conv_first.3.low.high = bf16[2,5,48,384]{3,2,1,0:T(8,128)(2,1)S(1)} custom-call(s32[1]{0:T(128)} %bitcast.tile, bf16[2,7,48,384]{3,2,1,0:T(8,128)(2,1)S(1)} %copy-done.1, bf16[2,7,48,384]{3,2,1,0:T(8,128)(2,1)S(1)} %copy-done.2, bf16[9,1152,384]{2,1,0:T(8,128)(2,1)S(1)} %bitcast.50, f32[1,384]{1,0:T(1,128)S(1)} %reshape.44.bias, f32[1,384]{1,0:T(1,128)S(1)} %reshape.45.gain), custom_call_target="tpu_custom_call" | custom-call | flops 3822059520 | bytes 7962624 | tf_op jit(solution)/shard_map/conv_first/pallas_call | solution.py:204
  115.3 3.3 %assemble.1.weight = bf16[8,1296,384]{2,1,0:T(8,128)(2,1)S(1)} custom-call(s32[8]{0:T(128)S(1)} %stack.90.where, bf16[8,160,384]{2,1,0:T(8,128)(2,1)S(1)} %bitcast.48, bf16[8,160,384]{2,1,0:T(8,128)(2,1)S(1)} %collective-permute-done.16.refs_1_, bf16[8,160,384]{2,1,0:T(8,128)(2,1)S(1)} %collective-permute-done.17.refs_2_, ...), custom_call_target="tpu_custom_call" | custom-call | tf_op jit(solution)/shard_map/assemble/pallas_call | solution.py:146
  118.6 3.7 %second_late.1.refs_0_ = bf16[576,384]{1,0:T(8,128)(2,1)} custom-call(bf16[2,5,48,384]{3,2,1,0:T(8,128)(2,1)S(1)} %conv_first.3.low.high, bf16[2,5,48,384]{3,2,1,0:T(8,128)(2,1)S(1)} %conv_first.2.high, bf16[8,1296,384]{2,1,0:T(8,128)(2,1)S(1)} %assemble.1.weight, bf16[576,384]{1,0:T(8,128)(2,1)S(1)} %bitcast.43, f32[1,384]{1,0:T(1,128)S(1)} %reshape.47.bias), custom_call_target="tpu_custom_call" | custom-call | flops 2293235712 | bytes 7962624 | tf_op jit(solution)/shard_map/second_late/pallas_call | solution.py:236
  122.3 3.7 %second_early.1 = bf16[576,384]{1,0:T(8,128)(2,1)} custom-call(bf16[2,5,48,384]{3,2,1,0:T(8,128)(2,1)S(1)} %collective-permute-done.12.low, bf16[2,5,48,384]{3,2,1,0:T(8,128)(2,1)S(1)} %conv_first.3.low.high, bf16[8,1296,384]{2,1,0:T(8,128)(2,1)S(1)} %assemble.1.weight, bf16[576,384]{1,0:T(8,128)(2,1)S(1)} %bitcast.44, ...), custom_call_target="tpu_custom_call", output_to_operand_aliasing={{}: (5, {})} | custom-call | flops 2293235712 | bytes 7962624 | tf_op jit(solution)/shard_map/second_early/pallas_call | solution.py:236
  (104 shorter events, 29.8 us)
Async XLA Ops:
  6.5 88.3 %all-gather.2.cloned.1.call-start = ((), (), s32[]{:S(2)}) async-start(), calls=%async_computation | async-start | bytes 8460288 | tf_op jit(solution)/shard_map/all_gather | solution.py:272
  7.3 5.0 %collective-permute-start = (bf16[9,72,384]{2,1,0:T(8,128)(2,1)}, bf16[9,72,384]{2,1,0:T(8,128)(2,1)S(1)}, u32[]{:S(2)}, u32[]{:S(2)}) collective-permute-start(bf16[9,72,384]{2,1,0:T(8,128)(2,1)} %bitcast.62), channel_id=1, source_target_pairs={{0,1},{1,0},{2,3},{3,2},{4,5},{5,4},{6,7},{7,6},{8,9},{9,8},{10,11... | collective-permute-start | bytes 1493000 | tf_op jit(solution)/shard_map/ppermute | solution.py:59
  13.6 6.5 %collective-permute-start.2 = (bf16[96,384]{1,0:T(8,128)(2,1)S(1)}, bf16[96,384]{1,0:T(8,128)(2,1)S(1)}, u32[]{:S(2)}, u32[]{:S(2)}) collective-permute-start(bf16[96,384]{1,0:T(8,128)(2,1)S(1)} %pad_maximum_fusion.5), channel_id=1, source_target_pairs={{0,4},{1,13},{2,6},{3,15},{4,8},{5,1},{6,10},{7,3},{8,12},{9,5},{1... | collective-permute-start | bytes 221192 | tf_op jit(solution)/shard_map/ppermute | solution.py:59
  18.0 5.0 %collective-permute-start.1 = (bf16[96,384]{1,0:T(8,128)(2,1)S(1)}, bf16[96,384]{1,0:T(8,128)(2,1)S(1)}, u32[]{:S(2)}, u32[]{:S(2)}) collective-permute-start(bf16[96,384]{1,0:T(8,128)(2,1)S(1)} %pad_maximum_fusion.5), channel_id=1, source_target_pairs={{0,2},{1,15},{2,4},{3,1},{4,6},{5,3},{6,8},{7,5},{8,10},{9,7},{10,... | collective-permute-start | bytes 221192 | tf_op jit(solution)/shard_map/ppermute | solution.py:59
  26.7 6.9 %collective-permute-start.5 = (bf16[96,384]{1,0:T(8,128)(2,1)S(1)}, bf16[96,384]{1,0:T(8,128)(2,1)S(1)}, u32[]{:S(2)}, u32[]{:S(2)}) collective-permute-start(bf16[96,384]{1,0:T(8,128)(2,1)S(1)} %collective-permute-done.2), channel_id=1, source_target_pairs={{0,4},{1,13},{2,6},{3,15},{4,8},{5,1},{6,10},{7,3},{8,12},{9,5},{1... | collective-permute-start | bytes 221192 | tf_op jit(solution)/shard_map/ppermute | solution.py:59
  35.1 5.9 %collective-permute-start.6 = (bf16[8,40,384]{2,1,0:T(8,128)(2,1)S(1)}, bf16[8,40,384]{2,1,0:T(8,128)(2,1)S(1)}, u32[]{:S(2)}, u32[]{:S(2)}) collective-permute-start(bf16[8,40,384]{2,1,0:T(8,128)(2,1)S(1)} %get-tuple-element.30), channel_id=1, source_target_pairs={{0,48},{1,193},{2,50},{3,195},{4,52},{5,197},{6,54},{7,199},{8,56}... | collective-permute-start | bytes 737288 | tf_op jit(solution)/shard_map/ppermute | solution.py:59
  37.8 6.8 %collective-permute-start.7 = (bf16[8,40,384]{2,1,0:T(8,128)(2,1)S(1)}, bf16[8,40,384]{2,1,0:T(8,128)(2,1)S(1)}, u32[]{:S(2)}, u32[]{:S(2)}) collective-permute-start(bf16[8,40,384]{2,1,0:T(8,128)(2,1)S(1)} %get-tuple-element.30), channel_id=1, source_target_pairs={{0,16},{1,65},{2,18},{3,67},{4,20},{5,69},{6,22},{7,71},{8,24},{9,... | collective-permute-start | bytes 737288 | tf_op jit(solution)/shard_map/ppermute | solution.py:59
  40.9 5.5 %collective-permute-start.9 = (bf16[4,40,384]{2,1,0:T(8,128)(2,1)S(1)}, bf16[4,40,384]{2,1,0:T(8,128)(2,1)S(1)}, u32[]{:S(2)}, u32[]{:S(2)}) collective-permute-start(bf16[4,40,384]{2,1,0:T(8,128)(2,1)S(1)} %slice.97), channel_id=1, source_target_pairs={{0,48},{1,193},{2,50},{3,195},{4,52},{5,197},{6,54},{7,199},{8,56}... | collective-permute-start | bytes 368648 | tf_op jit(solution)/shard_map/ppermute | solution.py:59
  44.6 5.4 %collective-permute-start.8 = (bf16[4,40,384]{2,1,0:T(8,128)(2,1)S(1)}, bf16[4,40,384]{2,1,0:T(8,128)(2,1)S(1)}, u32[]{:S(2)}, u32[]{:S(2)}) collective-permute-start(bf16[4,40,384]{2,1,0:T(8,128)(2,1)S(1)} %slice.96), channel_id=1, source_target_pairs={{0,16},{1,65},{2,18},{3,67},{4,20},{5,69},{6,22},{7,71},{8,24},{9,... | collective-permute-start | bytes 368648 | tf_op jit(solution)/shard_map/ppermute | solution.py:59
  50.5 29.6 %collective-permute-start.16 = (bf16[8,160,384]{2,1,0:T(8,128)(2,1)S(1)}, bf16[8,160,384]{2,1,0:T(8,128)(2,1)S(1)}, u32[]{:S(2)}, u32[]{:S(2)}) collective-permute-start(bf16[8,160,384]{2,1,0:T(8,128)(2,1)S(1)} %bitcast.45), channel_id=1, source_target_pairs={{0,64},{1,17},{2,66},{3,19},{4,68},{5,21},{6,70},{7,23},{8,72},{9,... | collective-permute-start | bytes 2949128 | tf_op jit(solution)/shard_map/ppermute | solution.py:59
  51.8 29.6 %collective-permute-start.17 = (bf16[8,160,384]{2,1,0:T(8,128)(2,1)S(1)}, bf16[8,160,384]{2,1,0:T(8,128)(2,1)S(1)}, u32[]{:S(2)}, u32[]{:S(2)}) collective-permute-start(bf16[8,160,384]{2,1,0:T(8,128)(2,1)S(1)} %bitcast.46), channel_id=1, source_target_pairs={{0,192},{1,49},{2,194},{3,51},{4,196},{5,53},{6,198},{7,55},{8,200... | collective-permute-start | bytes 2949128 | tf_op jit(solution)/shard_map/ppermute | solution.py:59
  54.5 12.1 %collective-permute-start.15 = (bf16[2,2,48,384]{3,2,1,0:T(8,128)(2,1)S(1)}, bf16[2,2,48,384]{3,2,1,0:T(8,128)(2,1)}, u32[]{:S(2)}, u32[]{:S(2)}) collective-permute-start(bf16[2,2,48,384]{3,2,1,0:T(8,128)(2,1)S(1)} %get-tuple-element.36), channel_id=1, source_target_pairs={{16,1},{17,2},{18,3},{19,4},{20,5},{21,6},{22,7},{23,8},{24,9},{25... | collective-permute-start | bytes 442376 | tf_op jit(solution)/shard_map/ppermute | solution.py:59
  56.8 17.5 %collective-permute-start.14 = (bf16[2,3,48,384]{3,2,1,0:T(8,128)(2,1)}, bf16[2,3,48,384]{3,2,1,0:T(8,128)(2,1)}, u32[]{:S(2)}, u32[]{:S(2)}) collective-permute-start(bf16[2,3,48,384]{3,2,1,0:T(8,128)(2,1)} %get-tuple-element.37), channel_id=1, source_target_pairs={{0,1},{1,2},{2,3},{3,4},{4,5},{5,6},{6,7},{7,8},{8,9},{9,10},{10,1... | collective-permute-start | bytes 663560 | tf_op jit(solution)/shard_map/ppermute | solution.py:59
  65.3 18.6 %collective-permute-start.11 = (bf16[4,2,48,384]{3,2,1,0:T(8,128)(2,1)}, bf16[4,2,48,384]{3,2,1,0:T(8,128)(2,1)}, u32[]{:S(2)}, u32[]{:S(2)}) collective-permute-start(bf16[4,2,48,384]{3,2,1,0:T(8,128)(2,1)} %get-tuple-element.40), channel_id=1, source_target_pairs={{16,0},{17,1},{18,2},{19,3},{20,4},{21,5},{22,6},{23,7},{24,8},{25... | collective-permute-start | bytes 884744 | tf_op jit(solution)/shard_map/ppermute | solution.py:59
  66.6 6.5 %collective-permute-start.13 = (bf16[2,2,48,384]{3,2,1,0:T(8,128)(2,1)}, bf16[2,2,48,384]{3,2,1,0:T(8,128)(2,1)}, u32[]{:S(2)}, u32[]{:S(2)}) collective-permute-start(bf16[2,2,48,384]{3,2,1,0:T(8,128)(2,1)} %get-tuple-element.35), channel_id=1, source_target_pairs={{0,17},{1,18},{2,19},{3,20},{4,21},{5,22},{6,23},{7,24},{8,25},{9,... | collective-permute-start | bytes 442376 | tf_op jit(solution)/shard_map/ppermute | solution.py:59
  73.1 32.2 %collective-permute-start.20 = (bf16[8,160,384]{2,1,0:T(8,128)(2,1)S(1)}, bf16[8,160,384]{2,1,0:T(8,128)(2,1)}, u32[]{:S(2)}, u32[]{:S(2)}) collective-permute-start(bf16[8,160,384]{2,1,0:T(8,128)(2,1)S(1)} %bitcast.47), channel_id=1, source_target_pairs={{0,1},{1,0},{2,3},{3,2},{4,5},{5,4},{6,7},{7,6},{8,9},{9,8},{10,11... | collective-permute-start | bytes 2949128 | tf_op jit(solution)/shard_map/ppermute | solution.py:59
  74.3 11.2 %collective-permute-start.10 = (bf16[4,2,48,384]{3,2,1,0:T(8,128)(2,1)}, bf16[4,2,48,384]{3,2,1,0:T(8,128)(2,1)S(1)}, u32[]{:S(2)}, u32[]{:S(2)}) collective-permute-start(bf16[4,2,48,384]{3,2,1,0:T(8,128)(2,1)} %get-tuple-element.39), channel_id=1, source_target_pairs={{0,16},{1,17},{2,18},{3,19},{4,20},{5,21},{6,22},{7,23},{8,24},{9,... | collective-permute-start | bytes 884744 | tf_op jit(solution)/shard_map/ppermute | solution.py:59
  80.2 14.1 %collective-permute-start.18 = (bf16[4,160,384]{2,1,0:T(8,128)(2,1)S(1)}, bf16[4,160,384]{2,1,0:T(8,128)(2,1)}, u32[]{:S(2)}, u32[]{:S(2)}) collective-permute-start(bf16[4,160,384]{2,1,0:T(8,128)(2,1)S(1)} %slice.108), channel_id=1, source_target_pairs={{0,64},{1,17},{2,66},{3,19},{4,68},{5,21},{6,70},{7,23},{8,72},{9,... | collective-permute-start | bytes 1474568 | tf_op jit(solution)/shard_map/ppermute | solution.py:59
  81.5 12.9 %collective-permute-start.19 = (bf16[4,160,384]{2,1,0:T(8,128)(2,1)S(1)}, bf16[4,160,384]{2,1,0:T(8,128)(2,1)}, u32[]{:S(2)}, u32[]{:S(2)}) collective-permute-start(bf16[4,160,384]{2,1,0:T(8,128)(2,1)S(1)} %slice.109), channel_id=1, source_target_pairs={{0,192},{1,49},{2,194},{3,51},{4,196},{5,53},{6,198},{7,55},{8,200... | collective-permute-start | bytes 1474568 | tf_op jit(solution)/shard_map/ppermute | solution.py:59
  84.9 30.3 %collective-permute-start.21 = (bf16[8,160,384]{2,1,0:T(8,128)(2,1)S(1)}, bf16[8,160,384]{2,1,0:T(8,128)(2,1)}, u32[]{:S(2)}, u32[]{:S(2)}) collective-permute-start(bf16[8,160,384]{2,1,0:T(8,128)(2,1)S(1)} %collective-permute-done.16.refs_1_), channel_id=1, source_target_pairs={{0,1},{1,0},{2,3},{3,2},{4,5},{5,4},{6,7},{7,6},{8,9},{9,8},{10,11... | collective-permute-start | bytes 2949128 | tf_op jit(solution)/shard_map/ppermute | solution.py:59
  85.5 29.7 %collective-permute-start.22 = (bf16[8,160,384]{2,1,0:T(8,128)(2,1)S(1)}, bf16[8,160,384]{2,1,0:T(8,128)(2,1)}, u32[]{:S(2)}, u32[]{:S(2)}) collective-permute-start(bf16[8,160,384]{2,1,0:T(8,128)(2,1)S(1)} %collective-permute-done.17.refs_2_), channel_id=1, source_target_pairs={{0,1},{1,0},{2,3},{3,2},{4,5},{5,4},{6,7},{7,6},{8,9},{9,8},{10,11... | collective-permute-start | bytes 2949128 | tf_op jit(solution)/shard_map/ppermute | solution.py:59
  94.3 20.9 %collective-permute-start.23 = (bf16[4,160,384]{2,1,0:T(8,128)(2,1)}, bf16[4,160,384]{2,1,0:T(8,128)(2,1)}, u32[]{:S(2)}, u32[]{:S(2)}) collective-permute-start(bf16[4,160,384]{2,1,0:T(8,128)(2,1)} %collective-permute-done.18.refs_3_), channel_id=1, source_target_pairs={{0,1},{1,0},{2,3},{3,2},{4,5},{5,4},{6,7},{7,6},{8,9},{9,8},{10,11... | collective-permute-start | bytes 1474568 | tf_op jit(solution)/shard_map/ppermute | solution.py:59
  94.3 20.9 %collective-permute-start.24 = (bf16[4,160,384]{2,1,0:T(8,128)(2,1)}, bf16[4,160,384]{2,1,0:T(8,128)(2,1)}, u32[]{:S(2)}, u32[]{:S(2)}) collective-permute-start(bf16[4,160,384]{2,1,0:T(8,128)(2,1)} %collective-permute-done.19.refs_4_), channel_id=1, source_target_pairs={{0,1},{1,0},{2,3},{3,2},{4,5},{5,4},{6,7},{7,6},{8,9},{9,8},{10,11... | collective-permute-start | bytes 1474568 | tf_op jit(solution)/shard_map/ppermute | solution.py:59
  105.3 17.0 %collective-permute-start.12 = (bf16[2,5,48,384]{3,2,1,0:T(8,128)(2,1)S(1)}, bf16[2,5,48,384]{3,2,1,0:T(8,128)(2,1)S(1)}, u32[]{:S(2)}, u32[]{:S(2)}) collective-permute-start(bf16[2,5,48,384]{3,2,1,0:T(8,128)(2,1)S(1)} %conv_first.2.high), channel_id=1, source_target_pairs={{0,1},{1,2},{2,3},{3,4},{4,5},{5,6},{6,7},{7,8},{8,9},{9,10},{10,1... | collective-permute-start | bytes 1105928 | tf_op jit(solution)/shard_map/ppermute | solution.py:59
  (13 other events, 88.7 us)
Sparse Core Ops, SparseCore 0:
  9.1 59.6 all-gather.1

commit v3 on v2

--- a/solution.py
+++ b/solution.py
@@ -69,21 +69,13 @@
     return lax.optimization_barrier((value, others))[0]
 
 
-def grow(own):
-    tail = own[2:]
+def grow_rows(own):
     above = send(own[:, 1:], neighbours(1, 0))
     below = send(own[:, :2], neighbours(-1, 0))
-    earlier = send(tail, neighbours(0, 1))
-    corner_above = send(tail[:, 1:], neighbours(1, 1))
-    corner_below = send(tail[:, :2], neighbours(-1, 1))
-    return [
-        jnp.concatenate([corner_above, earlier, corner_below], axis=1),
-        jnp.concatenate([above[:2], own[:2], below[:2]], axis=1),
-        jnp.concatenate([above[2:], own[2:], below[2:]], axis=1),
-    ]
-
-
-def gather(weight, y, x, z, core):
+    return jnp.concatenate([above, own, below], axis=1)
+
+
+def gather(weight, y, x, z, core, rows):
     first_core = core == 0
     other = send(weight, SWAP)
     slab = jnp.concatenate(
@@ -95,6 +87,7 @@
         axis=0,
     )
     one, two = send(both, Z1), send(both, Z2)
+    two = after(two, rows)
     three, four = send(two, Z1), send(two, Z2)
     sent = jnp.stack([one, two, three])
     other = send(sent, SWAP)
@@ -114,8 +107,7 @@
     spot = lax.rem(4 - jnp.where(first_core, x, y), 4)
     turned = lax.dynamic_slice_in_dim(jnp.stack(parts + parts), spot, 4, axis=0)
     chunk = turned.transpose(1, 0, 2, 3).reshape(NZ, BLOCK, C)
-    pieces = [chunk, *ring(chunk, CROSS_UP, CROSS_DOWN)]
-    return [*pieces, *(send(v, SWAP) for v in pieces), last], chunk
+    return [chunk, *ring(chunk, CROSS_UP, CROSS_DOWN)], last
 
 
 def assemble_kernel(where, *refs):
@@ -270,16 +262,20 @@
     row = lambda v: v.reshape(1, C)
 
     whole_first = lax.all_gather(weight_first, ("z", "c"), axis=2, tiled=True)
-    pieces, chunk = gather(weight_second.reshape(9, 72, C), y, x, z, core)
-    first = activate(after(latent, chunk), gain_first).astype(BF)
-    earlier, low, high = grow(first)
+    first = activate(latent, gain_first).astype(BF)
+    grown = grow_rows(first)
+    low, high = grown[:2], grown[2:]
+    pieces, last = gather(weight_second.reshape(9, 72, C), y, x, z, core, grown)
+    earlier = send(after(high, pieces[0]), neighbours(0, 1))
+    others = [send(v, SWAP) for v in pieces[:3]]
 
     scales = row(bias_first), row(gain_second), tile
     whole_first = whole_first.reshape(9, 3 * C, C)
     second_high = conv_first(low, high, whole_first, *scales)
     second_earlier = send(second_high, neighbours(0, 1))
+    others += [send(v, SWAP) for v in after(pieces[3:], second_high)]
     second_low = conv_first(earlier, low, whole_first, *scales)
-    whole_second = assemble(after(pieces, second_low), where)
+    whole_second = assemble(after([*pieces, *others, last], second_low), where)
     rest = whole_second, latent.reshape(576, C), row(bias_second)
     partial = conv_second(second_low, second_high, *rest, None)
     return conv_second(second_earlier, second_low, *rest, partial).reshape(4, 3, 48, C)

time: 134 us -> 136 us (1.015)
  waiting for transfers between devices: 23.9 us -> 30.8 us
  starting transfers between devices: 55.9 us -> 49.8 us
  other arithmetic: 6.8 us -> 4.05 us
  local copies, waits for them, and re-layouts: 11.5 us -> 14 us
  Pallas kernels: 20.9 us -> 22.9 us
    ppermute x25 -> x23, waiting for transfers between devices: 23.2 us -> 30.1 us  [send(): return lax.ppermute(value, AXES, pairs)]
    ppermute x25 -> x23, starting transfers between devices: 55.9 us -> 49.8 us  [send(): return lax.ppermute(value, AXES, pairs)]
    unnamed x33 -> x37, local copies, waits for them, and re-layouts: 6.67 us -> 10.6 us
    concatenate x3 -> x1, other arithmetic: 4.64 us -> 1.13 us  [grow_rows(): return jnp.concatenate([above, own, below], axis=1)]
    slice x5 -> x2, local copies, waits for them, and re-layouts: 3.43 us -> 1.13 us  [the longest x1 1.07 us: local(): low, high = (grown[:2], grown[2:])]
    pallas_call x2, Pallas kernels: 10.2 us -> 12.2 us  [conv_first(): pl.pallas_call(first_kernel, out_shape=jax.ShapeDtypeStruct((2, 5, 48, C)...]
  transfers between devices with their start and end apart: 26 -> 24, of which waited for: 9 -> 9; matrix products, arithmetic and copies ran while one was open for 9% -> 6% of each run, Pallas kernels for 13% -> 14%
where the time goes in v3:
time: 136 us; the launch traced here: 135 us
  starting transfers between devices  49.8 us (37%)
  waiting for transfers between devices  30.8 us (23%)
  Pallas kernels  22.9 us (17%)
  local copies, waits for them, and re-layouts  14 us (10%)
  between operations  13.9 us (10%)
  other arithmetic  4.05 us (3%)
    ppermute x23, starting transfers between devices, send(): return lax.ppermute(value, AXES, pairs)  49.8 us
    ppermute x23, waiting for transfers between devices, send(): return lax.ppermute(value, AXES, pairs)  30.1 us
    pallas_call x2, Pallas kernels, conv_first(): pl.pallas_call(first_kernel, out_shape=jax.ShapeDtypeStruct((2, 5, 48, C)...  12.2 us
    unnamed x37, local copies, waits for them, and re-layouts  10.6 us
    pallas_call x2, Pallas kernels, conv_second(): pl.pallas_call(functools.partial(second_kernel, start), out_shape=jax.Sha...  7.42 us
    pallas_call x1, Pallas kernels, assemble(): pl.pallas_call(assemble_kernel, out_shape=jax.ShapeDtypeStruct((NZ, 9 * S...  3.28 us
  transfers between devices with their start and end apart: 24, of which 9 were waited for; matrix products, arithmetic and copies ran while one was open for 6% of the time, Pallas kernels for 14%

profile of v3, /device:TPU:1, one launch (start us, length us, event | category | flops | bytes accessed | tf_op | source)
XLA Modules:
  0.0 135.4 jit_solution(8514284063922240029)
XLA Ops:
  7.3 3.3 %collective-permute-start.3 = (bf16[9,72,384]{2,1,0:T(8,128)(2,1)}, bf16[9,72,384]{2,1,0:T(8,128)(2,1)S(1)}, u32[]{:S(2)}, u32[]{:S(2)}) collective-permute-start(bf16[9,72,384]{2,1,0:T(8,128)(2,1)} %bitcast.62), channel_id=1, source_target_pairs={{0,1},{1,0},{2,3},{3,2},{4,5},{5,4},{6,7},{7,6},{8,9},{9,8},{10,11... | collective-permute-start | bytes 1493000 | tf_op jit(solution)/shard_map/ppermute | solution.py:59
  14.2 4.0 %collective-permute-start = (bf16[4,2,48,384]{3,2,1,0:T(8,128)(2,1)S(1)}, bf16[4,2,48,384]{3,2,1,0:T(8,128)(2,1)S(1)}, u32[]{:S(2)}, u32[]{:S(2)}) collective-permute-start(bf16[4,2,48,384]{3,2,1,0:T(8,128)(2,1)S(1)} %get-tuple-element.45), channel_id=1, source_target_pairs={{0,16},{1,17},{2,18},{3,19},{4,20},{5,21},{6,22},{7,23},{8,24},{9,... | collective-permute-start | bytes 884744 | tf_op jit(solution)/shard_map/ppermute | solution.py:59
  18.6 4.4 %collective-permute-start.5 = (bf16[96,384]{1,0:T(8,128)(2,1)S(1)}, bf16[96,384]{1,0:T(8,128)(2,1)S(1)}, u32[]{:S(2)}, u32[]{:S(2)}) collective-permute-start(bf16[96,384]{1,0:T(8,128)(2,1)S(1)} %pad_maximum_fusion.3), channel_id=1, source_target_pairs={{0,4},{1,13},{2,6},{3,15},{4,8},{5,1},{6,10},{7,3},{8,12},{9,5},{1... | collective-permute-start | bytes 221192 | tf_op jit(solution)/shard_map/ppermute | solution.py:59
  25.5 3.8 %collective-permute-start.4 = (bf16[96,384]{1,0:T(8,128)(2,1)S(1)}, bf16[96,384]{1,0:T(8,128)(2,1)S(1)}, u32[]{:S(2)}, u32[]{:S(2)}) collective-permute-start(bf16[96,384]{1,0:T(8,128)(2,1)S(1)} %pad_maximum_fusion.3), channel_id=1, source_target_pairs={{0,2},{1,15},{2,4},{3,1},{4,6},{5,3},{6,8},{7,5},{8,10},{9,7},{10,... | collective-permute-start | bytes 221192 | tf_op jit(solution)/shard_map/ppermute | solution.py:59
  31.9 2.5 %collective-permute-done.6 = bf16[96,384]{1,0:T(8,128)(2,1)S(1)} collective-permute-done((bf16[96,384]{1,0:T(8,128)(2,1)S(1)}, bf16[96,384]{1,0:T(8,128)(2,1)S(1)}, u32[]{:S(2)}, u32[]{:S(2)}) %collective-permute-start.6) | collective-permute-done | bytes 73760 | tf_op jit(solution)/shard_map/ppermute | solution.py:59
  34.5 2.6 %collective-permute-start.7 = (bf16[3,96,384]{2,1,0:T(8,128)(2,1)S(1)}, bf16[3,96,384]{2,1,0:T(8,128)(2,1)S(1)}, u32[]{:S(2)}, u32[]{:S(2)}) collective-permute-start(bf16[3,96,384]{2,1,0:T(8,128)(2,1)S(1)} %pad_maximum_fusion.2), channel_id=1, source_target_pairs={{0,1},{1,0},{2,3},{3,2},{4,5},{5,4},{6,7},{7,6},{8,9},{9,8},{10,11... | collective-permute-start | bytes 663560 | tf_op jit(solution)/shard_map/ppermute | solution.py:59
  37.1 2.3 %collective-permute-start.8 = (bf16[96,384]{1,0:T(8,128)(2,1)S(1)}, bf16[96,384]{1,0:T(8,128)(2,1)S(1)}, u32[]{:S(2)}, u32[]{:S(2)}) collective-permute-start(bf16[96,384]{1,0:T(8,128)(2,1)S(1)} %collective-permute-done.5), channel_id=1, source_target_pairs={{0,4},{1,13},{2,6},{3,15},{4,8},{5,1},{6,10},{7,3},{8,12},{9,5},{1... | collective-permute-start | bytes 221192 | tf_op jit(solution)/shard_map/ppermute | solution.py:59
  39.5 4.1 %collective-permute-done.8 = bf16[96,384]{1,0:T(8,128)(2,1)S(1)} collective-permute-done((bf16[96,384]{1,0:T(8,128)(2,1)S(1)}, bf16[96,384]{1,0:T(8,128)(2,1)S(1)}, u32[]{:S(2)}, u32[]{:S(2)}) %collective-permute-start.8) | collective-permute-done | bytes 73760 | tf_op jit(solution)/shard_map/ppermute | solution.py:59
  44.9 8.4 %collective-permute-start.9 = (bf16[8,40,384]{2,1,0:T(8,128)(2,1)S(1)}, bf16[8,40,384]{2,1,0:T(8,128)(2,1)S(1)}, u32[]{:S(2)}, u32[]{:S(2)}) collective-permute-start(bf16[8,40,384]{2,1,0:T(8,128)(2,1)S(1)} %get-tuple-element.36), channel_id=1, source_target_pairs={{0,48},{1,193},{2,50},{3,195},{4,52},{5,197},{6,54},{7,199},{8,56}... | collective-permute-start | bytes 737288 | tf_op jit(solution)/shard_map/ppermute | solution.py:59
  53.3 3.1 %collective-permute-done.9 = bf16[8,40,384]{2,1,0:T(8,128)(2,1)S(1)} collective-permute-done((bf16[8,40,384]{2,1,0:T(8,128)(2,1)S(1)}, bf16[8,40,384]{2,1,0:T(8,128)(2,1)S(1)}, u32[]{:S(2)}, u32[]{:S(2)}) %collective-permute-start.9) | collective-permute-done | bytes 245792 | tf_op jit(solution)/shard_map/ppermute | solution.py:59
  56.4 3.6 %collective-permute-start.12 = (bf16[4,40,384]{2,1,0:T(8,128)(2,1)S(1)}, bf16[4,40,384]{2,1,0:T(8,128)(2,1)S(1)}, u32[]{:S(2)}, u32[]{:S(2)}) collective-permute-start(bf16[4,40,384]{2,1,0:T(8,128)(2,1)S(1)} %slice.74), channel_id=1, source_target_pairs={{0,48},{1,193},{2,50},{3,195},{4,52},{5,197},{6,54},{7,199},{8,56}... | collective-permute-start | bytes 368648 | tf_op jit(solution)/shard_map/ppermute | solution.py:59
  61.9 3.6 %collective-permute-done.11 = bf16[4,40,384]{2,1,0:T(8,128)(2,1)S(1)} collective-permute-done((bf16[4,40,384]{2,1,0:T(8,128)(2,1)S(1)}, bf16[4,40,384]{2,1,0:T(8,128)(2,1)S(1)}, u32[]{:S(2)}, u32[]{:S(2)}) %collective-permute-start.11) | collective-permute-done | bytes 122912 | tf_op jit(solution)/shard_map/ppermute | solution.py:59
  66.1 2.7 %collective-permute-start.15 = (bf16[8,160,384]{2,1,0:T(8,128)(2,1)S(1)}, bf16[8,160,384]{2,1,0:T(8,128)(2,1)S(1)}, u32[]{:S(2)}, u32[]{:S(2)}) collective-permute-start(bf16[8,160,384]{2,1,0:T(8,128)(2,1)S(1)} %bitcast.46), channel_id=1, source_target_pairs={{0,192},{1,49},{2,194},{3,51},{4,196},{5,53},{6,198},{7,55},{8,200... | collective-permute-start | bytes 2949128 | tf_op jit(solution)/shard_map/ppermute | solution.py:59
  68.7 11.8 %collective-permute-done.14.refs_1_ = bf16[8,160,384]{2,1,0:T(8,128)(2,1)S(1)} collective-permute-done((bf16[8,160,384]{2,1,0:T(8,128)(2,1)S(1)}, bf16[8,160,384]{2,1,0:T(8,128)(2,1)S(1)}, u32[]{:S(2)}, u32[]{:S(2)}) %collective-permute-start.14) | collective-permute-done | bytes 983072 | tf_op jit(solution)/shard_map/ppermute | solution.py:59
  80.7 1.9 %collective-permute-start.18 = (bf16[8,160,384]{2,1,0:T(8,128)(2,1)S(1)}, bf16[8,160,384]{2,1,0:T(8,128)(2,1)}, u32[]{:S(2)}, u32[]{:S(2)}) collective-permute-start(bf16[8,160,384]{2,1,0:T(8,128)(2,1)S(1)} %bitcast.47), channel_id=1, source_target_pairs={{0,1},{1,0},{2,3},{3,2},{4,5},{5,4},{6,7},{7,6},{8,9},{9,8},{10,11... | collective-permute-start | bytes 2949128 | tf_op jit(solution)/shard_map/ppermute | solution.py:59
  87.2 3.5 %collective-permute-start.19 = (bf16[8,160,384]{2,1,0:T(8,128)(2,1)S(1)}, bf16[8,160,384]{2,1,0:T(8,128)(2,1)}, u32[]{:S(2)}, u32[]{:S(2)}) collective-permute-start(bf16[8,160,384]{2,1,0:T(8,128)(2,1)S(1)} %collective-permute-done.14.refs_1_), channel_id=1, source_target_pairs={{0,1},{1,0},{2,3},{3,2},{4,5},{5,4},{6,7},{7,6},{8,9},{9,8},{10,11... | collective-permute-start | bytes 2949128 | tf_op jit(solution)/shard_map/ppermute | solution.py:59
  93.5 3.3 %copy-done.5 = bf16[3,3,1152,384]{3,2,1,0:T(8,128)(2,1)S(1)} copy-done((bf16[3,3,1152,384]{3,2,1,0:T(8,128)(2,1)S(1)}, bf16[3,3,1152,384]{3,2,1,0:T(8,128)(2,1)}, u32[]{:S(2)}) %copy-start.5) | copy-done | bytes 7962648
  96.8 6.1 %conv_first.2.high = bf16[2,5,48,384]{3,2,1,0:T(8,128)(2,1)S(1)} custom-call(s32[1]{0:T(128)} %bitcast.tile, bf16[2,7,48,384]{3,2,1,0:T(8,128)(2,1)S(1)} %copy-done.1, bf16[2,7,48,384]{3,2,1,0:T(8,128)(2,1)} %get-tuple-element.21.high, bf16[9,1152,384]{2,1,0:T(8,128)(2,1)S(1)} %bitcast.49, f32[1,384]{1,0:T(1,128)S(1)} %reshape.41.bias, ...), custom_call_target="tpu_custom_call" | custom-call | flops 3822059520 | bytes 7962624 | tf_op jit(solution)/shard_map/conv_first/pallas_call | solution.py:196
  105.2 2.1 %collective-permute-start.2 = (bf16[2,5,48,384]{3,2,1,0:T(8,128)(2,1)}, bf16[2,5,48,384]{3,2,1,0:T(8,128)(2,1)S(1)}, u32[]{:S(2)}, u32[]{:S(2)}) collective-permute-start(bf16[2,5,48,384]{3,2,1,0:T(8,128)(2,1)} %copy-done.3), channel_id=1, source_target_pairs={{0,1},{1,2},{2,3},{3,4},{4,5},{5,6},{6,7},{7,8},{8,9},{9,10},{10,1... | collective-permute-start | bytes 1105928 | tf_op jit(solution)/shard_map/ppermute | solution.py:59
  108.4 3.3 %copy-done.6 = bf16[3,3,1152,384]{3,2,1,0:T(8,128)(2,1)S(1)} copy-done((bf16[3,3,1152,384]{3,2,1,0:T(8,128)(2,1)S(1)}, bf16[3,3,1152,384]{3,2,1,0:T(8,128)(2,1)}, u32[]{:S(2)}) %copy-start.6) | copy-done | bytes 7962648
  111.6 6.1 %conv_first.3.low.high = bf16[2,5,48,384]{3,2,1,0:T(8,128)(2,1)S(1)} custom-call(s32[1]{0:T(128)} %bitcast.tile, bf16[2,7,48,384]{3,2,1,0:T(8,128)(2,1)} %collective-permute-done.13.low, bf16[2,7,48,384]{3,2,1,0:T(8,128)(2,1)S(1)} %copy-done.2, bf16[9,1152,384]{2,1,0:T(8,128)(2,1)S(1)} %bitcast.50, f32[1,384]{1,0:T(1,128)S(1)} %reshape.41.bias, ...), custom_call_target="tpu_custom_call" | custom-call | flops 3822059520 | bytes 7962624 | tf_op jit(solution)/shard_map/conv_first/pallas_call | solution.py:196
  117.8 3.3 %assemble.1.weight = bf16[8,1296,384]{2,1,0:T(8,128)(2,1)S(1)} custom-call(s32[8]{0:T(128)S(1)} %stack.90.where, bf16[8,160,384]{2,1,0:T(8,128)(2,1)S(1)} %bitcast.48, bf16[8,160,384]{2,1,0:T(8,128)(2,1)S(1)} %collective-permute-done.14.refs_1_, bf16[8,160,384]{2,1,0:T(8,128)(2,1)S(1)} %collective-permute-done.15.refs_2_, ...), custom_call_target="tpu_custom_call" | custom-call | tf_op jit(solution)/shard_map/assemble/pallas_call | solution.py:138
  121.1 3.7 %second_late.1.refs_0_ = bf16[576,384]{1,0:T(8,128)(2,1)} custom-call(bf16[2,5,48,384]{3,2,1,0:T(8,128)(2,1)S(1)} %conv_first.3.low.high, bf16[2,5,48,384]{3,2,1,0:T(8,128)(2,1)S(1)} %copy-done.4, bf16[8,1296,384]{2,1,0:T(8,128)(2,1)S(1)} %assemble.1.weight, bf16[576,384]{1,0:T(8,128)(2,1)S(1)} %bitcast.43, f32[1,384]{1,0:T(1,128)S(1)} %reshape.47.bias), custom_call_target="tpu_custom_call" | custom-call | flops 2293235712 | bytes 7962624 | tf_op jit(solution)/shard_map/second_late/pallas_call | solution.py:228
  124.8 3.7 %second_early.1 = bf16[576,384]{1,0:T(8,128)(2,1)} custom-call(bf16[2,5,48,384]{3,2,1,0:T(8,128)(2,1)S(1)} %collective-permute-done.2.low, bf16[2,5,48,384]{3,2,1,0:T(8,128)(2,1)S(1)} %conv_first.3.low.high, bf16[8,1296,384]{2,1,0:T(8,128)(2,1)S(1)} %assemble.1.weight, bf16[576,384]{1,0:T(8,128)(2,1)S(1)} %bitcast.44, ...), custom_call_target="tpu_custom_call", output_to_operand_aliasing={{}: (5, {})} | custom-call | flops 2293235712 | bytes 7962624 | tf_op jit(solution)/shard_map/second_early/pallas_call | solution.py:228
  (99 shorter events, 24.4 us)
Async XLA Ops:
  6.5 86.0 %all-gather.2.cloned.1.call-start = ((), (), s32[]{:S(2)}) async-start(), calls=%async_computation | async-start | bytes 8460288 | tf_op jit(solution)/shard_map/all_gather | solution.py:264
  7.3 11.0 %collective-permute-start.3 = (bf16[9,72,384]{2,1,0:T(8,128)(2,1)}, bf16[9,72,384]{2,1,0:T(8,128)(2,1)S(1)}, u32[]{:S(2)}, u32[]{:S(2)}) collective-permute-start(bf16[9,72,384]{2,1,0:T(8,128)(2,1)} %bitcast.62), channel_id=1, source_target_pairs={{0,1},{1,0},{2,3},{3,2},{4,5},{5,4},{6,7},{7,6},{8,9},{9,8},{10,11... | collective-permute-start | bytes 1493000 | tf_op jit(solution)/shard_map/ppermute | solution.py:59
  12.9 10.5 %collective-permute-start.1 = (bf16[4,2,48,384]{3,2,1,0:T(8,128)(2,1)S(1)}, bf16[4,2,48,384]{3,2,1,0:T(8,128)(2,1)S(1)}, u32[]{:S(2)}, u32[]{:S(2)}) collective-permute-start(bf16[4,2,48,384]{3,2,1,0:T(8,128)(2,1)S(1)} %get-tuple-element.46), channel_id=1, source_target_pairs={{16,0},{17,1},{18,2},{19,3},{20,4},{21,5},{22,6},{23,7},{24,8},{25... | collective-permute-start | bytes 884744 | tf_op jit(solution)/shard_map/ppermute | solution.py:59
  14.2 10.1 %collective-permute-start = (bf16[4,2,48,384]{3,2,1,0:T(8,128)(2,1)S(1)}, bf16[4,2,48,384]{3,2,1,0:T(8,128)(2,1)S(1)}, u32[]{:S(2)}, u32[]{:S(2)}) collective-permute-start(bf16[4,2,48,384]{3,2,1,0:T(8,128)(2,1)S(1)} %get-tuple-element.45), channel_id=1, source_target_pairs={{0,16},{1,17},{2,18},{3,19},{4,20},{5,21},{6,22},{7,23},{8,24},{9,... | collective-permute-start | bytes 884744 | tf_op jit(solution)/shard_map/ppermute | solution.py:59
  18.6 10.7 %collective-permute-start.5 = (bf16[96,384]{1,0:T(8,128)(2,1)S(1)}, bf16[96,384]{1,0:T(8,128)(2,1)S(1)}, u32[]{:S(2)}, u32[]{:S(2)}) collective-permute-start(bf16[96,384]{1,0:T(8,128)(2,1)S(1)} %pad_maximum_fusion.3), channel_id=1, source_target_pairs={{0,4},{1,13},{2,6},{3,15},{4,8},{5,1},{6,10},{7,3},{8,12},{9,5},{1... | collective-permute-start | bytes 221192 | tf_op jit(solution)/shard_map/ppermute | solution.py:59
  25.5 6.5 %collective-permute-start.4 = (bf16[96,384]{1,0:T(8,128)(2,1)S(1)}, bf16[96,384]{1,0:T(8,128)(2,1)S(1)}, u32[]{:S(2)}, u32[]{:S(2)}) collective-permute-start(bf16[96,384]{1,0:T(8,128)(2,1)S(1)} %pad_maximum_fusion.3), channel_id=1, source_target_pairs={{0,2},{1,15},{2,4},{3,1},{4,6},{5,3},{6,8},{7,5},{8,10},{9,7},{10,... | collective-permute-start | bytes 221192 | tf_op jit(solution)/shard_map/ppermute | solution.py:59
  29.3 5.2 %collective-permute-start.6 = (bf16[96,384]{1,0:T(8,128)(2,1)S(1)}, bf16[96,384]{1,0:T(8,128)(2,1)S(1)}, u32[]{:S(2)}, u32[]{:S(2)}) collective-permute-start(bf16[96,384]{1,0:T(8,128)(2,1)S(1)} %collective-permute-done.5), channel_id=1, source_target_pairs={{0,2},{1,15},{2,4},{3,1},{4,6},{5,3},{6,8},{7,5},{8,10},{9,7},{10,... | collective-permute-start | bytes 221192 | tf_op jit(solution)/shard_map/ppermute | solution.py:59
  34.5 4.9 %collective-permute-start.7 = (bf16[3,96,384]{2,1,0:T(8,128)(2,1)S(1)}, bf16[3,96,384]{2,1,0:T(8,128)(2,1)S(1)}, u32[]{:S(2)}, u32[]{:S(2)}) collective-permute-start(bf16[3,96,384]{2,1,0:T(8,128)(2,1)S(1)} %pad_maximum_fusion.2), channel_id=1, source_target_pairs={{0,1},{1,0},{2,3},{3,2},{4,5},{5,4},{6,7},{7,6},{8,9},{9,8},{10,11... | collective-permute-start | bytes 663560 | tf_op jit(solution)/shard_map/ppermute | solution.py:59
  37.1 6.5 %collective-permute-start.8 = (bf16[96,384]{1,0:T(8,128)(2,1)S(1)}, bf16[96,384]{1,0:T(8,128)(2,1)S(1)}, u32[]{:S(2)}, u32[]{:S(2)}) collective-permute-start(bf16[96,384]{1,0:T(8,128)(2,1)S(1)} %collective-permute-done.5), channel_id=1, source_target_pairs={{0,4},{1,13},{2,6},{3,15},{4,8},{5,1},{6,10},{7,3},{8,12},{9,5},{1... | collective-permute-start | bytes 221192 | tf_op jit(solution)/shard_map/ppermute | solution.py:59
  44.9 11.5 %collective-permute-start.9 = (bf16[8,40,384]{2,1,0:T(8,128)(2,1)S(1)}, bf16[8,40,384]{2,1,0:T(8,128)(2,1)S(1)}, u32[]{:S(2)}, u32[]{:S(2)}) collective-permute-start(bf16[8,40,384]{2,1,0:T(8,128)(2,1)S(1)} %get-tuple-element.36), channel_id=1, source_target_pairs={{0,48},{1,193},{2,50},{3,195},{4,52},{5,197},{6,54},{7,199},{8,56}... | collective-permute-start | bytes 737288 | tf_op jit(solution)/shard_map/ppermute | solution.py:59
  53.3 6.8 %collective-permute-start.10 = (bf16[8,40,384]{2,1,0:T(8,128)(2,1)S(1)}, bf16[8,40,384]{2,1,0:T(8,128)(2,1)S(1)}, u32[]{:S(2)}, u32[]{:S(2)}) collective-permute-start(bf16[8,40,384]{2,1,0:T(8,128)(2,1)S(1)} %get-tuple-element.36), channel_id=1, source_target_pairs={{0,16},{1,65},{2,18},{3,67},{4,20},{5,69},{6,22},{7,71},{8,24},{9,... | collective-permute-start | bytes 737288 | tf_op jit(solution)/shard_map/ppermute | solution.py:59
  56.4 5.5 %collective-permute-start.12 = (bf16[4,40,384]{2,1,0:T(8,128)(2,1)S(1)}, bf16[4,40,384]{2,1,0:T(8,128)(2,1)S(1)}, u32[]{:S(2)}, u32[]{:S(2)}) collective-permute-start(bf16[4,40,384]{2,1,0:T(8,128)(2,1)S(1)} %slice.74), channel_id=1, source_target_pairs={{0,48},{1,193},{2,50},{3,195},{4,52},{5,197},{6,54},{7,199},{8,56}... | collective-permute-start | bytes 368648 | tf_op jit(solution)/shard_map/ppermute | solution.py:59
  60.0 5.4 %collective-permute-start.11 = (bf16[4,40,384]{2,1,0:T(8,128)(2,1)S(1)}, bf16[4,40,384]{2,1,0:T(8,128)(2,1)S(1)}, u32[]{:S(2)}, u32[]{:S(2)}) collective-permute-start(bf16[4,40,384]{2,1,0:T(8,128)(2,1)S(1)} %slice.73), channel_id=1, source_target_pairs={{0,16},{1,65},{2,18},{3,67},{4,20},{5,69},{6,22},{7,71},{8,24},{9,... | collective-permute-start | bytes 368648 | tf_op jit(solution)/shard_map/ppermute | solution.py:59
  66.0 14.5 %collective-permute-start.14 = (bf16[8,160,384]{2,1,0:T(8,128)(2,1)S(1)}, bf16[8,160,384]{2,1,0:T(8,128)(2,1)S(1)}, u32[]{:S(2)}, u32[]{:S(2)}) collective-permute-start(bf16[8,160,384]{2,1,0:T(8,128)(2,1)S(1)} %bitcast.45), channel_id=1, source_target_pairs={{0,64},{1,17},{2,66},{3,19},{4,68},{5,21},{6,70},{7,23},{8,72},{9,... | collective-permute-start | bytes 2949128 | tf_op jit(solution)/shard_map/ppermute | solution.py:59
  66.1 19.5 %collective-permute-start.15 = (bf16[8,160,384]{2,1,0:T(8,128)(2,1)S(1)}, bf16[8,160,384]{2,1,0:T(8,128)(2,1)S(1)}, u32[]{:S(2)}, u32[]{:S(2)}) collective-permute-start(bf16[8,160,384]{2,1,0:T(8,128)(2,1)S(1)} %bitcast.46), channel_id=1, source_target_pairs={{0,192},{1,49},{2,194},{3,51},{4,196},{5,53},{6,198},{7,55},{8,200... | collective-permute-start | bytes 2949128 | tf_op jit(solution)/shard_map/ppermute | solution.py:59
  80.6 10.1 %collective-permute-start.16 = (bf16[4,160,384]{2,1,0:T(8,128)(2,1)S(1)}, bf16[4,160,384]{2,1,0:T(8,128)(2,1)}, u32[]{:S(2)}, u32[]{:S(2)}) collective-permute-start(bf16[4,160,384]{2,1,0:T(8,128)(2,1)S(1)} %slice.75), channel_id=1, source_target_pairs={{0,64},{1,17},{2,66},{3,19},{4,68},{5,21},{6,70},{7,23},{8,72},{9,... | collective-permute-start | bytes 1474568 | tf_op jit(solution)/shard_map/ppermute | solution.py:59
  80.7 24.5 %collective-permute-start.18 = (bf16[8,160,384]{2,1,0:T(8,128)(2,1)S(1)}, bf16[8,160,384]{2,1,0:T(8,128)(2,1)}, u32[]{:S(2)}, u32[]{:S(2)}) collective-permute-start(bf16[8,160,384]{2,1,0:T(8,128)(2,1)S(1)} %bitcast.47), channel_id=1, source_target_pairs={{0,1},{1,0},{2,3},{3,2},{4,5},{5,4},{6,7},{7,6},{8,9},{9,8},{10,11... | collective-permute-start | bytes 2949128 | tf_op jit(solution)/shard_map/ppermute | solution.py:59
  83.7 20.0 %collective-permute-start.13 = (bf16[2,7,48,384]{3,2,1,0:T(8,128)(2,1)}, bf16[2,7,48,384]{3,2,1,0:T(8,128)(2,1)}, u32[]{:S(2)}, u32[]{:S(2)}) collective-permute-start(bf16[2,7,48,384]{3,2,1,0:T(8,128)(2,1)} %get-tuple-element.21.high), channel_id=1, source_target_pairs={{0,1},{1,2},{2,3},{3,4},{4,5},{5,6},{6,7},{7,8},{8,9},{9,10},{10,1... | collective-permute-start | bytes 1548296 | tf_op jit(solution)/shard_map/ppermute | solution.py:59
  86.4 17.2 %collective-permute-start.17 = (bf16[4,160,384]{2,1,0:T(8,128)(2,1)}, bf16[4,160,384]{2,1,0:T(8,128)(2,1)}, u32[]{:S(2)}, u32[]{:S(2)}) collective-permute-start(bf16[4,160,384]{2,1,0:T(8,128)(2,1)} %slice.76), channel_id=1, source_target_pairs={{0,192},{1,49},{2,194},{3,51},{4,196},{5,53},{6,198},{7,55},{8,200... | collective-permute-start | bytes 1474568 | tf_op jit(solution)/shard_map/ppermute | solution.py:59
  87.2 30.6 %collective-permute-start.19 = (bf16[8,160,384]{2,1,0:T(8,128)(2,1)S(1)}, bf16[8,160,384]{2,1,0:T(8,128)(2,1)}, u32[]{:S(2)}, u32[]{:S(2)}) collective-permute-start(bf16[8,160,384]{2,1,0:T(8,128)(2,1)S(1)} %collective-permute-done.14.refs_1_), channel_id=1, source_target_pairs={{0,1},{1,0},{2,3},{3,2},{4,5},{5,4},{6,7},{7,6},{8,9},{9,8},{10,11... | collective-permute-start | bytes 2949128 | tf_op jit(solution)/shard_map/ppermute | solution.py:59
  90.7 27.1 %collective-permute-start.20 = (bf16[8,160,384]{2,1,0:T(8,128)(2,1)S(1)}, bf16[8,160,384]{2,1,0:T(8,128)(2,1)}, u32[]{:S(2)}, u32[]{:S(2)}) collective-permute-start(bf16[8,160,384]{2,1,0:T(8,128)(2,1)S(1)} %collective-permute-done.15.refs_2_), channel_id=1, source_target_pairs={{0,1},{1,0},{2,3},{3,2},{4,5},{5,4},{6,7},{7,6},{8,9},{9,8},{10,11... | collective-permute-start | bytes 2949128 | tf_op jit(solution)/shard_map/ppermute | solution.py:59
  103.6 14.1 %collective-permute-start.21 = (bf16[4,160,384]{2,1,0:T(8,128)(2,1)}, bf16[4,160,384]{2,1,0:T(8,128)(2,1)}, u32[]{:S(2)}, u32[]{:S(2)}) collective-permute-start(bf16[4,160,384]{2,1,0:T(8,128)(2,1)} %collective-permute-done.16.refs_3_), channel_id=1, source_target_pairs={{0,1},{1,0},{2,3},{3,2},{4,5},{5,4},{6,7},{7,6},{8,9},{9,8},{10,11... | collective-permute-start | bytes 1474568 | tf_op jit(solution)/shard_map/ppermute | solution.py:59
  103.7 14.1 %collective-permute-start.22 = (bf16[4,160,384]{2,1,0:T(8,128)(2,1)}, bf16[4,160,384]{2,1,0:T(8,128)(2,1)}, u32[]{:S(2)}, u32[]{:S(2)}) collective-permute-start(bf16[4,160,384]{2,1,0:T(8,128)(2,1)} %collective-permute-done.17.refs_4_), channel_id=1, source_target_pairs={{0,1},{1,0},{2,3},{3,2},{4,5},{5,4},{6,7},{7,6},{8,9},{9,8},{10,11... | collective-permute-start | bytes 1474568 | tf_op jit(solution)/shard_map/ppermute | solution.py:59
  105.2 19.6 %collective-permute-start.2 = (bf16[2,5,48,384]{3,2,1,0:T(8,128)(2,1)}, bf16[2,5,48,384]{3,2,1,0:T(8,128)(2,1)S(1)}, u32[]{:S(2)}, u32[]{:S(2)}) collective-permute-start(bf16[2,5,48,384]{3,2,1,0:T(8,128)(2,1)} %copy-done.3), channel_id=1, source_target_pairs={{0,1},{1,2},{2,3},{3,4},{4,5},{5,6},{6,7},{7,8},{8,9},{9,10},{10,1... | collective-permute-start | bytes 1105928 | tf_op jit(solution)/shard_map/ppermute | solution.py:59
  (13 other events, 73.5 us)
Sparse Core Ops, SparseCore 0:
  9.1 61.2 all-gather.1

commit v4 on v3

--- a/solution.py
+++ b/solution.py
@@ -36,11 +36,11 @@
     return perm(lambda y, x, z, c: (y, x, z + steps if c == 0 else z - steps, c))
 
 
-Z1, Z2 = along_z(1), along_z(2)
 SWAP = perm(lambda y, x, z, c: (y, x, z, 1 - c))
 RING_UP = perm(lambda y, x, z, c: (y, x + 1, z, c) if c == 0 else (y + 1, x, z, c))
 RING_DOWN = perm(lambda y, x, z, c: (y, x - 1, z, c) if c == 0 else (y - 1, x, z, c))
 
+RING_FAR = perm(lambda y, x, z, c: (y, x + 2, z, c) if c == 0 else (y + 2, x, z, c))
 CROSS_UP = perm(lambda y, x, z, c: (y + 1, x, z, c) if c == 0 else (y, x + 1, z, c))
 CROSS_DOWN = perm(lambda y, x, z, c: (y - 1, x, z, c) if c == 0 else (y, x - 1, z, c))
 
@@ -86,9 +86,7 @@
         [*(lax.dynamic_slice_in_dim(slab, at, PART, axis=0) for at in starts), slab[8 * BLOCK :]],
         axis=0,
     )
-    one, two = send(both, Z1), send(both, Z2)
-    two = after(two, rows)
-    three, four = send(two, Z1), send(two, Z2)
+    one, two, three, four = (send(both, along_z(steps)) for steps in (1, 2, 3, 4))
     sent = jnp.stack([one, two, three])
     other = send(sent, SWAP)
     plus, minus = jnp.where(first_core, other, sent), jnp.where(first_core, sent, other)
@@ -97,17 +95,15 @@
     last = slabs[:, 2 * PART :]
     chunk = jnp.where(first_core, slabs[:, :PART], slabs[:, PART : 2 * PART])
 
-    def ring(chunk, up_pairs, down_pairs):
-        half = NZ // 2
-        up, down = send(chunk, up_pairs), send(chunk, down_pairs)
-        return up, down, send(up[:half], up_pairs), send(down[half:], down_pairs)
-
-    up, down, far_up, far_down = ring(chunk, RING_UP, RING_DOWN)
-    parts = [chunk, down, jnp.concatenate([far_up, far_down], axis=0), up]
+    chunk = after(chunk, rows)
+    parts = [chunk, *(send(chunk, pairs) for pairs in (RING_DOWN, RING_FAR, RING_UP))]
     spot = lax.rem(4 - jnp.where(first_core, x, y), 4)
     turned = lax.dynamic_slice_in_dim(jnp.stack(parts + parts), spot, 4, axis=0)
     chunk = turned.transpose(1, 0, 2, 3).reshape(NZ, BLOCK, C)
-    return [chunk, *ring(chunk, CROSS_UP, CROSS_DOWN)], last
+    half = NZ // 2
+    up, down = send(chunk, CROSS_UP), send(chunk, CROSS_DOWN)
+    far_up, far_down = send(up[:half], CROSS_UP), send(down[half:], CROSS_DOWN)
+    return [chunk, up, down, far_up, far_down], last
 
 
 def assemble_kernel(where, *refs):
@@ -147,12 +143,12 @@
 
 
 def convolve(frames, rows, whole, wide):
-    size = 2 * rows * 48
+    count = len(frames) - 2
     for t in range(3):
         left = jnp.concatenate(
             [
                 jnp.concatenate(
-                    [frames[f][k : k + rows].reshape(rows * 48, C) for f in (t, t + 1)], axis=0
+                    [frames[t + f][k : k + rows].reshape(rows * 48, C) for f in range(count)], axis=0
                 )
                 for k in range(3)
             ],
@@ -172,7 +168,7 @@
             wide[...] += part
     column = lax.broadcasted_iota(jnp.int32, (48, C), 0)
     lines = []
-    for i in range(2 * rows):
+    for i in range(count * rows):
         line = wide[48 * i : 48 * i + 48]
         before = jnp.where(column == 0, 0.0, pltpu.roll(line[:, :C], 1, 0))
         behind = jnp.where(column == 47, 0.0, pltpu.roll(line[:, 2 * C :], 47, 0))
@@ -180,8 +176,8 @@
     return lines
 
 
-def first_kernel(tile, low, high, weight, bias, gain, out, wide):
-    frames = [low[0], low[1], high[0], high[1]]
+def first_kernel(tile, earlier, grown, weight, bias, gain, out, wide):
+    frames = [earlier[0], earlier[1], *(grown[f] for f in range(4))]
     lines = convolve(frames, 5, lambda tap: weight[tap], wide)
     for i, line in enumerate(lines):
         result = activate(line + bias[...], gain[...])
@@ -192,17 +188,17 @@
         out[i // 5, i % 5] = result.astype(BF)
 
 
-def conv_first(low, high, weight, bias, gain, tile):
+def conv_first(earlier, grown, weight, bias, gain, tile):
     return pl.pallas_call(
         first_kernel,
-        out_shape=jax.ShapeDtypeStruct((2, 5, 48, C), BF),
+        out_shape=jax.ShapeDtypeStruct((4, 5, 48, C), BF),
         in_specs=[SMEM] + [VMEM] * 5,
         out_specs=VMEM,
-        scratch_shapes=[pltpu.VMEM((480, 3 * C), F32)],
-        compiler_params=pltpu.CompilerParams(vmem_limit_bytes=12 * 2**20),
-        cost_estimate=cost(480),
+        scratch_shapes=[pltpu.VMEM((960, 3 * C), F32)],
+        compiler_params=pltpu.CompilerParams(vmem_limit_bytes=20 * 2**20),
+        cost_estimate=cost(960),
         name="conv_first",
-    )(tile, low, high, weight, bias, gain)
+    )(tile, earlier, grown, weight, bias, gain)
 
 
 def slab_rows(weight, tap):
@@ -264,18 +260,17 @@
     whole_first = lax.all_gather(weight_first, ("z", "c"), axis=2, tiled=True)
     first = activate(latent, gain_first).astype(BF)
     grown = grow_rows(first)
-    low, high = grown[:2], grown[2:]
     pieces, last = gather(weight_second.reshape(9, 72, C), y, x, z, core, grown)
-    earlier = send(after(high, pieces[0]), neighbours(0, 1))
+    earlier = send(after(grown[2:], pieces[0]), neighbours(0, 1))
     others = [send(v, SWAP) for v in pieces[:3]]
 
     scales = row(bias_first), row(gain_second), tile
-    whole_first = whole_first.reshape(9, 3 * C, C)
-    second_high = conv_first(low, high, whole_first, *scales)
+    second = conv_first(earlier, grown, whole_first.reshape(9, 3 * C, C), *scales)
+    second_low, second_high = second[:2], second[2:]
     second_earlier = send(second_high, neighbours(0, 1))
-    others += [send(v, SWAP) for v in after(pieces[3:], second_high)]
-    second_low = conv_first(earlier, low, whole_first, *scales)
-    whole_second = assemble(after([*pieces, *others, last], second_low), where)
+    far = after(pieces[3:], second)
+    others += [send(v, SWAP) for v in far]
+    whole_second = assemble([*pieces[:3], *far, *others, last], where)
     rest = whole_second, latent.reshape(576, C), row(bias_second)
     partial = conv_second(second_low, second_high, *rest, None)
     return conv_second(second_earlier, second_low, *rest, partial).reshape(4, 3, 48, C)

time: 136 us -> 123 us (0.904)
  waiting for transfers between devices: 30.8 us -> 23.8 us
  local copies, waits for them, and re-layouts: 14 us -> 9.77 us
  starting transfers between devices: 49.8 us -> 48.2 us
    ppermute x23 -> x22, waiting for transfers between devices: 30.1 us -> 23 us  [send(): return lax.ppermute(value, AXES, pairs)]
    unnamed x37 -> x28, local copies, waits for them, and re-layouts: 10.6 us -> 4.76 us
    slice x5 -> x4, local copies, waits for them, and re-layouts: 1.99 us -> 3.66 us  [the longest x1 1.88 us: gather(): down[half:]]
    ppermute x23 -> x22, starting transfers between devices: 49.8 us -> 48.2 us  [send(): return lax.ppermute(value, AXES, pairs)]
    pallas_call x2 -> x1, Pallas kernels: 12.2 us -> 10.9 us  [conv_first(): pl.pallas_call(first_kernel, out_shape=jax.ShapeDtypeStruct((4, 5, 48, C)...]
  transfers between devices with their start and end apart: 24 -> 23, of which waited for: 9 -> 7; matrix products, arithmetic and copies ran while one was open for 6% -> 8% of each run, Pallas kernels for 14% -> 15%
where the time goes in v4:
time: 123 us; the launch traced here: 122 us
  starting transfers between devices  48.2 us (39%)
  waiting for transfers between devices  23.8 us (19%)
  Pallas kernels  22.8 us (19%)
  between operations  14 us (11%)
  local copies, waits for them, and re-layouts  9.77 us (8%)
  other arithmetic  3.93 us (3%)
    ppermute x22, starting transfers between devices, send(): return lax.ppermute(value, AXES, pairs)  48.2 us
    ppermute x22, waiting for transfers between devices, send(): return lax.ppermute(value, AXES, pairs)  23 us
    pallas_call x1, Pallas kernels, conv_first(): pl.pallas_call(first_kernel, out_shape=jax.ShapeDtypeStruct((4, 5, 48, C)...  10.9 us
    pallas_call x2, Pallas kernels, conv_second(): pl.pallas_call(functools.partial(second_kernel, start), out_shape=jax.Sha...  8.35 us
    unnamed x28, local copies, waits for them, and re-layouts  4.76 us
    pallas_call x1, Pallas kernels, assemble(): pl.pallas_call(assemble_kernel, out_shape=jax.ShapeDtypeStruct((NZ, 9 * S...  3.48 us
  transfers between devices with their start and end apart: 23, of which 7 were waited for; matrix products, arithmetic and copies ran while one was open for 8% of the time, Pallas kernels for 15%

profile of v4, /device:TPU:1, one launch (start us, length us, event | category | flops | bytes accessed | tf_op | source)
XLA Modules:
  0.0 122.3 jit_solution(7062979396434448923)
XLA Ops:
  7.3 3.3 %collective-permute-start.2 = (bf16[9,72,384]{2,1,0:T(8,128)(2,1)}, bf16[9,72,384]{2,1,0:T(8,128)(2,1)S(1)}, u32[]{:S(2)}, u32[]{:S(2)}) collective-permute-start(bf16[9,72,384]{2,1,0:T(8,128)(2,1)} %bitcast.58), channel_id=1, source_target_pairs={{0,1},{1,0},{2,3},{3,2},{4,5},{5,4},{6,7},{7,6},{8,9},{9,8},{10,11... | collective-permute-start | bytes 1493000 | tf_op jit(solution)/shard_map/ppermute | solution.py:59
  12.9 1.4 %collective-permute-start = (bf16[4,2,48,384]{3,2,1,0:T(8,128)(2,1)S(1)}, bf16[4,2,48,384]{3,2,1,0:T(8,128)(2,1)S(1)}, u32[]{:S(2)}, u32[]{:S(2)}) collective-permute-start(bf16[4,2,48,384]{3,2,1,0:T(8,128)(2,1)S(1)} %get-tuple-element.21), channel_id=1, source_target_pairs={{0,16},{1,17},{2,18},{3,19},{4,20},{5,21},{6,22},{7,23},{8,24},{9,... | collective-permute-start | bytes 884744 | tf_op jit(solution)/shard_map/ppermute | solution.py:59
  14.3 1.3 %collective-permute-start.1 = (bf16[4,2,48,384]{3,2,1,0:T(8,128)(2,1)S(1)}, bf16[4,2,48,384]{3,2,1,0:T(8,128)(2,1)}, u32[]{:S(2)}, u32[]{:S(2)}) collective-permute-start(bf16[4,2,48,384]{3,2,1,0:T(8,128)(2,1)S(1)} %get-tuple-element.22), channel_id=1, source_target_pairs={{16,0},{17,1},{18,2},{19,3},{20,4},{21,5},{22,6},{23,7},{24,8},{25... | collective-permute-start | bytes 884744 | tf_op jit(solution)/shard_map/ppermute | solution.py:59
  16.0 5.7 %collective-permute-start.3 = (bf16[96,384]{1,0:T(8,128)(2,1)S(1)}, bf16[96,384]{1,0:T(8,128)(2,1)S(1)}, u32[]{:S(2)}, u32[]{:S(2)}) collective-permute-start(bf16[96,384]{1,0:T(8,128)(2,1)S(1)} %pad_maximum_fusion.3), channel_id=1, source_target_pairs={{0,2},{1,15},{2,4},{3,1},{4,6},{5,3},{6,8},{7,5},{8,10},{9,7},{10,... | collective-permute-start | bytes 221192 | tf_op jit(solution)/shard_map/ppermute | solution.py:59
  21.6 1.2 collective-permute-start.4
  23.3 2.8 %collective-permute-done.4 = bf16[96,384]{1,0:T(8,128)(2,1)S(1)} collective-permute-done((bf16[96,384]{1,0:T(8,128)(2,1)S(1)}, bf16[96,384]{1,0:T(8,128)(2,1)S(1)}, u32[]{:S(2)}, u32[]{:S(2)}) %collective-permute-start.4) | collective-permute-done | bytes 73760 | tf_op jit(solution)/shard_map/ppermute | solution.py:59
  26.0 2.5 %collective-permute-done.5 = bf16[96,384]{1,0:T(8,128)(2,1)S(1)} collective-permute-done((bf16[96,384]{1,0:T(8,128)(2,1)S(1)}, bf16[96,384]{1,0:T(8,128)(2,1)S(1)}, u32[]{:S(2)}, u32[]{:S(2)}) %collective-permute-start.5) | collective-permute-done | bytes 73760 | tf_op jit(solution)/shard_map/ppermute | solution.py:59
  28.6 1.6 %collective-permute-start.6 = (bf16[3,96,384]{2,1,0:T(8,128)(2,1)S(1)}, bf16[3,96,384]{2,1,0:T(8,128)(2,1)S(1)}, u32[]{:S(2)}, u32[]{:S(2)}) collective-permute-start(bf16[3,96,384]{2,1,0:T(8,128)(2,1)S(1)} %pad_maximum_fusion.2), channel_id=1, source_target_pairs={{0,1},{1,0},{2,3},{3,2},{4,5},{5,4},{6,7},{7,6},{8,9},{9,8},{10,11... | collective-permute-start | bytes 663560 | tf_op jit(solution)/shard_map/ppermute | solution.py:59
  31.3 5.5 %collective-permute-start.7 = (bf16[96,384]{1,0:T(8,128)(2,1)S(1)}, bf16[96,384]{1,0:T(8,128)(2,1)S(1)}, u32[]{:S(2)}, u32[]{:S(2)}) collective-permute-start(bf16[96,384]{1,0:T(8,128)(2,1)S(1)} %pad_maximum_fusion.3), channel_id=1, source_target_pairs={{0,8},{1,9},{2,10},{3,11},{4,12},{5,13},{6,14},{7,15},{8,0},{9,1},... | collective-permute-start | bytes 221192 | tf_op jit(solution)/shard_map/ppermute | solution.py:59
  37.0 4.1 %collective-permute-done.7 = bf16[96,384]{1,0:T(8,128)(2,1)S(1)} collective-permute-done((bf16[96,384]{1,0:T(8,128)(2,1)S(1)}, bf16[96,384]{1,0:T(8,128)(2,1)S(1)}, u32[]{:S(2)}, u32[]{:S(2)}) %collective-permute-start.7) | collective-permute-done | bytes 73760 | tf_op jit(solution)/shard_map/ppermute | solution.py:59
  42.5 8.3 %collective-permute-start.8 = (bf16[8,40,384]{2,1,0:T(8,128)(2,1)S(1)}, bf16[8,40,384]{2,1,0:T(8,128)(2,1)S(1)}, u32[]{:S(2)}, u32[]{:S(2)}) collective-permute-start(bf16[8,40,384]{2,1,0:T(8,128)(2,1)S(1)} %dynamic-slice_select_fusion), channel_id=1, source_target_pairs={{0,48},{1,193},{2,50},{3,195},{4,52},{5,197},{6,54},{7,199},{8,56}... | collective-permute-start | bytes 737288 | tf_op jit(solution)/shard_map/ppermute | solution.py:59
  51.6 4.9 %collective-permute-done.8 = bf16[8,40,384]{2,1,0:T(8,128)(2,1)S(1)} collective-permute-done((bf16[8,40,384]{2,1,0:T(8,128)(2,1)S(1)}, bf16[8,40,384]{2,1,0:T(8,128)(2,1)S(1)}, u32[]{:S(2)}, u32[]{:S(2)}) %collective-permute-start.8) | collective-permute-done | bytes 245792 | tf_op jit(solution)/shard_map/ppermute | solution.py:59
  57.4 2.7 %collective-permute-done.10 = bf16[8,40,384]{2,1,0:T(8,128)(2,1)S(1)} collective-permute-done((bf16[8,40,384]{2,1,0:T(8,128)(2,1)S(1)}, bf16[8,40,384]{2,1,0:T(8,128)(2,1)S(1)}, u32[]{:S(2)}, u32[]{:S(2)}) %collective-permute-start.10) | collective-permute-done | bytes 245792 | tf_op jit(solution)/shard_map/ppermute | solution.py:59
  60.7 2.7 %collective-permute-start.14 = (bf16[8,160,384]{2,1,0:T(8,128)(2,1)S(1)}, bf16[8,160,384]{2,1,0:T(8,128)(2,1)}, u32[]{:S(2)}, u32[]{:S(2)}) collective-permute-start(bf16[8,160,384]{2,1,0:T(8,128)(2,1)S(1)} %bitcast.43), channel_id=1, source_target_pairs={{0,192},{1,49},{2,194},{3,51},{4,196},{5,53},{6,198},{7,55},{8,200... | collective-permute-start | bytes 2949128 | tf_op jit(solution)/shard_map/ppermute | solution.py:59
  64.2 5.5 %collective-permute-start.11 = (bf16[2,7,48,384]{3,2,1,0:T(8,128)(2,1)}, bf16[2,7,48,384]{3,2,1,0:T(8,128)(2,1)}, u32[]{:S(2)}, u32[]{:S(2)}) collective-permute-start(bf16[2,7,48,384]{3,2,1,0:T(8,128)(2,1)} %slice.63), channel_id=1, source_target_pairs={{0,1},{1,2},{2,3},{3,4},{4,5},{5,6},{6,7},{7,8},{8,9},{9,10},{10,1... | collective-permute-start | bytes 1548296 | tf_op jit(solution)/shard_map/ppermute | solution.py:59
  69.9 5.2 %collective-permute-done.13.refs_1_ = bf16[8,160,384]{2,1,0:T(8,128)(2,1)S(1)} collective-permute-done((bf16[8,160,384]{2,1,0:T(8,128)(2,1)S(1)}, bf16[8,160,384]{2,1,0:T(8,128)(2,1)S(1)}, u32[]{:S(2)}, u32[]{:S(2)}) %collective-permute-start.13) | collective-permute-done | bytes 983072 | tf_op jit(solution)/shard_map/ppermute | solution.py:59
  75.9 1.9 %slice.71 = bf16[4,160,384]{2,1,0:T(8,128)(2,1)} slice(bf16[8,160,384]{2,1,0:T(8,128)(2,1)} %collective-permute-done.14.refs_2_), slice={[4:8], [0:160], [0:384]} | slice | bytes 983040 | tf_op jit(solution)/shard_map/slice | solution.py:105
  77.8 2.7 %collective-permute-start.16 = (bf16[4,160,384]{2,1,0:T(8,128)(2,1)}, bf16[4,160,384]{2,1,0:T(8,128)(2,1)}, u32[]{:S(2)}, u32[]{:S(2)}) collective-permute-start(bf16[4,160,384]{2,1,0:T(8,128)(2,1)} %slice.71), channel_id=1, source_target_pairs={{0,192},{1,49},{2,194},{3,51},{4,196},{5,53},{6,198},{7,55},{8,200... | collective-permute-start | bytes 1474568 | tf_op jit(solution)/shard_map/ppermute | solution.py:59
  81.4 3.3 %copy-done.1 = bf16[3,3,1152,384]{3,2,1,0:T(8,128)(2,1)S(1)} copy-done((bf16[3,3,1152,384]{3,2,1,0:T(8,128)(2,1)S(1)}, bf16[3,3,1152,384]{3,2,1,0:T(8,128)(2,1)}, u32[]{:S(2)}) %copy-start.1) | copy-done | bytes 7962648
  84.7 10.9 %conv_first.1 = bf16[4,5,48,384]{3,2,1,0:T(8,128)(2,1)S(1)} custom-call(s32[1]{0:T(128)} %bitcast.tile, bf16[2,7,48,384]{3,2,1,0:T(8,128)(2,1)} %collective-permute-done.11.earlier, bf16[4,7,48,384]{3,2,1,0:T(8,128)(2,1)S(1)} %pad_maximum_fusion.grown, bf16[9,1152,384]{2,1,0:T(8,128)(2,1)S(1)} %bitcast.46, f32[1,384]{1,0:T(1,128)S(1)} %reshape.44.bias, ...), custom_call_target="tpu_custom_call" | custom-call | flops 7644119040 | bytes 7962624 | tf_op jit(solution)/shard_map/conv_first/pallas_call | solution.py:192
  96.5 6.0 %collective-permute-start.12 = (bf16[2,5,48,384]{3,2,1,0:T(8,128)(2,1)S(1)}, bf16[2,5,48,384]{3,2,1,0:T(8,128)(2,1)}, u32[]{:S(2)}, u32[]{:S(2)}) collective-permute-start(bf16[2,5,48,384]{3,2,1,0:T(8,128)(2,1)S(1)} %get-tuple-element.18.high), channel_id=1, source_target_pairs={{0,1},{1,2},{2,3},{3,4},{4,5},{5,6},{6,7},{7,8},{8,9},{9,10},{10,1... | collective-permute-start | bytes 1105928 | tf_op jit(solution)/shard_map/ppermute | solution.py:59
  103.6 3.5 %assemble.1.weight = bf16[8,1296,384]{2,1,0:T(8,128)(2,1)S(1)} custom-call(s32[8]{0:T(128)S(1)} %stack.90.where, bf16[8,160,384]{2,1,0:T(8,128)(2,1)S(1)} %bitcast.45, bf16[8,160,384]{2,1,0:T(8,128)(2,1)S(1)} %collective-permute-done.13.refs_1_, bf16[8,160,384]{2,1,0:T(8,128)(2,1)} %collective-permute-done.14.refs_2_, ...), custom_call_target="tpu_custom_call" | custom-call | tf_op jit(solution)/shard_map/assemble/pallas_call | solution.py:134
  107.1 3.7 %second_late.1.refs_0_ = bf16[576,384]{1,0:T(8,128)(2,1)} custom-call(bf16[2,5,48,384]{3,2,1,0:T(8,128)(2,1)S(1)} %get-tuple-element.17.low.high, bf16[2,5,48,384]{3,2,1,0:T(8,128)(2,1)S(1)} %get-tuple-element.18.high, bf16[8,1296,384]{2,1,0:T(8,128)(2,1)S(1)} %assemble.1.weight, bf16[576,384]{1,0:T(8,128)(2,1)S(1)} %bitcast.40, f32[1,384]{1,0:T(1,128)S(1)} %reshape.47.bias), custom_call_target="tpu_custom_call" | custom-call | flops 2293235712 | bytes 7962624 | tf_op jit(solution)/shard_map/second_late/pallas_call | solution.py:224
  110.8 4.7 %second_early.1 = bf16[576,384]{1,0:T(8,128)(2,1)} custom-call(bf16[2,5,48,384]{3,2,1,0:T(8,128)(2,1)} %collective-permute-done.12.low, bf16[2,5,48,384]{3,2,1,0:T(8,128)(2,1)S(1)} %get-tuple-element.17.low.high, bf16[8,1296,384]{2,1,0:T(8,128)(2,1)S(1)} %assemble.1.weight, bf16[576,384]{1,0:T(8,128)(2,1)S(1)} %bitcast.41, ...), custom_call_target="tpu_custom_call", output_to_operand_aliasing={{}: (5, {})} | custom-call | flops 2293235712 | bytes 7962624 | tf_op jit(solution)/shard_map/second_early/pallas_call | solution.py:224
  (84 shorter events, 13.3 us)
Async XLA Ops:
  6.5 74.9 %all-gather.2.cloned.1.call-start = ((), (), s32[]{:S(2)}) async-start(), calls=%async_computation | async-start | bytes 8460288 | tf_op jit(solution)/shard_map/all_gather | solution.py:260
  7.3 8.4 %collective-permute-start.2 = (bf16[9,72,384]{2,1,0:T(8,128)(2,1)}, bf16[9,72,384]{2,1,0:T(8,128)(2,1)S(1)}, u32[]{:S(2)}, u32[]{:S(2)}) collective-permute-start(bf16[9,72,384]{2,1,0:T(8,128)(2,1)} %bitcast.58), channel_id=1, source_target_pairs={{0,1},{1,0},{2,3},{3,2},{4,5},{5,4},{6,7},{7,6},{8,9},{9,8},{10,11... | collective-permute-start | bytes 1493000 | tf_op jit(solution)/shard_map/ppermute | solution.py:59
  12.9 17.3 %collective-permute-start = (bf16[4,2,48,384]{3,2,1,0:T(8,128)(2,1)S(1)}, bf16[4,2,48,384]{3,2,1,0:T(8,128)(2,1)S(1)}, u32[]{:S(2)}, u32[]{:S(2)}) collective-permute-start(bf16[4,2,48,384]{3,2,1,0:T(8,128)(2,1)S(1)} %get-tuple-element.21), channel_id=1, source_target_pairs={{0,16},{1,17},{2,18},{3,19},{4,20},{5,21},{6,22},{7,23},{8,24},{9,... | collective-permute-start | bytes 884744 | tf_op jit(solution)/shard_map/ppermute | solution.py:59
  14.3 15.9 %collective-permute-start.1 = (bf16[4,2,48,384]{3,2,1,0:T(8,128)(2,1)S(1)}, bf16[4,2,48,384]{3,2,1,0:T(8,128)(2,1)}, u32[]{:S(2)}, u32[]{:S(2)}) collective-permute-start(bf16[4,2,48,384]{3,2,1,0:T(8,128)(2,1)S(1)} %get-tuple-element.22), channel_id=1, source_target_pairs={{16,0},{17,1},{18,2},{19,3},{20,4},{21,5},{22,6},{23,7},{24,8},{25... | collective-permute-start | bytes 884744 | tf_op jit(solution)/shard_map/ppermute | solution.py:59
  16.0 7.3 %collective-permute-start.3 = (bf16[96,384]{1,0:T(8,128)(2,1)S(1)}, bf16[96,384]{1,0:T(8,128)(2,1)S(1)}, u32[]{:S(2)}, u32[]{:S(2)}) collective-permute-start(bf16[96,384]{1,0:T(8,128)(2,1)S(1)} %pad_maximum_fusion.3), channel_id=1, source_target_pairs={{0,2},{1,15},{2,4},{3,1},{4,6},{5,3},{6,8},{7,5},{8,10},{9,7},{10,... | collective-permute-start | bytes 221192 | tf_op jit(solution)/shard_map/ppermute | solution.py:59
  21.6 4.4 %collective-permute-start.4 = (bf16[96,384]{1,0:T(8,128)(2,1)S(1)}, bf16[96,384]{1,0:T(8,128)(2,1)S(1)}, u32[]{:S(2)}, u32[]{:S(2)}) collective-permute-start(bf16[96,384]{1,0:T(8,128)(2,1)S(1)} %pad_maximum_fusion.3), channel_id=1, source_target_pairs={{0,4},{1,13},{2,6},{3,15},{4,8},{5,1},{6,10},{7,3},{8,12},{9,5},{1... | collective-permute-start | bytes 221192 | tf_op jit(solution)/shard_map/ppermute | solution.py:59
  22.8 5.7 %collective-permute-start.5 = (bf16[96,384]{1,0:T(8,128)(2,1)S(1)}, bf16[96,384]{1,0:T(8,128)(2,1)S(1)}, u32[]{:S(2)}, u32[]{:S(2)}) collective-permute-start(bf16[96,384]{1,0:T(8,128)(2,1)S(1)} %pad_maximum_fusion.3), channel_id=1, source_target_pairs={{0,6},{1,11},{2,8},{3,13},{4,10},{5,15},{6,12},{7,1},{8,14},{9,3},... | collective-permute-start | bytes 221192 | tf_op jit(solution)/shard_map/ppermute | solution.py:59
  28.6 8.2 %collective-permute-start.6 = (bf16[3,96,384]{2,1,0:T(8,128)(2,1)S(1)}, bf16[3,96,384]{2,1,0:T(8,128)(2,1)S(1)}, u32[]{:S(2)}, u32[]{:S(2)}) collective-permute-start(bf16[3,96,384]{2,1,0:T(8,128)(2,1)S(1)} %pad_maximum_fusion.2), channel_id=1, source_target_pairs={{0,1},{1,0},{2,3},{3,2},{4,5},{5,4},{6,7},{7,6},{8,9},{9,8},{10,11... | collective-permute-start | bytes 663560 | tf_op jit(solution)/shard_map/ppermute | solution.py:59
  31.3 9.7 %collective-permute-start.7 = (bf16[96,384]{1,0:T(8,128)(2,1)S(1)}, bf16[96,384]{1,0:T(8,128)(2,1)S(1)}, u32[]{:S(2)}, u32[]{:S(2)}) collective-permute-start(bf16[96,384]{1,0:T(8,128)(2,1)S(1)} %pad_maximum_fusion.3), channel_id=1, source_target_pairs={{0,8},{1,9},{2,10},{3,11},{4,12},{5,13},{6,14},{7,15},{8,0},{9,1},... | collective-permute-start | bytes 221192 | tf_op jit(solution)/shard_map/ppermute | solution.py:59
  42.5 14.0 %collective-permute-start.8 = (bf16[8,40,384]{2,1,0:T(8,128)(2,1)S(1)}, bf16[8,40,384]{2,1,0:T(8,128)(2,1)S(1)}, u32[]{:S(2)}, u32[]{:S(2)}) collective-permute-start(bf16[8,40,384]{2,1,0:T(8,128)(2,1)S(1)} %dynamic-slice_select_fusion), channel_id=1, source_target_pairs={{0,48},{1,193},{2,50},{3,195},{4,52},{5,197},{6,54},{7,199},{8,56}... | collective-permute-start | bytes 737288 | tf_op jit(solution)/shard_map/ppermute | solution.py:59
  50.7 6.7 %collective-permute-start.9 = (bf16[8,40,384]{2,1,0:T(8,128)(2,1)S(1)}, bf16[8,40,384]{2,1,0:T(8,128)(2,1)S(1)}, u32[]{:S(2)}, u32[]{:S(2)}) collective-permute-start(bf16[8,40,384]{2,1,0:T(8,128)(2,1)S(1)} %dynamic-slice_select_fusion), channel_id=1, source_target_pairs={{0,32},{1,129},{2,34},{3,131},{4,36},{5,133},{6,38},{7,135},{8,40}... | collective-permute-start | bytes 737288 | tf_op jit(solution)/shard_map/ppermute | solution.py:59
  50.8 9.4 %collective-permute-start.10 = (bf16[8,40,384]{2,1,0:T(8,128)(2,1)S(1)}, bf16[8,40,384]{2,1,0:T(8,128)(2,1)S(1)}, u32[]{:S(2)}, u32[]{:S(2)}) collective-permute-start(bf16[8,40,384]{2,1,0:T(8,128)(2,1)S(1)} %dynamic-slice_select_fusion), channel_id=1, source_target_pairs={{0,16},{1,65},{2,18},{3,67},{4,20},{5,69},{6,22},{7,71},{8,24},{9,... | collective-permute-start | bytes 737288 | tf_op jit(solution)/shard_map/ppermute | solution.py:59
  60.5 9.3 %copy-start.5 = (f32[384]{0:T(512)S(1)}, f32[384]{0:T(512)}, u32[]{:S(2)}) copy-start(f32[384]{0:T(512)} %param.11) | copy-start | bytes 4612
  60.6 14.4 %collective-permute-start.13 = (bf16[8,160,384]{2,1,0:T(8,128)(2,1)S(1)}, bf16[8,160,384]{2,1,0:T(8,128)(2,1)S(1)}, u32[]{:S(2)}, u32[]{:S(2)}) collective-permute-start(bf16[8,160,384]{2,1,0:T(8,128)(2,1)S(1)} %bitcast.42), channel_id=1, source_target_pairs={{0,64},{1,17},{2,66},{3,19},{4,68},{5,21},{6,70},{7,23},{8,72},{9,... | collective-permute-start | bytes 2949128 | tf_op jit(solution)/shard_map/ppermute | solution.py:59
  60.7 15.2 %collective-permute-start.14 = (bf16[8,160,384]{2,1,0:T(8,128)(2,1)S(1)}, bf16[8,160,384]{2,1,0:T(8,128)(2,1)}, u32[]{:S(2)}, u32[]{:S(2)}) collective-permute-start(bf16[8,160,384]{2,1,0:T(8,128)(2,1)S(1)} %bitcast.43), channel_id=1, source_target_pairs={{0,192},{1,49},{2,194},{3,51},{4,196},{5,53},{6,198},{7,55},{8,200... | collective-permute-start | bytes 2949128 | tf_op jit(solution)/shard_map/ppermute | solution.py:59
  64.2 17.2 %collective-permute-start.11 = (bf16[2,7,48,384]{3,2,1,0:T(8,128)(2,1)}, bf16[2,7,48,384]{3,2,1,0:T(8,128)(2,1)}, u32[]{:S(2)}, u32[]{:S(2)}) collective-permute-start(bf16[2,7,48,384]{3,2,1,0:T(8,128)(2,1)} %slice.63), channel_id=1, source_target_pairs={{0,1},{1,2},{2,3},{3,4},{4,5},{5,6},{6,7},{7,8},{8,9},{9,10},{10,1... | collective-permute-start | bytes 1548296 | tf_op jit(solution)/shard_map/ppermute | solution.py:59
  69.8 26.7 %collective-permute-start.17 = (bf16[8,160,384]{2,1,0:T(8,128)(2,1)S(1)}, bf16[8,160,384]{2,1,0:T(8,128)(2,1)}, u32[]{:S(2)}, u32[]{:S(2)}) collective-permute-start(bf16[8,160,384]{2,1,0:T(8,128)(2,1)S(1)} %bitcast.44), channel_id=1, source_target_pairs={{0,1},{1,0},{2,3},{3,2},{4,5},{5,4},{6,7},{7,6},{8,9},{9,8},{10,11... | collective-permute-start | bytes 2949128 | tf_op jit(solution)/shard_map/ppermute | solution.py:59
  75.9 19.8 %collective-permute-start.15 = (bf16[4,160,384]{2,1,0:T(8,128)(2,1)}, bf16[4,160,384]{2,1,0:T(8,128)(2,1)}, u32[]{:S(2)}, u32[]{:S(2)}) collective-permute-start(bf16[4,160,384]{2,1,0:T(8,128)(2,1)} %slice.70), channel_id=1, source_target_pairs={{0,64},{1,17},{2,66},{3,19},{4,68},{5,21},{6,70},{7,23},{8,72},{9,... | collective-permute-start | bytes 1474568 | tf_op jit(solution)/shard_map/ppermute | solution.py:59
  77.8 17.9 %collective-permute-start.16 = (bf16[4,160,384]{2,1,0:T(8,128)(2,1)}, bf16[4,160,384]{2,1,0:T(8,128)(2,1)}, u32[]{:S(2)}, u32[]{:S(2)}) collective-permute-start(bf16[4,160,384]{2,1,0:T(8,128)(2,1)} %slice.71), channel_id=1, source_target_pairs={{0,192},{1,49},{2,194},{3,51},{4,196},{5,53},{6,198},{7,55},{8,200... | collective-permute-start | bytes 1474568 | tf_op jit(solution)/shard_map/ppermute | solution.py:59
  80.5 23.1 %collective-permute-start.18 = (bf16[8,160,384]{2,1,0:T(8,128)(2,1)S(1)}, bf16[8,160,384]{2,1,0:T(8,128)(2,1)}, u32[]{:S(2)}, u32[]{:S(2)}) collective-permute-start(bf16[8,160,384]{2,1,0:T(8,128)(2,1)S(1)} %collective-permute-done.13.refs_1_), channel_id=1, source_target_pairs={{0,1},{1,0},{2,3},{3,2},{4,5},{5,4},{6,7},{7,6},{8,9},{9,8},{10,11... | collective-permute-start | bytes 2949128 | tf_op jit(solution)/shard_map/ppermute | solution.py:59
  81.4 22.2 %collective-permute-start.19 = (bf16[8,160,384]{2,1,0:T(8,128)(2,1)}, bf16[8,160,384]{2,1,0:T(8,128)(2,1)}, u32[]{:S(2)}, u32[]{:S(2)}) collective-permute-start(bf16[8,160,384]{2,1,0:T(8,128)(2,1)} %collective-permute-done.14.refs_2_), channel_id=1, source_target_pairs={{0,1},{1,0},{2,3},{3,2},{4,5},{5,4},{6,7},{7,6},{8,9},{9,8},{10,11... | collective-permute-start | bytes 2949128 | tf_op jit(solution)/shard_map/ppermute | solution.py:59
  95.7 7.9 %collective-permute-start.20 = (bf16[4,160,384]{2,1,0:T(8,128)(2,1)}, bf16[4,160,384]{2,1,0:T(8,128)(2,1)}, u32[]{:S(2)}, u32[]{:S(2)}) collective-permute-start(bf16[4,160,384]{2,1,0:T(8,128)(2,1)} %collective-permute-done.15.refs_3_), channel_id=1, source_target_pairs={{0,1},{1,0},{2,3},{3,2},{4,5},{5,4},{6,7},{7,6},{8,9},{9,8},{10,11... | collective-permute-start | bytes 1474568 | tf_op jit(solution)/shard_map/ppermute | solution.py:59
  96.3 7.3 %collective-permute-start.21 = (bf16[4,160,384]{2,1,0:T(8,128)(2,1)}, bf16[4,160,384]{2,1,0:T(8,128)(2,1)}, u32[]{:S(2)}, u32[]{:S(2)}) collective-permute-start(bf16[4,160,384]{2,1,0:T(8,128)(2,1)} %collective-permute-done.16.refs_4_), channel_id=1, source_target_pairs={{0,1},{1,0},{2,3},{3,2},{4,5},{5,4},{6,7},{7,6},{8,9},{9,8},{10,11... | collective-permute-start | bytes 1474568 | tf_op jit(solution)/shard_map/ppermute | solution.py:59
  96.5 14.3 %collective-permute-start.12 = (bf16[2,5,48,384]{3,2,1,0:T(8,128)(2,1)S(1)}, bf16[2,5,48,384]{3,2,1,0:T(8,128)(2,1)}, u32[]{:S(2)}, u32[]{:S(2)}) collective-permute-start(bf16[2,5,48,384]{3,2,1,0:T(8,128)(2,1)S(1)} %get-tuple-element.18.high), channel_id=1, source_target_pairs={{0,1},{1,2},{2,3},{3,4},{4,5},{5,6},{6,7},{7,8},{8,9},{9,10},{10,1... | collective-permute-start | bytes 1105928 | tf_op jit(solution)/shard_map/ppermute | solution.py:59
  (6 other events, 29.7 us)
Sparse Core Ops, SparseCore 0:
  9.1 63.7 all-gather.1

commit v5 on v4

--- a/solution.py
+++ b/solution.py
@@ -72,10 +72,12 @@
 def grow_rows(own):
     above = send(own[:, 1:], neighbours(1, 0))
     below = send(own[:, :2], neighbours(-1, 0))
-    return jnp.concatenate([above, own, below], axis=1)
-
-
-def gather(weight, y, x, z, core, rows):
+    return [
+        jnp.concatenate([above[k : k + 2], own[k : k + 2], below[k : k + 2]], axis=1) for k in (0, 2)
+    ]
+
+
+def gather(weight, y, x, z, core):
     first_core = core == 0
     other = send(weight, SWAP)
     slab = jnp.concatenate(
@@ -95,15 +97,16 @@
     last = slabs[:, 2 * PART :]
     chunk = jnp.where(first_core, slabs[:, :PART], slabs[:, PART : 2 * PART])
 
-    chunk = after(chunk, rows)
+    chunk, last = lax.optimization_barrier((chunk, last))
     parts = [chunk, *(send(chunk, pairs) for pairs in (RING_DOWN, RING_FAR, RING_UP))]
     spot = lax.rem(4 - jnp.where(first_core, x, y), 4)
     turned = lax.dynamic_slice_in_dim(jnp.stack(parts + parts), spot, 4, axis=0)
     chunk = turned.transpose(1, 0, 2, 3).reshape(NZ, BLOCK, C)
-    half = NZ // 2
-    up, down = send(chunk, CROSS_UP), send(chunk, CROSS_DOWN)
-    far_up, far_down = send(up[:half], CROSS_UP), send(down[half:], CROSS_DOWN)
-    return [chunk, up, down, far_up, far_down], last
+    low, high = chunk[: NZ // 2], chunk[NZ // 2 :]
+    up_low, down_high = send(low, CROSS_UP), send(high, CROSS_DOWN)
+    up_high, down_low = send(high, CROSS_UP), send(low, CROSS_DOWN)
+    far = send(up_low, CROSS_UP), send(down_high, CROSS_DOWN)
+    return [low, high, up_low, up_high, down_low, down_high, *far], last, both
 
 
 def assemble_kernel(where, *refs):
@@ -117,9 +120,8 @@
 
     half = NZ // 2
     for k, src in enumerate(arrays):
-        at = pl.multiple_of(where[k - k // 5 - k % 5 // 4], BLOCK)
-        slabs = {3: pl.ds(0, half), 4: pl.ds(half, half)}.get(k % 5, pl.ds(0, NZ))
-        fetch(src, whole.at[slabs, pl.ds(at, BLOCK)])
+        at = pl.multiple_of(where[k // 2], BLOCK)
+        fetch(src, whole.at[pl.ds(k % 2 * half, half), pl.ds(at, BLOCK)])
     fetch(last, whole.at[:, pl.ds(8 * BLOCK, 9 * SLAB - 8 * BLOCK)])
     for copy in copies:
         copy.wait()
@@ -176,9 +178,24 @@
     return lines
 
 
-def first_kernel(tile, earlier, grown, weight, bias, gain, out, wide):
-    frames = [earlier[0], earlier[1], *(grown[f] for f in range(4))]
-    lines = convolve(frames, 5, lambda tap: weight[tap], wide)
+def first_kernel(tile, earlier, low, high, weight, bias, gain, out, wide, kept, sems):
+    copies = [
+        pltpu.make_async_copy(weight.at[pl.ds(3 * t, 3)], kept.at[pl.ds(3 * t, 3)], sems.at[t])
+        for t in range(3)
+    ]
+    for copy in copies:
+        copy.start()
+
+    arrived = set()
+
+    def whole(tap):
+        if tap // 3 not in arrived:
+            arrived.add(tap // 3)
+            copies[tap // 3].wait()
+        return kept[tap]
+
+    frames = [part[f] for part in (earlier, low, high) for f in range(2)]
+    lines = convolve(frames, 5, whole, wide)
     for i, line in enumerate(lines):
         result = activate(line + bias[...], gain[...])
         if i % 5 == 0:
@@ -188,17 +205,21 @@
         out[i // 5, i % 5] = result.astype(BF)
 
 
-def conv_first(earlier, grown, weight, bias, gain, tile):
+def conv_first(earlier, low, high, weight, bias, gain, tile):
     return pl.pallas_call(
         first_kernel,
         out_shape=jax.ShapeDtypeStruct((4, 5, 48, C), BF),
-        in_specs=[SMEM] + [VMEM] * 5,
+        in_specs=[SMEM, VMEM, VMEM, VMEM, ANY, VMEM, VMEM],
         out_specs=VMEM,
-        scratch_shapes=[pltpu.VMEM((960, 3 * C), F32)],
-        compiler_params=pltpu.CompilerParams(vmem_limit_bytes=20 * 2**20),
+        scratch_shapes=[
+            pltpu.VMEM((960, 3 * C), F32),
+            pltpu.VMEM((9, 3 * C, C), BF),
+            pltpu.SemaphoreType.DMA((3,)),
+        ],
+        compiler_params=pltpu.CompilerParams(vmem_limit_bytes=54 * 2**20),
         cost_estimate=cost(960),
         name="conv_first",
-    )(tile, earlier, grown, weight, bias, gain)
+    )(tile, earlier, low, high, weight, bias, gain)
 
 
 def slab_rows(weight, tap):
@@ -258,19 +279,19 @@
     row = lambda v: v.reshape(1, C)
 
     whole_first = lax.all_gather(weight_first, ("z", "c"), axis=2, tiled=True)
-    first = activate(latent, gain_first).astype(BF)
-    grown = grow_rows(first)
-    pieces, last = gather(weight_second.reshape(9, 72, C), y, x, z, core, grown)
-    earlier = send(after(grown[2:], pieces[0]), neighbours(0, 1))
-    others = [send(v, SWAP) for v in pieces[:3]]
+    pieces, last, both = gather(weight_second.reshape(9, 72, C), y, x, z, core)
+    first = activate(after(latent, both), gain_first).astype(BF)
+    low, high = grow_rows(first)
+    earlier = send(after(high, *pieces[:2]), neighbours(0, 1))
+    others = [send(v, SWAP) for v in pieces[:6]]
 
     scales = row(bias_first), row(gain_second), tile
-    second = conv_first(earlier, grown, whole_first.reshape(9, 3 * C, C), *scales)
+    second = conv_first(earlier, low, high, whole_first.reshape(9, 3 * C, C), *scales)
     second_low, second_high = second[:2], second[2:]
     second_earlier = send(second_high, neighbours(0, 1))
-    far = after(pieces[3:], second)
+    far = after(pieces[6:], second)
     others += [send(v, SWAP) for v in far]
-    whole_second = assemble([*pieces[:3], *far, *others, last], where)
+    whole_second = assemble([*pieces[:6], *far, *others, last], where)
     rest = whole_second, latent.reshape(576, C), row(bias_second)
     partial = conv_second(second_low, second_high, *rest, None)
     return conv_second(second_earlier, second_low, *rest, partial).reshape(4, 3, 48, C)

time: 123 us -> 118 us (0.959)
  local copies, waits for them, and re-layouts: 9.77 us -> 3.4 us
  Pallas kernels: 22.8 us -> 27.3 us
  waiting for transfers between devices: 23.8 us -> 20.5 us
    unnamed x28 -> x24, local copies, waits for them, and re-layouts: 4.76 us -> 0.42 us
    pallas_call x1, Pallas kernels: 10.9 us -> 15.2 us  [conv_first(): pl.pallas_call(first_kernel, out_shape=jax.ShapeDtypeStruct((4, 5, 48, C)...]
    slice x3 -> x6, local copies, waits for them, and re-layouts: 3.59 us -> 0.31 us  [the longest x3 0.2 us: gather(): low, high = (chunk[:NZ // 2], chunk[NZ // 2:])]
    ppermute x22 -> x27, waiting for transfers between devices: 23 us -> 19.8 us  [send(): return lax.ppermute(value, AXES, pairs)]
    ppermute x22 -> x27, starting transfers between devices: 48.2 us -> 48.9 us  [send(): return lax.ppermute(value, AXES, pairs)]
  transfers between devices with their start and end apart: 23 -> 28, of which waited for: 7 -> 8; matrix products, arithmetic and copies ran while one was open for 8% -> 6% of each run, Pallas kernels for 15% -> 19%
where the time goes in v5:
time: 118 us
  starting transfers between devices  48.9 us (41%)
  Pallas kernels  27.3 us (23%)
  waiting for transfers between devices  20.5 us (17%)
  between operations  13.9 us (12%)
  other arithmetic  3.83 us (3%)
  local copies, waits for them, and re-layouts  3.4 us (3%)
    ppermute x27, starting transfers between devices, send(): return lax.ppermute(value, AXES, pairs)  48.9 us
    ppermute x27, waiting for transfers between devices, send(): return lax.ppermute(value, AXES, pairs)  19.8 us
    pallas_call x1, Pallas kernels, conv_first(): pl.pallas_call(first_kernel, out_shape=jax.ShapeDtypeStruct((4, 5, 48, C)...  15.2 us
    pallas_call x2, Pallas kernels, conv_second(): pl.pallas_call(functools.partial(second_kernel, start), out_shape=jax.Sha...  8.42 us
    pallas_call x1, Pallas kernels, assemble(): pl.pallas_call(assemble_kernel, out_shape=jax.ShapeDtypeStruct((NZ, 9 * S...  3.7 us
  transfers between devices with their start and end apart: 28, of which 8 were waited for; matrix products, arithmetic and copies ran while one was open for 6% of the time, Pallas kernels for 19%

profile of v5, /device:TPU:1, one launch (start us, length us, event | category | flops | bytes accessed | tf_op | source)
XLA Modules:
  0.0 117.9 jit_solution(322016008031951731)
XLA Ops:
  7.3 3.3 %collective-permute-start = (bf16[9,72,384]{2,1,0:T(8,128)(2,1)}, bf16[9,72,384]{2,1,0:T(8,128)(2,1)S(1)}, u32[]{:S(2)}, u32[]{:S(2)}) collective-permute-start(bf16[9,72,384]{2,1,0:T(8,128)(2,1)} %bitcast.62), channel_id=1, source_target_pairs={{0,1},{1,0},{2,3},{3,2},{4,5},{5,4},{6,7},{7,6},{8,9},{9,8},{10,11... | collective-permute-start | bytes 1493000 | tf_op jit(solution)/shard_map/ppermute | solution.py:59
  10.6 1.7 %collective-permute-done = bf16[9,72,384]{2,1,0:T(8,128)(2,1)S(1)} collective-permute-done((bf16[9,72,384]{2,1,0:T(8,128)(2,1)}, bf16[9,72,384]{2,1,0:T(8,128)(2,1)S(1)}, u32[]{:S(2)}, u32[]{:S(2)}) %collective-permute-start) | collective-permute-done | bytes 497696 | tf_op jit(solution)/shard_map/ppermute | solution.py:59
  13.6 3.9 %collective-permute-start.3 = (bf16[96,384]{1,0:T(8,128)(2,1)S(1)}, bf16[96,384]{1,0:T(8,128)(2,1)S(1)}, u32[]{:S(2)}, u32[]{:S(2)}) collective-permute-start(bf16[96,384]{1,0:T(8,128)(2,1)S(1)} %pad_maximum_fusion.4), channel_id=1, source_target_pairs={{0,2},{1,15},{2,4},{3,1},{4,6},{5,3},{6,8},{7,5},{8,10},{9,7},{10,... | collective-permute-start | bytes 221192 | tf_op jit(solution)/shard_map/ppermute | solution.py:59
  17.5 1.2 collective-permute-start.4
  19.2 4.5 %collective-permute-start.7 = (bf16[96,384]{1,0:T(8,128)(2,1)S(1)}, bf16[96,384]{1,0:T(8,128)(2,1)S(1)}, u32[]{:S(2)}, u32[]{:S(2)}) collective-permute-start(bf16[96,384]{1,0:T(8,128)(2,1)S(1)} %pad_maximum_fusion.4), channel_id=1, source_target_pairs={{0,8},{1,9},{2,10},{3,11},{4,12},{5,13},{6,14},{7,15},{8,0},{9,1},... | collective-permute-start | bytes 221192 | tf_op jit(solution)/shard_map/ppermute | solution.py:59
  24.3 1.9 %collective-permute-start.6 = (bf16[3,96,384]{2,1,0:T(8,128)(2,1)S(1)}, bf16[3,96,384]{2,1,0:T(8,128)(2,1)S(1)}, u32[]{:S(2)}, u32[]{:S(2)}) collective-permute-start(bf16[3,96,384]{2,1,0:T(8,128)(2,1)S(1)} %pad_maximum_fusion.3), channel_id=1, source_target_pairs={{0,1},{1,0},{2,3},{3,2},{4,5},{5,4},{6,7},{7,6},{8,9},{9,8},{10,11... | collective-permute-start | bytes 663560 | tf_op jit(solution)/shard_map/ppermute | solution.py:59
  27.3 1.4 %collective-permute-done.7 = bf16[96,384]{1,0:T(8,128)(2,1)S(1)} collective-permute-done((bf16[96,384]{1,0:T(8,128)(2,1)S(1)}, bf16[96,384]{1,0:T(8,128)(2,1)S(1)}, u32[]{:S(2)}, u32[]{:S(2)}) %collective-permute-start.7) | collective-permute-done | bytes 73760 | tf_op jit(solution)/shard_map/ppermute | solution.py:59
  29.2 2.8 %collective-permute-start.8 = (bf16[8,40,384]{2,1,0:T(8,128)(2,1)S(1)}, bf16[8,40,384]{2,1,0:T(8,128)(2,1)S(1)}, u32[]{:S(2)}, u32[]{:S(2)}) collective-permute-start(bf16[8,40,384]{2,1,0:T(8,128)(2,1)S(1)} %dynamic-slice_select_fusion), channel_id=1, source_target_pairs={{0,48},{1,193},{2,50},{3,195},{4,52},{5,197},{6,54},{7,199},{8,56}... | collective-permute-start | bytes 737288 | tf_op jit(solution)/shard_map/ppermute | solution.py:59
  32.0 3.1 %collective-permute-start.1 = (bf16[4,2,48,384]{3,2,1,0:T(8,128)(2,1)S(1)}, bf16[4,2,48,384]{3,2,1,0:T(8,128)(2,1)S(1)}, u32[]{:S(2)}, u32[]{:S(2)}) collective-permute-start(bf16[4,2,48,384]{3,2,1,0:T(8,128)(2,1)S(1)} %get-tuple-element.29), channel_id=1, source_target_pairs={{0,16},{1,17},{2,18},{3,19},{4,20},{5,21},{6,22},{7,23},{8,24},{9,... | collective-permute-start | bytes 884744 | tf_op jit(solution)/shard_map/ppermute | solution.py:59
  35.1 1.3 %collective-permute-start.2 = (bf16[4,2,48,384]{3,2,1,0:T(8,128)(2,1)S(1)}, bf16[4,2,48,384]{3,2,1,0:T(8,128)(2,1)S(1)}, u32[]{:S(2)}, u32[]{:S(2)}) collective-permute-start(bf16[4,2,48,384]{3,2,1,0:T(8,128)(2,1)S(1)} %get-tuple-element.30), channel_id=1, source_target_pairs={{16,0},{17,1},{18,2},{19,3},{20,4},{21,5},{22,6},{23,7},{24,8},{25... | collective-permute-start | bytes 884744 | tf_op jit(solution)/shard_map/ppermute | solution.py:59
  36.4 3.3 %collective-permute-start.9 = (bf16[8,40,384]{2,1,0:T(8,128)(2,1)S(1)}, bf16[8,40,384]{2,1,0:T(8,128)(2,1)S(1)}, u32[]{:S(2)}, u32[]{:S(2)}) collective-permute-start(bf16[8,40,384]{2,1,0:T(8,128)(2,1)S(1)} %dynamic-slice_select_fusion), channel_id=1, source_target_pairs={{0,32},{1,129},{2,34},{3,131},{4,36},{5,133},{6,38},{7,135},{8,40}... | collective-permute-start | bytes 737288 | tf_op jit(solution)/shard_map/ppermute | solution.py:59
  40.7 7.0 %collective-permute-done.9 = bf16[8,40,384]{2,1,0:T(8,128)(2,1)S(1)} collective-permute-done((bf16[8,40,384]{2,1,0:T(8,128)(2,1)S(1)}, bf16[8,40,384]{2,1,0:T(8,128)(2,1)S(1)}, u32[]{:S(2)}, u32[]{:S(2)}) %collective-permute-start.9) | collective-permute-done | bytes 245792 | tf_op jit(solution)/shard_map/ppermute | solution.py:59
  48.9 2.7 %collective-permute-start.16 = (bf16[4,160,384]{2,1,0:T(8,128)(2,1)S(1)}, bf16[4,160,384]{2,1,0:T(8,128)(2,1)S(1)}, u32[]{:S(2)}, u32[]{:S(2)}) collective-permute-start(bf16[4,160,384]{2,1,0:T(8,128)(2,1)S(1)} %bitcast.47), channel_id=1, source_target_pairs={{0,192},{1,49},{2,194},{3,51},{4,196},{5,53},{6,198},{7,55},{8,200... | collective-permute-start | bytes 1474568 | tf_op jit(solution)/shard_map/ppermute | solution.py:59
  52.6 8.1 %collective-permute-start.11 = (bf16[2,7,48,384]{3,2,1,0:T(8,128)(2,1)}, bf16[2,7,48,384]{3,2,1,0:T(8,128)(2,1)}, u32[]{:S(2)}, u32[]{:S(2)}) collective-permute-start(bf16[2,7,48,384]{3,2,1,0:T(8,128)(2,1)} %pad_maximum_fusion.1.high), channel_id=1, source_target_pairs={{0,1},{1,2},{2,3},{3,4},{4,5},{5,6},{6,7},{7,8},{8,9},{9,10},{10,1... | collective-permute-start | bytes 1548296 | tf_op jit(solution)/shard_map/ppermute | solution.py:59
  61.9 1.8 %collective-permute-start.18 = (bf16[4,160,384]{2,1,0:T(8,128)(2,1)S(1)}, bf16[4,160,384]{2,1,0:T(8,128)(2,1)}, u32[]{:S(2)}, u32[]{:S(2)}) collective-permute-start(bf16[4,160,384]{2,1,0:T(8,128)(2,1)S(1)} %collective-permute-done.16.refs_5_), channel_id=1, source_target_pairs={{0,192},{1,49},{2,194},{3,51},{4,196},{5,53},{6,198},{7,55},{8,200... | collective-permute-start | bytes 1474568 | tf_op jit(solution)/shard_map/ppermute | solution.py:59
  65.8 1.2 %collective-permute-start.15 = (bf16[4,160,384]{2,1,0:T(8,128)(2,1)S(1)}, bf16[4,160,384]{2,1,0:T(8,128)(2,1)}, u32[]{:S(2)}, u32[]{:S(2)}) collective-permute-start(bf16[4,160,384]{2,1,0:T(8,128)(2,1)S(1)} %bitcast.44), channel_id=1, source_target_pairs={{0,192},{1,49},{2,194},{3,51},{4,196},{5,53},{6,198},{7,55},{8,200... | collective-permute-start | bytes 1474568 | tf_op jit(solution)/shard_map/ppermute | solution.py:59
  67.0 3.1 %collective-permute-done.14.refs_3_ = bf16[4,160,384]{2,1,0:T(8,128)(2,1)} collective-permute-done((bf16[4,160,384]{2,1,0:T(8,128)(2,1)S(1)}, bf16[4,160,384]{2,1,0:T(8,128)(2,1)}, u32[]{:S(2)}, u32[]{:S(2)}) %collective-permute-start.14) | collective-permute-done | bytes 491552 | tf_op jit(solution)/shard_map/ppermute | solution.py:59
  71.0 4.0 %collective-permute-done.17.refs_6_ = bf16[4,160,384]{2,1,0:T(8,128)(2,1)} collective-permute-done((bf16[4,160,384]{2,1,0:T(8,128)(2,1)S(1)}, bf16[4,160,384]{2,1,0:T(8,128)(2,1)}, u32[]{:S(2)}, u32[]{:S(2)}) %collective-permute-start.17) | collective-permute-done | bytes 491552 | tf_op jit(solution)/shard_map/ppermute | solution.py:59
  75.6 15.2 %conv_first.1 = bf16[4,5,48,384]{3,2,1,0:T(8,128)(2,1)} custom-call(s32[1]{0:T(128)} %bitcast.tile, bf16[2,7,48,384]{3,2,1,0:T(8,128)(2,1)} %collective-permute-done.11.earlier, bf16[2,7,48,384]{3,2,1,0:T(8,128)(2,1)} %pad_maximum_fusion.2.low, bf16[2,7,48,384]{3,2,1,0:T(8,128)(2,1)} %pad_maximum_fusion.1.high, bf16[9,1152,384]{2,1,0:T(8,128)(2,1)} %bitcast.63, ...), custom_call_target="tpu_custom_call" | custom-call | flops 7644119040 | bytes 7962624 | tf_op jit(solution)/shard_map/conv_first/pallas_call | solution.py:209
  91.9 1.2 fusion.11
  93.1 5.6 %collective-permute-start.12 = (bf16[2,5,48,384]{3,2,1,0:T(8,128)(2,1)S(1)}, bf16[2,5,48,384]{3,2,1,0:T(8,128)(2,1)}, u32[]{:S(2)}, u32[]{:S(2)}) collective-permute-start(bf16[2,5,48,384]{3,2,1,0:T(8,128)(2,1)S(1)} %get-tuple-element.24.high), channel_id=1, source_target_pairs={{0,1},{1,2},{2,3},{3,4},{4,5},{5,6},{6,7},{7,8},{8,9},{9,10},{10,1... | collective-permute-start | bytes 1105928 | tf_op jit(solution)/shard_map/ppermute | solution.py:59
  98.9 3.7 %assemble.1.weight = bf16[8,1296,384]{2,1,0:T(8,128)(2,1)S(1)} custom-call(s32[8]{0:T(128)S(1)} %stack.90.where, bf16[4,160,384]{2,1,0:T(8,128)(2,1)S(1)} %bitcast.46, bf16[4,160,384]{2,1,0:T(8,128)(2,1)S(1)} %bitcast.50, bf16[4,160,384]{2,1,0:T(8,128)(2,1)S(1)} %collective-permute-done.13.refs_2_, bf16[4,160,384]{2,1,0:T(8,128)(2,1)} %collective-permute-done.14.refs_3_, ...), custom_call_target="tpu_custom_call" | custom-call | tf_op jit(solution)/shard_map/assemble/pallas_call | solution.py:136
  102.6 3.7 %second_late.1.refs_0_ = bf16[576,384]{1,0:T(8,128)(2,1)} custom-call(bf16[2,5,48,384]{3,2,1,0:T(8,128)(2,1)S(1)} %get-tuple-element.23.low.high, bf16[2,5,48,384]{3,2,1,0:T(8,128)(2,1)S(1)} %get-tuple-element.24.high, bf16[8,1296,384]{2,1,0:T(8,128)(2,1)S(1)} %assemble.1.weight, bf16[576,384]{1,0:T(8,128)(2,1)S(1)} %bitcast.41, f32[1,384]{1,0:T(1,128)S(1)} %reshape.46.bias), custom_call_target="tpu_custom_call" | custom-call | flops 2293235712 | bytes 7962624 | tf_op jit(solution)/shard_map/second_late/pallas_call | solution.py:245
  106.3 4.7 %second_early.1 = bf16[576,384]{1,0:T(8,128)(2,1)} custom-call(bf16[2,5,48,384]{3,2,1,0:T(8,128)(2,1)} %collective-permute-done.12.low, bf16[2,5,48,384]{3,2,1,0:T(8,128)(2,1)S(1)} %get-tuple-element.23.low.high, bf16[8,1296,384]{2,1,0:T(8,128)(2,1)S(1)} %assemble.1.weight, bf16[576,384]{1,0:T(8,128)(2,1)S(1)} %bitcast.42, ...), custom_call_target="tpu_custom_call", output_to_operand_aliasing={{}: (5, {})} | custom-call | flops 2293235712 | bytes 7962624 | tf_op jit(solution)/shard_map/second_early/pallas_call | solution.py:245
  (93 shorter events, 13.5 us)
Async XLA Ops:
  6.5 69.0 %all-gather.2.cloned.1.call-start = ((), (), s32[]{:S(2)}) async-start(), calls=%async_computation | async-start | bytes 8460288 | tf_op jit(solution)/shard_map/all_gather | solution.py:281
  13.6 10.6 %collective-permute-start.3 = (bf16[96,384]{1,0:T(8,128)(2,1)S(1)}, bf16[96,384]{1,0:T(8,128)(2,1)S(1)}, u32[]{:S(2)}, u32[]{:S(2)}) collective-permute-start(bf16[96,384]{1,0:T(8,128)(2,1)S(1)} %pad_maximum_fusion.4), channel_id=1, source_target_pairs={{0,2},{1,15},{2,4},{3,1},{4,6},{5,3},{6,8},{7,5},{8,10},{9,7},{10,... | collective-permute-start | bytes 221192 | tf_op jit(solution)/shard_map/ppermute | solution.py:59
  19.2 9.6 %collective-permute-start.7 = (bf16[96,384]{1,0:T(8,128)(2,1)S(1)}, bf16[96,384]{1,0:T(8,128)(2,1)S(1)}, u32[]{:S(2)}, u32[]{:S(2)}) collective-permute-start(bf16[96,384]{1,0:T(8,128)(2,1)S(1)} %pad_maximum_fusion.4), channel_id=1, source_target_pairs={{0,8},{1,9},{2,10},{3,11},{4,12},{5,13},{6,14},{7,15},{8,0},{9,1},... | collective-permute-start | bytes 221192 | tf_op jit(solution)/shard_map/ppermute | solution.py:59
  29.2 11.5 %collective-permute-start.8 = (bf16[8,40,384]{2,1,0:T(8,128)(2,1)S(1)}, bf16[8,40,384]{2,1,0:T(8,128)(2,1)S(1)}, u32[]{:S(2)}, u32[]{:S(2)}) collective-permute-start(bf16[8,40,384]{2,1,0:T(8,128)(2,1)S(1)} %dynamic-slice_select_fusion), channel_id=1, source_target_pairs={{0,48},{1,193},{2,50},{3,195},{4,52},{5,197},{6,54},{7,199},{8,56}... | collective-permute-start | bytes 737288 | tf_op jit(solution)/shard_map/ppermute | solution.py:59
  32.0 19.6 %collective-permute-start.1 = (bf16[4,2,48,384]{3,2,1,0:T(8,128)(2,1)S(1)}, bf16[4,2,48,384]{3,2,1,0:T(8,128)(2,1)S(1)}, u32[]{:S(2)}, u32[]{:S(2)}) collective-permute-start(bf16[4,2,48,384]{3,2,1,0:T(8,128)(2,1)S(1)} %get-tuple-element.29), channel_id=1, source_target_pairs={{0,16},{1,17},{2,18},{3,19},{4,20},{5,21},{6,22},{7,23},{8,24},{9,... | collective-permute-start | bytes 884744 | tf_op jit(solution)/shard_map/ppermute | solution.py:59
  35.1 16.5 %collective-permute-start.2 = (bf16[4,2,48,384]{3,2,1,0:T(8,128)(2,1)S(1)}, bf16[4,2,48,384]{3,2,1,0:T(8,128)(2,1)S(1)}, u32[]{:S(2)}, u32[]{:S(2)}) collective-permute-start(bf16[4,2,48,384]{3,2,1,0:T(8,128)(2,1)S(1)} %get-tuple-element.30), channel_id=1, source_target_pairs={{16,0},{17,1},{18,2},{19,3},{20,4},{21,5},{22,6},{23,7},{24,8},{25... | collective-permute-start | bytes 884744 | tf_op jit(solution)/shard_map/ppermute | solution.py:59
  36.4 11.2 %collective-permute-start.9 = (bf16[8,40,384]{2,1,0:T(8,128)(2,1)S(1)}, bf16[8,40,384]{2,1,0:T(8,128)(2,1)S(1)}, u32[]{:S(2)}, u32[]{:S(2)}) collective-permute-start(bf16[8,40,384]{2,1,0:T(8,128)(2,1)S(1)} %dynamic-slice_select_fusion), channel_id=1, source_target_pairs={{0,32},{1,129},{2,34},{3,131},{4,36},{5,133},{6,38},{7,135},{8,40}... | collective-permute-start | bytes 737288 | tf_op jit(solution)/shard_map/ppermute | solution.py:59
  39.7 8.5 %collective-permute-start.10 = (bf16[8,40,384]{2,1,0:T(8,128)(2,1)S(1)}, bf16[8,40,384]{2,1,0:T(8,128)(2,1)S(1)}, u32[]{:S(2)}, u32[]{:S(2)}) collective-permute-start(bf16[8,40,384]{2,1,0:T(8,128)(2,1)S(1)} %dynamic-slice_select_fusion), channel_id=1, source_target_pairs={{0,16},{1,65},{2,18},{3,67},{4,20},{5,69},{6,22},{7,71},{8,24},{9,... | collective-permute-start | bytes 737288 | tf_op jit(solution)/shard_map/ppermute | solution.py:59
  48.9 12.0 %collective-permute-start.13 = (bf16[4,160,384]{2,1,0:T(8,128)(2,1)S(1)}, bf16[4,160,384]{2,1,0:T(8,128)(2,1)S(1)}, u32[]{:S(2)}, u32[]{:S(2)}) collective-permute-start(bf16[4,160,384]{2,1,0:T(8,128)(2,1)S(1)} %bitcast.43), channel_id=1, source_target_pairs={{0,64},{1,17},{2,66},{3,19},{4,68},{5,21},{6,70},{7,23},{8,72},{9,... | collective-permute-start | bytes 1474568 | tf_op jit(solution)/shard_map/ppermute | solution.py:59
  48.9 13.0 %collective-permute-start.16 = (bf16[4,160,384]{2,1,0:T(8,128)(2,1)S(1)}, bf16[4,160,384]{2,1,0:T(8,128)(2,1)S(1)}, u32[]{:S(2)}, u32[]{:S(2)}) collective-permute-start(bf16[4,160,384]{2,1,0:T(8,128)(2,1)S(1)} %bitcast.47), channel_id=1, source_target_pairs={{0,192},{1,49},{2,194},{3,51},{4,196},{5,53},{6,198},{7,55},{8,200... | collective-permute-start | bytes 1474568 | tf_op jit(solution)/shard_map/ppermute | solution.py:59
  52.6 18.5 %collective-permute-start.11 = (bf16[2,7,48,384]{3,2,1,0:T(8,128)(2,1)}, bf16[2,7,48,384]{3,2,1,0:T(8,128)(2,1)}, u32[]{:S(2)}, u32[]{:S(2)}) collective-permute-start(bf16[2,7,48,384]{3,2,1,0:T(8,128)(2,1)} %pad_maximum_fusion.1.high), channel_id=1, source_target_pairs={{0,1},{1,2},{2,3},{3,4},{4,5},{5,6},{6,7},{7,8},{8,9},{9,10},{10,1... | collective-permute-start | bytes 1548296 | tf_op jit(solution)/shard_map/ppermute | solution.py:59
  60.7 9.4 %collective-permute-start.14 = (bf16[4,160,384]{2,1,0:T(8,128)(2,1)S(1)}, bf16[4,160,384]{2,1,0:T(8,128)(2,1)}, u32[]{:S(2)}, u32[]{:S(2)}) collective-permute-start(bf16[4,160,384]{2,1,0:T(8,128)(2,1)S(1)} %bitcast.48), channel_id=1, source_target_pairs={{0,64},{1,17},{2,66},{3,19},{4,68},{5,21},{6,70},{7,23},{8,72},{9,... | collective-permute-start | bytes 1474568 | tf_op jit(solution)/shard_map/ppermute | solution.py:59
  60.8 14.2 %collective-permute-start.17 = (bf16[4,160,384]{2,1,0:T(8,128)(2,1)S(1)}, bf16[4,160,384]{2,1,0:T(8,128)(2,1)}, u32[]{:S(2)}, u32[]{:S(2)}) collective-permute-start(bf16[4,160,384]{2,1,0:T(8,128)(2,1)S(1)} %collective-permute-done.13.refs_2_), channel_id=1, source_target_pairs={{0,64},{1,17},{2,66},{3,19},{4,68},{5,21},{6,70},{7,23},{8,72},{9,... | collective-permute-start | bytes 1474568 | tf_op jit(solution)/shard_map/ppermute | solution.py:59
  61.9 13.2 %collective-permute-start.18 = (bf16[4,160,384]{2,1,0:T(8,128)(2,1)S(1)}, bf16[4,160,384]{2,1,0:T(8,128)(2,1)}, u32[]{:S(2)}, u32[]{:S(2)}) collective-permute-start(bf16[4,160,384]{2,1,0:T(8,128)(2,1)S(1)} %collective-permute-done.16.refs_5_), channel_id=1, source_target_pairs={{0,192},{1,49},{2,194},{3,51},{4,196},{5,53},{6,198},{7,55},{8,200... | collective-permute-start | bytes 1474568 | tf_op jit(solution)/shard_map/ppermute | solution.py:59
  65.8 25.0 %collective-permute-start.15 = (bf16[4,160,384]{2,1,0:T(8,128)(2,1)S(1)}, bf16[4,160,384]{2,1,0:T(8,128)(2,1)}, u32[]{:S(2)}, u32[]{:S(2)}) collective-permute-start(bf16[4,160,384]{2,1,0:T(8,128)(2,1)S(1)} %bitcast.44), channel_id=1, source_target_pairs={{0,192},{1,49},{2,194},{3,51},{4,196},{5,53},{6,198},{7,55},{8,200... | collective-permute-start | bytes 1474568 | tf_op jit(solution)/shard_map/ppermute | solution.py:59
  70.1 20.8 %collective-permute-start.19 = (bf16[4,160,384]{2,1,0:T(8,128)(2,1)S(1)}, bf16[4,160,384]{2,1,0:T(8,128)(2,1)}, u32[]{:S(2)}, u32[]{:S(2)}) collective-permute-start(bf16[4,160,384]{2,1,0:T(8,128)(2,1)S(1)} %bitcast.45), channel_id=1, source_target_pairs={{0,1},{1,0},{2,3},{3,2},{4,5},{5,4},{6,7},{7,6},{8,9},{9,8},{10,11... | collective-permute-start | bytes 1474568 | tf_op jit(solution)/shard_map/ppermute | solution.py:59
  71.0 20.4 %collective-permute-start.20 = (bf16[4,160,384]{2,1,0:T(8,128)(2,1)S(1)}, bf16[4,160,384]{2,1,0:T(8,128)(2,1)}, u32[]{:S(2)}, u32[]{:S(2)}) collective-permute-start(bf16[4,160,384]{2,1,0:T(8,128)(2,1)S(1)} %bitcast.49), channel_id=1, source_target_pairs={{0,1},{1,0},{2,3},{3,2},{4,5},{5,4},{6,7},{7,6},{8,9},{9,8},{10,11... | collective-permute-start | bytes 1474568 | tf_op jit(solution)/shard_map/ppermute | solution.py:59
  75.1 16.5 %collective-permute-start.21 = (bf16[4,160,384]{2,1,0:T(8,128)(2,1)S(1)}, bf16[4,160,384]{2,1,0:T(8,128)(2,1)}, u32[]{:S(2)}, u32[]{:S(2)}) collective-permute-start(bf16[4,160,384]{2,1,0:T(8,128)(2,1)S(1)} %collective-permute-done.13.refs_2_), channel_id=1, source_target_pairs={{0,1},{1,0},{2,3},{3,2},{4,5},{5,4},{6,7},{7,6},{8,9},{9,8},{10,11... | collective-permute-start | bytes 1474568 | tf_op jit(solution)/shard_map/ppermute | solution.py:59
  75.1 18.0 %collective-permute-start.22 = (bf16[4,160,384]{2,1,0:T(8,128)(2,1)}, bf16[4,160,384]{2,1,0:T(8,128)(2,1)}, u32[]{:S(2)}, u32[]{:S(2)}) collective-permute-start(bf16[4,160,384]{2,1,0:T(8,128)(2,1)} %collective-permute-done.14.refs_3_), channel_id=1, source_target_pairs={{0,1},{1,0},{2,3},{3,2},{4,5},{5,4},{6,7},{7,6},{8,9},{9,8},{10,11... | collective-permute-start | bytes 1474568 | tf_op jit(solution)/shard_map/ppermute | solution.py:59
  90.8 8.0 %collective-permute-start.24 = (bf16[4,160,384]{2,1,0:T(8,128)(2,1)S(1)}, bf16[4,160,384]{2,1,0:T(8,128)(2,1)}, u32[]{:S(2)}, u32[]{:S(2)}) collective-permute-start(bf16[4,160,384]{2,1,0:T(8,128)(2,1)S(1)} %collective-permute-done.16.refs_5_), channel_id=1, source_target_pairs={{0,1},{1,0},{2,3},{3,2},{4,5},{5,4},{6,7},{7,6},{8,9},{9,8},{10,11... | collective-permute-start | bytes 1474568 | tf_op jit(solution)/shard_map/ppermute | solution.py:59
  90.9 7.9 %collective-permute-start.23 = (bf16[4,160,384]{2,1,0:T(8,128)(2,1)}, bf16[4,160,384]{2,1,0:T(8,128)(2,1)}, u32[]{:S(2)}, u32[]{:S(2)}) collective-permute-start(bf16[4,160,384]{2,1,0:T(8,128)(2,1)} %collective-permute-done.15.refs_4_), channel_id=1, source_target_pairs={{0,1},{1,0},{2,3},{3,2},{4,5},{5,4},{6,7},{7,6},{8,9},{9,8},{10,11... | collective-permute-start | bytes 1474568 | tf_op jit(solution)/shard_map/ppermute | solution.py:59
  91.4 7.4 %collective-permute-start.25 = (bf16[4,160,384]{2,1,0:T(8,128)(2,1)}, bf16[4,160,384]{2,1,0:T(8,128)(2,1)}, u32[]{:S(2)}, u32[]{:S(2)}) collective-permute-start(bf16[4,160,384]{2,1,0:T(8,128)(2,1)} %collective-permute-done.17.refs_6_), channel_id=1, source_target_pairs={{0,1},{1,0},{2,3},{3,2},{4,5},{5,4},{6,7},{7,6},{8,9},{9,8},{10,11... | collective-permute-start | bytes 1474568 | tf_op jit(solution)/shard_map/ppermute | solution.py:59
  91.5 7.3 %collective-permute-start.26 = (bf16[4,160,384]{2,1,0:T(8,128)(2,1)}, bf16[4,160,384]{2,1,0:T(8,128)(2,1)}, u32[]{:S(2)}, u32[]{:S(2)}) collective-permute-start(bf16[4,160,384]{2,1,0:T(8,128)(2,1)} %collective-permute-done.18.refs_7_), channel_id=1, source_target_pairs={{0,1},{1,0},{2,3},{3,2},{4,5},{5,4},{6,7},{7,6},{8,9},{9,8},{10,11... | collective-permute-start | bytes 1474568 | tf_op jit(solution)/shard_map/ppermute | solution.py:59
  93.1 13.2 %collective-permute-start.12 = (bf16[2,5,48,384]{3,2,1,0:T(8,128)(2,1)S(1)}, bf16[2,5,48,384]{3,2,1,0:T(8,128)(2,1)}, u32[]{:S(2)}, u32[]{:S(2)}) collective-permute-start(bf16[2,5,48,384]{3,2,1,0:T(8,128)(2,1)S(1)} %get-tuple-element.24.high), channel_id=1, source_target_pairs={{0,1},{1,2},{2,3},{3,4},{4,5},{5,6},{6,7},{7,8},{8,9},{9,10},{10,1... | collective-permute-start | bytes 1105928 | tf_op jit(solution)/shard_map/ppermute | solution.py:59
  (9 other events, 79.1 us)
Sparse Core Ops, SparseCore 0:
  9.1 60.2 all-gather.1

commit v6 on v4

--- a/solution.py
+++ b/solution.py
@@ -72,7 +72,9 @@
 def grow_rows(own):
     above = send(own[:, 1:], neighbours(1, 0))
     below = send(own[:, :2], neighbours(-1, 0))
-    return jnp.concatenate([above, own, below], axis=1)
+    return [
+        jnp.concatenate([above[k : k + 2], own[k : k + 2], below[k : k + 2]], axis=1) for k in (0, 2)
+    ]
 
 
 def gather(weight, y, x, z, core, rows):
@@ -95,19 +97,19 @@
     last = slabs[:, 2 * PART :]
     chunk = jnp.where(first_core, slabs[:, :PART], slabs[:, PART : 2 * PART])
 
-    chunk = after(chunk, rows)
+    chunk, last, _ = lax.optimization_barrier((chunk, last, rows(both)))
     parts = [chunk, *(send(chunk, pairs) for pairs in (RING_DOWN, RING_FAR, RING_UP))]
     spot = lax.rem(4 - jnp.where(first_core, x, y), 4)
     turned = lax.dynamic_slice_in_dim(jnp.stack(parts + parts), spot, 4, axis=0)
     chunk = turned.transpose(1, 0, 2, 3).reshape(NZ, BLOCK, C)
-    half = NZ // 2
-    up, down = send(chunk, CROSS_UP), send(chunk, CROSS_DOWN)
-    far_up, far_down = send(up[:half], CROSS_UP), send(down[half:], CROSS_DOWN)
-    return [chunk, up, down, far_up, far_down], last
-
-
-def assemble_kernel(where, *refs):
-    *arrays, last, whole, sems = refs
+    low, high = chunk[: NZ // 2], chunk[NZ // 2 :]
+    up_low, down_high = send(low, CROSS_UP), send(high, CROSS_DOWN)
+    up_high, down_low = send(high, CROSS_UP), send(low, CROSS_DOWN)
+    far = send(up_low, CROSS_UP), send(down_high, CROSS_DOWN)
+    return [low, high, up_low, up_high, down_low, down_high, *far], last
+
+
+def start_assembly(where, arrays, last, whole, sems):
     copies = []
 
     def fetch(src, dst):
@@ -117,29 +119,15 @@
 
     half = NZ // 2
     for k, src in enumerate(arrays):
-        at = pl.multiple_of(where[k - k // 5 - k % 5 // 4], BLOCK)
-        slabs = {3: pl.ds(0, half), 4: pl.ds(half, half)}.get(k % 5, pl.ds(0, NZ))
-        fetch(src, whole.at[slabs, pl.ds(at, BLOCK)])
+        at = pl.multiple_of(where[k // 2], BLOCK)
+        fetch(src, whole.at[pl.ds(k % 2 * half, half), pl.ds(at, BLOCK)])
     fetch(last, whole.at[:, pl.ds(8 * BLOCK, 9 * SLAB - 8 * BLOCK)])
-    for copy in copies:
-        copy.wait()
+    return copies
 
 
 ANY = pl.BlockSpec(memory_space=pl.ANY)
 VMEM = pl.BlockSpec(memory_space=pltpu.VMEM)
 SMEM = pl.BlockSpec(memory_space=pltpu.SMEM)
-
-
-def assemble(arrays, where):
-    return pl.pallas_call(
-        assemble_kernel,
-        out_shape=jax.ShapeDtypeStruct((NZ, 9 * SLAB, C), BF),
-        in_specs=[SMEM, *[ANY] * len(arrays)],
-        out_specs=VMEM,
-        scratch_shapes=[pltpu.SemaphoreType.DMA((len(arrays),))],
-        compiler_params=pltpu.CompilerParams(vmem_limit_bytes=12 * 2**20),
-        name="assemble",
-    )(where, *arrays)
 
 
 def convolve(frames, rows, whole, wide):
@@ -176,8 +164,10 @@
     return lines
 
 
-def first_kernel(tile, earlier, grown, weight, bias, gain, out, wide):
-    frames = [earlier[0], earlier[1], *(grown[f] for f in range(4))]
+def first_kernel(tile, where, earlier, low, high, weight, bias, gain, *refs):
+    *arrays, last, out_low, out_high, next_weight, wide, sems = refs
+    copies = start_assembly(where, arrays, last, next_weight, sems)
+    frames = [part[f] for part in (earlier, low, high) for f in range(2)]
     lines = convolve(frames, 5, lambda tap: weight[tap], wide)
     for i, line in enumerate(lines):
         result = activate(line + bias[...], gain[...])
@@ -185,20 +175,24 @@
             result = jnp.where(tile[0] == 0, 0.0, result)
         if i % 5 == 4:
             result = jnp.where(tile[0] == NY * NX - 1, 0.0, result)
-        out[i // 5, i % 5] = result.astype(BF)
-
-
-def conv_first(earlier, grown, weight, bias, gain, tile):
+        out = out_low if i < 10 else out_high
+        out[i // 5 % 2, i % 5] = result.astype(BF)
+    for copy in copies:
+        copy.wait()
+
+
+def conv_first(tile, where, earlier, low, high, weight, bias, gain, pieces):
+    half = jax.ShapeDtypeStruct((2, 5, 48, C), BF)
     return pl.pallas_call(
         first_kernel,
-        out_shape=jax.ShapeDtypeStruct((4, 5, 48, C), BF),
-        in_specs=[SMEM] + [VMEM] * 5,
-        out_specs=VMEM,
-        scratch_shapes=[pltpu.VMEM((960, 3 * C), F32)],
-        compiler_params=pltpu.CompilerParams(vmem_limit_bytes=20 * 2**20),
+        out_shape=[half, half, jax.ShapeDtypeStruct((NZ, 9 * SLAB, C), BF)],
+        in_specs=[SMEM, SMEM] + [VMEM] * 6 + [ANY] * len(pieces),
+        out_specs=[VMEM] * 3,
+        scratch_shapes=[pltpu.VMEM((960, 3 * C), F32), pltpu.SemaphoreType.DMA((len(pieces),))],
+        compiler_params=pltpu.CompilerParams(vmem_limit_bytes=30 * 2**20),
         cost_estimate=cost(960),
         name="conv_first",
-    )(tile, earlier, grown, weight, bias, gain)
+    )(tile, where, earlier, low, high, weight, bias, gain, *pieces)
 
 
 def slab_rows(weight, tap):
@@ -258,19 +252,29 @@
     row = lambda v: v.reshape(1, C)
 
     whole_first = lax.all_gather(weight_first, ("z", "c"), axis=2, tiled=True)
-    first = activate(latent, gain_first).astype(BF)
-    grown = grow_rows(first)
-    pieces, last = gather(weight_second.reshape(9, 72, C), y, x, z, core, grown)
-    earlier = send(after(grown[2:], pieces[0]), neighbours(0, 1))
-    others = [send(v, SWAP) for v in pieces[:3]]
-
-    scales = row(bias_first), row(gain_second), tile
-    second = conv_first(earlier, grown, whole_first.reshape(9, 3 * C, C), *scales)
-    second_low, second_high = second[:2], second[2:]
+    halo = []
+
+    def rows(before):
+        halo.extend(grow_rows(activate(after(latent, before), gain_first).astype(BF)))
+        return halo
+
+    pieces, last = gather(weight_second.reshape(9, 72, C), y, x, z, core, rows)
+    low, high = halo
+    earlier = send(high, neighbours(0, 1))
+    pieces = [*pieces, *(send(v, SWAP) for v in pieces), last]
+
+    second_low, second_high, whole_second = conv_first(
+        tile,
+        where,
+        earlier,
+        low,
+        high,
+        whole_first.reshape(9, 3 * C, C),
+        row(bias_first),
+        row(gain_second),
+        pieces,
+    )
     second_earlier = send(second_high, neighbours(0, 1))
-    far = after(pieces[3:], second)
-    others += [send(v, SWAP) for v in far]
-    whole_second = assemble([*pieces[:3], *far, *others, last], where)
     rest = whole_second, latent.reshape(576, C), row(bias_second)
     partial = conv_second(second_low, second_high, *rest, None)
     return conv_second(second_earlier, second_low, *rest, partial).reshape(4, 3, 48, C)

time: 123 us -> 119 us (0.967)
  waiting for transfers between devices: 23.8 us -> 27 us
  starting transfers between devices: 48.2 us -> 45.2 us
  other arithmetic: 3.93 us -> 2.23 us
  local copies, waits for them, and re-layouts: 9.77 us -> 8.34 us
  Pallas kernels: 22.8 us -> 21.5 us
    slice x4 -> x6, local copies, waits for them, and re-layouts: 3.66 us -> 0.31 us  [the longest x3 0.2 us: gather(): low, high = (chunk[:NZ // 2], chunk[NZ // 2:])]
    ppermute x22 -> x27, waiting for transfers between devices: 23 us -> 26.3 us  [send(): return lax.ppermute(value, AXES, pairs)]
    ppermute x22 -> x27, starting transfers between devices: 48.2 us -> 45.2 us  [send(): return lax.ppermute(value, AXES, pairs)]
    unnamed x28 -> x40, local copies, waits for them, and re-layouts: 4.76 us -> 7.67 us
    pallas_call x2 -> x1, Pallas kernels: 14.4 us -> 14.1 us  [conv_first(): pl.pallas_call(first_kernel, out_shape=[half, half, jax.ShapeDtypeStruct(...]
  transfers between devices with their start and end apart: 23 -> 28, of which waited for: 7 -> 12; matrix products, arithmetic and copies ran while one was open for 8% -> 3% of each run, Pallas kernels for 15% -> 3%
where the time goes in v6:
time: 119 us; the launch traced here: 118 us
  starting transfers between devices  45.2 us (38%)
  waiting for transfers between devices  27 us (23%)
  Pallas kernels  21.5 us (18%)
  between operations  13.9 us (12%)
  local copies, waits for them, and re-layouts  8.34 us (7%)
  other arithmetic  2.23 us (2%)
    ppermute x27, starting transfers between devices, send(): return lax.ppermute(value, AXES, pairs)  45.2 us
    ppermute x27, waiting for transfers between devices, send(): return lax.ppermute(value, AXES, pairs)  26.3 us
    pallas_call x1, Pallas kernels, conv_first(): pl.pallas_call(first_kernel, out_shape=[half, half, jax.ShapeDtypeStruct(...  14.1 us
    unnamed x40, local copies, waits for them, and re-layouts  7.67 us
    pallas_call x2, Pallas kernels, conv_second(): pl.pallas_call(functools.partial(second_kernel, start), out_shape=jax.Sha...  7.42 us
  transfers between devices with their start and end apart: 28, of which 12 were waited for; matrix products, arithmetic and copies ran while one was open for 3% of the time, Pallas kernels for 3%

profile of v6, /device:TPU:1, one launch (start us, length us, event | category | flops | bytes accessed | tf_op | source)
XLA Modules:
  0.0 118.1 jit_solution(4117490690205119406)
XLA Ops:
  7.3 3.3 %collective-permute-start = (bf16[9,72,384]{2,1,0:T(8,128)(2,1)}, bf16[9,72,384]{2,1,0:T(8,128)(2,1)S(1)}, u32[]{:S(2)}, u32[]{:S(2)}) collective-permute-start(bf16[9,72,384]{2,1,0:T(8,128)(2,1)} %bitcast.62), channel_id=1, source_target_pairs={{0,1},{1,0},{2,3},{3,2},{4,5},{5,4},{6,7},{7,6},{8,9},{9,8},{10,11... | collective-permute-start | bytes 1493000 | tf_op jit(solution)/shard_map/ppermute | solution.py:59
  10.6 1.7 %collective-permute-done = bf16[9,72,384]{2,1,0:T(8,128)(2,1)S(1)} collective-permute-done((bf16[9,72,384]{2,1,0:T(8,128)(2,1)}, bf16[9,72,384]{2,1,0:T(8,128)(2,1)S(1)}, u32[]{:S(2)}, u32[]{:S(2)}) %collective-permute-start) | collective-permute-done | bytes 497696 | tf_op jit(solution)/shard_map/ppermute | solution.py:59
  13.6 3.9 %collective-permute-start.4 = (bf16[96,384]{1,0:T(8,128)(2,1)S(1)}, bf16[96,384]{1,0:T(8,128)(2,1)S(1)}, u32[]{:S(2)}, u32[]{:S(2)}) collective-permute-start(bf16[96,384]{1,0:T(8,128)(2,1)S(1)} %pad_maximum_fusion.4), channel_id=1, source_target_pairs={{0,2},{1,15},{2,4},{3,1},{4,6},{5,3},{6,8},{7,5},{8,10},{9,7},{10,... | collective-permute-start | bytes 221192 | tf_op jit(solution)/shard_map/ppermute | solution.py:59
  19.2 4.5 %collective-permute-start.8 = (bf16[96,384]{1,0:T(8,128)(2,1)S(1)}, bf16[96,384]{1,0:T(8,128)(2,1)S(1)}, u32[]{:S(2)}, u32[]{:S(2)}) collective-permute-start(bf16[96,384]{1,0:T(8,128)(2,1)S(1)} %pad_maximum_fusion.4), channel_id=1, source_target_pairs={{0,8},{1,9},{2,10},{3,11},{4,12},{5,13},{6,14},{7,15},{8,0},{9,1},... | collective-permute-start | bytes 221192 | tf_op jit(solution)/shard_map/ppermute | solution.py:59
  24.2 3.1 %collective-permute-start.1 = (bf16[4,2,48,384]{3,2,1,0:T(8,128)(2,1)S(1)}, bf16[4,2,48,384]{3,2,1,0:T(8,128)(2,1)S(1)}, u32[]{:S(2)}, u32[]{:S(2)}) collective-permute-start(bf16[4,2,48,384]{3,2,1,0:T(8,128)(2,1)S(1)} %get-tuple-element.27), channel_id=1, source_target_pairs={{0,16},{1,17},{2,18},{3,19},{4,20},{5,21},{6,22},{7,23},{8,24},{9,... | collective-permute-start | bytes 884744 | tf_op jit(solution)/shard_map/ppermute | solution.py:59
  27.4 1.3 %collective-permute-start.2 = (bf16[4,2,48,384]{3,2,1,0:T(8,128)(2,1)S(1)}, bf16[4,2,48,384]{3,2,1,0:T(8,128)(2,1)S(1)}, u32[]{:S(2)}, u32[]{:S(2)}) collective-permute-start(bf16[4,2,48,384]{3,2,1,0:T(8,128)(2,1)S(1)} %get-tuple-element.28), channel_id=1, source_target_pairs={{16,0},{17,1},{18,2},{19,3},{20,4},{21,5},{22,6},{23,7},{24,8},{25... | collective-permute-start | bytes 884744 | tf_op jit(solution)/shard_map/ppermute | solution.py:59
  28.9 1.4 %collective-permute-done.7 = bf16[3,96,384]{2,1,0:T(8,128)(2,1)S(1)} collective-permute-done((bf16[3,96,384]{2,1,0:T(8,128)(2,1)S(1)}, bf16[3,96,384]{2,1,0:T(8,128)(2,1)S(1)}, u32[]{:S(2)}, u32[]{:S(2)}) %collective-permute-start.7) | collective-permute-done | bytes 221216 | tf_op jit(solution)/shard_map/ppermute | solution.py:59
  30.8 2.2 %collective-permute-done.1 = bf16[4,2,48,384]{3,2,1,0:T(8,128)(2,1)S(1)} collective-permute-done((bf16[4,2,48,384]{3,2,1,0:T(8,128)(2,1)S(1)}, bf16[4,2,48,384]{3,2,1,0:T(8,128)(2,1)S(1)}, u32[]{:S(2)}, u32[]{:S(2)}) %collective-permute-start.1) | collective-permute-done | bytes 294944 | tf_op jit(solution)/shard_map/ppermute | solution.py:59
  33.1 4.5 %collective-permute-done.2 = bf16[4,2,48,384]{3,2,1,0:T(8,128)(2,1)S(1)} collective-permute-done((bf16[4,2,48,384]{3,2,1,0:T(8,128)(2,1)S(1)}, bf16[4,2,48,384]{3,2,1,0:T(8,128)(2,1)S(1)}, u32[]{:S(2)}, u32[]{:S(2)}) %collective-permute-start.2) | collective-permute-done | bytes 294944 | tf_op jit(solution)/shard_map/ppermute | solution.py:59
  37.8 2.9 %collective-permute-start.9 = (bf16[8,40,384]{2,1,0:T(8,128)(2,1)S(1)}, bf16[8,40,384]{2,1,0:T(8,128)(2,1)S(1)}, u32[]{:S(2)}, u32[]{:S(2)}) collective-permute-start(bf16[8,40,384]{2,1,0:T(8,128)(2,1)S(1)} %dynamic-slice_select_fusion), channel_id=1, source_target_pairs={{0,48},{1,193},{2,50},{3,195},{4,52},{5,197},{6,54},{7,199},{8,56}... | collective-permute-start | bytes 737288 | tf_op jit(solution)/shard_map/ppermute | solution.py:59
  41.8 5.6 %collective-permute-start.3 = (bf16[2,7,48,384]{3,2,1,0:T(8,128)(2,1)S(1)}, bf16[2,7,48,384]{3,2,1,0:T(8,128)(2,1)S(1)}, u32[]{:S(2)}, u32[]{:S(2)}) collective-permute-start(bf16[2,7,48,384]{3,2,1,0:T(8,128)(2,1)S(1)} %pad_maximum_fusion.1.high), channel_id=1, source_target_pairs={{0,1},{1,2},{2,3},{3,4},{4,5},{5,6},{6,7},{7,8},{8,9},{9,10},{10,1... | collective-permute-start | bytes 1548296 | tf_op jit(solution)/shard_map/ppermute | solution.py:59
  47.6 2.7 %collective-permute-done.11 = bf16[8,40,384]{2,1,0:T(8,128)(2,1)S(1)} collective-permute-done((bf16[8,40,384]{2,1,0:T(8,128)(2,1)S(1)}, bf16[8,40,384]{2,1,0:T(8,128)(2,1)S(1)}, u32[]{:S(2)}, u32[]{:S(2)}) %collective-permute-start.11) | collective-permute-done | bytes 245792 | tf_op jit(solution)/shard_map/ppermute | solution.py:59
  50.8 1.2 %collective-permute-start.12 = (bf16[4,160,384]{2,1,0:T(8,128)(2,1)S(1)}, bf16[4,160,384]{2,1,0:T(8,128)(2,1)S(1)}, u32[]{:S(2)}, u32[]{:S(2)}) collective-permute-start(bf16[4,160,384]{2,1,0:T(8,128)(2,1)S(1)} %bitcast.43), channel_id=1, source_target_pairs={{0,64},{1,17},{2,66},{3,19},{4,68},{5,21},{6,70},{7,23},{8,72},{9,... | collective-permute-start | bytes 1474568 | tf_op jit(solution)/shard_map/ppermute | solution.py:59
  52.1 1.6 %collective-permute-start.15 = (bf16[4,160,384]{2,1,0:T(8,128)(2,1)S(1)}, bf16[4,160,384]{2,1,0:T(8,128)(2,1)}, u32[]{:S(2)}, u32[]{:S(2)}) collective-permute-start(bf16[4,160,384]{2,1,0:T(8,128)(2,1)S(1)} %bitcast.47), channel_id=1, source_target_pairs={{0,192},{1,49},{2,194},{3,51},{4,196},{5,53},{6,198},{7,55},{8,200... | collective-permute-start | bytes 1474568 | tf_op jit(solution)/shard_map/ppermute | solution.py:59
  53.7 2.7 %collective-permute-start.14 = (bf16[4,160,384]{2,1,0:T(8,128)(2,1)S(1)}, bf16[4,160,384]{2,1,0:T(8,128)(2,1)}, u32[]{:S(2)}, u32[]{:S(2)}) collective-permute-start(bf16[4,160,384]{2,1,0:T(8,128)(2,1)S(1)} %bitcast.44), channel_id=1, source_target_pairs={{0,192},{1,49},{2,194},{3,51},{4,196},{5,53},{6,198},{7,55},{8,200... | collective-permute-start | bytes 1474568 | tf_op jit(solution)/shard_map/ppermute | solution.py:59
  56.4 8.1 %collective-permute-done.3.earlier = bf16[2,7,48,384]{3,2,1,0:T(8,128)(2,1)S(1)} collective-permute-done((bf16[2,7,48,384]{3,2,1,0:T(8,128)(2,1)S(1)}, bf16[2,7,48,384]{3,2,1,0:T(8,128)(2,1)S(1)}, u32[]{:S(2)}, u32[]{:S(2)}) %collective-permute-start.3) | collective-permute-done | bytes 516128 | tf_op jit(solution)/shard_map/ppermute | solution.py:59
  65.0 2.2 %collective-permute-start.16 = (bf16[4,160,384]{2,1,0:T(8,128)(2,1)S(1)}, bf16[4,160,384]{2,1,0:T(8,128)(2,1)}, u32[]{:S(2)}, u32[]{:S(2)}) collective-permute-start(bf16[4,160,384]{2,1,0:T(8,128)(2,1)S(1)} %collective-permute-done.12.refs_2_), channel_id=1, source_target_pairs={{0,64},{1,17},{2,66},{3,19},{4,68},{5,21},{6,70},{7,23},{8,72},{9,... | collective-permute-start | bytes 1474568 | tf_op jit(solution)/shard_map/ppermute | solution.py:59
  67.7 1.3 %collective-permute-start.20 = (bf16[4,160,384]{2,1,0:T(8,128)(2,1)S(1)}, bf16[4,160,384]{2,1,0:T(8,128)(2,1)S(1)}, u32[]{:S(2)}, u32[]{:S(2)}) collective-permute-start(bf16[4,160,384]{2,1,0:T(8,128)(2,1)S(1)} %collective-permute-done.12.refs_2_), channel_id=1, source_target_pairs={{0,1},{1,0},{2,3},{3,2},{4,5},{5,4},{6,7},{7,6},{8,9},{9,8},{10,11... | collective-permute-start | bytes 1474568 | tf_op jit(solution)/shard_map/ppermute | solution.py:59
  71.8 2.5 %collective-permute-done.16.refs_6_ = bf16[4,160,384]{2,1,0:T(8,128)(2,1)} collective-permute-done((bf16[4,160,384]{2,1,0:T(8,128)(2,1)S(1)}, bf16[4,160,384]{2,1,0:T(8,128)(2,1)}, u32[]{:S(2)}, u32[]{:S(2)}) %collective-permute-start.16) | collective-permute-done | bytes 491552 | tf_op jit(solution)/shard_map/ppermute | solution.py:59
  75.5 2.1 %collective-permute-start.24 = (bf16[4,160,384]{2,1,0:T(8,128)(2,1)}, bf16[4,160,384]{2,1,0:T(8,128)(2,1)}, u32[]{:S(2)}, u32[]{:S(2)}) collective-permute-start(bf16[4,160,384]{2,1,0:T(8,128)(2,1)} %collective-permute-done.16.refs_6_), channel_id=1, source_target_pairs={{0,1},{1,0},{2,3},{3,2},{4,5},{5,4},{6,7},{7,6},{8,9},{9,8},{10,11... | collective-permute-start | bytes 1474568 | tf_op jit(solution)/shard_map/ppermute | solution.py:59
  84.7 14.1 %conv_first.1 = (bf16[2,5,48,384]{3,2,1,0:T(8,128)(2,1)S(1)}, bf16[2,5,48,384]{3,2,1,0:T(8,128)(2,1)S(1)}, bf16[8,1296,384]{2,1,0:T(8,128)(2,1)S(1)}) custom-call(s32[1]{0:T(128)} %bitcast.tile, s32[8]{0:T(128)S(1)} %stack.78.where, bf16[2,7,48,384]{3,2,1,0:T(8,128)(2,1)S(1)} %collective-permute-done.3.earlier, ...), custom_call_target="tpu_custom_call" | custom-call | flops 7644119040 | bytes 7962624 | tf_op jit(solution)/shard_map/conv_first/pallas_call | solution.py:186
  98.9 4.2 %collective-permute-start.26 = (bf16[2,5,48,384]{3,2,1,0:T(8,128)(2,1)S(1)}, bf16[2,5,48,384]{3,2,1,0:T(8,128)(2,1)S(1)}, u32[]{:S(2)}, u32[]{:S(2)}) collective-permute-start(bf16[2,5,48,384]{3,2,1,0:T(8,128)(2,1)S(1)} %get-tuple-element.14.high), channel_id=1, source_target_pairs={{0,1},{1,2},{2,3},{3,4},{4,5},{5,6},{6,7},{7,8},{8,9},{9,10},{10,1... | collective-permute-start | bytes 1105928 | tf_op jit(solution)/shard_map/ppermute | solution.py:59
  103.1 3.7 %second_late.1.refs_0_ = bf16[576,384]{1,0:T(8,128)(2,1)} custom-call(bf16[2,5,48,384]{3,2,1,0:T(8,128)(2,1)S(1)} %get-tuple-element.15.low.high, bf16[2,5,48,384]{3,2,1,0:T(8,128)(2,1)S(1)} %get-tuple-element.14.high, bf16[8,1296,384]{2,1,0:T(8,128)(2,1)S(1)} %get-tuple-element.16.weight, bf16[576,384]{1,0:T(8,128)(2,1)S(1)} %bitcast.41, ...), custom_call_target="tpu_custom_call" | custom-call | flops 2293235712 | bytes 7962624 | tf_op jit(solution)/shard_map/second_late/pallas_call | solution.py:218
  107.5 3.7 %second_early.1 = bf16[576,384]{1,0:T(8,128)(2,1)} custom-call(bf16[2,5,48,384]{3,2,1,0:T(8,128)(2,1)S(1)} %collective-permute-done.26.low, bf16[2,5,48,384]{3,2,1,0:T(8,128)(2,1)S(1)} %get-tuple-element.15.low.high, bf16[8,1296,384]{2,1,0:T(8,128)(2,1)S(1)} %get-tuple-element.16.weight, ...), custom_call_target="tpu_custom_call", output_to_operand_aliasing={{}: (5, {})} | custom-call | flops 2293235712 | bytes 7962624 | tf_op jit(solution)/shard_map/second_early/pallas_call | solution.py:218
  (107 shorter events, 19.7 us)
Async XLA Ops:
  6.5 74.1 %all-gather.2.cloned.1.call-start = ((), (), s32[]{:S(2)}) async-start(), calls=%async_computation | async-start | bytes 8460288 | tf_op jit(solution)/shard_map/all_gather | solution.py:254
  7.3 5.0 %collective-permute-start = (bf16[9,72,384]{2,1,0:T(8,128)(2,1)}, bf16[9,72,384]{2,1,0:T(8,128)(2,1)S(1)}, u32[]{:S(2)}, u32[]{:S(2)}) collective-permute-start(bf16[9,72,384]{2,1,0:T(8,128)(2,1)} %bitcast.62), channel_id=1, source_target_pairs={{0,1},{1,0},{2,3},{3,2},{4,5},{5,4},{6,7},{7,6},{8,9},{9,8},{10,11... | collective-permute-start | bytes 1493000 | tf_op jit(solution)/shard_map/ppermute | solution.py:59
  13.6 13.8 %collective-permute-start.4 = (bf16[96,384]{1,0:T(8,128)(2,1)S(1)}, bf16[96,384]{1,0:T(8,128)(2,1)S(1)}, u32[]{:S(2)}, u32[]{:S(2)}) collective-permute-start(bf16[96,384]{1,0:T(8,128)(2,1)S(1)} %pad_maximum_fusion.4), channel_id=1, source_target_pairs={{0,2},{1,15},{2,4},{3,1},{4,6},{5,3},{6,8},{7,5},{8,10},{9,7},{10,... | collective-permute-start | bytes 221192 | tf_op jit(solution)/shard_map/ppermute | solution.py:59
  17.5 11.2 %collective-permute-start.5 = (bf16[96,384]{1,0:T(8,128)(2,1)S(1)}, bf16[96,384]{1,0:T(8,128)(2,1)S(1)}, u32[]{:S(2)}, u32[]{:S(2)}) collective-permute-start(bf16[96,384]{1,0:T(8,128)(2,1)S(1)} %pad_maximum_fusion.4), channel_id=1, source_target_pairs={{0,4},{1,13},{2,6},{3,15},{4,8},{5,1},{6,10},{7,3},{8,12},{9,5},{1... | collective-permute-start | bytes 221192 | tf_op jit(solution)/shard_map/ppermute | solution.py:59
  18.7 10.0 %collective-permute-start.6 = (bf16[96,384]{1,0:T(8,128)(2,1)S(1)}, bf16[96,384]{1,0:T(8,128)(2,1)S(1)}, u32[]{:S(2)}, u32[]{:S(2)}) collective-permute-start(bf16[96,384]{1,0:T(8,128)(2,1)S(1)} %pad_maximum_fusion.4), channel_id=1, source_target_pairs={{0,6},{1,11},{2,8},{3,13},{4,10},{5,15},{6,12},{7,1},{8,14},{9,3},... | collective-permute-start | bytes 221192 | tf_op jit(solution)/shard_map/ppermute | solution.py:59
  19.2 11.3 %collective-permute-start.8 = (bf16[96,384]{1,0:T(8,128)(2,1)S(1)}, bf16[96,384]{1,0:T(8,128)(2,1)S(1)}, u32[]{:S(2)}, u32[]{:S(2)}) collective-permute-start(bf16[96,384]{1,0:T(8,128)(2,1)S(1)} %pad_maximum_fusion.4), channel_id=1, source_target_pairs={{0,8},{1,9},{2,10},{3,11},{4,12},{5,13},{6,14},{7,15},{8,0},{9,1},... | collective-permute-start | bytes 221192 | tf_op jit(solution)/shard_map/ppermute | solution.py:59
  24.2 8.9 %collective-permute-start.1 = (bf16[4,2,48,384]{3,2,1,0:T(8,128)(2,1)S(1)}, bf16[4,2,48,384]{3,2,1,0:T(8,128)(2,1)S(1)}, u32[]{:S(2)}, u32[]{:S(2)}) collective-permute-start(bf16[4,2,48,384]{3,2,1,0:T(8,128)(2,1)S(1)} %get-tuple-element.27), channel_id=1, source_target_pairs={{0,16},{1,17},{2,18},{3,19},{4,20},{5,21},{6,22},{7,23},{8,24},{9,... | collective-permute-start | bytes 884744 | tf_op jit(solution)/shard_map/ppermute | solution.py:59
  27.4 10.2 %collective-permute-start.2 = (bf16[4,2,48,384]{3,2,1,0:T(8,128)(2,1)S(1)}, bf16[4,2,48,384]{3,2,1,0:T(8,128)(2,1)S(1)}, u32[]{:S(2)}, u32[]{:S(2)}) collective-permute-start(bf16[4,2,48,384]{3,2,1,0:T(8,128)(2,1)S(1)} %get-tuple-element.28), channel_id=1, source_target_pairs={{16,0},{17,1},{18,2},{19,3},{20,4},{21,5},{22,6},{23,7},{24,8},{25... | collective-permute-start | bytes 884744 | tf_op jit(solution)/shard_map/ppermute | solution.py:59
  37.8 9.6 %collective-permute-start.9 = (bf16[8,40,384]{2,1,0:T(8,128)(2,1)S(1)}, bf16[8,40,384]{2,1,0:T(8,128)(2,1)S(1)}, u32[]{:S(2)}, u32[]{:S(2)}) collective-permute-start(bf16[8,40,384]{2,1,0:T(8,128)(2,1)S(1)} %dynamic-slice_select_fusion), channel_id=1, source_target_pairs={{0,48},{1,193},{2,50},{3,195},{4,52},{5,197},{6,54},{7,199},{8,56}... | collective-permute-start | bytes 737288 | tf_op jit(solution)/shard_map/ppermute | solution.py:59
  40.7 6.9 %collective-permute-start.10 = (bf16[8,40,384]{2,1,0:T(8,128)(2,1)S(1)}, bf16[8,40,384]{2,1,0:T(8,128)(2,1)S(1)}, u32[]{:S(2)}, u32[]{:S(2)}) collective-permute-start(bf16[8,40,384]{2,1,0:T(8,128)(2,1)S(1)} %dynamic-slice_select_fusion), channel_id=1, source_target_pairs={{0,32},{1,129},{2,34},{3,131},{4,36},{5,133},{6,38},{7,135},{8,40}... | collective-permute-start | bytes 737288 | tf_op jit(solution)/shard_map/ppermute | solution.py:59
  41.1 9.2 %collective-permute-start.11 = (bf16[8,40,384]{2,1,0:T(8,128)(2,1)S(1)}, bf16[8,40,384]{2,1,0:T(8,128)(2,1)S(1)}, u32[]{:S(2)}, u32[]{:S(2)}) collective-permute-start(bf16[8,40,384]{2,1,0:T(8,128)(2,1)S(1)} %dynamic-slice_select_fusion), channel_id=1, source_target_pairs={{0,16},{1,65},{2,18},{3,67},{4,20},{5,69},{6,22},{7,71},{8,24},{9,... | collective-permute-start | bytes 737288 | tf_op jit(solution)/shard_map/ppermute | solution.py:59
  41.8 22.7 %collective-permute-start.3 = (bf16[2,7,48,384]{3,2,1,0:T(8,128)(2,1)S(1)}, bf16[2,7,48,384]{3,2,1,0:T(8,128)(2,1)S(1)}, u32[]{:S(2)}, u32[]{:S(2)}) collective-permute-start(bf16[2,7,48,384]{3,2,1,0:T(8,128)(2,1)S(1)} %pad_maximum_fusion.1.high), channel_id=1, source_target_pairs={{0,1},{1,2},{2,3},{3,4},{4,5},{5,6},{6,7},{7,8},{8,9},{9,10},{10,1... | collective-permute-start | bytes 1548296 | tf_op jit(solution)/shard_map/ppermute | solution.py:59
  50.8 13.7 %collective-permute-start.12 = (bf16[4,160,384]{2,1,0:T(8,128)(2,1)S(1)}, bf16[4,160,384]{2,1,0:T(8,128)(2,1)S(1)}, u32[]{:S(2)}, u32[]{:S(2)}) collective-permute-start(bf16[4,160,384]{2,1,0:T(8,128)(2,1)S(1)} %bitcast.43), channel_id=1, source_target_pairs={{0,64},{1,17},{2,66},{3,19},{4,68},{5,21},{6,70},{7,23},{8,72},{9,... | collective-permute-start | bytes 1474568 | tf_op jit(solution)/shard_map/ppermute | solution.py:59
  52.1 12.9 %collective-permute-start.15 = (bf16[4,160,384]{2,1,0:T(8,128)(2,1)S(1)}, bf16[4,160,384]{2,1,0:T(8,128)(2,1)}, u32[]{:S(2)}, u32[]{:S(2)}) collective-permute-start(bf16[4,160,384]{2,1,0:T(8,128)(2,1)S(1)} %bitcast.47), channel_id=1, source_target_pairs={{0,192},{1,49},{2,194},{3,51},{4,196},{5,53},{6,198},{7,55},{8,200... | collective-permute-start | bytes 1474568 | tf_op jit(solution)/shard_map/ppermute | solution.py:59
  53.7 13.5 %collective-permute-start.13 = (bf16[4,160,384]{2,1,0:T(8,128)(2,1)S(1)}, bf16[4,160,384]{2,1,0:T(8,128)(2,1)}, u32[]{:S(2)}, u32[]{:S(2)}) collective-permute-start(bf16[4,160,384]{2,1,0:T(8,128)(2,1)S(1)} %bitcast.48), channel_id=1, source_target_pairs={{0,64},{1,17},{2,66},{3,19},{4,68},{5,21},{6,70},{7,23},{8,72},{9,... | collective-permute-start | bytes 1474568 | tf_op jit(solution)/shard_map/ppermute | solution.py:59
  53.7 14.0 %collective-permute-start.14 = (bf16[4,160,384]{2,1,0:T(8,128)(2,1)S(1)}, bf16[4,160,384]{2,1,0:T(8,128)(2,1)}, u32[]{:S(2)}, u32[]{:S(2)}) collective-permute-start(bf16[4,160,384]{2,1,0:T(8,128)(2,1)S(1)} %bitcast.44), channel_id=1, source_target_pairs={{0,192},{1,49},{2,194},{3,51},{4,196},{5,53},{6,198},{7,55},{8,200... | collective-permute-start | bytes 1474568 | tf_op jit(solution)/shard_map/ppermute | solution.py:59
  64.5 5.3 %collective-permute-start.18 = (bf16[4,160,384]{2,1,0:T(8,128)(2,1)S(1)}, bf16[4,160,384]{2,1,0:T(8,128)(2,1)S(1)}, u32[]{:S(2)}, u32[]{:S(2)}) collective-permute-start(bf16[4,160,384]{2,1,0:T(8,128)(2,1)S(1)} %bitcast.45), channel_id=1, source_target_pairs={{0,1},{1,0},{2,3},{3,2},{4,5},{5,4},{6,7},{7,6},{8,9},{9,8},{10,11... | collective-permute-start | bytes 1474568 | tf_op jit(solution)/shard_map/ppermute | solution.py:59
  64.5 6.0 %collective-permute-start.19 = (bf16[4,160,384]{2,1,0:T(8,128)(2,1)S(1)}, bf16[4,160,384]{2,1,0:T(8,128)(2,1)S(1)}, u32[]{:S(2)}, u32[]{:S(2)}) collective-permute-start(bf16[4,160,384]{2,1,0:T(8,128)(2,1)S(1)} %bitcast.49), channel_id=1, source_target_pairs={{0,1},{1,0},{2,3},{3,2},{4,5},{5,4},{6,7},{7,6},{8,9},{9,8},{10,11... | collective-permute-start | bytes 1474568 | tf_op jit(solution)/shard_map/ppermute | solution.py:59
  65.0 9.3 %collective-permute-start.16 = (bf16[4,160,384]{2,1,0:T(8,128)(2,1)S(1)}, bf16[4,160,384]{2,1,0:T(8,128)(2,1)}, u32[]{:S(2)}, u32[]{:S(2)}) collective-permute-start(bf16[4,160,384]{2,1,0:T(8,128)(2,1)S(1)} %collective-permute-done.12.refs_2_), channel_id=1, source_target_pairs={{0,64},{1,17},{2,66},{3,19},{4,68},{5,21},{6,70},{7,23},{8,72},{9,... | collective-permute-start | bytes 1474568 | tf_op jit(solution)/shard_map/ppermute | solution.py:59
  67.2 8.3 %collective-permute-start.17 = (bf16[4,160,384]{2,1,0:T(8,128)(2,1)}, bf16[4,160,384]{2,1,0:T(8,128)(2,1)}, u32[]{:S(2)}, u32[]{:S(2)}) collective-permute-start(bf16[4,160,384]{2,1,0:T(8,128)(2,1)} %collective-permute-done.15.refs_5_), channel_id=1, source_target_pairs={{0,192},{1,49},{2,194},{3,51},{4,196},{5,53},{6,198},{7,55},{8,200... | collective-permute-start | bytes 1474568 | tf_op jit(solution)/shard_map/ppermute | solution.py:59
  67.7 9.9 %collective-permute-start.20 = (bf16[4,160,384]{2,1,0:T(8,128)(2,1)S(1)}, bf16[4,160,384]{2,1,0:T(8,128)(2,1)S(1)}, u32[]{:S(2)}, u32[]{:S(2)}) collective-permute-start(bf16[4,160,384]{2,1,0:T(8,128)(2,1)S(1)} %collective-permute-done.12.refs_2_), channel_id=1, source_target_pairs={{0,1},{1,0},{2,3},{3,2},{4,5},{5,4},{6,7},{7,6},{8,9},{9,8},{10,11... | collective-permute-start | bytes 1474568 | tf_op jit(solution)/shard_map/ppermute | solution.py:59
  70.5 8.0 %collective-permute-start.23 = (bf16[4,160,384]{2,1,0:T(8,128)(2,1)}, bf16[4,160,384]{2,1,0:T(8,128)(2,1)}, u32[]{:S(2)}, u32[]{:S(2)}) collective-permute-start(bf16[4,160,384]{2,1,0:T(8,128)(2,1)} %collective-permute-done.15.refs_5_), channel_id=1, source_target_pairs={{0,1},{1,0},{2,3},{3,2},{4,5},{5,4},{6,7},{7,6},{8,9},{9,8},{10,11... | collective-permute-start | bytes 1474568 | tf_op jit(solution)/shard_map/ppermute | solution.py:59
  71.3 7.2 %collective-permute-start.21 = (bf16[4,160,384]{2,1,0:T(8,128)(2,1)}, bf16[4,160,384]{2,1,0:T(8,128)(2,1)}, u32[]{:S(2)}, u32[]{:S(2)}) collective-permute-start(bf16[4,160,384]{2,1,0:T(8,128)(2,1)} %collective-permute-done.13.refs_3_), channel_id=1, source_target_pairs={{0,1},{1,0},{2,3},{3,2},{4,5},{5,4},{6,7},{7,6},{8,9},{9,8},{10,11... | collective-permute-start | bytes 1474568 | tf_op jit(solution)/shard_map/ppermute | solution.py:59
  98.9 8.7 %collective-permute-start.26 = (bf16[2,5,48,384]{3,2,1,0:T(8,128)(2,1)S(1)}, bf16[2,5,48,384]{3,2,1,0:T(8,128)(2,1)S(1)}, u32[]{:S(2)}, u32[]{:S(2)}) collective-permute-start(bf16[2,5,48,384]{3,2,1,0:T(8,128)(2,1)S(1)} %get-tuple-element.14.high), channel_id=1, source_target_pairs={{0,1},{1,2},{2,3},{3,4},{4,5},{5,6},{6,7},{7,8},{8,9},{9,10},{10,1... | collective-permute-start | bytes 1105928 | tf_op jit(solution)/shard_map/ppermute | solution.py:59
  (17 other events, 113.5 us)
Sparse Core Ops, SparseCore 0:
  9.1 63.5 all-gather.1

commit v7 on v6

--- a/solution.py
+++ b/solution.py
@@ -42,6 +42,7 @@
 
 RING_FAR = perm(lambda y, x, z, c: (y, x + 2, z, c) if c == 0 else (y + 2, x, z, c))
 CROSS_UP = perm(lambda y, x, z, c: (y + 1, x, z, c) if c == 0 else (y, x + 1, z, c))
+CROSS_FAR = perm(lambda y, x, z, c: (y + 2, x, z, c) if c == 0 else (y, x + 2, z, c))
 CROSS_DOWN = perm(lambda y, x, z, c: (y - 1, x, z, c) if c == 0 else (y, x - 1, z, c))
 
 
@@ -97,32 +98,15 @@
     last = slabs[:, 2 * PART :]
     chunk = jnp.where(first_core, slabs[:, :PART], slabs[:, PART : 2 * PART])
 
-    chunk, last, _ = lax.optimization_barrier((chunk, last, rows(both)))
+    halo = rows(both)
+    chunk, last, _ = lax.optimization_barrier((chunk, last, halo))
     parts = [chunk, *(send(chunk, pairs) for pairs in (RING_DOWN, RING_FAR, RING_UP))]
     spot = lax.rem(4 - jnp.where(first_core, x, y), 4)
     turned = lax.dynamic_slice_in_dim(jnp.stack(parts + parts), spot, 4, axis=0)
     chunk = turned.transpose(1, 0, 2, 3).reshape(NZ, BLOCK, C)
-    low, high = chunk[: NZ // 2], chunk[NZ // 2 :]
-    up_low, down_high = send(low, CROSS_UP), send(high, CROSS_DOWN)
-    up_high, down_low = send(high, CROSS_UP), send(low, CROSS_DOWN)
-    far = send(up_low, CROSS_UP), send(down_high, CROSS_DOWN)
-    return [low, high, up_low, up_high, down_low, down_high, *far], last
-
-
-def start_assembly(where, arrays, last, whole, sems):
-    copies = []
-
-    def fetch(src, dst):
-        copy = pltpu.make_async_copy(src, dst, sems.at[len(copies)])
-        copy.start()
-        copies.append(copy)
-
-    half = NZ // 2
-    for k, src in enumerate(arrays):
-        at = pl.multiple_of(where[k // 2], BLOCK)
-        fetch(src, whole.at[pl.ds(k % 2 * half, half), pl.ds(at, BLOCK)])
-    fetch(last, whole.at[:, pl.ds(8 * BLOCK, 9 * SLAB - 8 * BLOCK)])
-    return copies
+    up, down = send(chunk, CROSS_UP), send(chunk, CROSS_DOWN)
+    far = send(after(chunk, up, down), CROSS_FAR)
+    return [chunk, up, down, far], last, halo
 
 
 ANY = pl.BlockSpec(memory_space=pl.ANY)
@@ -164,9 +148,7 @@
     return lines
 
 
-def first_kernel(tile, where, earlier, low, high, weight, bias, gain, *refs):
-    *arrays, last, out_low, out_high, next_weight, wide, sems = refs
-    copies = start_assembly(where, arrays, last, next_weight, sems)
+def first_kernel(tile, earlier, low, high, weight, bias, gain, out_low, out_high, wide):
     frames = [part[f] for part in (earlier, low, high) for f in range(2)]
     lines = convolve(frames, 5, lambda tap: weight[tap], wide)
     for i, line in enumerate(lines):
@@ -177,32 +159,52 @@
             result = jnp.where(tile[0] == NY * NX - 1, 0.0, result)
         out = out_low if i < 10 else out_high
         out[i // 5 % 2, i % 5] = result.astype(BF)
-    for copy in copies:
-        copy.wait()
-
-
-def conv_first(tile, where, earlier, low, high, weight, bias, gain, pieces):
+
+
+def conv_first(tile, earlier, low, high, weight, bias, gain):
     half = jax.ShapeDtypeStruct((2, 5, 48, C), BF)
     return pl.pallas_call(
         first_kernel,
-        out_shape=[half, half, jax.ShapeDtypeStruct((NZ, 9 * SLAB, C), BF)],
-        in_specs=[SMEM, SMEM] + [VMEM] * 6 + [ANY] * len(pieces),
-        out_specs=[VMEM] * 3,
-        scratch_shapes=[pltpu.VMEM((960, 3 * C), F32), pltpu.SemaphoreType.DMA((len(pieces),))],
-        compiler_params=pltpu.CompilerParams(vmem_limit_bytes=30 * 2**20),
+        out_shape=[half, half],
+        in_specs=[SMEM] + [VMEM] * 6,
+        out_specs=[VMEM, VMEM],
+        scratch_shapes=[pltpu.VMEM((960, 3 * C), F32)],
+        compiler_params=pltpu.CompilerParams(vmem_limit_bytes=20 * 2**20),
         cost_estimate=cost(960),
         name="conv_first",
-    )(tile, where, earlier, low, high, weight, bias, gain, *pieces)
+    )(tile, earlier, low, high, weight, bias, gain)
 
 
 def slab_rows(weight, tap):
     return weight[:, SLAB * tap : SLAB * (tap + 1)].reshape(3 * C, C)
 
 
-def second_kernel(start, low, high, weight, latent, bias, *refs):
-    out, wide, done, sem = refs[-4:]
-    frames = [low[0], low[1], high[0], high[1]]
-    lines = convolve(frames, 3, lambda tap: slab_rows(weight, tap), wide)
+def assembled(where, arrays, last, whole, sems):
+    def start(block, index):
+        @pl.when(where[index] == block * BLOCK)
+        def _():
+            rows = whole.at[:, pl.ds(block * BLOCK, BLOCK)]
+            pltpu.make_async_copy(arrays[index], rows, sems.at[block]).start()
+
+    for block in range(8):
+        for index in range(8):
+            start(block, index)
+    rest = whole.at[:, pl.ds(8 * BLOCK, 9 * SLAB - 8 * BLOCK)]
+    pltpu.make_async_copy(last, rest, sems.at[8]).start()
+    arrived = set()
+
+    def rows(tap):
+        for block in range(SLAB * tap // BLOCK, -(-SLAB * (tap + 1) // BLOCK)):
+            if block not in arrived:
+                arrived.add(block)
+                at = whole.at[:, pl.ds(block * BLOCK, BLOCK)] if block < 8 else rest
+                pltpu.make_async_copy(at, at, sems.at[block]).wait()
+        return slab_rows(whole, tap)
+
+    return rows
+
+
+def finish(lines, start, latent, bias, out, done, sem):
     for i, line in enumerate(lines):
         at = start + 48 * i
         done[48 * i : 48 * i + 48] = (
@@ -213,23 +215,50 @@
     copy.wait()
 
 
-def conv_second(low, high, weight, latent, bias, partial):
-    start = 288 if partial is None else 0
+def late_kernel(where, low, high, latent, bias, *refs):
+    *arrays, last, out, whole, wide, done, sems, sem = refs
+    rows = assembled(where, arrays, last, whole, sems)
+    frames = [part[f] for part in (low, high) for f in range(2)]
+    finish(convolve(frames, 3, rows, wide), 288, latent, bias, out, done, sem)
+
+
+def early_kernel(low, high, latent, bias, weight, partial, out, wide, done, sem):
+    frames = [part[f] for part in (low, high) for f in range(2)]
+    lines = convolve(frames, 3, lambda tap: slab_rows(weight, tap), wide)
+    finish(lines, 0, latent, bias, out, done, sem)
+
+
+SCRATCH = [pltpu.VMEM((288, 3 * C), F32), pltpu.VMEM((288, C), BF)]
+
+
+def conv_late(where, low, high, latent, bias, pieces):
     return pl.pallas_call(
-        functools.partial(second_kernel, start),
+        late_kernel,
+        out_shape=[
+            jax.ShapeDtypeStruct((576, C), BF),
+            jax.ShapeDtypeStruct((NZ, 9 * SLAB, C), BF),
+        ],
+        in_specs=[SMEM] + [VMEM] * 4 + [ANY] * len(pieces),
+        out_specs=[ANY, VMEM],
+        scratch_shapes=[*SCRATCH, pltpu.SemaphoreType.DMA((9,)), pltpu.SemaphoreType.DMA],
+        compiler_params=pltpu.CompilerParams(vmem_limit_bytes=20 * 2**20),
+        cost_estimate=cost(288),
+        name="second_late",
+    )(where, low, high, latent, bias, *pieces)
+
+
+def conv_early(low, high, latent, bias, weight, partial):
+    return pl.pallas_call(
+        early_kernel,
         out_shape=jax.ShapeDtypeStruct((576, C), BF),
-        in_specs=[VMEM] * 5 + ([] if partial is None else [ANY]),
+        in_specs=[VMEM] * 5 + [ANY],
         out_specs=ANY,
-        input_output_aliases={} if partial is None else {5: 0},
-        scratch_shapes=[
-            pltpu.VMEM((288, 3 * C), F32),
-            pltpu.VMEM((288, C), BF),
-            pltpu.SemaphoreType.DMA,
-        ],
+        input_output_aliases={5: 0},
+        scratch_shapes=[*SCRATCH, pltpu.SemaphoreType.DMA],
         compiler_params=pltpu.CompilerParams(vmem_limit_bytes=12 * 2**20),
         cost_estimate=cost(288),
-        name="second_late" if start else "second_early",
-    )(low, high, weight, latent, bias, *([] if partial is None else [partial]))
+        name="second_early",
+    )(low, high, latent, bias, weight, partial)
 
 
 def cost(size):
@@ -252,32 +281,26 @@
     row = lambda v: v.reshape(1, C)
 
     whole_first = lax.all_gather(weight_first, ("z", "c"), axis=2, tiled=True)
-    halo = []
 
     def rows(before):
-        halo.extend(grow_rows(activate(after(latent, before), gain_first).astype(BF)))
-        return halo
-
-    pieces, last = gather(weight_second.reshape(9, 72, C), y, x, z, core, rows)
-    low, high = halo
-    earlier = send(high, neighbours(0, 1))
-    pieces = [*pieces, *(send(v, SWAP) for v in pieces), last]
-
-    second_low, second_high, whole_second = conv_first(
-        tile,
-        where,
-        earlier,
-        low,
-        high,
-        whole_first.reshape(9, 3 * C, C),
-        row(bias_first),
-        row(gain_second),
-        pieces,
+        return grow_rows(activate(after(latent, before), gain_first).astype(BF))
+
+    pieces, last, (low, high) = gather(weight_second.reshape(9, 72, C), y, x, z, core, rows)
+    earlier = send(after(high, pieces[0]), neighbours(0, 1))
+    others = [send(v, SWAP) for v in pieces[:3]]
+
+    second_low, second_high = conv_first(
+        tile, earlier, low, high, whole_first.reshape(9, 3 * C, C), row(bias_first), row(gain_second)
     )
     second_earlier = send(second_high, neighbours(0, 1))
-    rest = whole_second, latent.reshape(576, C), row(bias_second)
-    partial = conv_second(second_low, second_high, *rest, None)
-    return conv_second(second_earlier, second_low, *rest, partial).reshape(4, 3, 48, C)
+    pieces[3] = after(pieces[3], second_high)
+    others.append(send(pieces[3], SWAP))
+    rest = latent.reshape(576, C), row(bias_second)
+    partial, whole_second = conv_late(
+        where, second_low, second_high, *rest, [*pieces, *others, last]
+    )
+    result = conv_early(second_earlier, second_low, *rest, whole_second, partial)
+    return result.reshape(4, 3, 48, C)
 
 
 def solution(mesh):

time: 119 us -> 112 us (0.941)
  starting transfers between devices: 45.2 us -> 41.3 us
  local copies, waits for them, and re-layouts: 8.34 us -> 5.28 us
  waiting for transfers between devices: 27 us -> 24 us
  Pallas kernels: 21.5 us -> 22.7 us
    ppermute x27 -> x20, starting transfers between devices: 45.2 us -> 41.3 us  [send(): return lax.ppermute(value, AXES, pairs)]
    unnamed x40 -> x28, local copies, waits for them, and re-layouts: 7.67 us -> 4.72 us
    ppermute x27 -> x20, waiting for transfers between devices: 26.3 us -> 23.3 us  [send(): return lax.ppermute(value, AXES, pairs)]
  transfers between devices with their start and end apart: 28 -> 21, of which waited for: 12 -> 8; matrix products, arithmetic and copies ran while one was open for 3% -> 4% of each run, Pallas kernels for 3% -> 17%
where the time goes in v7:
time: 112 us; the launch traced here: 110 us
  starting transfers between devices  41.3 us (37%)
  waiting for transfers between devices  24 us (21%)
  Pallas kernels  22.7 us (20%)
  between operations  13.9 us (12%)
  local copies, waits for them, and re-layouts  5.28 us (5%)
  other arithmetic  3.01 us (3%)
    ppermute x20, starting transfers between devices, send(): return lax.ppermute(value, AXES, pairs)  41.3 us
    ppermute x20, waiting for transfers between devices, send(): return lax.ppermute(value, AXES, pairs)  23.3 us
    pallas_call x1, Pallas kernels, conv_first(): pl.pallas_call(first_kernel, out_shape=[half, half], in_specs=[SMEM] + [V...  11.8 us
    pallas_call x1, Pallas kernels, conv_late(): pl.pallas_call(late_kernel, out_shape=[jax.ShapeDtypeStruct((576, C), BF)...  7.13 us
    unnamed x28, local copies, waits for them, and re-layouts  4.72 us
    pallas_call x1, Pallas kernels, conv_early(): pl.pallas_call(early_kernel, out_shape=jax.ShapeDtypeStruct((576, C), BF)...  3.7 us
  transfers between devices with their start and end apart: 21, of which 8 were waited for; matrix products, arithmetic and copies ran while one was open for 4% of the time, Pallas kernels for 17%

profile of v7, /device:TPU:1, one launch (start us, length us, event | category | flops | bytes accessed | tf_op | source)
XLA Modules:
  0.0 110.2 jit_solution(7401691976424914647)
XLA Ops:
  7.3 3.3 %collective-permute-start = (bf16[9,72,384]{2,1,0:T(8,128)(2,1)}, bf16[9,72,384]{2,1,0:T(8,128)(2,1)S(1)}, u32[]{:S(2)}, u32[]{:S(2)}) collective-permute-start(bf16[9,72,384]{2,1,0:T(8,128)(2,1)} %bitcast.59), channel_id=1, source_target_pairs={{0,1},{1,0},{2,3},{3,2},{4,5},{5,4},{6,7},{7,6},{8,9},{9,8},{10,11... | collective-permute-start | bytes 1493000 | tf_op jit(solution)/shard_map/ppermute | solution.py:60
  10.6 1.7 %collective-permute-done = bf16[9,72,384]{2,1,0:T(8,128)(2,1)S(1)} collective-permute-done((bf16[9,72,384]{2,1,0:T(8,128)(2,1)}, bf16[9,72,384]{2,1,0:T(8,128)(2,1)S(1)}, u32[]{:S(2)}, u32[]{:S(2)}) %collective-permute-start) | collective-permute-done | bytes 497696 | tf_op jit(solution)/shard_map/ppermute | solution.py:60
  13.6 3.9 %collective-permute-start.3 = (bf16[96,384]{1,0:T(8,128)(2,1)S(1)}, bf16[96,384]{1,0:T(8,128)(2,1)S(1)}, u32[]{:S(2)}, u32[]{:S(2)}) collective-permute-start(bf16[96,384]{1,0:T(8,128)(2,1)S(1)} %pad_maximum_fusion.4), channel_id=1, source_target_pairs={{0,2},{1,15},{2,4},{3,1},{4,6},{5,3},{6,8},{7,5},{8,10},{9,7},{10,... | collective-permute-start | bytes 221192 | tf_op jit(solution)/shard_map/ppermute | solution.py:60
  17.5 1.2 %collective-permute-start.4 = (bf16[96,384]{1,0:T(8,128)(2,1)S(1)}, bf16[96,384]{1,0:T(8,128)(2,1)S(1)}, u32[]{:S(2)}, u32[]{:S(2)}) collective-permute-start(bf16[96,384]{1,0:T(8,128)(2,1)S(1)} %pad_maximum_fusion.4), channel_id=1, source_target_pairs={{0,4},{1,13},{2,6},{3,15},{4,8},{5,1},{6,10},{7,3},{8,12},{9,5},{1... | collective-permute-start | bytes 221192 | tf_op jit(solution)/shard_map/ppermute | solution.py:60
  19.2 4.5 %collective-permute-start.7 = (bf16[96,384]{1,0:T(8,128)(2,1)S(1)}, bf16[96,384]{1,0:T(8,128)(2,1)S(1)}, u32[]{:S(2)}, u32[]{:S(2)}) collective-permute-start(bf16[96,384]{1,0:T(8,128)(2,1)S(1)} %pad_maximum_fusion.4), channel_id=1, source_target_pairs={{0,8},{1,9},{2,10},{3,11},{4,12},{5,13},{6,14},{7,15},{8,0},{9,1},... | collective-permute-start | bytes 221192 | tf_op jit(solution)/shard_map/ppermute | solution.py:60
  24.2 3.1 %collective-permute-start.1 = (bf16[4,2,48,384]{3,2,1,0:T(8,128)(2,1)S(1)}, bf16[4,2,48,384]{3,2,1,0:T(8,128)(2,1)S(1)}, u32[]{:S(2)}, u32[]{:S(2)}) collective-permute-start(bf16[4,2,48,384]{3,2,1,0:T(8,128)(2,1)S(1)} %get-tuple-element.33), channel_id=1, source_target_pairs={{0,16},{1,17},{2,18},{3,19},{4,20},{5,21},{6,22},{7,23},{8,24},{9,... | collective-permute-start | bytes 884744 | tf_op jit(solution)/shard_map/ppermute | solution.py:60
  27.4 1.3 %collective-permute-start.2 = (bf16[4,2,48,384]{3,2,1,0:T(8,128)(2,1)S(1)}, bf16[4,2,48,384]{3,2,1,0:T(8,128)(2,1)S(1)}, u32[]{:S(2)}, u32[]{:S(2)}) collective-permute-start(bf16[4,2,48,384]{3,2,1,0:T(8,128)(2,1)S(1)} %get-tuple-element.34), channel_id=1, source_target_pairs={{16,0},{17,1},{18,2},{19,3},{20,4},{21,5},{22,6},{23,7},{24,8},{25... | collective-permute-start | bytes 884744 | tf_op jit(solution)/shard_map/ppermute | solution.py:60
  28.9 1.4 %collective-permute-done.6 = bf16[3,96,384]{2,1,0:T(8,128)(2,1)S(1)} collective-permute-done((bf16[3,96,384]{2,1,0:T(8,128)(2,1)S(1)}, bf16[3,96,384]{2,1,0:T(8,128)(2,1)S(1)}, u32[]{:S(2)}, u32[]{:S(2)}) %collective-permute-start.6) | collective-permute-done | bytes 221216 | tf_op jit(solution)/shard_map/ppermute | solution.py:60
  30.8 2.2 %collective-permute-done.1 = bf16[4,2,48,384]{3,2,1,0:T(8,128)(2,1)S(1)} collective-permute-done((bf16[4,2,48,384]{3,2,1,0:T(8,128)(2,1)S(1)}, bf16[4,2,48,384]{3,2,1,0:T(8,128)(2,1)S(1)}, u32[]{:S(2)}, u32[]{:S(2)}) %collective-permute-start.1) | collective-permute-done | bytes 294944 | tf_op jit(solution)/shard_map/ppermute | solution.py:60
  33.1 4.5 %collective-permute-done.2 = bf16[4,2,48,384]{3,2,1,0:T(8,128)(2,1)S(1)} collective-permute-done((bf16[4,2,48,384]{3,2,1,0:T(8,128)(2,1)S(1)}, bf16[4,2,48,384]{3,2,1,0:T(8,128)(2,1)S(1)}, u32[]{:S(2)}, u32[]{:S(2)}) %collective-permute-start.2) | collective-permute-done | bytes 294944 | tf_op jit(solution)/shard_map/ppermute | solution.py:60
  38.6 2.8 %collective-permute-start.8 = (bf16[8,40,384]{2,1,0:T(8,128)(2,1)S(1)}, bf16[8,40,384]{2,1,0:T(8,128)(2,1)S(1)}, u32[]{:S(2)}, u32[]{:S(2)}) collective-permute-start(bf16[8,40,384]{2,1,0:T(8,128)(2,1)S(1)} %dynamic-slice_select_fusion), channel_id=1, source_target_pairs={{0,48},{1,193},{2,50},{3,195},{4,52},{5,197},{6,54},{7,199},{8,56}... | collective-permute-start | bytes 737288 | tf_op jit(solution)/shard_map/ppermute | solution.py:60
  42.5 4.6 %collective-permute-done.8 = bf16[8,40,384]{2,1,0:T(8,128)(2,1)S(1)} collective-permute-done((bf16[8,40,384]{2,1,0:T(8,128)(2,1)S(1)}, bf16[8,40,384]{2,1,0:T(8,128)(2,1)S(1)}, u32[]{:S(2)}, u32[]{:S(2)}) %collective-permute-start.8) | collective-permute-done | bytes 245792 | tf_op jit(solution)/shard_map/ppermute | solution.py:60
  48.3 2.7 %collective-permute-done.10 = bf16[8,40,384]{2,1,0:T(8,128)(2,1)S(1)} collective-permute-done((bf16[8,40,384]{2,1,0:T(8,128)(2,1)S(1)}, bf16[8,40,384]{2,1,0:T(8,128)(2,1)S(1)}, u32[]{:S(2)}, u32[]{:S(2)}) %collective-permute-start.10) | collective-permute-done | bytes 245792 | tf_op jit(solution)/shard_map/ppermute | solution.py:60
  51.5 1.2 %collective-permute-start.13 = (bf16[8,160,384]{2,1,0:T(8,128)(2,1)S(1)}, bf16[8,160,384]{2,1,0:T(8,128)(2,1)S(1)}, u32[]{:S(2)}, u32[]{:S(2)}) collective-permute-start(bf16[8,160,384]{2,1,0:T(8,128)(2,1)S(1)} %bitcast.42), channel_id=1, source_target_pairs={{0,64},{1,17},{2,66},{3,19},{4,68},{5,21},{6,70},{7,23},{8,72},{9,... | collective-permute-start | bytes 2949128 | tf_op jit(solution)/shard_map/ppermute | solution.py:60
  52.7 1.5 %collective-permute-start.14 = (bf16[8,160,384]{2,1,0:T(8,128)(2,1)S(1)}, bf16[8,160,384]{2,1,0:T(8,128)(2,1)}, u32[]{:S(2)}, u32[]{:S(2)}) collective-permute-start(bf16[8,160,384]{2,1,0:T(8,128)(2,1)S(1)} %bitcast.43), channel_id=1, source_target_pairs={{0,192},{1,49},{2,194},{3,51},{4,196},{5,53},{6,198},{7,55},{8,200... | collective-permute-start | bytes 2949128 | tf_op jit(solution)/shard_map/ppermute | solution.py:60
  54.2 6.8 %collective-permute-start.11 = (bf16[2,7,48,384]{3,2,1,0:T(8,128)(2,1)S(1)}, bf16[2,7,48,384]{3,2,1,0:T(8,128)(2,1)}, u32[]{:S(2)}, u32[]{:S(2)}) collective-permute-start(bf16[2,7,48,384]{3,2,1,0:T(8,128)(2,1)S(1)} %get-tuple-element.17.high), channel_id=1, source_target_pairs={{0,1},{1,2},{2,3},{3,4},{4,5},{5,6},{6,7},{7,8},{8,9},{9,10},{10,1... | collective-permute-start | bytes 1548296 | tf_op jit(solution)/shard_map/ppermute | solution.py:60
  61.0 5.1 %collective-permute-done.13.refs_1_ = bf16[8,160,384]{2,1,0:T(8,128)(2,1)S(1)} collective-permute-done((bf16[8,160,384]{2,1,0:T(8,128)(2,1)S(1)}, bf16[8,160,384]{2,1,0:T(8,128)(2,1)S(1)}, u32[]{:S(2)}, u32[]{:S(2)}) %collective-permute-start.13) | collective-permute-done | bytes 983072 | tf_op jit(solution)/shard_map/ppermute | solution.py:60
  66.1 1.7 %collective-permute-start.15 = (bf16[8,160,384]{2,1,0:T(8,128)(2,1)S(1)}, bf16[8,160,384]{2,1,0:T(8,128)(2,1)}, u32[]{:S(2)}, u32[]{:S(2)}) collective-permute-start(bf16[8,160,384]{2,1,0:T(8,128)(2,1)S(1)} %bitcast.44), channel_id=1, source_target_pairs={{0,128},{1,33},{2,130},{3,35},{4,132},{5,37},{6,134},{7,39},{8,136... | collective-permute-start | bytes 2949128 | tf_op jit(solution)/shard_map/ppermute | solution.py:60
  67.8 3.2 %collective-permute-start.16 = (bf16[8,160,384]{2,1,0:T(8,128)(2,1)S(1)}, bf16[8,160,384]{2,1,0:T(8,128)(2,1)}, u32[]{:S(2)}, u32[]{:S(2)}) collective-permute-start(bf16[8,160,384]{2,1,0:T(8,128)(2,1)S(1)} %bitcast.45), channel_id=1, source_target_pairs={{0,1},{1,0},{2,3},{3,2},{4,5},{5,4},{6,7},{7,6},{8,9},{9,8},{10,11... | collective-permute-start | bytes 2949128 | tf_op jit(solution)/shard_map/ppermute | solution.py:60
  72.6 3.3 %copy-done.2 = bf16[3,3,1152,384]{3,2,1,0:T(8,128)(2,1)S(1)} copy-done((bf16[3,3,1152,384]{3,2,1,0:T(8,128)(2,1)S(1)}, bf16[3,3,1152,384]{3,2,1,0:T(8,128)(2,1)}, u32[]{:S(2)}) %copy-start.2) | copy-done | bytes 7962648
  75.8 11.8 %conv_first.1 = (bf16[2,5,48,384]{3,2,1,0:T(8,128)(2,1)S(1)}, bf16[2,5,48,384]{3,2,1,0:T(8,128)(2,1)}) custom-call(s32[1]{0:T(128)} %bitcast.tile, bf16[2,7,48,384]{3,2,1,0:T(8,128)(2,1)} %collective-permute-done.11.earlier, bf16[2,7,48,384]{3,2,1,0:T(8,128)(2,1)S(1)} %copy-done.1, bf16[2,7,48,384]{3,2,1,0:T(8,128)(2,1)S(1)} %get-tuple-element.17.high, ...), custom_call_target="tpu_custom_call" | custom-call | flops 7644119040 | bytes 7962624 | tf_op jit(solution)/shard_map/conv_first/pallas_call | solution.py:166
  87.8 4.5 %collective-permute-start.12 = (bf16[2,5,48,384]{3,2,1,0:T(8,128)(2,1)}, bf16[2,5,48,384]{3,2,1,0:T(8,128)(2,1)S(1)}, u32[]{:S(2)}, u32[]{:S(2)}) collective-permute-start(bf16[2,5,48,384]{3,2,1,0:T(8,128)(2,1)} %get-tuple-element.18.high), channel_id=1, source_target_pairs={{0,1},{1,2},{2,3},{3,4},{4,5},{5,6},{6,7},{7,8},{8,9},{9,10},{10,1... | collective-permute-start | bytes 1105928 | tf_op jit(solution)/shard_map/ppermute | solution.py:60
  92.4 7.1 %second_late.1 = (bf16[576,384]{1,0:T(8,128)(2,1)}, bf16[8,1296,384]{2,1,0:T(8,128)(2,1)S(1)}) custom-call(s32[8]{0:T(128)S(1)} %stack.90.where, bf16[2,5,48,384]{3,2,1,0:T(8,128)(2,1)S(1)} %get-tuple-element.19.low.high, bf16[2,5,48,384]{3,2,1,0:T(8,128)(2,1)} %get-tuple-element.18.high, bf16[576,384]{1,0:T(8,128)(2,1)S(1)} %bitcast.40, ...), custom_call_target="tpu_custom_call" | custom-call | flops 2293235712 | bytes 7962624 | tf_op jit(solution)/shard_map/second_late/pallas_call | solution.py:235
  99.6 3.7 %second_early.1 = bf16[576,384]{1,0:T(8,128)(2,1)} custom-call(bf16[2,5,48,384]{3,2,1,0:T(8,128)(2,1)S(1)} %collective-permute-done.12.low, bf16[2,5,48,384]{3,2,1,0:T(8,128)(2,1)S(1)} %get-tuple-element.19.low.high, bf16[576,384]{1,0:T(8,128)(2,1)S(1)} %bitcast.41, f32[1,384]{1,0:T(1,128)S(1)} %reshape.47.bias, ...), custom_call_target="tpu_custom_call", output_to_operand_aliasing={{}: (5, {})} | custom-call | flops 2293235712 | bytes 7962624 | tf_op jit(solution)/shard_map/second_early/pallas_call | solution.py:251
  (78 shorter events, 9.1 us)
Async XLA Ops:
  6.5 65.0 %all-gather.2.cloned.1.call-start = ((), (), s32[]{:S(2)}) async-start(), calls=%async_computation | async-start | bytes 8460288 | tf_op jit(solution)/shard_map/all_gather | solution.py:283
  7.3 5.0 %collective-permute-start = (bf16[9,72,384]{2,1,0:T(8,128)(2,1)}, bf16[9,72,384]{2,1,0:T(8,128)(2,1)S(1)}, u32[]{:S(2)}, u32[]{:S(2)}) collective-permute-start(bf16[9,72,384]{2,1,0:T(8,128)(2,1)} %bitcast.59), channel_id=1, source_target_pairs={{0,1},{1,0},{2,3},{3,2},{4,5},{5,4},{6,7},{7,6},{8,9},{9,8},{10,11... | collective-permute-start | bytes 1493000 | tf_op jit(solution)/shard_map/ppermute | solution.py:60
  13.6 13.8 %collective-permute-start.3 = (bf16[96,384]{1,0:T(8,128)(2,1)S(1)}, bf16[96,384]{1,0:T(8,128)(2,1)S(1)}, u32[]{:S(2)}, u32[]{:S(2)}) collective-permute-start(bf16[96,384]{1,0:T(8,128)(2,1)S(1)} %pad_maximum_fusion.4), channel_id=1, source_target_pairs={{0,2},{1,15},{2,4},{3,1},{4,6},{5,3},{6,8},{7,5},{8,10},{9,7},{10,... | collective-permute-start | bytes 221192 | tf_op jit(solution)/shard_map/ppermute | solution.py:60
  17.5 11.2 %collective-permute-start.4 = (bf16[96,384]{1,0:T(8,128)(2,1)S(1)}, bf16[96,384]{1,0:T(8,128)(2,1)S(1)}, u32[]{:S(2)}, u32[]{:S(2)}) collective-permute-start(bf16[96,384]{1,0:T(8,128)(2,1)S(1)} %pad_maximum_fusion.4), channel_id=1, source_target_pairs={{0,4},{1,13},{2,6},{3,15},{4,8},{5,1},{6,10},{7,3},{8,12},{9,5},{1... | collective-permute-start | bytes 221192 | tf_op jit(solution)/shard_map/ppermute | solution.py:60
  18.7 10.0 %collective-permute-start.5 = (bf16[96,384]{1,0:T(8,128)(2,1)S(1)}, bf16[96,384]{1,0:T(8,128)(2,1)S(1)}, u32[]{:S(2)}, u32[]{:S(2)}) collective-permute-start(bf16[96,384]{1,0:T(8,128)(2,1)S(1)} %pad_maximum_fusion.4), channel_id=1, source_target_pairs={{0,6},{1,11},{2,8},{3,13},{4,10},{5,15},{6,12},{7,1},{8,14},{9,3},... | collective-permute-start | bytes 221192 | tf_op jit(solution)/shard_map/ppermute | solution.py:60
  19.2 11.3 %collective-permute-start.7 = (bf16[96,384]{1,0:T(8,128)(2,1)S(1)}, bf16[96,384]{1,0:T(8,128)(2,1)S(1)}, u32[]{:S(2)}, u32[]{:S(2)}) collective-permute-start(bf16[96,384]{1,0:T(8,128)(2,1)S(1)} %pad_maximum_fusion.4), channel_id=1, source_target_pairs={{0,8},{1,9},{2,10},{3,11},{4,12},{5,13},{6,14},{7,15},{8,0},{9,1},... | collective-permute-start | bytes 221192 | tf_op jit(solution)/shard_map/ppermute | solution.py:60
  24.2 8.9 %collective-permute-start.1 = (bf16[4,2,48,384]{3,2,1,0:T(8,128)(2,1)S(1)}, bf16[4,2,48,384]{3,2,1,0:T(8,128)(2,1)S(1)}, u32[]{:S(2)}, u32[]{:S(2)}) collective-permute-start(bf16[4,2,48,384]{3,2,1,0:T(8,128)(2,1)S(1)} %get-tuple-element.33), channel_id=1, source_target_pairs={{0,16},{1,17},{2,18},{3,19},{4,20},{5,21},{6,22},{7,23},{8,24},{9,... | collective-permute-start | bytes 884744 | tf_op jit(solution)/shard_map/ppermute | solution.py:60
  27.4 10.2 %collective-permute-start.2 = (bf16[4,2,48,384]{3,2,1,0:T(8,128)(2,1)S(1)}, bf16[4,2,48,384]{3,2,1,0:T(8,128)(2,1)S(1)}, u32[]{:S(2)}, u32[]{:S(2)}) collective-permute-start(bf16[4,2,48,384]{3,2,1,0:T(8,128)(2,1)S(1)} %get-tuple-element.34), channel_id=1, source_target_pairs={{16,0},{17,1},{18,2},{19,3},{20,4},{21,5},{22,6},{23,7},{24,8},{25... | collective-permute-start | bytes 884744 | tf_op jit(solution)/shard_map/ppermute | solution.py:60
  28.8 1.6 %collective-permute-start.6 = (bf16[3,96,384]{2,1,0:T(8,128)(2,1)S(1)}, bf16[3,96,384]{2,1,0:T(8,128)(2,1)S(1)}, u32[]{:S(2)}, u32[]{:S(2)}) collective-permute-start(bf16[3,96,384]{2,1,0:T(8,128)(2,1)S(1)} %pad_maximum_fusion.3), channel_id=1, source_target_pairs={{0,1},{1,0},{2,3},{3,2},{4,5},{5,4},{6,7},{7,6},{8,9},{9,8},{10,11... | collective-permute-start | bytes 663560 | tf_op jit(solution)/shard_map/ppermute | solution.py:60
  38.6 8.6 %collective-permute-start.8 = (bf16[8,40,384]{2,1,0:T(8,128)(2,1)S(1)}, bf16[8,40,384]{2,1,0:T(8,128)(2,1)S(1)}, u32[]{:S(2)}, u32[]{:S(2)}) collective-permute-start(bf16[8,40,384]{2,1,0:T(8,128)(2,1)S(1)} %dynamic-slice_select_fusion), channel_id=1, source_target_pairs={{0,48},{1,193},{2,50},{3,195},{4,52},{5,197},{6,54},{7,199},{8,56}... | collective-permute-start | bytes 737288 | tf_op jit(solution)/shard_map/ppermute | solution.py:60
  41.4 6.9 %collective-permute-start.9 = (bf16[8,40,384]{2,1,0:T(8,128)(2,1)S(1)}, bf16[8,40,384]{2,1,0:T(8,128)(2,1)S(1)}, u32[]{:S(2)}, u32[]{:S(2)}) collective-permute-start(bf16[8,40,384]{2,1,0:T(8,128)(2,1)S(1)} %dynamic-slice_select_fusion), channel_id=1, source_target_pairs={{0,32},{1,129},{2,34},{3,131},{4,36},{5,133},{6,38},{7,135},{8,40}... | collective-permute-start | bytes 737288 | tf_op jit(solution)/shard_map/ppermute | solution.py:60
  41.8 9.2 %collective-permute-start.10 = (bf16[8,40,384]{2,1,0:T(8,128)(2,1)S(1)}, bf16[8,40,384]{2,1,0:T(8,128)(2,1)S(1)}, u32[]{:S(2)}, u32[]{:S(2)}) collective-permute-start(bf16[8,40,384]{2,1,0:T(8,128)(2,1)S(1)} %dynamic-slice_select_fusion), channel_id=1, source_target_pairs={{0,16},{1,65},{2,18},{3,67},{4,20},{5,69},{6,22},{7,71},{8,24},{9,... | collective-permute-start | bytes 737288 | tf_op jit(solution)/shard_map/ppermute | solution.py:60
  51.3 16.4 %copy-start.4 = (f32[384]{0:T(512)S(1)}, f32[384]{0:T(512)}, u32[]{:S(2)}) copy-start(f32[384]{0:T(512)} %param.10) | copy-start | bytes 4612
  51.3 16.4 %copy-start.5 = (f32[384]{0:T(512)S(1)}, f32[384]{0:T(512)}, u32[]{:S(2)}) copy-start(f32[384]{0:T(512)} %param.11) | copy-start | bytes 4612
  51.5 14.6 %collective-permute-start.13 = (bf16[8,160,384]{2,1,0:T(8,128)(2,1)S(1)}, bf16[8,160,384]{2,1,0:T(8,128)(2,1)S(1)}, u32[]{:S(2)}, u32[]{:S(2)}) collective-permute-start(bf16[8,160,384]{2,1,0:T(8,128)(2,1)S(1)} %bitcast.42), channel_id=1, source_target_pairs={{0,64},{1,17},{2,66},{3,19},{4,68},{5,21},{6,70},{7,23},{8,72},{9,... | collective-permute-start | bytes 2949128 | tf_op jit(solution)/shard_map/ppermute | solution.py:60
  52.7 13.4 %collective-permute-start.14 = (bf16[8,160,384]{2,1,0:T(8,128)(2,1)S(1)}, bf16[8,160,384]{2,1,0:T(8,128)(2,1)}, u32[]{:S(2)}, u32[]{:S(2)}) collective-permute-start(bf16[8,160,384]{2,1,0:T(8,128)(2,1)S(1)} %bitcast.43), channel_id=1, source_target_pairs={{0,192},{1,49},{2,194},{3,51},{4,196},{5,53},{6,198},{7,55},{8,200... | collective-permute-start | bytes 2949128 | tf_op jit(solution)/shard_map/ppermute | solution.py:60
  54.2 17.3 %collective-permute-start.11 = (bf16[2,7,48,384]{3,2,1,0:T(8,128)(2,1)S(1)}, bf16[2,7,48,384]{3,2,1,0:T(8,128)(2,1)}, u32[]{:S(2)}, u32[]{:S(2)}) collective-permute-start(bf16[2,7,48,384]{3,2,1,0:T(8,128)(2,1)S(1)} %get-tuple-element.17.high), channel_id=1, source_target_pairs={{0,1},{1,2},{2,3},{3,4},{4,5},{5,6},{6,7},{7,8},{8,9},{9,10},{10,1... | collective-permute-start | bytes 1548296 | tf_op jit(solution)/shard_map/ppermute | solution.py:60
  66.1 21.6 %collective-permute-start.15 = (bf16[8,160,384]{2,1,0:T(8,128)(2,1)S(1)}, bf16[8,160,384]{2,1,0:T(8,128)(2,1)}, u32[]{:S(2)}, u32[]{:S(2)}) collective-permute-start(bf16[8,160,384]{2,1,0:T(8,128)(2,1)S(1)} %bitcast.44), channel_id=1, source_target_pairs={{0,128},{1,33},{2,130},{3,35},{4,132},{5,37},{6,134},{7,39},{8,136... | collective-permute-start | bytes 2949128 | tf_op jit(solution)/shard_map/ppermute | solution.py:60
  67.8 24.6 %collective-permute-start.16 = (bf16[8,160,384]{2,1,0:T(8,128)(2,1)S(1)}, bf16[8,160,384]{2,1,0:T(8,128)(2,1)}, u32[]{:S(2)}, u32[]{:S(2)}) collective-permute-start(bf16[8,160,384]{2,1,0:T(8,128)(2,1)S(1)} %bitcast.45), channel_id=1, source_target_pairs={{0,1},{1,0},{2,3},{3,2},{4,5},{5,4},{6,7},{7,6},{8,9},{9,8},{10,11... | collective-permute-start | bytes 2949128 | tf_op jit(solution)/shard_map/ppermute | solution.py:60
  71.0 21.4 %collective-permute-start.17 = (bf16[8,160,384]{2,1,0:T(8,128)(2,1)S(1)}, bf16[8,160,384]{2,1,0:T(8,128)(2,1)}, u32[]{:S(2)}, u32[]{:S(2)}) collective-permute-start(bf16[8,160,384]{2,1,0:T(8,128)(2,1)S(1)} %collective-permute-done.13.refs_1_), channel_id=1, source_target_pairs={{0,1},{1,0},{2,3},{3,2},{4,5},{5,4},{6,7},{7,6},{8,9},{9,8},{10,11... | collective-permute-start | bytes 2949128 | tf_op jit(solution)/shard_map/ppermute | solution.py:60
  71.1 21.3 %collective-permute-start.18 = (bf16[8,160,384]{2,1,0:T(8,128)(2,1)}, bf16[8,160,384]{2,1,0:T(8,128)(2,1)}, u32[]{:S(2)}, u32[]{:S(2)}) collective-permute-start(bf16[8,160,384]{2,1,0:T(8,128)(2,1)} %collective-permute-done.14.refs_2_), channel_id=1, source_target_pairs={{0,1},{1,0},{2,3},{3,2},{4,5},{5,4},{6,7},{7,6},{8,9},{9,8},{10,11... | collective-permute-start | bytes 2949128 | tf_op jit(solution)/shard_map/ppermute | solution.py:60
  75.8 16.5 %copy-start.6 = (f32[384]{0:T(512)S(1)}, f32[384]{0:T(512)}, u32[]{:S(2)}) copy-start(f32[384]{0:T(512)} %param.13) | copy-start | bytes 4612
  87.7 4.8 %collective-permute-start.19 = (bf16[8,160,384]{2,1,0:T(8,128)(2,1)}, bf16[8,160,384]{2,1,0:T(8,128)(2,1)}, u32[]{:S(2)}, u32[]{:S(2)}) collective-permute-start(bf16[8,160,384]{2,1,0:T(8,128)(2,1)} %collective-permute-done.15.refs_3_), channel_id=1, source_target_pairs={{0,1},{1,0},{2,3},{3,2},{4,5},{5,4},{6,7},{7,6},{8,9},{9,8},{10,11... | collective-permute-start | bytes 2949128 | tf_op jit(solution)/shard_map/ppermute | solution.py:60
  87.8 11.8 %collective-permute-start.12 = (bf16[2,5,48,384]{3,2,1,0:T(8,128)(2,1)}, bf16[2,5,48,384]{3,2,1,0:T(8,128)(2,1)S(1)}, u32[]{:S(2)}, u32[]{:S(2)}) collective-permute-start(bf16[2,5,48,384]{3,2,1,0:T(8,128)(2,1)} %get-tuple-element.18.high), channel_id=1, source_target_pairs={{0,1},{1,2},{2,3},{3,4},{4,5},{5,6},{6,7},{7,8},{8,9},{9,10},{10,1... | collective-permute-start | bytes 1105928 | tf_op jit(solution)/shard_map/ppermute | solution.py:60
  (4 other events, 24.9 us)
Sparse Core Ops, SparseCore 0:
  9.1 60.2 all-gather.1

commit v8 on v7

--- a/solution.py
+++ b/solution.py
@@ -70,15 +70,14 @@
     return lax.optimization_barrier((value, others))[0]
 
 
-def grow_rows(own):
+def grow(own, before):
+    own = after(jnp.concatenate([send(own[2:], neighbours(0, 1)), own], axis=0), before)
     above = send(own[:, 1:], neighbours(1, 0))
     below = send(own[:, :2], neighbours(-1, 0))
-    return [
-        jnp.concatenate([above[k : k + 2], own[k : k + 2], below[k : k + 2]], axis=1) for k in (0, 2)
-    ]
-
-
-def gather(weight, y, x, z, core, rows):
+    return jnp.concatenate([above, own, below], axis=1)
+
+
+def gather(weight, y, x, z, core, first):
     first_core = core == 0
     other = send(weight, SWAP)
     slab = jnp.concatenate(
@@ -98,15 +97,17 @@
     last = slabs[:, 2 * PART :]
     chunk = jnp.where(first_core, slabs[:, :PART], slabs[:, PART : 2 * PART])
 
-    halo = rows(both)
-    chunk, last, _ = lax.optimization_barrier((chunk, last, halo))
+    grown = grow(first, both)
+    chunk, last = lax.optimization_barrier((chunk, last))
     parts = [chunk, *(send(chunk, pairs) for pairs in (RING_DOWN, RING_FAR, RING_UP))]
     spot = lax.rem(4 - jnp.where(first_core, x, y), 4)
     turned = lax.dynamic_slice_in_dim(jnp.stack(parts + parts), spot, 4, axis=0)
     chunk = turned.transpose(1, 0, 2, 3).reshape(NZ, BLOCK, C)
+    chunk = after(chunk, grown)
     up, down = send(chunk, CROSS_UP), send(chunk, CROSS_DOWN)
     far = send(after(chunk, up, down), CROSS_FAR)
-    return [chunk, up, down, far], last, halo
+    others = [send(v, SWAP) for v in (chunk, up, down)]
+    return [chunk, up, down, *others, last], far, grown
 
 
 ANY = pl.BlockSpec(memory_space=pl.ANY)
@@ -148,9 +149,17 @@
     return lines
 
 
-def first_kernel(tile, earlier, low, high, weight, bias, gain, out_low, out_high, wide):
-    frames = [part[f] for part in (earlier, low, high) for f in range(2)]
-    lines = convolve(frames, 5, lambda tap: weight[tap], wide)
+def first_kernel(tile, where, grown, weight, bias, gain, *refs):
+    *arrays, last, out_low, out_high, next_weight, wide, sems = refs
+    copies = []
+    for k, src in enumerate([*arrays, last]):
+        if src is last:
+            rows = pl.ds(8 * BLOCK, 9 * SLAB - 8 * BLOCK)
+        else:
+            rows = pl.ds(pl.multiple_of(where[k + k // 3], BLOCK), BLOCK)
+        copies.append(pltpu.make_async_copy(src, next_weight.at[:, rows], sems.at[k]))
+        copies[k].start()
+    lines = convolve([grown[f] for f in range(6)], 5, lambda tap: weight[tap], wide)
     for i, line in enumerate(lines):
         result = activate(line + bias[...], gain[...])
         if i % 5 == 0:
@@ -159,49 +168,26 @@
             result = jnp.where(tile[0] == NY * NX - 1, 0.0, result)
         out = out_low if i < 10 else out_high
         out[i // 5 % 2, i % 5] = result.astype(BF)
-
-
-def conv_first(tile, earlier, low, high, weight, bias, gain):
+    for copy in copies:
+        copy.wait()
+
+
+def conv_first(tile, where, grown, weight, bias, gain, pieces):
     half = jax.ShapeDtypeStruct((2, 5, 48, C), BF)
     return pl.pallas_call(
         first_kernel,
-        out_shape=[half, half],
-        in_specs=[SMEM] + [VMEM] * 6,
-        out_specs=[VMEM, VMEM],
-        scratch_shapes=[pltpu.VMEM((960, 3 * C), F32)],
-        compiler_params=pltpu.CompilerParams(vmem_limit_bytes=20 * 2**20),
+        out_shape=[half, half, jax.ShapeDtypeStruct((NZ, 9 * SLAB, C), BF)],
+        in_specs=[SMEM, SMEM] + [VMEM] * 4 + [ANY] * len(pieces),
+        out_specs=[VMEM] * 3,
+        scratch_shapes=[pltpu.VMEM((960, 3 * C), F32), pltpu.SemaphoreType.DMA((len(pieces),))],
+        compiler_params=pltpu.CompilerParams(vmem_limit_bytes=30 * 2**20),
         cost_estimate=cost(960),
         name="conv_first",
-    )(tile, earlier, low, high, weight, bias, gain)
+    )(tile, where, grown, weight, bias, gain, *pieces)
 
 
 def slab_rows(weight, tap):
     return weight[:, SLAB * tap : SLAB * (tap + 1)].reshape(3 * C, C)
-
-
-def assembled(where, arrays, last, whole, sems):
-    def start(block, index):
-        @pl.when(where[index] == block * BLOCK)
-        def _():
-            rows = whole.at[:, pl.ds(block * BLOCK, BLOCK)]
-            pltpu.make_async_copy(arrays[index], rows, sems.at[block]).start()
-
-    for block in range(8):
-        for index in range(8):
-            start(block, index)
-    rest = whole.at[:, pl.ds(8 * BLOCK, 9 * SLAB - 8 * BLOCK)]
-    pltpu.make_async_copy(last, rest, sems.at[8]).start()
-    arrived = set()
-
-    def rows(tap):
-        for block in range(SLAB * tap // BLOCK, -(-SLAB * (tap + 1) // BLOCK)):
-            if block not in arrived:
-                arrived.add(block)
-                at = whole.at[:, pl.ds(block * BLOCK, BLOCK)] if block < 8 else rest
-                pltpu.make_async_copy(at, at, sems.at[block]).wait()
-        return slab_rows(whole, tap)
-
-    return rows
 
 
 def finish(lines, start, latent, bias, out, done, sem):
@@ -215,11 +201,14 @@
     copy.wait()
 
 
-def late_kernel(where, low, high, latent, bias, *refs):
-    *arrays, last, out, whole, wide, done, sems, sem = refs
-    rows = assembled(where, arrays, last, whole, sems)
+def late_kernel(where, low, high, latent, bias, weight, far, other_far, out, whole, wide, done, sem):
+    whole[...] = weight[...]
+    for k, src in enumerate((far, other_far)):
+        rows = pl.ds(pl.multiple_of(where[3 + 4 * k], BLOCK), BLOCK)
+        whole[:, rows] = src[...]
     frames = [part[f] for part in (low, high) for f in range(2)]
-    finish(convolve(frames, 3, rows, wide), 288, latent, bias, out, done, sem)
+    lines = convolve(frames, 3, lambda tap: slab_rows(whole, tap), wide)
+    finish(lines, 288, latent, bias, out, done, sem)
 
 
 def early_kernel(low, high, latent, bias, weight, partial, out, wide, done, sem):
@@ -231,20 +220,17 @@
 SCRATCH = [pltpu.VMEM((288, 3 * C), F32), pltpu.VMEM((288, C), BF)]
 
 
-def conv_late(where, low, high, latent, bias, pieces):
+def conv_late(where, low, high, latent, bias, weight, far, other_far):
     return pl.pallas_call(
         late_kernel,
-        out_shape=[
-            jax.ShapeDtypeStruct((576, C), BF),
-            jax.ShapeDtypeStruct((NZ, 9 * SLAB, C), BF),
-        ],
-        in_specs=[SMEM] + [VMEM] * 4 + [ANY] * len(pieces),
+        out_shape=[jax.ShapeDtypeStruct((576, C), BF), jax.ShapeDtypeStruct(weight.shape, BF)],
+        in_specs=[SMEM] + [VMEM] * 7,
         out_specs=[ANY, VMEM],
-        scratch_shapes=[*SCRATCH, pltpu.SemaphoreType.DMA((9,)), pltpu.SemaphoreType.DMA],
+        scratch_shapes=[*SCRATCH, pltpu.SemaphoreType.DMA],
         compiler_params=pltpu.CompilerParams(vmem_limit_bytes=20 * 2**20),
         cost_estimate=cost(288),
         name="second_late",
-    )(where, low, high, latent, bias, *pieces)
+    )(where, low, high, latent, bias, weight, far, other_far)
 
 
 def conv_early(low, high, latent, bias, weight, partial):
@@ -281,23 +267,23 @@
     row = lambda v: v.reshape(1, C)
 
     whole_first = lax.all_gather(weight_first, ("z", "c"), axis=2, tiled=True)
-
-    def rows(before):
-        return grow_rows(activate(after(latent, before), gain_first).astype(BF))
-
-    pieces, last, (low, high) = gather(weight_second.reshape(9, 72, C), y, x, z, core, rows)
-    earlier = send(after(high, pieces[0]), neighbours(0, 1))
-    others = [send(v, SWAP) for v in pieces[:3]]
-
-    second_low, second_high = conv_first(
-        tile, earlier, low, high, whole_first.reshape(9, 3 * C, C), row(bias_first), row(gain_second)
+    first = activate(latent, gain_first).astype(BF)
+    pieces, far, grown = gather(weight_second.reshape(9, 72, C), y, x, z, core, first)
+
+    second_low, second_high, most = conv_first(
+        tile,
+        where,
+        grown,
+        whole_first.reshape(9, 3 * C, C),
+        row(bias_first),
+        row(gain_second),
+        pieces,
     )
     second_earlier = send(second_high, neighbours(0, 1))
-    pieces[3] = after(pieces[3], second_high)
-    others.append(send(pieces[3], SWAP))
+    far = after(far, second_high)
     rest = latent.reshape(576, C), row(bias_second)
     partial, whole_second = conv_late(
-        where, second_low, second_high, *rest, [*pieces, *others, last]
+        where, second_low, second_high, *rest, most, far, send(far, SWAP)
     )
     result = conv_early(second_earlier, second_low, *rest, whole_second, partial)
     return result.reshape(4, 3, 48, C)

time: 112 us -> 107 us (0.955); the launches traced: 110 us -> 106 us
  Pallas kernels: 22.7 us -> 19.5 us
  starting transfers between devices: 41.3 us -> 38.3 us
  waiting for transfers between devices: 24 us -> 25.6 us
    ppermute x20, starting transfers between devices: 41.3 us -> 38.3 us  [send(): return lax.ppermute(value, AXES, pairs)]
    pallas_call x1, Pallas kernels: 7.13 us -> 5.1 us  [conv_late(): pl.pallas_call(late_kernel, out_shape=[jax.ShapeDtypeStruct((576, C), BF)...]
    ppermute x20, waiting for transfers between devices: 23.3 us -> 24.9 us  [send(): return lax.ppermute(value, AXES, pairs)]
    pallas_call x1, Pallas kernels: 11.8 us -> 10.7 us  [conv_first(): pl.pallas_call(first_kernel, out_shape=[half, half, jax.ShapeDtypeStruct(...]
    unnamed x28 -> x30, local copies, waits for them, and re-layouts: 4.72 us -> 4.73 us
  transfers between devices with their start and end apart: 21 -> 21, of which waited for: 8 -> 7; matrix products, arithmetic and copies ran while one was open for 4% -> 5% of each run, Pallas kernels for 17% -> 15%
where the time goes in v8:
time: 107 us; the launch traced here: 106 us
  starting transfers between devices  38.3 us (36%)
  waiting for transfers between devices  25.6 us (24%)
  Pallas kernels  19.5 us (18%)
  between operations  13.9 us (13%)
  local copies, waits for them, and re-layouts  5.95 us (6%)
  other arithmetic  3.21 us (3%)
    ppermute x20, starting transfers between devices, send(): return lax.ppermute(value, AXES, pairs)  38.3 us
    ppermute x20, waiting for transfers between devices, send(): return lax.ppermute(value, AXES, pairs)  24.9 us
    pallas_call x1, Pallas kernels, conv_first(): pl.pallas_call(first_kernel, out_shape=[half, half, jax.ShapeDtypeStruct(...  10.7 us
    pallas_call x1, Pallas kernels, conv_late(): pl.pallas_call(late_kernel, out_shape=[jax.ShapeDtypeStruct((576, C), BF)...  5.1 us
    unnamed x30, local copies, waits for them, and re-layouts  4.73 us
    pallas_call x1, Pallas kernels, conv_early(): pl.pallas_call(early_kernel, out_shape=jax.ShapeDtypeStruct((576, C), BF)...  3.72 us
  transfers between devices with their start and end apart: 21, of which 7 were waited for; matrix products, arithmetic and copies ran while one was open for 5% of the time, Pallas kernels for 15%

profile of v8, /device:TPU:1, one launch (start us, length us, event | category | flops | bytes accessed | tf_op | source)
XLA Modules:
  0.0 106.4 jit_solution(15141318489875568382)
XLA Ops:
  7.3 3.3 %collective-permute-start.1 = (bf16[9,72,384]{2,1,0:T(8,128)(2,1)}, bf16[9,72,384]{2,1,0:T(8,128)(2,1)S(1)}, u32[]{:S(2)}, u32[]{:S(2)}) collective-permute-start(bf16[9,72,384]{2,1,0:T(8,128)(2,1)} %bitcast.59), channel_id=1, source_target_pairs={{0,1},{1,0},{2,3},{3,2},{4,5},{5,4},{6,7},{7,6},{8,9},{9,8},{10,11... | collective-permute-start | bytes 1493000 | tf_op jit(solution)/shard_map/ppermute | solution.py:60
  10.6 1.2 %fusion = f32[4,3,48]{2,1,0:T(4,128)S(1)} fusion(bf16[4,3,48,384]{3,2,1,0:T(8,128)(2,1)} %param.7), kind=kLoop, calls=%fused_computation.4 | loop fusion | flops 662976 | bytes 444672 | tf_op jit(solution)/shard_map/reduce_sum | solution.py:65
  11.8 1.4 %fusion.7 = bf16[4,3,48,384]{3,2,1,0:T(8,128)(2,1)S(1)} fusion(bf16[4,3,48,384]{3,2,1,0:T(8,128)(2,1)} %param.7, f32[384]{0:T(512)} %param.8, f32[4,3,48]{2,1,0:T(4,128)S(1)} %add_rsqrt_fusion), kind=kLoop, calls=%fused_computation.11 | loop fusion | flops 1769472 | bytes 888576 | tf_op jit(solution)/shard_map/convert_element_type | solution.py:270
  13.2 1.9 %collective-permute-start = (bf16[2,3,48,384]{3,2,1,0:T(8,128)(2,1)S(1)}, bf16[2,3,48,384]{3,2,1,0:T(8,128)(2,1)S(1)}, u32[]{:S(2)}, u32[]{:S(2)}) collective-permute-start(bf16[2,3,48,384]{3,2,1,0:T(8,128)(2,1)S(1)} %slice.45), channel_id=1, source_target_pairs={{0,1},{1,2},{2,3},{3,4},{4,5},{5,6},{6,7},{7,8},{8,9},{9,10},{10,1... | collective-permute-start | bytes 663560 | tf_op jit(solution)/shard_map/ppermute | solution.py:60
  15.5 5.4 %collective-permute-start.6 = (bf16[96,384]{1,0:T(8,128)(2,1)S(1)}, bf16[96,384]{1,0:T(8,128)(2,1)S(1)}, u32[]{:S(2)}, u32[]{:S(2)}) collective-permute-start(bf16[96,384]{1,0:T(8,128)(2,1)S(1)} %pad_maximum_fusion.3), channel_id=1, source_target_pairs={{0,6},{1,11},{2,8},{3,13},{4,10},{5,15},{6,12},{7,1},{8,14},{9,3},... | collective-permute-start | bytes 221192 | tf_op jit(solution)/shard_map/ppermute | solution.py:60
  20.9 2.4 %collective-permute-start.5 = (bf16[96,384]{1,0:T(8,128)(2,1)S(1)}, bf16[96,384]{1,0:T(8,128)(2,1)S(1)}, u32[]{:S(2)}, u32[]{:S(2)}) collective-permute-start(bf16[96,384]{1,0:T(8,128)(2,1)S(1)} %pad_maximum_fusion.3), channel_id=1, source_target_pairs={{0,4},{1,13},{2,6},{3,15},{4,8},{5,1},{6,10},{7,3},{8,12},{9,5},{1... | collective-permute-start | bytes 221192 | tf_op jit(solution)/shard_map/ppermute | solution.py:60
  23.4 2.9 %collective-permute-start.8 = (bf16[96,384]{1,0:T(8,128)(2,1)S(1)}, bf16[96,384]{1,0:T(8,128)(2,1)S(1)}, u32[]{:S(2)}, u32[]{:S(2)}) collective-permute-start(bf16[96,384]{1,0:T(8,128)(2,1)S(1)} %pad_maximum_fusion.3), channel_id=1, source_target_pairs={{0,8},{1,9},{2,10},{3,11},{4,12},{5,13},{6,14},{7,15},{8,0},{9,1},... | collective-permute-start | bytes 221192 | tf_op jit(solution)/shard_map/ppermute | solution.py:60
  26.3 3.7 %collective-permute-done.4 = bf16[96,384]{1,0:T(8,128)(2,1)S(1)} collective-permute-done((bf16[96,384]{1,0:T(8,128)(2,1)S(1)}, bf16[96,384]{1,0:T(8,128)(2,1)S(1)}, u32[]{:S(2)}, u32[]{:S(2)}) %collective-permute-start.4) | collective-permute-done | bytes 73760 | tf_op jit(solution)/shard_map/ppermute | solution.py:60
  30.3 3.1 %collective-permute-start.2 = (bf16[6,2,48,384]{3,2,1,0:T(8,128)(2,1)S(1)}, bf16[6,2,48,384]{3,2,1,0:T(8,128)(2,1)S(1)}, u32[]{:S(2)}, u32[]{:S(2)}) collective-permute-start(bf16[6,2,48,384]{3,2,1,0:T(8,128)(2,1)S(1)} %get-tuple-element.32), channel_id=1, source_target_pairs={{0,16},{1,17},{2,18},{3,19},{4,20},{5,21},{6,22},{7,23},{8,24},{9,... | collective-permute-start | bytes 1327112 | tf_op jit(solution)/shard_map/ppermute | solution.py:60
  33.4 1.3 %collective-permute-start.3 = (bf16[6,2,48,384]{3,2,1,0:T(8,128)(2,1)S(1)}, bf16[6,2,48,384]{3,2,1,0:T(8,128)(2,1)S(1)}, u32[]{:S(2)}, u32[]{:S(2)}) collective-permute-start(bf16[6,2,48,384]{3,2,1,0:T(8,128)(2,1)S(1)} %get-tuple-element.31), channel_id=1, source_target_pairs={{16,0},{17,1},{18,2},{19,3},{20,4},{21,5},{22,6},{23,7},{24,8},{25... | collective-permute-start | bytes 1327112 | tf_op jit(solution)/shard_map/ppermute | solution.py:60
  35.9 5.6 %collective-permute-start.9 = (bf16[8,40,384]{2,1,0:T(8,128)(2,1)S(1)}, bf16[8,40,384]{2,1,0:T(8,128)(2,1)S(1)}, u32[]{:S(2)}, u32[]{:S(2)}) collective-permute-start(bf16[8,40,384]{2,1,0:T(8,128)(2,1)S(1)} %dynamic-slice_select_fusion), channel_id=1, source_target_pairs={{0,48},{1,193},{2,50},{3,195},{4,52},{5,197},{6,54},{7,199},{8,56}... | collective-permute-start | bytes 737288 | tf_op jit(solution)/shard_map/ppermute | solution.py:60
  42.9 3.5 %collective-permute-done.3 = bf16[6,2,48,384]{3,2,1,0:T(8,128)(2,1)S(1)} collective-permute-done((bf16[6,2,48,384]{3,2,1,0:T(8,128)(2,1)S(1)}, bf16[6,2,48,384]{3,2,1,0:T(8,128)(2,1)S(1)}, u32[]{:S(2)}, u32[]{:S(2)}) %collective-permute-start.3) | collective-permute-done | bytes 442400 | tf_op jit(solution)/shard_map/ppermute | solution.py:60
  47.4 3.8 %collective-permute-done.10 = bf16[8,40,384]{2,1,0:T(8,128)(2,1)S(1)} collective-permute-done((bf16[8,40,384]{2,1,0:T(8,128)(2,1)S(1)}, bf16[8,40,384]{2,1,0:T(8,128)(2,1)S(1)}, u32[]{:S(2)}, u32[]{:S(2)}) %collective-permute-start.10) | collective-permute-done | bytes 245792 | tf_op jit(solution)/shard_map/ppermute | solution.py:60
  51.8 3.2 %collective-permute-start.13 = (bf16[8,160,384]{2,1,0:T(8,128)(2,1)S(1)}, bf16[8,160,384]{2,1,0:T(8,128)(2,1)}, u32[]{:S(2)}, u32[]{:S(2)}) collective-permute-start(bf16[8,160,384]{2,1,0:T(8,128)(2,1)S(1)} %bitcast.43), channel_id=1, source_target_pairs={{0,192},{1,49},{2,194},{3,51},{4,196},{5,53},{6,198},{7,55},{8,200... | collective-permute-start | bytes 2949128 | tf_op jit(solution)/shard_map/ppermute | solution.py:60
  55.0 2.1 %collective-permute-start.14 = (bf16[8,160,384]{2,1,0:T(8,128)(2,1)S(1)}, bf16[8,160,384]{2,1,0:T(8,128)(2,1)}, u32[]{:S(2)}, u32[]{:S(2)}) collective-permute-start(bf16[8,160,384]{2,1,0:T(8,128)(2,1)S(1)} %bitcast.44), channel_id=1, source_target_pairs={{0,1},{1,0},{2,3},{3,2},{4,5},{5,4},{6,7},{7,6},{8,9},{9,8},{10,11... | collective-permute-start | bytes 2949128 | tf_op jit(solution)/shard_map/ppermute | solution.py:60
  57.0 9.7 %collective-permute-done.12.refs_1_ = bf16[8,160,384]{2,1,0:T(8,128)(2,1)} collective-permute-done((bf16[8,160,384]{2,1,0:T(8,128)(2,1)S(1)}, bf16[8,160,384]{2,1,0:T(8,128)(2,1)}, u32[]{:S(2)}, u32[]{:S(2)}) %collective-permute-start.12) | collective-permute-done | bytes 983072 | tf_op jit(solution)/shard_map/ppermute | solution.py:60
  66.8 2.4 %collective-permute-start.15 = (bf16[8,160,384]{2,1,0:T(8,128)(2,1)}, bf16[8,160,384]{2,1,0:T(8,128)(2,1)}, u32[]{:S(2)}, u32[]{:S(2)}) collective-permute-start(bf16[8,160,384]{2,1,0:T(8,128)(2,1)} %collective-permute-done.12.refs_1_), channel_id=1, source_target_pairs={{0,1},{1,0},{2,3},{3,2},{4,5},{5,4},{6,7},{7,6},{8,9},{9,8},{10,11... | collective-permute-start | bytes 2949128 | tf_op jit(solution)/shard_map/ppermute | solution.py:60
  70.0 1.7 %collective-permute-done.15.refs_4_ = bf16[8,160,384]{2,1,0:T(8,128)(2,1)} collective-permute-done((bf16[8,160,384]{2,1,0:T(8,128)(2,1)}, bf16[8,160,384]{2,1,0:T(8,128)(2,1)}, u32[]{:S(2)}, u32[]{:S(2)}) %collective-permute-start.15) | collective-permute-done | bytes 983072 | tf_op jit(solution)/shard_map/ppermute | solution.py:60
  71.7 1.4 %collective-permute-done.16.refs_5_ = bf16[8,160,384]{2,1,0:T(8,128)(2,1)} collective-permute-done((bf16[8,160,384]{2,1,0:T(8,128)(2,1)}, bf16[8,160,384]{2,1,0:T(8,128)(2,1)}, u32[]{:S(2)}, u32[]{:S(2)}) %collective-permute-start.16) | collective-permute-done | bytes 983072 | tf_op jit(solution)/shard_map/ppermute | solution.py:60
  74.0 3.3 %copy-done.2 = bf16[3,3,1152,384]{3,2,1,0:T(8,128)(2,1)S(1)} copy-done((bf16[3,3,1152,384]{3,2,1,0:T(8,128)(2,1)S(1)}, bf16[3,3,1152,384]{3,2,1,0:T(8,128)(2,1)}, u32[]{:S(2)}) %copy-start.2) | copy-done | bytes 7962648
  77.3 10.7 %conv_first.1 = (bf16[2,5,48,384]{3,2,1,0:T(8,128)(2,1)S(1)}, bf16[2,5,48,384]{3,2,1,0:T(8,128)(2,1)S(1)}, bf16[8,1296,384]{2,1,0:T(8,128)(2,1)S(1)}) custom-call(s32[1]{0:T(128)} %bitcast.tile, s32[8]{0:T(128)S(1)} %stack.78.where, bf16[6,7,48,384]{3,2,1,0:T(8,128)(2,1)S(1)} %constant_dynamic-update-slice_fusion.grown, bf16[9,1152,384]{2,1,0:T(8,128)(2,1)S(1)} %bitcast.47, ...), custom_call_target="tpu_custom_call" | custom-call | flops 7644119040 | bytes 7962624 | tf_op jit(solution)/shard_map/conv_first/pallas_call | solution.py:177
  88.4 2.2 %collective-permute-start.17 = (bf16[2,5,48,384]{3,2,1,0:T(8,128)(2,1)S(1)}, bf16[2,5,48,384]{3,2,1,0:T(8,128)(2,1)S(1)}, u32[]{:S(2)}, u32[]{:S(2)}) collective-permute-start(bf16[2,5,48,384]{3,2,1,0:T(8,128)(2,1)S(1)} %get-tuple-element.20.high), channel_id=1, source_target_pairs={{0,1},{1,2},{2,3},{3,4},{4,5},{5,6},{6,7},{7,8},{8,9},{9,10},{10,1... | collective-permute-start | bytes 1105928 | tf_op jit(solution)/shard_map/ppermute | solution.py:60
  90.7 5.1 %second_late.1 = (bf16[576,384]{1,0:T(8,128)(2,1)}, bf16[8,1296,384]{2,1,0:T(8,128)(2,1)S(1)}) custom-call(s32[8]{0:T(128)S(1)} %stack.78.where, bf16[2,5,48,384]{3,2,1,0:T(8,128)(2,1)S(1)} %get-tuple-element.21.low.high, bf16[2,5,48,384]{3,2,1,0:T(8,128)(2,1)S(1)} %get-tuple-element.20.high, bf16[576,384]{1,0:T(8,128)(2,1)S(1)} %bitcast.40, ...), custom_call_target="tpu_custom_call" | custom-call | flops 2293235712 | bytes 7962624 | tf_op jit(solution)/shard_map/second_late/pallas_call | solution.py:224
  95.8 3.7 %second_early.1 = bf16[576,384]{1,0:T(8,128)(2,1)} custom-call(bf16[2,5,48,384]{3,2,1,0:T(8,128)(2,1)S(1)} %collective-permute-done.17.low, bf16[2,5,48,384]{3,2,1,0:T(8,128)(2,1)S(1)} %get-tuple-element.21.low.high, bf16[576,384]{1,0:T(8,128)(2,1)S(1)} %bitcast.41, f32[1,384]{1,0:T(1,128)S(1)} %reshape.47.bias, ...), custom_call_target="tpu_custom_call", output_to_operand_aliasing={{}: (5, {})} | custom-call | flops 2293235712 | bytes 7962624 | tf_op jit(solution)/shard_map/second_early/pallas_call | solution.py:237
  (79 shorter events, 7.4 us)
Async XLA Ops:
  6.5 66.6 %all-gather.2.cloned.1.call-start = ((), (), s32[]{:S(2)}) async-start(), calls=%async_computation | async-start | bytes 8460288 | tf_op jit(solution)/shard_map/all_gather | solution.py:269
  7.3 7.9 %collective-permute-start.1 = (bf16[9,72,384]{2,1,0:T(8,128)(2,1)}, bf16[9,72,384]{2,1,0:T(8,128)(2,1)S(1)}, u32[]{:S(2)}, u32[]{:S(2)}) collective-permute-start(bf16[9,72,384]{2,1,0:T(8,128)(2,1)} %bitcast.59), channel_id=1, source_target_pairs={{0,1},{1,0},{2,3},{3,2},{4,5},{5,4},{6,7},{7,6},{8,9},{9,8},{10,11... | collective-permute-start | bytes 1493000 | tf_op jit(solution)/shard_map/ppermute | solution.py:60
  13.2 10.1 %collective-permute-start = (bf16[2,3,48,384]{3,2,1,0:T(8,128)(2,1)S(1)}, bf16[2,3,48,384]{3,2,1,0:T(8,128)(2,1)S(1)}, u32[]{:S(2)}, u32[]{:S(2)}) collective-permute-start(bf16[2,3,48,384]{3,2,1,0:T(8,128)(2,1)S(1)} %slice.45), channel_id=1, source_target_pairs={{0,1},{1,2},{2,3},{3,4},{4,5},{5,6},{6,7},{7,8},{8,9},{9,10},{10,1... | collective-permute-start | bytes 663560 | tf_op jit(solution)/shard_map/ppermute | solution.py:60
  15.5 10.8 %collective-permute-start.6 = (bf16[96,384]{1,0:T(8,128)(2,1)S(1)}, bf16[96,384]{1,0:T(8,128)(2,1)S(1)}, u32[]{:S(2)}, u32[]{:S(2)}) collective-permute-start(bf16[96,384]{1,0:T(8,128)(2,1)S(1)} %pad_maximum_fusion.3), channel_id=1, source_target_pairs={{0,6},{1,11},{2,8},{3,13},{4,10},{5,15},{6,12},{7,1},{8,14},{9,3},... | collective-permute-start | bytes 221192 | tf_op jit(solution)/shard_map/ppermute | solution.py:60
  20.9 5.4 %collective-permute-start.5 = (bf16[96,384]{1,0:T(8,128)(2,1)S(1)}, bf16[96,384]{1,0:T(8,128)(2,1)S(1)}, u32[]{:S(2)}, u32[]{:S(2)}) collective-permute-start(bf16[96,384]{1,0:T(8,128)(2,1)S(1)} %pad_maximum_fusion.3), channel_id=1, source_target_pairs={{0,4},{1,13},{2,6},{3,15},{4,8},{5,1},{6,10},{7,3},{8,12},{9,5},{1... | collective-permute-start | bytes 221192 | tf_op jit(solution)/shard_map/ppermute | solution.py:60
  23.3 6.7 %collective-permute-start.4 = (bf16[96,384]{1,0:T(8,128)(2,1)S(1)}, bf16[96,384]{1,0:T(8,128)(2,1)S(1)}, u32[]{:S(2)}, u32[]{:S(2)}) collective-permute-start(bf16[96,384]{1,0:T(8,128)(2,1)S(1)} %pad_maximum_fusion.3), channel_id=1, source_target_pairs={{0,2},{1,15},{2,4},{3,1},{4,6},{5,3},{6,8},{7,5},{8,10},{9,7},{10,... | collective-permute-start | bytes 221192 | tf_op jit(solution)/shard_map/ppermute | solution.py:60
  23.4 11.5 %collective-permute-start.8 = (bf16[96,384]{1,0:T(8,128)(2,1)S(1)}, bf16[96,384]{1,0:T(8,128)(2,1)S(1)}, u32[]{:S(2)}, u32[]{:S(2)}) collective-permute-start(bf16[96,384]{1,0:T(8,128)(2,1)S(1)} %pad_maximum_fusion.3), channel_id=1, source_target_pairs={{0,8},{1,9},{2,10},{3,11},{4,12},{5,13},{6,14},{7,15},{8,0},{9,1},... | collective-permute-start | bytes 221192 | tf_op jit(solution)/shard_map/ppermute | solution.py:60
  30.1 4.7 %collective-permute-start.7 = (bf16[3,96,384]{2,1,0:T(8,128)(2,1)S(1)}, bf16[3,96,384]{2,1,0:T(8,128)(2,1)S(1)}, u32[]{:S(2)}, u32[]{:S(2)}) collective-permute-start(bf16[3,96,384]{2,1,0:T(8,128)(2,1)S(1)} %pad_maximum_fusion.2), channel_id=1, source_target_pairs={{0,1},{1,0},{2,3},{3,2},{4,5},{5,4},{6,7},{7,6},{8,9},{9,8},{10,11... | collective-permute-start | bytes 663560 | tf_op jit(solution)/shard_map/ppermute | solution.py:60
  30.3 12.4 %collective-permute-start.2 = (bf16[6,2,48,384]{3,2,1,0:T(8,128)(2,1)S(1)}, bf16[6,2,48,384]{3,2,1,0:T(8,128)(2,1)S(1)}, u32[]{:S(2)}, u32[]{:S(2)}) collective-permute-start(bf16[6,2,48,384]{3,2,1,0:T(8,128)(2,1)S(1)} %get-tuple-element.32), channel_id=1, source_target_pairs={{0,16},{1,17},{2,18},{3,19},{4,20},{5,21},{6,22},{7,23},{8,24},{9,... | collective-permute-start | bytes 1327112 | tf_op jit(solution)/shard_map/ppermute | solution.py:60
  33.4 12.9 %collective-permute-start.3 = (bf16[6,2,48,384]{3,2,1,0:T(8,128)(2,1)S(1)}, bf16[6,2,48,384]{3,2,1,0:T(8,128)(2,1)S(1)}, u32[]{:S(2)}, u32[]{:S(2)}) collective-permute-start(bf16[6,2,48,384]{3,2,1,0:T(8,128)(2,1)S(1)} %get-tuple-element.31), channel_id=1, source_target_pairs={{16,0},{17,1},{18,2},{19,3},{20,4},{21,5},{22,6},{23,7},{24,8},{25... | collective-permute-start | bytes 1327112 | tf_op jit(solution)/shard_map/ppermute | solution.py:60
  35.9 11.4 %collective-permute-start.9 = (bf16[8,40,384]{2,1,0:T(8,128)(2,1)S(1)}, bf16[8,40,384]{2,1,0:T(8,128)(2,1)S(1)}, u32[]{:S(2)}, u32[]{:S(2)}) collective-permute-start(bf16[8,40,384]{2,1,0:T(8,128)(2,1)S(1)} %dynamic-slice_select_fusion), channel_id=1, source_target_pairs={{0,48},{1,193},{2,50},{3,195},{4,52},{5,197},{6,54},{7,199},{8,56}... | collective-permute-start | bytes 737288 | tf_op jit(solution)/shard_map/ppermute | solution.py:60
  41.5 9.6 %collective-permute-start.10 = (bf16[8,40,384]{2,1,0:T(8,128)(2,1)S(1)}, bf16[8,40,384]{2,1,0:T(8,128)(2,1)S(1)}, u32[]{:S(2)}, u32[]{:S(2)}) collective-permute-start(bf16[8,40,384]{2,1,0:T(8,128)(2,1)S(1)} %dynamic-slice_select_fusion), channel_id=1, source_target_pairs={{0,32},{1,129},{2,34},{3,131},{4,36},{5,133},{6,38},{7,135},{8,40}... | collective-permute-start | bytes 737288 | tf_op jit(solution)/shard_map/ppermute | solution.py:60
  42.0 9.2 %collective-permute-start.11 = (bf16[8,40,384]{2,1,0:T(8,128)(2,1)S(1)}, bf16[8,40,384]{2,1,0:T(8,128)(2,1)S(1)}, u32[]{:S(2)}, u32[]{:S(2)}) collective-permute-start(bf16[8,40,384]{2,1,0:T(8,128)(2,1)S(1)} %dynamic-slice_select_fusion), channel_id=1, source_target_pairs={{0,16},{1,65},{2,18},{3,67},{4,20},{5,69},{6,22},{7,71},{8,24},{9,... | collective-permute-start | bytes 737288 | tf_op jit(solution)/shard_map/ppermute | solution.py:60
  51.6 18.3 %copy-start.4 = (f32[384]{0:T(512)S(1)}, f32[384]{0:T(512)}, u32[]{:S(2)}) copy-start(f32[384]{0:T(512)} %param.10) | copy-start | bytes 4612
  51.6 18.2 %copy-start.5 = (f32[384]{0:T(512)S(1)}, f32[384]{0:T(512)}, u32[]{:S(2)}) copy-start(f32[384]{0:T(512)} %param.11) | copy-start | bytes 4612
  51.7 15.1 %collective-permute-start.12 = (bf16[8,160,384]{2,1,0:T(8,128)(2,1)S(1)}, bf16[8,160,384]{2,1,0:T(8,128)(2,1)}, u32[]{:S(2)}, u32[]{:S(2)}) collective-permute-start(bf16[8,160,384]{2,1,0:T(8,128)(2,1)S(1)} %bitcast.42), channel_id=1, source_target_pairs={{0,64},{1,17},{2,66},{3,19},{4,68},{5,21},{6,70},{7,23},{8,72},{9,... | collective-permute-start | bytes 2949128 | tf_op jit(solution)/shard_map/ppermute | solution.py:60
  51.8 17.3 %collective-permute-start.13 = (bf16[8,160,384]{2,1,0:T(8,128)(2,1)S(1)}, bf16[8,160,384]{2,1,0:T(8,128)(2,1)}, u32[]{:S(2)}, u32[]{:S(2)}) collective-permute-start(bf16[8,160,384]{2,1,0:T(8,128)(2,1)S(1)} %bitcast.43), channel_id=1, source_target_pairs={{0,192},{1,49},{2,194},{3,51},{4,196},{5,53},{6,198},{7,55},{8,200... | collective-permute-start | bytes 2949128 | tf_op jit(solution)/shard_map/ppermute | solution.py:60
  55.0 15.0 %collective-permute-start.14 = (bf16[8,160,384]{2,1,0:T(8,128)(2,1)S(1)}, bf16[8,160,384]{2,1,0:T(8,128)(2,1)}, u32[]{:S(2)}, u32[]{:S(2)}) collective-permute-start(bf16[8,160,384]{2,1,0:T(8,128)(2,1)S(1)} %bitcast.44), channel_id=1, source_target_pairs={{0,1},{1,0},{2,3},{3,2},{4,5},{5,4},{6,7},{7,6},{8,9},{9,8},{10,11... | collective-permute-start | bytes 2949128 | tf_op jit(solution)/shard_map/ppermute | solution.py:60
  66.8 4.9 %collective-permute-start.15 = (bf16[8,160,384]{2,1,0:T(8,128)(2,1)}, bf16[8,160,384]{2,1,0:T(8,128)(2,1)}, u32[]{:S(2)}, u32[]{:S(2)}) collective-permute-start(bf16[8,160,384]{2,1,0:T(8,128)(2,1)} %collective-permute-done.12.refs_1_), channel_id=1, source_target_pairs={{0,1},{1,0},{2,3},{3,2},{4,5},{5,4},{6,7},{7,6},{8,9},{9,8},{10,11... | collective-permute-start | bytes 2949128 | tf_op jit(solution)/shard_map/ppermute | solution.py:60
  69.1 4.0 %collective-permute-start.16 = (bf16[8,160,384]{2,1,0:T(8,128)(2,1)}, bf16[8,160,384]{2,1,0:T(8,128)(2,1)}, u32[]{:S(2)}, u32[]{:S(2)}) collective-permute-start(bf16[8,160,384]{2,1,0:T(8,128)(2,1)} %collective-permute-done.13.refs_2_), channel_id=1, source_target_pairs={{0,1},{1,0},{2,3},{3,2},{4,5},{5,4},{6,7},{7,6},{8,9},{9,8},{10,11... | collective-permute-start | bytes 2949128 | tf_op jit(solution)/shard_map/ppermute | solution.py:60
  69.8 18.2 %collective-permute-start.18 = (bf16[8,160,384]{2,1,0:T(8,128)(2,1)S(1)}, bf16[8,160,384]{2,1,0:T(8,128)(2,1)S(1)}, u32[]{:S(2)}, u32[]{:S(2)}) collective-permute-start(bf16[8,160,384]{2,1,0:T(8,128)(2,1)S(1)} %bitcast.45), channel_id=1, source_target_pairs={{0,128},{1,33},{2,130},{3,35},{4,132},{5,37},{6,134},{7,39},{8,136... | collective-permute-start | bytes 2949128 | tf_op jit(solution)/shard_map/ppermute | solution.py:60
  77.3 13.4 %copy-start = (bf16[4,3,48,384]{3,2,1,0:T(8,128)(2,1)S(1)}, bf16[4,3,48,384]{3,2,1,0:T(8,128)(2,1)}, u32[]{:S(2)}) copy-start(bf16[4,3,48,384]{3,2,1,0:T(8,128)(2,1)} %param.7) | copy-start | bytes 1327108
  88.0 2.7 %collective-permute-start.19 = (bf16[8,160,384]{2,1,0:T(8,128)(2,1)S(1)}, bf16[8,160,384]{2,1,0:T(8,128)(2,1)S(1)}, u32[]{:S(2)}, u32[]{:S(2)}) collective-permute-start(bf16[8,160,384]{2,1,0:T(8,128)(2,1)S(1)} %collective-permute-done.18.far), channel_id=1, source_target_pairs={{0,1},{1,0},{2,3},{3,2},{4,5},{5,4},{6,7},{7,6},{8,9},{9,8},{10,11... | collective-permute-start | bytes 2949128 | tf_op jit(solution)/shard_map/ppermute | solution.py:60
  88.4 7.4 %collective-permute-start.17 = (bf16[2,5,48,384]{3,2,1,0:T(8,128)(2,1)S(1)}, bf16[2,5,48,384]{3,2,1,0:T(8,128)(2,1)S(1)}, u32[]{:S(2)}, u32[]{:S(2)}) collective-permute-start(bf16[2,5,48,384]{3,2,1,0:T(8,128)(2,1)S(1)} %get-tuple-element.20.high), channel_id=1, source_target_pairs={{0,1},{1,2},{2,3},{3,4},{4,5},{5,6},{6,7},{7,8},{8,9},{9,10},{10,1... | collective-permute-start | bytes 1105928 | tf_op jit(solution)/shard_map/ppermute | solution.py:60
  (4 other events, 26.1 us)
Sparse Core Ops, SparseCore 0:
  9.1 62.5 all-gather.1

commit v9 on v8

--- a/solution.py
+++ b/solution.py
@@ -117,28 +117,21 @@
 
 def convolve(frames, rows, whole, wide):
     count = len(frames) - 2
-    for t in range(3):
-        left = jnp.concatenate(
-            [
-                jnp.concatenate(
-                    [frames[t + f][k : k + rows].reshape(rows * 48, C) for f in range(count)], axis=0
-                )
-                for k in range(3)
-            ],
-            axis=1,
-        )
-        right = jnp.concatenate(
-            [
-                jnp.concatenate([whole(3 * t + k)[d * C : (d + 1) * C] for d in range(3)], axis=1)
-                for k in range(3)
-            ],
-            axis=0,
-        )
-        part = jnp.dot(left, right, preferred_element_type=F32)
-        if t == 0:
-            wide[...] = part
-        else:
-            wide[...] += part
+
+    def left(t, k):
+        shown = [frames[t + f][k : k + rows].reshape(rows * 48, C) for f in range(count)]
+        return jnp.concatenate(shown, axis=0)
+
+    def right(t, k):
+        tap = whole(3 * t + k)
+        return jnp.concatenate([tap[d * C : (d + 1) * C] for d in range(3)], axis=1)
+
+    taps = [(t, k) for t in range(3) for k in range(3)]
+    wide[...] = jnp.dot(
+        jnp.concatenate([left(t, k) for t, k in taps], axis=1),
+        jnp.concatenate([right(t, k) for t, k in taps], axis=0),
+        preferred_element_type=F32,
+    )
     column = lax.broadcasted_iota(jnp.int32, (48, C), 0)
     lines = []
     for i in range(count * rows):

time: 107 us -> 106 us (level)
  transfers between devices with their start and end apart: 21 -> 21, of which waited for: 7 -> 8; matrix products, arithmetic and copies ran while one was open for 5% -> 5% of each run, Pallas kernels for 15% -> 14%
where the time goes in v9:
time: 106 us; the launch traced here: 105 us
  starting transfers between devices  38 us (36%)
  waiting for transfers between devices  25.8 us (24%)
  Pallas kernels  18.6 us (18%)
  between operations  13.9 us (13%)
  local copies, waits for them, and re-layouts  5.95 us (6%)
  other arithmetic  3.21 us (3%)
    ppermute x20, starting transfers between devices, send(): return lax.ppermute(value, AXES, pairs)  38 us
    ppermute x20, waiting for transfers between devices, send(): return lax.ppermute(value, AXES, pairs)  25.1 us
    pallas_call x1, Pallas kernels, conv_first(): pl.pallas_call(first_kernel, out_shape=[half, half, jax.ShapeDtypeStruct(...  10.1 us
    pallas_call x1, Pallas kernels, conv_late(): pl.pallas_call(late_kernel, out_shape=[jax.ShapeDtypeStruct((576, C), BF)...  4.94 us
    unnamed x30, local copies, waits for them, and re-layouts  4.73 us
    pallas_call x1, Pallas kernels, conv_early(): pl.pallas_call(early_kernel, out_shape=jax.ShapeDtypeStruct((576, C), BF)...  3.56 us
  transfers between devices with their start and end apart: 21, of which 8 were waited for; matrix products, arithmetic and copies ran while one was open for 5% of the time, Pallas kernels for 14%

profile of v9, /device:TPU:1, one launch (start us, length us, event | category | flops | bytes accessed | tf_op | source)
XLA Modules:
  0.0 105.4 jit_solution(7558342106482641660)
XLA Ops:
  7.3 3.3 %collective-permute-start.1 = (bf16[9,72,384]{2,1,0:T(8,128)(2,1)}, bf16[9,72,384]{2,1,0:T(8,128)(2,1)S(1)}, u32[]{:S(2)}, u32[]{:S(2)}) collective-permute-start(bf16[9,72,384]{2,1,0:T(8,128)(2,1)} %bitcast.59), channel_id=1, source_target_pairs={{0,1},{1,0},{2,3},{3,2},{4,5},{5,4},{6,7},{7,6},{8,9},{9,8},{10,11... | collective-permute-start | bytes 1493000 | tf_op jit(solution)/shard_map/ppermute | solution.py:60
  10.6 1.2 %fusion = f32[4,3,48]{2,1,0:T(4,128)S(1)} fusion(bf16[4,3,48,384]{3,2,1,0:T(8,128)(2,1)} %param.7), kind=kLoop, calls=%fused_computation.4 | loop fusion | flops 662976 | bytes 444672 | tf_op jit(solution)/shard_map/reduce_sum | solution.py:65
  11.8 1.4 %fusion.7 = bf16[4,3,48,384]{3,2,1,0:T(8,128)(2,1)S(1)} fusion(bf16[4,3,48,384]{3,2,1,0:T(8,128)(2,1)} %param.7, f32[384]{0:T(512)} %param.8, f32[4,3,48]{2,1,0:T(4,128)S(1)} %add_rsqrt_fusion), kind=kLoop, calls=%fused_computation.11 | loop fusion | flops 1769472 | bytes 888576 | tf_op jit(solution)/shard_map/convert_element_type | solution.py:263
  13.2 1.9 %collective-permute-start = (bf16[2,3,48,384]{3,2,1,0:T(8,128)(2,1)S(1)}, bf16[2,3,48,384]{3,2,1,0:T(8,128)(2,1)S(1)}, u32[]{:S(2)}, u32[]{:S(2)}) collective-permute-start(bf16[2,3,48,384]{3,2,1,0:T(8,128)(2,1)S(1)} %slice.45), channel_id=1, source_target_pairs={{0,1},{1,2},{2,3},{3,4},{4,5},{5,6},{6,7},{7,8},{8,9},{9,10},{10,1... | collective-permute-start | bytes 663560 | tf_op jit(solution)/shard_map/ppermute | solution.py:60
  15.5 5.4 %collective-permute-start.6 = (bf16[96,384]{1,0:T(8,128)(2,1)S(1)}, bf16[96,384]{1,0:T(8,128)(2,1)S(1)}, u32[]{:S(2)}, u32[]{:S(2)}) collective-permute-start(bf16[96,384]{1,0:T(8,128)(2,1)S(1)} %pad_maximum_fusion.3), channel_id=1, source_target_pairs={{0,6},{1,11},{2,8},{3,13},{4,10},{5,15},{6,12},{7,1},{8,14},{9,3},... | collective-permute-start | bytes 221192 | tf_op jit(solution)/shard_map/ppermute | solution.py:60
  20.9 2.4 %collective-permute-start.5 = (bf16[96,384]{1,0:T(8,128)(2,1)S(1)}, bf16[96,384]{1,0:T(8,128)(2,1)S(1)}, u32[]{:S(2)}, u32[]{:S(2)}) collective-permute-start(bf16[96,384]{1,0:T(8,128)(2,1)S(1)} %pad_maximum_fusion.3), channel_id=1, source_target_pairs={{0,4},{1,13},{2,6},{3,15},{4,8},{5,1},{6,10},{7,3},{8,12},{9,5},{1... | collective-permute-start | bytes 221192 | tf_op jit(solution)/shard_map/ppermute | solution.py:60
  23.4 2.9 %collective-permute-start.8 = (bf16[96,384]{1,0:T(8,128)(2,1)S(1)}, bf16[96,384]{1,0:T(8,128)(2,1)S(1)}, u32[]{:S(2)}, u32[]{:S(2)}) collective-permute-start(bf16[96,384]{1,0:T(8,128)(2,1)S(1)} %pad_maximum_fusion.3), channel_id=1, source_target_pairs={{0,8},{1,9},{2,10},{3,11},{4,12},{5,13},{6,14},{7,15},{8,0},{9,1},... | collective-permute-start | bytes 221192 | tf_op jit(solution)/shard_map/ppermute | solution.py:60
  26.3 3.7 %collective-permute-done.4 = bf16[96,384]{1,0:T(8,128)(2,1)S(1)} collective-permute-done((bf16[96,384]{1,0:T(8,128)(2,1)S(1)}, bf16[96,384]{1,0:T(8,128)(2,1)S(1)}, u32[]{:S(2)}, u32[]{:S(2)}) %collective-permute-start.4) | collective-permute-done | bytes 73760 | tf_op jit(solution)/shard_map/ppermute | solution.py:60
  30.3 3.1 %collective-permute-start.2 = (bf16[6,2,48,384]{3,2,1,0:T(8,128)(2,1)S(1)}, bf16[6,2,48,384]{3,2,1,0:T(8,128)(2,1)S(1)}, u32[]{:S(2)}, u32[]{:S(2)}) collective-permute-start(bf16[6,2,48,384]{3,2,1,0:T(8,128)(2,1)S(1)} %get-tuple-element.32), channel_id=1, source_target_pairs={{0,16},{1,17},{2,18},{3,19},{4,20},{5,21},{6,22},{7,23},{8,24},{9,... | collective-permute-start | bytes 1327112 | tf_op jit(solution)/shard_map/ppermute | solution.py:60
  33.4 1.3 %collective-permute-start.3 = (bf16[6,2,48,384]{3,2,1,0:T(8,128)(2,1)S(1)}, bf16[6,2,48,384]{3,2,1,0:T(8,128)(2,1)S(1)}, u32[]{:S(2)}, u32[]{:S(2)}) collective-permute-start(bf16[6,2,48,384]{3,2,1,0:T(8,128)(2,1)S(1)} %get-tuple-element.31), channel_id=1, source_target_pairs={{16,0},{17,1},{18,2},{19,3},{20,4},{21,5},{22,6},{23,7},{24,8},{25... | collective-permute-start | bytes 1327112 | tf_op jit(solution)/shard_map/ppermute | solution.py:60
  35.9 5.6 %collective-permute-start.9 = (bf16[8,40,384]{2,1,0:T(8,128)(2,1)S(1)}, bf16[8,40,384]{2,1,0:T(8,128)(2,1)S(1)}, u32[]{:S(2)}, u32[]{:S(2)}) collective-permute-start(bf16[8,40,384]{2,1,0:T(8,128)(2,1)S(1)} %dynamic-slice_select_fusion), channel_id=1, source_target_pairs={{0,48},{1,193},{2,50},{3,195},{4,52},{5,197},{6,54},{7,199},{8,56}... | collective-permute-start | bytes 737288 | tf_op jit(solution)/shard_map/ppermute | solution.py:60
  42.9 3.5 %collective-permute-done.3 = bf16[6,2,48,384]{3,2,1,0:T(8,128)(2,1)S(1)} collective-permute-done((bf16[6,2,48,384]{3,2,1,0:T(8,128)(2,1)S(1)}, bf16[6,2,48,384]{3,2,1,0:T(8,128)(2,1)S(1)}, u32[]{:S(2)}, u32[]{:S(2)}) %collective-permute-start.3) | collective-permute-done | bytes 442400 | tf_op jit(solution)/shard_map/ppermute | solution.py:60
  47.4 3.8 %collective-permute-done.10 = bf16[8,40,384]{2,1,0:T(8,128)(2,1)S(1)} collective-permute-done((bf16[8,40,384]{2,1,0:T(8,128)(2,1)S(1)}, bf16[8,40,384]{2,1,0:T(8,128)(2,1)S(1)}, u32[]{:S(2)}, u32[]{:S(2)}) %collective-permute-start.10) | collective-permute-done | bytes 245792 | tf_op jit(solution)/shard_map/ppermute | solution.py:60
  51.8 3.2 %collective-permute-start.13 = (bf16[8,160,384]{2,1,0:T(8,128)(2,1)S(1)}, bf16[8,160,384]{2,1,0:T(8,128)(2,1)}, u32[]{:S(2)}, u32[]{:S(2)}) collective-permute-start(bf16[8,160,384]{2,1,0:T(8,128)(2,1)S(1)} %bitcast.43), channel_id=1, source_target_pairs={{0,192},{1,49},{2,194},{3,51},{4,196},{5,53},{6,198},{7,55},{8,200... | collective-permute-start | bytes 2949128 | tf_op jit(solution)/shard_map/ppermute | solution.py:60
  55.0 2.1 %collective-permute-start.14 = (bf16[8,160,384]{2,1,0:T(8,128)(2,1)S(1)}, bf16[8,160,384]{2,1,0:T(8,128)(2,1)}, u32[]{:S(2)}, u32[]{:S(2)}) collective-permute-start(bf16[8,160,384]{2,1,0:T(8,128)(2,1)S(1)} %bitcast.44), channel_id=1, source_target_pairs={{0,1},{1,0},{2,3},{3,2},{4,5},{5,4},{6,7},{7,6},{8,9},{9,8},{10,11... | collective-permute-start | bytes 2949128 | tf_op jit(solution)/shard_map/ppermute | solution.py:60
  57.0 9.7 %collective-permute-done.12.refs_1_ = bf16[8,160,384]{2,1,0:T(8,128)(2,1)} collective-permute-done((bf16[8,160,384]{2,1,0:T(8,128)(2,1)S(1)}, bf16[8,160,384]{2,1,0:T(8,128)(2,1)}, u32[]{:S(2)}, u32[]{:S(2)}) %collective-permute-start.12) | collective-permute-done | bytes 983072 | tf_op jit(solution)/shard_map/ppermute | solution.py:60
  66.8 2.4 %collective-permute-start.15 = (bf16[8,160,384]{2,1,0:T(8,128)(2,1)}, bf16[8,160,384]{2,1,0:T(8,128)(2,1)}, u32[]{:S(2)}, u32[]{:S(2)}) collective-permute-start(bf16[8,160,384]{2,1,0:T(8,128)(2,1)} %collective-permute-done.12.refs_1_), channel_id=1, source_target_pairs={{0,1},{1,0},{2,3},{3,2},{4,5},{5,4},{6,7},{7,6},{8,9},{9,8},{10,11... | collective-permute-start | bytes 2949128 | tf_op jit(solution)/shard_map/ppermute | solution.py:60
  70.0 1.7 %collective-permute-done.15.refs_4_ = bf16[8,160,384]{2,1,0:T(8,128)(2,1)} collective-permute-done((bf16[8,160,384]{2,1,0:T(8,128)(2,1)}, bf16[8,160,384]{2,1,0:T(8,128)(2,1)}, u32[]{:S(2)}, u32[]{:S(2)}) %collective-permute-start.15) | collective-permute-done | bytes 983072 | tf_op jit(solution)/shard_map/ppermute | solution.py:60
  71.7 1.4 %collective-permute-done.16.refs_5_ = bf16[8,160,384]{2,1,0:T(8,128)(2,1)} collective-permute-done((bf16[8,160,384]{2,1,0:T(8,128)(2,1)}, bf16[8,160,384]{2,1,0:T(8,128)(2,1)}, u32[]{:S(2)}, u32[]{:S(2)}) %collective-permute-start.16) | collective-permute-done | bytes 983072 | tf_op jit(solution)/shard_map/ppermute | solution.py:60
  74.0 3.3 %copy-done.2 = bf16[3,3,1152,384]{3,2,1,0:T(8,128)(2,1)S(1)} copy-done((bf16[3,3,1152,384]{3,2,1,0:T(8,128)(2,1)S(1)}, bf16[3,3,1152,384]{3,2,1,0:T(8,128)(2,1)}, u32[]{:S(2)}) %copy-start.2) | copy-done | bytes 7962648
  77.3 10.1 %conv_first.1 = (bf16[2,5,48,384]{3,2,1,0:T(8,128)(2,1)S(1)}, bf16[2,5,48,384]{3,2,1,0:T(8,128)(2,1)S(1)}, bf16[8,1296,384]{2,1,0:T(8,128)(2,1)S(1)}) custom-call(s32[1]{0:T(128)} %bitcast.tile, s32[8]{0:T(128)S(1)} %stack.78.where, bf16[6,7,48,384]{3,2,1,0:T(8,128)(2,1)S(1)} %constant_dynamic-update-slice_fusion.grown, bf16[9,1152,384]{2,1,0:T(8,128)(2,1)S(1)} %bitcast.47, ...), custom_call_target="tpu_custom_call" | custom-call | flops 7644119040 | bytes 7962624 | tf_op jit(solution)/shard_map/conv_first/pallas_call | solution.py:170
  87.8 2.0 %collective-permute-start.17 = (bf16[2,5,48,384]{3,2,1,0:T(8,128)(2,1)S(1)}, bf16[2,5,48,384]{3,2,1,0:T(8,128)(2,1)S(1)}, u32[]{:S(2)}, u32[]{:S(2)}) collective-permute-start(bf16[2,5,48,384]{3,2,1,0:T(8,128)(2,1)S(1)} %get-tuple-element.20.high), channel_id=1, source_target_pairs={{0,1},{1,2},{2,3},{3,4},{4,5},{5,6},{6,7},{7,8},{8,9},{9,10},{10,1... | collective-permute-start | bytes 1105928 | tf_op jit(solution)/shard_map/ppermute | solution.py:60
  90.1 4.9 %second_late.1 = (bf16[576,384]{1,0:T(8,128)(2,1)}, bf16[8,1296,384]{2,1,0:T(8,128)(2,1)S(1)}) custom-call(s32[8]{0:T(128)S(1)} %stack.78.where, bf16[2,5,48,384]{3,2,1,0:T(8,128)(2,1)S(1)} %get-tuple-element.21.low.high, bf16[2,5,48,384]{3,2,1,0:T(8,128)(2,1)S(1)} %get-tuple-element.20.high, bf16[576,384]{1,0:T(8,128)(2,1)S(1)} %bitcast.40, ...), custom_call_target="tpu_custom_call" | custom-call | flops 2293235712 | bytes 7962624 | tf_op jit(solution)/shard_map/second_late/pallas_call | solution.py:217
  95.0 3.6 %second_early.1 = bf16[576,384]{1,0:T(8,128)(2,1)} custom-call(bf16[2,5,48,384]{3,2,1,0:T(8,128)(2,1)S(1)} %collective-permute-done.17.low, bf16[2,5,48,384]{3,2,1,0:T(8,128)(2,1)S(1)} %get-tuple-element.21.low.high, bf16[576,384]{1,0:T(8,128)(2,1)S(1)} %bitcast.41, f32[1,384]{1,0:T(1,128)S(1)} %reshape.47.bias, ...), custom_call_target="tpu_custom_call", output_to_operand_aliasing={{}: (5, {})} | custom-call | flops 2293235712 | bytes 7962624 | tf_op jit(solution)/shard_map/second_early/pallas_call | solution.py:230
  (79 shorter events, 7.6 us)
Async XLA Ops:
  6.5 66.6 %all-gather.2.cloned.1.call-start = ((), (), s32[]{:S(2)}) async-start(), calls=%async_computation | async-start | bytes 8460288 | tf_op jit(solution)/shard_map/all_gather | solution.py:262
  7.3 7.9 %collective-permute-start.1 = (bf16[9,72,384]{2,1,0:T(8,128)(2,1)}, bf16[9,72,384]{2,1,0:T(8,128)(2,1)S(1)}, u32[]{:S(2)}, u32[]{:S(2)}) collective-permute-start(bf16[9,72,384]{2,1,0:T(8,128)(2,1)} %bitcast.59), channel_id=1, source_target_pairs={{0,1},{1,0},{2,3},{3,2},{4,5},{5,4},{6,7},{7,6},{8,9},{9,8},{10,11... | collective-permute-start | bytes 1493000 | tf_op jit(solution)/shard_map/ppermute | solution.py:60
  13.2 10.1 %collective-permute-start = (bf16[2,3,48,384]{3,2,1,0:T(8,128)(2,1)S(1)}, bf16[2,3,48,384]{3,2,1,0:T(8,128)(2,1)S(1)}, u32[]{:S(2)}, u32[]{:S(2)}) collective-permute-start(bf16[2,3,48,384]{3,2,1,0:T(8,128)(2,1)S(1)} %slice.45), channel_id=1, source_target_pairs={{0,1},{1,2},{2,3},{3,4},{4,5},{5,6},{6,7},{7,8},{8,9},{9,10},{10,1... | collective-permute-start | bytes 663560 | tf_op jit(solution)/shard_map/ppermute | solution.py:60
  15.5 10.8 %collective-permute-start.6 = (bf16[96,384]{1,0:T(8,128)(2,1)S(1)}, bf16[96,384]{1,0:T(8,128)(2,1)S(1)}, u32[]{:S(2)}, u32[]{:S(2)}) collective-permute-start(bf16[96,384]{1,0:T(8,128)(2,1)S(1)} %pad_maximum_fusion.3), channel_id=1, source_target_pairs={{0,6},{1,11},{2,8},{3,13},{4,10},{5,15},{6,12},{7,1},{8,14},{9,3},... | collective-permute-start | bytes 221192 | tf_op jit(solution)/shard_map/ppermute | solution.py:60
  20.9 5.4 %collective-permute-start.5 = (bf16[96,384]{1,0:T(8,128)(2,1)S(1)}, bf16[96,384]{1,0:T(8,128)(2,1)S(1)}, u32[]{:S(2)}, u32[]{:S(2)}) collective-permute-start(bf16[96,384]{1,0:T(8,128)(2,1)S(1)} %pad_maximum_fusion.3), channel_id=1, source_target_pairs={{0,4},{1,13},{2,6},{3,15},{4,8},{5,1},{6,10},{7,3},{8,12},{9,5},{1... | collective-permute-start | bytes 221192 | tf_op jit(solution)/shard_map/ppermute | solution.py:60
  23.3 6.7 %collective-permute-start.4 = (bf16[96,384]{1,0:T(8,128)(2,1)S(1)}, bf16[96,384]{1,0:T(8,128)(2,1)S(1)}, u32[]{:S(2)}, u32[]{:S(2)}) collective-permute-start(bf16[96,384]{1,0:T(8,128)(2,1)S(1)} %pad_maximum_fusion.3), channel_id=1, source_target_pairs={{0,2},{1,15},{2,4},{3,1},{4,6},{5,3},{6,8},{7,5},{8,10},{9,7},{10,... | collective-permute-start | bytes 221192 | tf_op jit(solution)/shard_map/ppermute | solution.py:60
  23.4 11.5 %collective-permute-start.8 = (bf16[96,384]{1,0:T(8,128)(2,1)S(1)}, bf16[96,384]{1,0:T(8,128)(2,1)S(1)}, u32[]{:S(2)}, u32[]{:S(2)}) collective-permute-start(bf16[96,384]{1,0:T(8,128)(2,1)S(1)} %pad_maximum_fusion.3), channel_id=1, source_target_pairs={{0,8},{1,9},{2,10},{3,11},{4,12},{5,13},{6,14},{7,15},{8,0},{9,1},... | collective-permute-start | bytes 221192 | tf_op jit(solution)/shard_map/ppermute | solution.py:60
  30.1 4.7 %collective-permute-start.7 = (bf16[3,96,384]{2,1,0:T(8,128)(2,1)S(1)}, bf16[3,96,384]{2,1,0:T(8,128)(2,1)S(1)}, u32[]{:S(2)}, u32[]{:S(2)}) collective-permute-start(bf16[3,96,384]{2,1,0:T(8,128)(2,1)S(1)} %pad_maximum_fusion.2), channel_id=1, source_target_pairs={{0,1},{1,0},{2,3},{3,2},{4,5},{5,4},{6,7},{7,6},{8,9},{9,8},{10,11... | collective-permute-start | bytes 663560 | tf_op jit(solution)/shard_map/ppermute | solution.py:60
  30.3 12.4 %collective-permute-start.2 = (bf16[6,2,48,384]{3,2,1,0:T(8,128)(2,1)S(1)}, bf16[6,2,48,384]{3,2,1,0:T(8,128)(2,1)S(1)}, u32[]{:S(2)}, u32[]{:S(2)}) collective-permute-start(bf16[6,2,48,384]{3,2,1,0:T(8,128)(2,1)S(1)} %get-tuple-element.32), channel_id=1, source_target_pairs={{0,16},{1,17},{2,18},{3,19},{4,20},{5,21},{6,22},{7,23},{8,24},{9,... | collective-permute-start | bytes 1327112 | tf_op jit(solution)/shard_map/ppermute | solution.py:60
  33.4 12.9 %collective-permute-start.3 = (bf16[6,2,48,384]{3,2,1,0:T(8,128)(2,1)S(1)}, bf16[6,2,48,384]{3,2,1,0:T(8,128)(2,1)S(1)}, u32[]{:S(2)}, u32[]{:S(2)}) collective-permute-start(bf16[6,2,48,384]{3,2,1,0:T(8,128)(2,1)S(1)} %get-tuple-element.31), channel_id=1, source_target_pairs={{16,0},{17,1},{18,2},{19,3},{20,4},{21,5},{22,6},{23,7},{24,8},{25... | collective-permute-start | bytes 1327112 | tf_op jit(solution)/shard_map/ppermute | solution.py:60
  35.9 11.4 %collective-permute-start.9 = (bf16[8,40,384]{2,1,0:T(8,128)(2,1)S(1)}, bf16[8,40,384]{2,1,0:T(8,128)(2,1)S(1)}, u32[]{:S(2)}, u32[]{:S(2)}) collective-permute-start(bf16[8,40,384]{2,1,0:T(8,128)(2,1)S(1)} %dynamic-slice_select_fusion), channel_id=1, source_target_pairs={{0,48},{1,193},{2,50},{3,195},{4,52},{5,197},{6,54},{7,199},{8,56}... | collective-permute-start | bytes 737288 | tf_op jit(solution)/shard_map/ppermute | solution.py:60
  41.5 9.6 %collective-permute-start.10 = (bf16[8,40,384]{2,1,0:T(8,128)(2,1)S(1)}, bf16[8,40,384]{2,1,0:T(8,128)(2,1)S(1)}, u32[]{:S(2)}, u32[]{:S(2)}) collective-permute-start(bf16[8,40,384]{2,1,0:T(8,128)(2,1)S(1)} %dynamic-slice_select_fusion), channel_id=1, source_target_pairs={{0,32},{1,129},{2,34},{3,131},{4,36},{5,133},{6,38},{7,135},{8,40}... | collective-permute-start | bytes 737288 | tf_op jit(solution)/shard_map/ppermute | solution.py:60
  42.0 9.2 %collective-permute-start.11 = (bf16[8,40,384]{2,1,0:T(8,128)(2,1)S(1)}, bf16[8,40,384]{2,1,0:T(8,128)(2,1)S(1)}, u32[]{:S(2)}, u32[]{:S(2)}) collective-permute-start(bf16[8,40,384]{2,1,0:T(8,128)(2,1)S(1)} %dynamic-slice_select_fusion), channel_id=1, source_target_pairs={{0,16},{1,65},{2,18},{3,67},{4,20},{5,69},{6,22},{7,71},{8,24},{9,... | collective-permute-start | bytes 737288 | tf_op jit(solution)/shard_map/ppermute | solution.py:60
  51.6 18.3 %copy-start.4 = (f32[384]{0:T(512)S(1)}, f32[384]{0:T(512)}, u32[]{:S(2)}) copy-start(f32[384]{0:T(512)} %param.10) | copy-start | bytes 4612
  51.6 18.2 %copy-start.5 = (f32[384]{0:T(512)S(1)}, f32[384]{0:T(512)}, u32[]{:S(2)}) copy-start(f32[384]{0:T(512)} %param.11) | copy-start | bytes 4612
  51.7 15.1 %collective-permute-start.12 = (bf16[8,160,384]{2,1,0:T(8,128)(2,1)S(1)}, bf16[8,160,384]{2,1,0:T(8,128)(2,1)}, u32[]{:S(2)}, u32[]{:S(2)}) collective-permute-start(bf16[8,160,384]{2,1,0:T(8,128)(2,1)S(1)} %bitcast.42), channel_id=1, source_target_pairs={{0,64},{1,17},{2,66},{3,19},{4,68},{5,21},{6,70},{7,23},{8,72},{9,... | collective-permute-start | bytes 2949128 | tf_op jit(solution)/shard_map/ppermute | solution.py:60
  51.8 17.3 %collective-permute-start.13 = (bf16[8,160,384]{2,1,0:T(8,128)(2,1)S(1)}, bf16[8,160,384]{2,1,0:T(8,128)(2,1)}, u32[]{:S(2)}, u32[]{:S(2)}) collective-permute-start(bf16[8,160,384]{2,1,0:T(8,128)(2,1)S(1)} %bitcast.43), channel_id=1, source_target_pairs={{0,192},{1,49},{2,194},{3,51},{4,196},{5,53},{6,198},{7,55},{8,200... | collective-permute-start | bytes 2949128 | tf_op jit(solution)/shard_map/ppermute | solution.py:60
  55.0 15.0 %collective-permute-start.14 = (bf16[8,160,384]{2,1,0:T(8,128)(2,1)S(1)}, bf16[8,160,384]{2,1,0:T(8,128)(2,1)}, u32[]{:S(2)}, u32[]{:S(2)}) collective-permute-start(bf16[8,160,384]{2,1,0:T(8,128)(2,1)S(1)} %bitcast.44), channel_id=1, source_target_pairs={{0,1},{1,0},{2,3},{3,2},{4,5},{5,4},{6,7},{7,6},{8,9},{9,8},{10,11... | collective-permute-start | bytes 2949128 | tf_op jit(solution)/shard_map/ppermute | solution.py:60
  66.8 4.9 %collective-permute-start.15 = (bf16[8,160,384]{2,1,0:T(8,128)(2,1)}, bf16[8,160,384]{2,1,0:T(8,128)(2,1)}, u32[]{:S(2)}, u32[]{:S(2)}) collective-permute-start(bf16[8,160,384]{2,1,0:T(8,128)(2,1)} %collective-permute-done.12.refs_1_), channel_id=1, source_target_pairs={{0,1},{1,0},{2,3},{3,2},{4,5},{5,4},{6,7},{7,6},{8,9},{9,8},{10,11... | collective-permute-start | bytes 2949128 | tf_op jit(solution)/shard_map/ppermute | solution.py:60
  69.1 4.0 %collective-permute-start.16 = (bf16[8,160,384]{2,1,0:T(8,128)(2,1)}, bf16[8,160,384]{2,1,0:T(8,128)(2,1)}, u32[]{:S(2)}, u32[]{:S(2)}) collective-permute-start(bf16[8,160,384]{2,1,0:T(8,128)(2,1)} %collective-permute-done.13.refs_2_), channel_id=1, source_target_pairs={{0,1},{1,0},{2,3},{3,2},{4,5},{5,4},{6,7},{7,6},{8,9},{9,8},{10,11... | collective-permute-start | bytes 2949128 | tf_op jit(solution)/shard_map/ppermute | solution.py:60
  69.8 17.6 %collective-permute-start.18 = (bf16[8,160,384]{2,1,0:T(8,128)(2,1)S(1)}, bf16[8,160,384]{2,1,0:T(8,128)(2,1)S(1)}, u32[]{:S(2)}, u32[]{:S(2)}) collective-permute-start(bf16[8,160,384]{2,1,0:T(8,128)(2,1)S(1)} %bitcast.45), channel_id=1, source_target_pairs={{0,128},{1,33},{2,130},{3,35},{4,132},{5,37},{6,134},{7,39},{8,136... | collective-permute-start | bytes 2949128 | tf_op jit(solution)/shard_map/ppermute | solution.py:60
  77.3 12.8 %copy-start = (bf16[4,3,48,384]{3,2,1,0:T(8,128)(2,1)S(1)}, bf16[4,3,48,384]{3,2,1,0:T(8,128)(2,1)}, u32[]{:S(2)}) copy-start(bf16[4,3,48,384]{3,2,1,0:T(8,128)(2,1)} %param.7) | copy-start | bytes 1327108
  87.4 2.7 %collective-permute-start.19 = (bf16[8,160,384]{2,1,0:T(8,128)(2,1)S(1)}, bf16[8,160,384]{2,1,0:T(8,128)(2,1)S(1)}, u32[]{:S(2)}, u32[]{:S(2)}) collective-permute-start(bf16[8,160,384]{2,1,0:T(8,128)(2,1)S(1)} %collective-permute-done.18.far), channel_id=1, source_target_pairs={{0,1},{1,0},{2,3},{3,2},{4,5},{5,4},{6,7},{7,6},{8,9},{9,8},{10,11... | collective-permute-start | bytes 2949128 | tf_op jit(solution)/shard_map/ppermute | solution.py:60
  87.8 7.2 %collective-permute-start.17 = (bf16[2,5,48,384]{3,2,1,0:T(8,128)(2,1)S(1)}, bf16[2,5,48,384]{3,2,1,0:T(8,128)(2,1)S(1)}, u32[]{:S(2)}, u32[]{:S(2)}) collective-permute-start(bf16[2,5,48,384]{3,2,1,0:T(8,128)(2,1)S(1)} %get-tuple-element.20.high), channel_id=1, source_target_pairs={{0,1},{1,2},{2,3},{3,4},{4,5},{5,6},{6,7},{7,8},{8,9},{9,10},{10,1... | collective-permute-start | bytes 1105928 | tf_op jit(solution)/shard_map/ppermute | solution.py:60
  (4 other events, 25.3 us)
Sparse Core Ops, SparseCore 0:
  9.1 62.5 all-gather.1

commit v10 on v9

--- a/solution.py
+++ b/solution.py
@@ -173,7 +173,7 @@
         in_specs=[SMEM, SMEM] + [VMEM] * 4 + [ANY] * len(pieces),
         out_specs=[VMEM] * 3,
         scratch_shapes=[pltpu.VMEM((960, 3 * C), F32), pltpu.SemaphoreType.DMA((len(pieces),))],
-        compiler_params=pltpu.CompilerParams(vmem_limit_bytes=30 * 2**20),
+        compiler_params=pltpu.CompilerParams(vmem_limit_bytes=38 * 2**20),
         cost_estimate=cost(960),
         name="conv_first",
     )(tile, where, grown, weight, bias, gain, *pieces)

time: 106 us -> 106 us (level)
  local copies, waits for them, and re-layouts: 5.95 us -> 2.69 us
  Pallas kernels: 18.6 us -> 21.4 us
    unnamed x30 -> x28, local copies, waits for them, and re-layouts: 4.73 us -> 1.47 us
    pallas_call x1, Pallas kernels: 10.1 us -> 12.9 us  [conv_first(): pl.pallas_call(first_kernel, out_shape=[half, half, jax.ShapeDtypeStruct(...]
  transfers between devices with their start and end apart: 21 -> 21, of which waited for: 8 -> 8; matrix products, arithmetic and copies ran while one was open for 5% -> 5% of each run, Pallas kernels for 14% -> 17%
where the time goes in v10:
time: 106 us; the launch traced here: 105 us
  starting transfers between devices  38 us (36%)
  waiting for transfers between devices  25.8 us (24%)
  Pallas kernels  21.4 us (20%)
  between operations  13.9 us (13%)
  other arithmetic  3.21 us (3%)
  local copies, waits for them, and re-layouts  2.69 us (3%)
    ppermute x20, starting transfers between devices, send(): return lax.ppermute(value, AXES, pairs)  38 us
    ppermute x20, waiting for transfers between devices, send(): return lax.ppermute(value, AXES, pairs)  25.1 us
    pallas_call x1, Pallas kernels, conv_first(): pl.pallas_call(first_kernel, out_shape=[half, half, jax.ShapeDtypeStruct(...  12.9 us
    pallas_call x1, Pallas kernels, conv_late(): pl.pallas_call(late_kernel, out_shape=[jax.ShapeDtypeStruct((576, C), BF)...  4.94 us
    pallas_call x1, Pallas kernels, conv_early(): pl.pallas_call(early_kernel, out_shape=jax.ShapeDtypeStruct((576, C), BF)...  3.56 us
  transfers between devices with their start and end apart: 21, of which 8 were waited for; matrix products, arithmetic and copies ran while one was open for 5% of the time, Pallas kernels for 17%

profile of v10, /device:TPU:1, one launch (start us, length us, event | category | flops | bytes accessed | tf_op | source)
XLA Modules:
  0.0 104.9 jit_solution(6301595090535092046)
XLA Ops:
  7.3 3.3 %collective-permute-start.1 = (bf16[9,72,384]{2,1,0:T(8,128)(2,1)}, bf16[9,72,384]{2,1,0:T(8,128)(2,1)S(1)}, u32[]{:S(2)}, u32[]{:S(2)}) collective-permute-start(bf16[9,72,384]{2,1,0:T(8,128)(2,1)} %bitcast.58), channel_id=1, source_target_pairs={{0,1},{1,0},{2,3},{3,2},{4,5},{5,4},{6,7},{7,6},{8,9},{9,8},{10,11... | collective-permute-start | bytes 1493000 | tf_op jit(solution)/shard_map/ppermute | solution.py:60
  10.6 1.2 %fusion = f32[4,3,48]{2,1,0:T(4,128)S(1)} fusion(bf16[4,3,48,384]{3,2,1,0:T(8,128)(2,1)} %param.7), kind=kLoop, calls=%fused_computation.4 | loop fusion | flops 662976 | bytes 444672 | tf_op jit(solution)/shard_map/reduce_sum | solution.py:65
  11.8 1.4 %fusion.7 = bf16[4,3,48,384]{3,2,1,0:T(8,128)(2,1)S(1)} fusion(bf16[4,3,48,384]{3,2,1,0:T(8,128)(2,1)} %param.7, f32[384]{0:T(512)} %param.8, f32[4,3,48]{2,1,0:T(4,128)S(1)} %add_rsqrt_fusion), kind=kLoop, calls=%fused_computation.11 | loop fusion | flops 1769472 | bytes 888576 | tf_op jit(solution)/shard_map/convert_element_type | solution.py:263
  13.2 1.9 %collective-permute-start = (bf16[2,3,48,384]{3,2,1,0:T(8,128)(2,1)S(1)}, bf16[2,3,48,384]{3,2,1,0:T(8,128)(2,1)S(1)}, u32[]{:S(2)}, u32[]{:S(2)}) collective-permute-start(bf16[2,3,48,384]{3,2,1,0:T(8,128)(2,1)S(1)} %slice.45), channel_id=1, source_target_pairs={{0,1},{1,2},{2,3},{3,4},{4,5},{5,6},{6,7},{7,8},{8,9},{9,10},{10,1... | collective-permute-start | bytes 663560 | tf_op jit(solution)/shard_map/ppermute | solution.py:60
  15.5 5.4 %collective-permute-start.6 = (bf16[96,384]{1,0:T(8,128)(2,1)S(1)}, bf16[96,384]{1,0:T(8,128)(2,1)S(1)}, u32[]{:S(2)}, u32[]{:S(2)}) collective-permute-start(bf16[96,384]{1,0:T(8,128)(2,1)S(1)} %pad_maximum_fusion.3), channel_id=1, source_target_pairs={{0,6},{1,11},{2,8},{3,13},{4,10},{5,15},{6,12},{7,1},{8,14},{9,3},... | collective-permute-start | bytes 221192 | tf_op jit(solution)/shard_map/ppermute | solution.py:60
  20.9 2.4 %collective-permute-start.5 = (bf16[96,384]{1,0:T(8,128)(2,1)S(1)}, bf16[96,384]{1,0:T(8,128)(2,1)S(1)}, u32[]{:S(2)}, u32[]{:S(2)}) collective-permute-start(bf16[96,384]{1,0:T(8,128)(2,1)S(1)} %pad_maximum_fusion.3), channel_id=1, source_target_pairs={{0,4},{1,13},{2,6},{3,15},{4,8},{5,1},{6,10},{7,3},{8,12},{9,5},{1... | collective-permute-start | bytes 221192 | tf_op jit(solution)/shard_map/ppermute | solution.py:60
  23.4 2.9 %collective-permute-start.8 = (bf16[96,384]{1,0:T(8,128)(2,1)S(1)}, bf16[96,384]{1,0:T(8,128)(2,1)S(1)}, u32[]{:S(2)}, u32[]{:S(2)}) collective-permute-start(bf16[96,384]{1,0:T(8,128)(2,1)S(1)} %pad_maximum_fusion.3), channel_id=1, source_target_pairs={{0,8},{1,9},{2,10},{3,11},{4,12},{5,13},{6,14},{7,15},{8,0},{9,1},... | collective-permute-start | bytes 221192 | tf_op jit(solution)/shard_map/ppermute | solution.py:60
  26.3 3.7 %collective-permute-done.4 = bf16[96,384]{1,0:T(8,128)(2,1)S(1)} collective-permute-done((bf16[96,384]{1,0:T(8,128)(2,1)S(1)}, bf16[96,384]{1,0:T(8,128)(2,1)S(1)}, u32[]{:S(2)}, u32[]{:S(2)}) %collective-permute-start.4) | collective-permute-done | bytes 73760 | tf_op jit(solution)/shard_map/ppermute | solution.py:60
  30.3 3.1 %collective-permute-start.2 = (bf16[6,2,48,384]{3,2,1,0:T(8,128)(2,1)S(1)}, bf16[6,2,48,384]{3,2,1,0:T(8,128)(2,1)S(1)}, u32[]{:S(2)}, u32[]{:S(2)}) collective-permute-start(bf16[6,2,48,384]{3,2,1,0:T(8,128)(2,1)S(1)} %get-tuple-element.32), channel_id=1, source_target_pairs={{0,16},{1,17},{2,18},{3,19},{4,20},{5,21},{6,22},{7,23},{8,24},{9,... | collective-permute-start | bytes 1327112 | tf_op jit(solution)/shard_map/ppermute | solution.py:60
  33.4 1.3 %collective-permute-start.3 = (bf16[6,2,48,384]{3,2,1,0:T(8,128)(2,1)S(1)}, bf16[6,2,48,384]{3,2,1,0:T(8,128)(2,1)S(1)}, u32[]{:S(2)}, u32[]{:S(2)}) collective-permute-start(bf16[6,2,48,384]{3,2,1,0:T(8,128)(2,1)S(1)} %get-tuple-element.31), channel_id=1, source_target_pairs={{16,0},{17,1},{18,2},{19,3},{20,4},{21,5},{22,6},{23,7},{24,8},{25... | collective-permute-start | bytes 1327112 | tf_op jit(solution)/shard_map/ppermute | solution.py:60
  35.9 5.6 %collective-permute-start.9 = (bf16[8,40,384]{2,1,0:T(8,128)(2,1)S(1)}, bf16[8,40,384]{2,1,0:T(8,128)(2,1)S(1)}, u32[]{:S(2)}, u32[]{:S(2)}) collective-permute-start(bf16[8,40,384]{2,1,0:T(8,128)(2,1)S(1)} %dynamic-slice_select_fusion), channel_id=1, source_target_pairs={{0,48},{1,193},{2,50},{3,195},{4,52},{5,197},{6,54},{7,199},{8,56}... | collective-permute-start | bytes 737288 | tf_op jit(solution)/shard_map/ppermute | solution.py:60
  42.9 3.5 %collective-permute-done.3 = bf16[6,2,48,384]{3,2,1,0:T(8,128)(2,1)S(1)} collective-permute-done((bf16[6,2,48,384]{3,2,1,0:T(8,128)(2,1)S(1)}, bf16[6,2,48,384]{3,2,1,0:T(8,128)(2,1)S(1)}, u32[]{:S(2)}, u32[]{:S(2)}) %collective-permute-start.3) | collective-permute-done | bytes 442400 | tf_op jit(solution)/shard_map/ppermute | solution.py:60
  47.4 3.8 %collective-permute-done.10 = bf16[8,40,384]{2,1,0:T(8,128)(2,1)S(1)} collective-permute-done((bf16[8,40,384]{2,1,0:T(8,128)(2,1)S(1)}, bf16[8,40,384]{2,1,0:T(8,128)(2,1)S(1)}, u32[]{:S(2)}, u32[]{:S(2)}) %collective-permute-start.10) | collective-permute-done | bytes 245792 | tf_op jit(solution)/shard_map/ppermute | solution.py:60
  51.8 3.2 %collective-permute-start.13 = (bf16[8,160,384]{2,1,0:T(8,128)(2,1)S(1)}, bf16[8,160,384]{2,1,0:T(8,128)(2,1)}, u32[]{:S(2)}, u32[]{:S(2)}) collective-permute-start(bf16[8,160,384]{2,1,0:T(8,128)(2,1)S(1)} %bitcast.43), channel_id=1, source_target_pairs={{0,192},{1,49},{2,194},{3,51},{4,196},{5,53},{6,198},{7,55},{8,200... | collective-permute-start | bytes 2949128 | tf_op jit(solution)/shard_map/ppermute | solution.py:60
  55.0 2.1 %collective-permute-start.14 = (bf16[8,160,384]{2,1,0:T(8,128)(2,1)S(1)}, bf16[8,160,384]{2,1,0:T(8,128)(2,1)}, u32[]{:S(2)}, u32[]{:S(2)}) collective-permute-start(bf16[8,160,384]{2,1,0:T(8,128)(2,1)S(1)} %bitcast.44), channel_id=1, source_target_pairs={{0,1},{1,0},{2,3},{3,2},{4,5},{5,4},{6,7},{7,6},{8,9},{9,8},{10,11... | collective-permute-start | bytes 2949128 | tf_op jit(solution)/shard_map/ppermute | solution.py:60
  57.0 9.7 %collective-permute-done.12.refs_1_ = bf16[8,160,384]{2,1,0:T(8,128)(2,1)} collective-permute-done((bf16[8,160,384]{2,1,0:T(8,128)(2,1)S(1)}, bf16[8,160,384]{2,1,0:T(8,128)(2,1)}, u32[]{:S(2)}, u32[]{:S(2)}) %collective-permute-start.12) | collective-permute-done | bytes 983072 | tf_op jit(solution)/shard_map/ppermute | solution.py:60
  66.8 2.4 %collective-permute-start.15 = (bf16[8,160,384]{2,1,0:T(8,128)(2,1)}, bf16[8,160,384]{2,1,0:T(8,128)(2,1)}, u32[]{:S(2)}, u32[]{:S(2)}) collective-permute-start(bf16[8,160,384]{2,1,0:T(8,128)(2,1)} %collective-permute-done.12.refs_1_), channel_id=1, source_target_pairs={{0,1},{1,0},{2,3},{3,2},{4,5},{5,4},{6,7},{7,6},{8,9},{9,8},{10,11... | collective-permute-start | bytes 2949128 | tf_op jit(solution)/shard_map/ppermute | solution.py:60
  70.0 1.7 %collective-permute-done.15.refs_4_ = bf16[8,160,384]{2,1,0:T(8,128)(2,1)} collective-permute-done((bf16[8,160,384]{2,1,0:T(8,128)(2,1)}, bf16[8,160,384]{2,1,0:T(8,128)(2,1)}, u32[]{:S(2)}, u32[]{:S(2)}) %collective-permute-start.15) | collective-permute-done | bytes 983072 | tf_op jit(solution)/shard_map/ppermute | solution.py:60
  71.7 1.4 %collective-permute-done.16.refs_5_ = bf16[8,160,384]{2,1,0:T(8,128)(2,1)} collective-permute-done((bf16[8,160,384]{2,1,0:T(8,128)(2,1)}, bf16[8,160,384]{2,1,0:T(8,128)(2,1)}, u32[]{:S(2)}, u32[]{:S(2)}) %collective-permute-start.16) | collective-permute-done | bytes 983072 | tf_op jit(solution)/shard_map/ppermute | solution.py:60
  73.1 0.9 copy-done.1
  74.0 12.9 %conv_first.1 = (bf16[2,5,48,384]{3,2,1,0:T(8,128)(2,1)S(1)}, bf16[2,5,48,384]{3,2,1,0:T(8,128)(2,1)S(1)}, bf16[8,1296,384]{2,1,0:T(8,128)(2,1)S(1)}) custom-call(s32[1]{0:T(128)} %bitcast.tile, s32[8]{0:T(128)S(1)} %stack.78.where, bf16[6,7,48,384]{3,2,1,0:T(8,128)(2,1)S(1)} %constant_dynamic-update-slice_fusion.grown, bf16[9,1152,384]{2,1,0:T(8,128)(2,1)} %bitcast.59, ...), custom_call_target="tpu_custom_call" | custom-call | flops 7644119040 | bytes 7962624 | tf_op jit(solution)/shard_map/conv_first/pallas_call | solution.py:170
  87.3 2.0 %collective-permute-start.17 = (bf16[2,5,48,384]{3,2,1,0:T(8,128)(2,1)S(1)}, bf16[2,5,48,384]{3,2,1,0:T(8,128)(2,1)S(1)}, u32[]{:S(2)}, u32[]{:S(2)}) collective-permute-start(bf16[2,5,48,384]{3,2,1,0:T(8,128)(2,1)S(1)} %get-tuple-element.20.high), channel_id=1, source_target_pairs={{0,1},{1,2},{2,3},{3,4},{4,5},{5,6},{6,7},{7,8},{8,9},{9,10},{10,1... | collective-permute-start | bytes 1105928 | tf_op jit(solution)/shard_map/ppermute | solution.py:60
  89.6 4.9 %second_late.1 = (bf16[576,384]{1,0:T(8,128)(2,1)}, bf16[8,1296,384]{2,1,0:T(8,128)(2,1)S(1)}) custom-call(s32[8]{0:T(128)S(1)} %stack.78.where, bf16[2,5,48,384]{3,2,1,0:T(8,128)(2,1)S(1)} %get-tuple-element.21.low.high, bf16[2,5,48,384]{3,2,1,0:T(8,128)(2,1)S(1)} %get-tuple-element.20.high, bf16[576,384]{1,0:T(8,128)(2,1)S(1)} %bitcast.40, ...), custom_call_target="tpu_custom_call" | custom-call | flops 2293235712 | bytes 7962624 | tf_op jit(solution)/shard_map/second_late/pallas_call | solution.py:217
  94.5 3.6 %second_early.1 = bf16[576,384]{1,0:T(8,128)(2,1)} custom-call(bf16[2,5,48,384]{3,2,1,0:T(8,128)(2,1)S(1)} %collective-permute-done.17.low, bf16[2,5,48,384]{3,2,1,0:T(8,128)(2,1)S(1)} %get-tuple-element.21.low.high, bf16[576,384]{1,0:T(8,128)(2,1)S(1)} %bitcast.41, f32[1,384]{1,0:T(1,128)S(1)} %reshape.47.bias, ...), custom_call_target="tpu_custom_call", output_to_operand_aliasing={{}: (5, {})} | custom-call | flops 2293235712 | bytes 7962624 | tf_op jit(solution)/shard_map/second_early/pallas_call | solution.py:230
  (77 shorter events, 6.7 us)
Async XLA Ops:
  6.5 66.6 %all-gather.2.cloned.1.call-start = ((), (), s32[]{:S(2)}) async-start(), calls=%async_computation | async-start | bytes 8460288 | tf_op jit(solution)/shard_map/all_gather | solution.py:262
  7.3 7.9 %collective-permute-start.1 = (bf16[9,72,384]{2,1,0:T(8,128)(2,1)}, bf16[9,72,384]{2,1,0:T(8,128)(2,1)S(1)}, u32[]{:S(2)}, u32[]{:S(2)}) collective-permute-start(bf16[9,72,384]{2,1,0:T(8,128)(2,1)} %bitcast.58), channel_id=1, source_target_pairs={{0,1},{1,0},{2,3},{3,2},{4,5},{5,4},{6,7},{7,6},{8,9},{9,8},{10,11... | collective-permute-start | bytes 1493000 | tf_op jit(solution)/shard_map/ppermute | solution.py:60
  13.2 10.1 %collective-permute-start = (bf16[2,3,48,384]{3,2,1,0:T(8,128)(2,1)S(1)}, bf16[2,3,48,384]{3,2,1,0:T(8,128)(2,1)S(1)}, u32[]{:S(2)}, u32[]{:S(2)}) collective-permute-start(bf16[2,3,48,384]{3,2,1,0:T(8,128)(2,1)S(1)} %slice.45), channel_id=1, source_target_pairs={{0,1},{1,2},{2,3},{3,4},{4,5},{5,6},{6,7},{7,8},{8,9},{9,10},{10,1... | collective-permute-start | bytes 663560 | tf_op jit(solution)/shard_map/ppermute | solution.py:60
  15.5 10.8 %collective-permute-start.6 = (bf16[96,384]{1,0:T(8,128)(2,1)S(1)}, bf16[96,384]{1,0:T(8,128)(2,1)S(1)}, u32[]{:S(2)}, u32[]{:S(2)}) collective-permute-start(bf16[96,384]{1,0:T(8,128)(2,1)S(1)} %pad_maximum_fusion.3), channel_id=1, source_target_pairs={{0,6},{1,11},{2,8},{3,13},{4,10},{5,15},{6,12},{7,1},{8,14},{9,3},... | collective-permute-start | bytes 221192 | tf_op jit(solution)/shard_map/ppermute | solution.py:60
  20.9 5.4 %collective-permute-start.5 = (bf16[96,384]{1,0:T(8,128)(2,1)S(1)}, bf16[96,384]{1,0:T(8,128)(2,1)S(1)}, u32[]{:S(2)}, u32[]{:S(2)}) collective-permute-start(bf16[96,384]{1,0:T(8,128)(2,1)S(1)} %pad_maximum_fusion.3), channel_id=1, source_target_pairs={{0,4},{1,13},{2,6},{3,15},{4,8},{5,1},{6,10},{7,3},{8,12},{9,5},{1... | collective-permute-start | bytes 221192 | tf_op jit(solution)/shard_map/ppermute | solution.py:60
  23.3 6.7 %collective-permute-start.4 = (bf16[96,384]{1,0:T(8,128)(2,1)S(1)}, bf16[96,384]{1,0:T(8,128)(2,1)S(1)}, u32[]{:S(2)}, u32[]{:S(2)}) collective-permute-start(bf16[96,384]{1,0:T(8,128)(2,1)S(1)} %pad_maximum_fusion.3), channel_id=1, source_target_pairs={{0,2},{1,15},{2,4},{3,1},{4,6},{5,3},{6,8},{7,5},{8,10},{9,7},{10,... | collective-permute-start | bytes 221192 | tf_op jit(solution)/shard_map/ppermute | solution.py:60
  23.4 11.5 %collective-permute-start.8 = (bf16[96,384]{1,0:T(8,128)(2,1)S(1)}, bf16[96,384]{1,0:T(8,128)(2,1)S(1)}, u32[]{:S(2)}, u32[]{:S(2)}) collective-permute-start(bf16[96,384]{1,0:T(8,128)(2,1)S(1)} %pad_maximum_fusion.3), channel_id=1, source_target_pairs={{0,8},{1,9},{2,10},{3,11},{4,12},{5,13},{6,14},{7,15},{8,0},{9,1},... | collective-permute-start | bytes 221192 | tf_op jit(solution)/shard_map/ppermute | solution.py:60
  30.1 4.7 %collective-permute-start.7 = (bf16[3,96,384]{2,1,0:T(8,128)(2,1)S(1)}, bf16[3,96,384]{2,1,0:T(8,128)(2,1)S(1)}, u32[]{:S(2)}, u32[]{:S(2)}) collective-permute-start(bf16[3,96,384]{2,1,0:T(8,128)(2,1)S(1)} %pad_maximum_fusion.2), channel_id=1, source_target_pairs={{0,1},{1,0},{2,3},{3,2},{4,5},{5,4},{6,7},{7,6},{8,9},{9,8},{10,11... | collective-permute-start | bytes 663560 | tf_op jit(solution)/shard_map/ppermute | solution.py:60
  30.3 12.4 %collective-permute-start.2 = (bf16[6,2,48,384]{3,2,1,0:T(8,128)(2,1)S(1)}, bf16[6,2,48,384]{3,2,1,0:T(8,128)(2,1)S(1)}, u32[]{:S(2)}, u32[]{:S(2)}) collective-permute-start(bf16[6,2,48,384]{3,2,1,0:T(8,128)(2,1)S(1)} %get-tuple-element.32), channel_id=1, source_target_pairs={{0,16},{1,17},{2,18},{3,19},{4,20},{5,21},{6,22},{7,23},{8,24},{9,... | collective-permute-start | bytes 1327112 | tf_op jit(solution)/shard_map/ppermute | solution.py:60
  33.4 12.9 %collective-permute-start.3 = (bf16[6,2,48,384]{3,2,1,0:T(8,128)(2,1)S(1)}, bf16[6,2,48,384]{3,2,1,0:T(8,128)(2,1)S(1)}, u32[]{:S(2)}, u32[]{:S(2)}) collective-permute-start(bf16[6,2,48,384]{3,2,1,0:T(8,128)(2,1)S(1)} %get-tuple-element.31), channel_id=1, source_target_pairs={{16,0},{17,1},{18,2},{19,3},{20,4},{21,5},{22,6},{23,7},{24,8},{25... | collective-permute-start | bytes 1327112 | tf_op jit(solution)/shard_map/ppermute | solution.py:60
  35.9 11.4 %collective-permute-start.9 = (bf16[8,40,384]{2,1,0:T(8,128)(2,1)S(1)}, bf16[8,40,384]{2,1,0:T(8,128)(2,1)S(1)}, u32[]{:S(2)}, u32[]{:S(2)}) collective-permute-start(bf16[8,40,384]{2,1,0:T(8,128)(2,1)S(1)} %dynamic-slice_select_fusion), channel_id=1, source_target_pairs={{0,48},{1,193},{2,50},{3,195},{4,52},{5,197},{6,54},{7,199},{8,56}... | collective-permute-start | bytes 737288 | tf_op jit(solution)/shard_map/ppermute | solution.py:60
  41.5 9.6 %collective-permute-start.10 = (bf16[8,40,384]{2,1,0:T(8,128)(2,1)S(1)}, bf16[8,40,384]{2,1,0:T(8,128)(2,1)S(1)}, u32[]{:S(2)}, u32[]{:S(2)}) collective-permute-start(bf16[8,40,384]{2,1,0:T(8,128)(2,1)S(1)} %dynamic-slice_select_fusion), channel_id=1, source_target_pairs={{0,32},{1,129},{2,34},{3,131},{4,36},{5,133},{6,38},{7,135},{8,40}... | collective-permute-start | bytes 737288 | tf_op jit(solution)/shard_map/ppermute | solution.py:60
  42.0 9.2 %collective-permute-start.11 = (bf16[8,40,384]{2,1,0:T(8,128)(2,1)S(1)}, bf16[8,40,384]{2,1,0:T(8,128)(2,1)S(1)}, u32[]{:S(2)}, u32[]{:S(2)}) collective-permute-start(bf16[8,40,384]{2,1,0:T(8,128)(2,1)S(1)} %dynamic-slice_select_fusion), channel_id=1, source_target_pairs={{0,16},{1,65},{2,18},{3,67},{4,20},{5,69},{6,22},{7,71},{8,24},{9,... | collective-permute-start | bytes 737288 | tf_op jit(solution)/shard_map/ppermute | solution.py:60
  51.6 18.3 %copy-start.3 = (f32[384]{0:T(512)S(1)}, f32[384]{0:T(512)}, u32[]{:S(2)}) copy-start(f32[384]{0:T(512)} %param.10) | copy-start | bytes 4612
  51.6 18.2 %copy-start.4 = (f32[384]{0:T(512)S(1)}, f32[384]{0:T(512)}, u32[]{:S(2)}) copy-start(f32[384]{0:T(512)} %param.11) | copy-start | bytes 4612
  51.7 15.1 %collective-permute-start.12 = (bf16[8,160,384]{2,1,0:T(8,128)(2,1)S(1)}, bf16[8,160,384]{2,1,0:T(8,128)(2,1)}, u32[]{:S(2)}, u32[]{:S(2)}) collective-permute-start(bf16[8,160,384]{2,1,0:T(8,128)(2,1)S(1)} %bitcast.42), channel_id=1, source_target_pairs={{0,64},{1,17},{2,66},{3,19},{4,68},{5,21},{6,70},{7,23},{8,72},{9,... | collective-permute-start | bytes 2949128 | tf_op jit(solution)/shard_map/ppermute | solution.py:60
  51.8 17.3 %collective-permute-start.13 = (bf16[8,160,384]{2,1,0:T(8,128)(2,1)S(1)}, bf16[8,160,384]{2,1,0:T(8,128)(2,1)}, u32[]{:S(2)}, u32[]{:S(2)}) collective-permute-start(bf16[8,160,384]{2,1,0:T(8,128)(2,1)S(1)} %bitcast.43), channel_id=1, source_target_pairs={{0,192},{1,49},{2,194},{3,51},{4,196},{5,53},{6,198},{7,55},{8,200... | collective-permute-start | bytes 2949128 | tf_op jit(solution)/shard_map/ppermute | solution.py:60
  55.0 15.0 %collective-permute-start.14 = (bf16[8,160,384]{2,1,0:T(8,128)(2,1)S(1)}, bf16[8,160,384]{2,1,0:T(8,128)(2,1)}, u32[]{:S(2)}, u32[]{:S(2)}) collective-permute-start(bf16[8,160,384]{2,1,0:T(8,128)(2,1)S(1)} %bitcast.44), channel_id=1, source_target_pairs={{0,1},{1,0},{2,3},{3,2},{4,5},{5,4},{6,7},{7,6},{8,9},{9,8},{10,11... | collective-permute-start | bytes 2949128 | tf_op jit(solution)/shard_map/ppermute | solution.py:60
  66.8 4.9 %collective-permute-start.15 = (bf16[8,160,384]{2,1,0:T(8,128)(2,1)}, bf16[8,160,384]{2,1,0:T(8,128)(2,1)}, u32[]{:S(2)}, u32[]{:S(2)}) collective-permute-start(bf16[8,160,384]{2,1,0:T(8,128)(2,1)} %collective-permute-done.12.refs_1_), channel_id=1, source_target_pairs={{0,1},{1,0},{2,3},{3,2},{4,5},{5,4},{6,7},{7,6},{8,9},{9,8},{10,11... | collective-permute-start | bytes 2949128 | tf_op jit(solution)/shard_map/ppermute | solution.py:60
  69.1 4.0 %collective-permute-start.16 = (bf16[8,160,384]{2,1,0:T(8,128)(2,1)}, bf16[8,160,384]{2,1,0:T(8,128)(2,1)}, u32[]{:S(2)}, u32[]{:S(2)}) collective-permute-start(bf16[8,160,384]{2,1,0:T(8,128)(2,1)} %collective-permute-done.13.refs_2_), channel_id=1, source_target_pairs={{0,1},{1,0},{2,3},{3,2},{4,5},{5,4},{6,7},{7,6},{8,9},{9,8},{10,11... | collective-permute-start | bytes 2949128 | tf_op jit(solution)/shard_map/ppermute | solution.py:60
  69.8 17.1 %collective-permute-start.18 = (bf16[8,160,384]{2,1,0:T(8,128)(2,1)S(1)}, bf16[8,160,384]{2,1,0:T(8,128)(2,1)S(1)}, u32[]{:S(2)}, u32[]{:S(2)}) collective-permute-start(bf16[8,160,384]{2,1,0:T(8,128)(2,1)S(1)} %bitcast.45), channel_id=1, source_target_pairs={{0,128},{1,33},{2,130},{3,35},{4,132},{5,37},{6,134},{7,39},{8,136... | collective-permute-start | bytes 2949128 | tf_op jit(solution)/shard_map/ppermute | solution.py:60
  74.0 15.5 %copy-start = (bf16[4,3,48,384]{3,2,1,0:T(8,128)(2,1)S(1)}, bf16[4,3,48,384]{3,2,1,0:T(8,128)(2,1)}, u32[]{:S(2)}) copy-start(bf16[4,3,48,384]{3,2,1,0:T(8,128)(2,1)} %param.7) | copy-start | bytes 1327108
  86.9 2.7 %collective-permute-start.19 = (bf16[8,160,384]{2,1,0:T(8,128)(2,1)S(1)}, bf16[8,160,384]{2,1,0:T(8,128)(2,1)S(1)}, u32[]{:S(2)}, u32[]{:S(2)}) collective-permute-start(bf16[8,160,384]{2,1,0:T(8,128)(2,1)S(1)} %collective-permute-done.18.far), channel_id=1, source_target_pairs={{0,1},{1,0},{2,3},{3,2},{4,5},{5,4},{6,7},{7,6},{8,9},{9,8},{10,11... | collective-permute-start | bytes 2949128 | tf_op jit(solution)/shard_map/ppermute | solution.py:60
  87.3 7.2 %collective-permute-start.17 = (bf16[2,5,48,384]{3,2,1,0:T(8,128)(2,1)S(1)}, bf16[2,5,48,384]{3,2,1,0:T(8,128)(2,1)S(1)}, u32[]{:S(2)}, u32[]{:S(2)}) collective-permute-start(bf16[2,5,48,384]{3,2,1,0:T(8,128)(2,1)S(1)} %get-tuple-element.20.high), channel_id=1, source_target_pairs={{0,1},{1,2},{2,3},{3,4},{4,5},{5,6},{6,7},{7,8},{8,9},{9,10},{10,1... | collective-permute-start | bytes 1105928 | tf_op jit(solution)/shard_map/ppermute | solution.py:60
  (3 other events, 24.8 us)
Sparse Core Ops, SparseCore 0:
  9.1 62.5 all-gather.1
